TPU v7x, 32 devices: a whole 2x2x4 slice. The times are simulated.
32 devices in a mesh: dp: 8 (over y, x, core), expert: 4 (over z).
Axes of the slice: x: 2, y: 2, z: 4, core: 2. Of those that a mesh axis runs over, the one named last changes fastest.
Arguments:
- tokens: bfloat16 [4096, 2048], P(('dp', 'expert')), may hold values from -6 to 6
- cotangent: bfloat16 [4096, 2048], P(('dp', 'expert')), may hold values from -6 to 6
- route: int32 [4096, 1], P(('dp', 'expert')), may hold values from 0 to 3; in each aligned block of 128 rows (0 to 127, 128 to 255, ...) at most 48 rows name the same one
- prob: bfloat16 [4096], P(('dp', 'expert')), may hold values from 0.049804688 to 1
- w_gate: float32 [4, 2048, 512], P('expert'), may hold values from -0.125 to 0.125
- w_up: float32 [4, 2048, 512], P('expert'), may hold values from -0.125 to 0.125
- w_down: float32 [4, 2048, 512], P('expert'), may hold values from -0.25 to 0.25
Outputs:
- grad_input: bfloat16 [4096, 2048], P(('dp', 'expert'))
- grad_prob: bfloat16 [4096], P(('dp', 'expert'))
- grad_gate: float32 [4, 2048, 512], P('expert', 'dp')
- grad_up: float32 [4, 2048, 512], P('expert', 'dp')
- grad_down: float32 [4, 2048, 512], P('expert', 'dp')
Inputs may be any that keep to these rules, and one draw needn't show every extreme that they name: `route`: within each device's aligned block of 128 rows (devices in the order of dp, then expert) each hot expert is named by at most 48 rows, a bound that some block reaches.
All inputs are finite; a program needn't handle non-finite values.
Results may differ from a plain program's by a relative error of at most 0.003.
Values may be sent and summed in bfloat16 or wider, within the bound.
No kernel may reach another device: no remote copies, remote signals or barrier semaphores. Data moves between devices by JAX's collectives and lax.ppermute only.
A program may use at most 128 MiB of HBM per device.

v0:
```python
import math

import jax
import jax.numpy as jnp
from jax import lax
from jax.sharding import PartitionSpec as P

D = 2048
HOT = 4
CAP = 48


highest = lax.Precision.HIGHEST


def expert_rows(row_tokens, row_cotangents, row_probs, gate_weight, up_weight, down_weight):
    probs_f32 = row_probs.astype(jnp.float32)
    gate_pre = jnp.dot(
        row_tokens, gate_weight, precision=highest, preferred_element_type=jnp.float32
    )
    up_pre = jnp.dot(row_tokens, up_weight, precision=highest, preferred_element_type=jnp.float32)
    sigmoid_val = jax.nn.sigmoid(gate_pre)
    activation = gate_pre * sigmoid_val
    hidden = activation * up_pre
    backward = jnp.dot(
        row_cotangents, down_weight, precision=highest, preferred_element_type=jnp.float32
    )
    prob_part = jnp.sum(hidden * backward, axis=1)
    d_hidden = probs_f32[:, None] * backward
    d_up = d_hidden * activation
    d_gate = d_hidden * up_pre * sigmoid_val * (1.0 + gate_pre * (1.0 - sigmoid_val))
    input_part = jnp.dot(d_gate, gate_weight.T, precision=highest) + jnp.dot(
        d_up, up_weight.T, precision=highest
    )
    grad_g = jnp.dot(row_tokens.T, d_gate, precision=highest, preferred_element_type=jnp.float32)
    grad_u = jnp.dot(row_tokens.T, d_up, precision=highest, preferred_element_type=jnp.float32)
    scaled_cot = probs_f32[:, None] * row_cotangents
    grad_d = jnp.dot(scaled_cot.T, hidden, precision=highest)
    return (input_part, prob_part, grad_g, grad_u, grad_d)


def slot_positions(route_column):
    onehot = (route_column[:, None] == jnp.arange(HOT, dtype=jnp.int32)[None, :]).astype(jnp.int32)
    earlier = jnp.cumsum(onehot, axis=0) - onehot
    rank_in_expert = jnp.sum(earlier * onehot, axis=1)
    return route_column * CAP + rank_in_expert


def shards(tokens, cotangent, route, prob, w_gate, w_up, w_down):
    quarters = lax.axis_size("expert") // HOT
    position = slot_positions(route[:, 0])
    placing = (jnp.arange(HOT * CAP, dtype=jnp.int32)[:, None] == position[None, :]).astype(
        jnp.bfloat16
    )
    slot_tok = jnp.dot(placing, tokens, preferred_element_type=jnp.float32).astype(jnp.bfloat16)
    slot_cot = jnp.dot(placing, cotangent, preferred_element_type=jnp.float32).astype(jnp.bfloat16)
    slot_prob = jnp.zeros((HOT * CAP,), jnp.bfloat16).at[position].set(prob)
    gate_weight = w_gate[0]
    up_weight = w_up[0]
    down_weight = w_down[0]
    send_tok = jnp.repeat(slot_tok.reshape(HOT, CAP, D), quarters, axis=0)
    send_cot = jnp.repeat(slot_cot.reshape(HOT, CAP, D), quarters, axis=0)
    send_prob = jnp.repeat(slot_prob.reshape(HOT, CAP), quarters, axis=0)
    recv_tok, recv_cot, recv_prob = (
        lax.all_to_all(send_tok, "expert", split_axis=0, concat_axis=0, tiled=True),
        lax.all_to_all(send_cot, "expert", split_axis=0, concat_axis=0, tiled=True),
        lax.all_to_all(send_prob, "expert", split_axis=0, concat_axis=0, tiled=True),
    )
    sources = recv_tok.shape[0]
    input_part, prob_part, grad_g, grad_u, grad_d = expert_rows(
        recv_tok.reshape(sources * CAP, D),
        recv_cot.reshape(sources * CAP, D),
        recv_prob.reshape(sources * CAP),
        gate_weight,
        up_weight,
        down_weight,
    )
    back_input, back_prob = (
        lax.all_to_all(
            input_part.reshape(sources, CAP, D), "expert", split_axis=0, concat_axis=0, tiled=True
        ),
        lax.all_to_all(
            prob_part.reshape(sources, CAP), "expert", split_axis=0, concat_axis=0, tiled=True
        ),
    )
    summed_input = (
        jnp.sum(back_input.reshape(HOT, quarters, CAP, D), axis=1)
        .astype(jnp.bfloat16)
        .reshape(HOT * CAP, D)
    )
    summed_prob = (
        jnp.sum(back_prob.reshape(HOT, quarters, CAP), axis=1)
        .astype(jnp.bfloat16)
        .reshape(HOT * CAP)
    )
    grad_input = summed_input[position]
    grad_prob = summed_prob[position]
    stacked = jnp.stack([grad_g, grad_u, grad_d])
    reduced = lax.psum_scatter(stacked, "dp", scatter_dimension=1, tiled=True)
    token_total = tokens.shape[0] * lax.axis_size("dp") * lax.axis_size("expert")
    reduced = reduced * (1.0 / math.sqrt(token_total))
    return (grad_input, grad_prob, reduced[0][None], reduced[1][None], reduced[2][None])


def solution(mesh):
    placed = (
        P(("dp", "expert"), None),
        P(("dp", "expert"), None),
        P(("dp", "expert"), None),
        P(("dp", "expert")),
        P("expert", None, None),
        P("expert", None, None),
        P("expert", None, None),
    )
    return jax.shard_map(
        shards,
        mesh=mesh,
        in_specs=placed,
        out_specs=(
            P(("dp", "expert"), None),
            P(("dp", "expert")),
            P("expert", "dp", None),
            P("expert", "dp", None),
            P("expert", "dp", None),
        ),
        check_vma=False,
    )
```

profile of v0, /device:TPU:0, one launch (start us, length us, event | category | flops | bytes accessed | tf_op | source)
XLA Modules:
  0.0 186.4 jit_solution(2570992438444946133)
XLA Ops:
  9.7 1.5 scatter_custom_fusion
  11.8 6.3 %all-to-all-start = ((bf16[4,1,48]{2,1,0:T(2,128)(2,1)}), bf16[4,1,48]{2,1,0:T(2,128)(2,1)S(1)}, u32[]{:S(2)}, u32[]{:S(2)}) async-start(bf16[4,1,48]{2,1,0:T(2,128)(2,1)} %all_to_all.28), calls=%async_computation | async-start | bytes 4096 | tf_op jit(solution)/shard_map/all_to_all | solution.py:67
  20.0 3.6 %all-to-all-done = bf16[4,1,48]{2,1,0:T(2,128)(2,1)S(1)} async-done(((bf16[4,1,48]{2,1,0:T(2,128)(2,1)}), bf16[4,1,48]{2,1,0:T(2,128)(2,1)S(1)}, u32[]{:S(2)}, u32[]{:S(2)}) %all-to-all-start) | async-done | bytes 416 | tf_op jit(solution)/shard_map/all_to_all | solution.py:67
  23.6 3.5 %all-to-all-start.2 = ((bf16[4,48,2048]{2,1,0:T(8,128)(2,1)}), bf16[4,48,2048]{2,1,0:T(8,128)(2,1)S(1)}, u32[]{:S(2)}, u32[]{:S(2)}) async-start(bf16[4,48,2048]{2,1,0:T(8,128)(2,1)} %bitcast.6), calls=%async_computation.2 | async-start | bytes 1572864 | tf_op jit(solution)/shard_map/all_to_all | solution.py:65
  27.1 2.3 %convolution_convert_fusion.1 = bf16[192,2048]{1,0:T(8,128)(2,1)} fusion(bf16[128,2048]{1,0:T(8,128)(2,1)} %param.8, s32[128]{0:T(128)S(1)} %multiply_add_fusion), kind=kOutput, calls=%fused_computation.19 | convolution fusion | flops 101081088 | bytes 1311232 | tf_op jit(solution)/shard_map/dot_general | solution.py:56
  29.4 16.6 %all-to-all-done.2 = bf16[4,48,2048]{2,1,0:T(8,128)(2,1)S(1)} async-done(((bf16[4,48,2048]{2,1,0:T(8,128)(2,1)}), bf16[4,48,2048]{2,1,0:T(8,128)(2,1)S(1)}, u32[]{:S(2)}, u32[]{:S(2)}) %all-to-all-start.2) | async-done | bytes 786464 | tf_op jit(solution)/shard_map/all_to_all | solution.py:65
  46.0 3.5 %all-to-all-start.1 = ((bf16[4,48,2048]{2,1,0:T(8,128)(2,1)}), bf16[4,48,2048]{2,1,0:T(8,128)(2,1)S(1)}, u32[]{:S(2)}, u32[]{:S(2)}) async-start(bf16[4,48,2048]{2,1,0:T(8,128)(2,1)} %bitcast.3), calls=%async_computation.1 | async-start | bytes 1572864 | tf_op jit(solution)/shard_map/all_to_all | solution.py:66
  49.8 4.1 %fusion.2 = f32[192,512]{1,0:T(8,128)S(1)} fusion(bf16[192,2048]{1,0:T(8,128)(2,1)S(1)} %bitcast.48, f32[1,2048,512]{2,1,0:T(8,128)} %param.11), kind=kOutput, calls=%fused_computation.6 | convolution fusion | flops 2415919104 | bytes 5373952 | tf_op jit(solution)/shard_map/dot_general | solution.py:18
  54.0 1.9 %fusion.6 = f32[192,512]{1,0:T(8,128)S(1)} fusion(bf16[192,2048]{1,0:T(8,128)(2,1)S(1)} %bitcast.49, f32[1,2048,512]{2,1,0:T(8,128)S(1)} %copy-done.1), kind=kOutput, calls=%fused_computation.10 | convolution fusion | flops 2415919104 | bytes 5373952 | tf_op jit(solution)/shard_map/dot_general | solution.py:21
  55.9 13.2 %all-to-all-done.1 = bf16[4,48,2048]{2,1,0:T(8,128)(2,1)S(1)} async-done(((bf16[4,48,2048]{2,1,0:T(8,128)(2,1)}), bf16[4,48,2048]{2,1,0:T(8,128)(2,1)S(1)}, u32[]{:S(2)}, u32[]{:S(2)}) %all-to-all-start.1) | async-done | bytes 786464 | tf_op jit(solution)/shard_map/all_to_all | solution.py:66
  69.1 3.6 %convolution_bitcast_fusion = f32[1,2048,512]{2,1,0:T(8,128)S(1)} fusion(bf16[192,2048]{1,0:T(8,128)(2,1)S(1)} %bitcast.52, f32[192]{0:T(256)S(1)} %reshape.60, f32[192,512]{1,0:T(8,128)S(1)} %fusion.6, f32[192,512]{1,0:T(8,128)S(1)} %fusion.2), kind=kOutput, calls=%fused_computation.14 | convolution fusion | flops 2417197056 | bytes 5767936 | tf_op jit(solution)/shard_map/dot_general | solution.py:38
  72.7 3.1 %multiply_reduce_fusion = (bf16[192]{0:T(256)(128)(2,1)S(1)}, f32[192,512]{1,0:T(8,128)S(1)}, f32[192,512]{1,0:T(8,128)S(1)}) fusion(f32[192,512]{1,0:T(8,128)} %copy-done.4, f32[192,512]{1,0:T(8,128)S(1)} %fusion.2, f32[192]{0:T(256)S(1)} %reshape.60, bf16[192,2048]{1,0:T(8,128)(2,1)S(1)} %bitcast.53, f32[1,2048,512]{2,1,0:T(8,128)S(1)} %copy-done.3), kind=kOutput, calls=%fused_computation.24 | convolution fusion | flops 2417295104 | bytes 6554752 | tf_op jit(solution)/shard_map/dot_general | solution.py:25
  75.8 2.0 %convolution_bitcast_fusion.1 = f32[1,2048,512]{2,1,0:T(8,128)S(1)} fusion(bf16[192,2048]{1,0:T(8,128)(2,1)S(1)} %bitcast.50, f32[192,512]{1,0:T(8,128)S(1)} %get-tuple-element.10, f32[192]{0:T(256)S(1)} %reshape.60, f32[192,512]{1,0:T(8,128)S(1)} %fusion.2), kind=kOutput, calls=%fused_computation.15 | convolution fusion | flops 2416508928 | bytes 5767936 | tf_op jit(solution)/shard_map/dot_general | solution.py:36
  77.8 2.1 %convolution_bitcast_fusion.2 = f32[1,2048,512]{2,1,0:T(8,128)S(1)} fusion(bf16[192,2048]{1,0:T(8,128)(2,1)S(1)} %bitcast.51, f32[192,512]{1,0:T(8,128)S(1)} %get-tuple-element.9), kind=kOutput, calls=%fused_computation.16 | convolution fusion | flops 2415919104 | bytes 5373952 | tf_op jit(solution)/shard_map/dot_general | solution.py:35
  80.0 5.2 %pad_maximum_fusion = f32[3,2048,512]{2,1,0:T(8,128)} fusion(f32[1,2048,512]{2,1,0:T(8,128)S(1)} %convolution_bitcast_fusion, f32[1,2048,512]{2,1,0:T(8,128)S(1)} %convolution_bitcast_fusion.1, f32[1,2048,512]{2,1,0:T(8,128)S(1)} %convolution_bitcast_fusion.2), kind=kLoop, calls=%fused_computation.3 | loop fusion | flops 6291456 | bytes 25165824 | tf_op jit(solution)/shard_map/stack | solution.py:98
  85.8 3.2 %all-to-all-start.4 = ((bf16[4,1,48]{2,1,0:T(2,128)(2,1)}), bf16[4,1,48]{2,1,0:T(2,128)(2,1)S(1)}, u32[]{:S(2)}, u32[]{:S(2)}) async-start(bf16[4,1,48]{2,1,0:T(2,128)(2,1)} %all_to_all.26), calls=%async_computation.4 | async-start | bytes 4096 | tf_op jit(solution)/shard_map/all_to_all | solution.py:82
  89.1 7.0 %fusion = f32[192,2048]{1,0:T(8,128)S(1)} fusion(f32[192,512]{1,0:T(8,128)S(1)} %get-tuple-element.9, f32[1,2048,512]{2,1,0:T(8,128)} %param.11), kind=kOutput, calls=%fused_computation.4 | convolution fusion | flops 2415919104 | bytes 6160384 | tf_op jit(solution)/shard_map/dot_general | solution.py:32
  96.1 5.4 %fusion.10 = bf16[192,2048]{1,0:T(8,128)(2,1)} fusion(f32[192,2048]{1,0:T(8,128)S(1)} %fusion, f32[1,2048,512]{2,1,0:T(8,128)S(1)} %copy-done.2, f32[192,512]{1,0:T(8,128)S(1)} %get-tuple-element.10, f32[192]{0:T(256)S(1)} %reshape.60, f32[192,512]{1,0:T(8,128)S(1)} %fusion.2), kind=kOutput, calls=%fused_computation.17 | convolution fusion | flops 2417295360 | bytes 7340800 | tf_op jit(solution)/shard_map/dot_general | solution.py:32
  101.5 5.0 %all-to-all-start.3 = ((bf16[4,48,2048]{2,1,0:T(8,128)(2,1)}), bf16[4,48,2048]{2,1,0:T(8,128)(2,1)S(1)}, u32[]{:S(2)}, u32[]{:S(2)}) async-start(bf16[4,48,2048]{2,1,0:T(8,128)(2,1)} %bitcast.10), calls=%async_computation.3 | async-start | bytes 1572864 | tf_op jit(solution)/shard_map/all_to_all | solution.py:79
  106.6 1.7 gather_fusion.1
  108.4 16.6 %all-to-all-done.3 = bf16[4,48,2048]{2,1,0:T(8,128)(2,1)S(1)} async-done(((bf16[4,48,2048]{2,1,0:T(8,128)(2,1)}), bf16[4,48,2048]{2,1,0:T(8,128)(2,1)S(1)}, u32[]{:S(2)}, u32[]{:S(2)}) %all-to-all-start.3) | async-done | bytes 786464 | tf_op jit(solution)/shard_map/all_to_all | solution.py:79
  124.9 1.7 gather_fusion
  126.7 50.2 %reduce-scatter.2.cloned.1.call-done = f32[3,256,512]{2,1,0:T(8,128)} async-done(((f32[3,2048,512]{2,1,0:T(8,128)}), f32[3,256,512]{2,1,0:T(8,128)}) %reduce-scatter.2.cloned.1.call-update) | async-done | bytes 1572880 | tf_op jit(solution)/shard_map/reduce_scatter | solution.py:99
  176.8 1.6 broadcast_multiply_fusion
  (27 shorter events, 7.3 us)
Async XLA Ops:
  7.2 11.6 %copy-start = (bf16[128,2048]{1,0:T(8,128)(2,1)S(1)}, bf16[128,2048]{1,0:T(8,128)(2,1)}, u32[]{:S(2)}) copy-start(bf16[128,2048]{1,0:T(8,128)(2,1)} %param.7) | copy-start | bytes 1572868
  11.8 11.8 %all-to-all-start = ((bf16[4,1,48]{2,1,0:T(2,128)(2,1)}), bf16[4,1,48]{2,1,0:T(2,128)(2,1)S(1)}, u32[]{:S(2)}, u32[]{:S(2)}) async-start(bf16[4,1,48]{2,1,0:T(2,128)(2,1)} %all_to_all.28), calls=%async_computation | async-start | bytes 4096 | tf_op jit(solution)/shard_map/all_to_all | solution.py:67
  23.6 22.4 %all-to-all-start.2 = ((bf16[4,48,2048]{2,1,0:T(8,128)(2,1)}), bf16[4,48,2048]{2,1,0:T(8,128)(2,1)S(1)}, u32[]{:S(2)}, u32[]{:S(2)}) async-start(bf16[4,48,2048]{2,1,0:T(8,128)(2,1)} %bitcast.6), calls=%async_computation.2 | async-start | bytes 1572864 | tf_op jit(solution)/shard_map/all_to_all | solution.py:65
  46.0 23.1 %all-to-all-start.1 = ((bf16[4,48,2048]{2,1,0:T(8,128)(2,1)}), bf16[4,48,2048]{2,1,0:T(8,128)(2,1)S(1)}, u32[]{:S(2)}, u32[]{:S(2)}) async-start(bf16[4,48,2048]{2,1,0:T(8,128)(2,1)} %bitcast.3), calls=%async_computation.1 | async-start | bytes 1572864 | tf_op jit(solution)/shard_map/all_to_all | solution.py:66
  49.5 127.3 %reduce-scatter.2.cloned.1.call-start = ((), (), s32[]{:S(2)}) async-start(), calls=%async_computation.6 | async-start | bytes 14155776 | tf_op jit(solution)/shard_map/reduce_scatter | solution.py:99
  49.8 4.2 %copy-start.1 = (f32[1,2048,512]{2,1,0:T(8,128)S(1)}, f32[1,2048,512]{2,1,0:T(8,128)}, u32[]{:S(2)}) copy-start(f32[1,2048,512]{2,1,0:T(8,128)} %param.12) | copy-start | bytes 12582916
  55.9 13.2 %copy-start.4 = (f32[192,512]{1,0:T(8,128)}, f32[192,512]{1,0:T(8,128)S(1)}, u32[]{:S(2)}) copy-start(f32[192,512]{1,0:T(8,128)S(1)} %fusion.6) | copy-start | bytes 1179652
  69.1 3.6 %copy-start.3 = (f32[1,2048,512]{2,1,0:T(8,128)S(1)}, f32[1,2048,512]{2,1,0:T(8,128)}, u32[]{:S(2)}) copy-start(f32[1,2048,512]{2,1,0:T(8,128)} %param.13) | copy-start | bytes 12582916
  85.8 15.7 %all-to-all-start.4 = ((bf16[4,1,48]{2,1,0:T(2,128)(2,1)}), bf16[4,1,48]{2,1,0:T(2,128)(2,1)S(1)}, u32[]{:S(2)}, u32[]{:S(2)}) async-start(bf16[4,1,48]{2,1,0:T(2,128)(2,1)} %all_to_all.26), calls=%async_computation.4 | async-start | bytes 4096 | tf_op jit(solution)/shard_map/all_to_all | solution.py:82
  89.1 7.0 %copy-start.2 = (f32[1,2048,512]{2,1,0:T(8,128)S(1)}, f32[1,2048,512]{2,1,0:T(8,128)}, u32[]{:S(2)}) copy-start(f32[1,2048,512]{2,1,0:T(8,128)} %param.12) | copy-start | bytes 12582916
  101.5 23.5 %all-to-all-start.3 = ((bf16[4,48,2048]{2,1,0:T(8,128)(2,1)}), bf16[4,48,2048]{2,1,0:T(8,128)(2,1)S(1)}, u32[]{:S(2)}, u32[]{:S(2)}) async-start(bf16[4,48,2048]{2,1,0:T(8,128)(2,1)} %bitcast.10), calls=%async_computation.3 | async-start | bytes 1572864 | tf_op jit(solution)/shard_map/all_to_all | solution.py:79
Sparse Core Ops, SparseCore 0:
  85.3 91.4 reduce-scatter.1
where the time goes:
time: 187 us; the launch traced here: 186 us
  waiting for transfers between devices  100 us (53%)
  matrix products  32.8 us (18%)
  starting transfers between devices  21.8 us (12%)
  between operations  14.2 us (8%)
  other arithmetic  9.88 us (5%)
  local copies, waits for them, and re-layouts  7.65 us (4%)
    reduce_scatter x1, waiting for transfers between devices, shards(): reduced = lax.psum_scatter(stacked, 'dp', scatter_dimension=1, tiled=True)  50.2 us
    all_to_all x1, waiting for transfers between devices, shards(): lax.all_to_all(send_tok, 'expert', split_axis=0, concat_axis=0, tiled=True)  16.6 us
    all_to_all x1, waiting for transfers between devices, shards(): lax.all_to_all(input_part.reshape(sources, CAP, D), 'expert', split_axis=...  16.6 us
    all_to_all x1, waiting for transfers between devices, shards(): lax.all_to_all(send_cot, 'expert', split_axis=0, concat_axis=0, tiled=True)  13.2 us
    dot_general x1, matrix products, expert_rows(): jnp.dot(d_gate, gate_weight.T, precision=highest)  6.96 us
    all_to_all x1, starting transfers between devices, shards(): lax.all_to_all(send_prob, 'expert', split_axis=0, concat_axis=0, tiled=True)  6.32 us
    dot_general x1, matrix products, expert_rows(): jnp.dot(d_up, up_weight.T, precision=highest)  5.42 us
    another operation x1, other arithmetic, shards(): stacked = jnp.stack([grad_g, grad_u, grad_d])  5.16 us
  transfers between devices with their start and end apart: 6, of which 5 were waited for; matrix products, arithmetic and copies ran while one was open for 14% of the time, Pallas kernels for 0%

commit v1 on v0

v1 whole, which is shorter than its diff:
```python
import math

import jax
import jax.numpy as jnp
from jax import lax
from jax.sharding import PartitionSpec as P

HOT = 4
CAP = 48
LANES = 128

highest = lax.Precision.HIGHEST
f32 = jnp.float32
bf16 = jnp.bfloat16


def shifted(values, axis, by):
    size = lax.axis_size(axis)
    return lax.ppermute(values, axis, [(i, (i + by) % size) for i in range(size)])


def placing_matrix(route_column, me, n_expert):
    quarters = n_expert // HOT
    onehot = (route_column[:, None] == jnp.arange(HOT, dtype=jnp.int32)[None, :]).astype(jnp.int32)
    earlier = jnp.cumsum(onehot, axis=0) - onehot
    rank = jnp.sum(earlier * onehot, axis=1)
    slots = jnp.arange(n_expert * CAP, dtype=jnp.int32)
    owner = lax.rem(me + slots // CAP, n_expert) // quarters
    wanted = (owner[:, None] == route_column[None, :]) & ((slots % CAP)[:, None] == rank[None, :])
    return wanted.astype(bf16)


def shards(tokens, cotangent, route, prob, w_gate, w_up, w_down):
    n_expert = lax.axis_size("expert")
    n_dp = lax.axis_size("dp")
    quarters = n_expert // HOT
    width = tokens.shape[1]
    rows = n_expert * CAP
    scale = 1.0 / math.sqrt(tokens.shape[0] * n_dp * n_expert)
    back_type = bf16 if quarters == 1 else f32
    me = lax.axis_index("expert")
    placing = placing_matrix(route[:, 0], me, n_expert)
    prob_lanes = jnp.broadcast_to(prob[:, None], (prob.shape[0], LANES))
    cot_prob = jnp.concatenate([cotangent, prob_lanes], axis=1)
    slot_tok = jnp.dot(placing, tokens, preferred_element_type=f32).astype(bf16)
    slot_cot = jnp.dot(placing, cot_prob, preferred_element_type=f32).astype(bf16)
    slot_tok = slot_tok.reshape(n_expert, CAP, width)
    slot_cot = slot_cot.reshape(n_expert, CAP, width + LANES)
    row_tok = jnp.concatenate(
        [slot_tok[0]] + [shifted(slot_tok[k], "expert", k) for k in range(1, n_expert)]
    )
    row_cotp = jnp.concatenate(
        [slot_cot[0]] + [shifted(slot_cot[k], "expert", k) for k in range(1, n_expert)]
    )
    row_cot = row_cotp[:, :width]
    row_prob = row_cotp[:, width : width + 1].astype(f32)

    gate_pre = jnp.dot(row_tok, w_gate[0], precision=highest, preferred_element_type=f32)
    up_pre = jnp.dot(row_tok, w_up[0], precision=highest, preferred_element_type=f32)
    sig = jax.nn.sigmoid(gate_pre)
    act = gate_pre * sig
    hidden = act * up_pre
    tok_cols = lax.all_to_all(
        row_tok.reshape(rows, n_dp, width // n_dp).transpose(1, 0, 2),
        "dp", split_axis=0, concat_axis=0, tiled=True,
    ).reshape(n_dp * rows, width // n_dp)
    backward = jnp.dot(row_cot, w_down[0], precision=highest, preferred_element_type=f32)
    cot_cols = lax.all_to_all(
        row_cot.reshape(rows, n_dp, width // n_dp).transpose(1, 0, 2),
        "dp", split_axis=0, concat_axis=0, tiled=True,
    ).reshape(n_dp * rows, width // n_dp)
    prob_part = jnp.sum(hidden * backward, axis=1)
    d_hidden = row_prob * backward
    d_up = d_hidden * act
    d_gate = d_hidden * up_pre * sig * (1.0 + gate_pre * (1.0 - sig))
    terms = jnp.stack(
        [(d_gate * scale).astype(bf16), (d_up * scale).astype(bf16), (row_prob * scale * hidden).astype(bf16)]
    )
    all_terms = lax.all_gather(terms, "dp", axis=1, tiled=True)
    input_part = jnp.dot(d_gate, w_gate[0].T, precision=highest) + jnp.dot(
        d_up, w_up[0].T, precision=highest
    )
    back = jnp.concatenate(
        [
            input_part.astype(back_type),
            jnp.broadcast_to(prob_part.astype(back_type)[:, None], (rows, LANES)),
        ],
        axis=1,
    ).reshape(n_expert, CAP, width + LANES)
    home = jnp.concatenate(
        [back[0]] + [shifted(back[k], "expert", n_expert - k) for k in range(1, n_expert)]
    )
    taken = lax.dot_general(
        placing.astype(back_type), home, (((0,), (0,)), ((), ())),
        precision=None if quarters == 1 else highest, preferred_element_type=f32,
    ).astype(bf16)
    grad_input = taken[:, :width]
    grad_prob = taken[:, width]

    def over_rows(cols, term):
        return lax.dot_general(
            cols, term, (((0,), (0,)), ((), ())), preferred_element_type=f32
        )[None]

    return (
        grad_input,
        grad_prob,
        over_rows(tok_cols, all_terms[0]),
        over_rows(tok_cols, all_terms[1]),
        over_rows(cot_cols, all_terms[2]),
    )


def solution(mesh):
    placed = (
        P(("dp", "expert"), None),
        P(("dp", "expert"), None),
        P(("dp", "expert"), None),
        P(("dp", "expert")),
        P("expert", None, None),
        P("expert", None, None),
        P("expert", None, None),
    )
    return jax.shard_map(
        shards,
        mesh=mesh,
        in_specs=placed,
        out_specs=(
            P(("dp", "expert"), None),
            P(("dp", "expert")),
            P("expert", "dp", None),
            P("expert", "dp", None),
            P("expert", "dp", None),
        ),
        check_vma=False,
    )
```

time: 187 us -> 124 us (0.66)
  waiting for transfers between devices: 100 us -> 49.6 us
  other arithmetic: 9.88 us -> 3.91 us
  local copies, waits for them, and re-layouts: 7.65 us -> 2.98 us
  matrix products: 32.8 us -> 28.7 us
  starting transfers between devices: 21.8 us -> 24.4 us
    reduce_scatter x1 -> x0, waiting for transfers between devices: 50.2 us -> none  [shards(): reduced = lax.psum_scatter(stacked, 'dp', scatter_dimension=1, tiled=True)]
    all_to_all x5 -> x2, waiting for transfers between devices: 49.9 us -> 0.48 us  [the longest x1 0.48 us: shards(): lax.all_to_all(row_tok.reshape(rows, n_dp, width // n_dp).transpose(1, 0,...]
    ppermute x0 -> x9, waiting for transfers between devices: none -> 33.6 us  [shifted(): lax.ppermute(values, axis, [(i, (i + by) % size) for i in range(size)])]
    ppermute x0 -> x9, starting transfers between devices: none -> 16.9 us  [shifted(): lax.ppermute(values, axis, [(i, (i + by) % size) for i in range(size)])]
    all_gather x0 -> x1, waiting for transfers between devices: none -> 15.5 us  [shards(): all_terms = lax.all_gather(terms, 'dp', axis=1, tiled=True)]
    all_to_all x5 -> x2, starting transfers between devices: 21.6 us -> 7.45 us  [the longest x1 3.73 us: shards(): lax.all_to_all(row_tok.reshape(rows, n_dp, width // n_dp).transpose(1, 0,...]
    another operation x2, other arithmetic: 5.33 us -> 1.06 us  [the longest x1 0.89 us: shards(): jnp.stack([(d_gate * scale).astype(bf16), (d_up * scale).astype(bf16), (r...]
    dot_general x10 -> x11, matrix products: 32.8 us -> 28.7 us  [the longest x3 8.38 us: over_rows(): lax.dot_general(cols, term, (((0,), (0,)), ((), ())), preferred_element_t...]
  transfers between devices with their start and end apart: 6 -> 12, of which waited for: 5 -> 5; matrix products, arithmetic and copies ran while one was open for 14% -> 19% of each run, Pallas kernels for 0% -> 0%
where the time goes in v1:
time: 124 us
  waiting for transfers between devices  49.6 us (40%)
  matrix products  28.7 us (23%)
  starting transfers between devices  24.4 us (20%)
  between operations  14.3 us (12%)
  other arithmetic  3.91 us (3%)
  local copies, waits for them, and re-layouts  2.98 us (2%)
    ppermute x9, waiting for transfers between devices, shifted(): lax.ppermute(values, axis, [(i, (i + by) % size) for i in range(size)])  33.6 us
    ppermute x9, starting transfers between devices, shifted(): lax.ppermute(values, axis, [(i, (i + by) % size) for i in range(size)])  16.9 us
    all_gather x1, waiting for transfers between devices, shards(): all_terms = lax.all_gather(terms, 'dp', axis=1, tiled=True)  15.5 us
    dot_general x3, matrix products, over_rows(): lax.dot_general(cols, term, (((0,), (0,)), ((), ())), preferred_element_t...  8.38 us
    dot_general x1, matrix products, shards(): jnp.dot(d_gate, w_gate[0].T, precision=highest)  6.34 us
    dot_general x1, matrix products, shards(): jnp.dot(d_up, w_up[0].T, precision=highest)  4.6 us
    all_to_all x1, starting transfers between devices, shards(): lax.all_to_all(row_tok.reshape(rows, n_dp, width // n_dp).transpose(1, 0,...  3.73 us
    all_to_all x1, starting transfers between devices, shards(): lax.all_to_all(row_cot.reshape(rows, n_dp, width // n_dp).transpose(1, 0,...  3.72 us
  transfers between devices with their start and end apart: 12, of which 5 were waited for; matrix products, arithmetic and copies ran while one was open for 19% of the time, Pallas kernels for 0%

profile of v1, /device:TPU:0, one launch (start us, length us, event | category | flops | bytes accessed | tf_op | source)
XLA Modules:
  0.0 123.9 jit_solution(14260580207086143977)
XLA Ops:
  9.1 1.1 convolution_convert_fusion.2
  10.2 5.1 %collective-permute-start.5 = (bf16[48,2048]{1,0:T(8,128)(2,1)S(1)}, bf16[48,2048]{1,0:T(8,128)(2,1)S(1)}, u32[]{:S(2)}, u32[]{:S(2)}) collective-permute-start(bf16[48,2048]{1,0:T(8,128)(2,1)S(1)} %get-tuple-element.21), channel_id=1, source_target_pairs={{0,3},{1,0},{2,1},{3,2},{4,7},{5,4},{6,5},{7,6},{8,11},{9,8},{10,9... | collective-permute-start | bytes 589832 | tf_op jit(solution)/shard_map/ppermute | solution.py:19
  15.3 1.0 collective-permute-start.3
  17.0 2.9 %collective-permute-start.2 = (bf16[48,2176]{1,0:T(8,128)(2,1)S(1)}, bf16[48,2176]{1,0:T(8,128)(2,1)S(1)}, u32[]{:S(2)}, u32[]{:S(2)}) collective-permute-start(bf16[48,2176]{1,0:T(8,128)(2,1)S(1)} %get-tuple-element.15), channel_id=1, source_target_pairs={{0,3},{1,0},{2,1},{3,2},{4,7},{5,4},{6,5},{7,6},{8,11},{9,8},{10,9... | collective-permute-start | bytes 626696 | tf_op jit(solution)/shard_map/ppermute | solution.py:19
  19.8 1.1 collective-permute-start.1
  21.0 1.0 collective-permute-start
  22.0 11.8 %collective-permute-done.4 = bf16[48,2048]{1,0:T(8,128)(2,1)S(1)} collective-permute-done((bf16[48,2048]{1,0:T(8,128)(2,1)S(1)}, bf16[48,2048]{1,0:T(8,128)(2,1)S(1)}, u32[]{:S(2)}, u32[]{:S(2)}) %collective-permute-start.4) | collective-permute-done | bytes 196640 | tf_op jit(solution)/shard_map/ppermute | solution.py:19
  33.8 1.9 %fusion.2 = f32[192,512]{1,0:T(8,128)S(1)} fusion(f32[1,2048,512]{2,1,0:T(8,128)S(1)} %copy-done.1, bf16[48,2048]{1,0:T(8,128)(2,1)S(1)} %collective-permute-done.5, bf16[48,2048]{1,0:T(8,128)(2,1)S(1)} %collective-permute-done.4, bf16[48,2048]{1,0:T(8,128)(2,1)S(1)} %collective-permute-done.3, bf16[48,2048]{1,0:T(8,128)(2,1)S(1)} %get-tuple-element.20), kind=kOutput, calls=%fused_computation.2 | convolution fusion | flops 2419064832 | bytes 5373952 | tf_op jit(solution)/shard_map/dot_general | solution.py:58
  35.6 14.3 %collective-permute-done.1 = bf16[48,2176]{1,0:T(8,128)(2,1)S(1)} collective-permute-done((bf16[48,2176]{1,0:T(8,128)(2,1)S(1)}, bf16[48,2176]{1,0:T(8,128)(2,1)S(1)}, u32[]{:S(2)}, u32[]{:S(2)}) %collective-permute-start.1) | collective-permute-done | bytes 208928 | tf_op jit(solution)/shard_map/ppermute | solution.py:19
  50.1 1.9 %fusion.8 = f32[192,512]{1,0:T(8,128)S(1)} fusion(bf16[192,2048]{1,0:T(8,128)(2,1)S(1)} %pad_maximum_fusion, f32[1,2048,512]{2,1,0:T(8,128)S(1)} %copy-done.2), kind=kOutput, calls=%fused_computation.8 | convolution fusion | flops 2415919104 | bytes 5373952 | tf_op jit(solution)/shard_map/dot_general | solution.py:67
  52.2 2.8 %fusion.36 = (bf16[1,192,512]{2,1,0:T(8,128)(2,1)S(1)}, f32[192,512]{1,0:T(8,128)}, bf16[192]{0:T(256)(128)(2,1)S(1)}, bf16[1,192,512]{2,1,0:T(8,128)(2,1)S(1)}, bf16[1,192,512]{2,1,0:T(8,128)(2,1)S(1)}) fusion(f32[192,512]{1,0:T(8,128)S(1)} %fusion.2, f32[192,512]{1,0:T(8,128)S(1)} %fusion.8, f32[192]{0:T(256)S(1)} %get-tuple-element.6, ...), kind=kOutput, calls=%fused_computation.59 | convolution fusion | flops 2421128960 | bytes 6752128 | tf_op jit(solution)/shard_map/dot_general | solution.py:59
  57.0 3.7 %all-to-all-start = ((bf16[8,192,256]{2,1,0:T(8,128)(2,1)}), bf16[8,192,256]{2,1,0:T(8,128)(2,1)S(1)}, u32[]{:S(2)}, u32[]{:S(2)}) async-start(bf16[8,192,256]{2,1,0:T(8,128)(2,1)} %maximum_bitcast_fusion), calls=%async_computation | async-start | bytes 1572864 | tf_op jit(solution)/shard_map/all_to_all | solution.py:63
  60.7 6.3 %fusion = f32[192,2048]{1,0:T(8,128)S(1)} fusion(f32[192,512]{1,0:T(8,128)S(1)} %copy-done.6, f32[1,2048,512]{2,1,0:T(8,128)} %param.11), kind=kOutput, calls=%fused_computation | convolution fusion | flops 2415919104 | bytes 6160384 | tf_op jit(solution)/shard_map/dot_general | solution.py:80
  67.1 4.6 %fusion.13 = bf16[192,2048]{1,0:T(8,128)(2,1)S(1)} fusion(f32[192,2048]{1,0:T(8,128)S(1)} %fusion, f32[1,2048,512]{2,1,0:T(8,128)S(1)} %copy-done.4, f32[192,512]{1,0:T(8,128)S(1)} %fusion.8, f32[192]{0:T(256)S(1)} %get-tuple-element.6, f32[192,512]{1,0:T(8,128)S(1)} %fusion.2), kind=kOutput, calls=%fused_computation.13 | convolution fusion | flops 2417295360 | bytes 7340800 | tf_op jit(solution)/shard_map/dot_general | solution.py:80
  71.9 1.0 collective-permute-start.8
  72.9 2.0 %collective-permute-start.7 = (bf16[48,2176]{1,0:T(8,128)(2,1)S(1)}, bf16[48,2176]{1,0:T(8,128)(2,1)S(1)}, u32[]{:S(2)}, u32[]{:S(2)}) collective-permute-start(bf16[48,2176]{1,0:T(8,128)(2,1)S(1)} %get-tuple-element.13), channel_id=1, source_target_pairs={{0,2},{1,3},{2,0},{3,1},{4,6},{5,7},{6,4},{7,5},{8,10},{9,11},{10,... | collective-permute-start | bytes 626696 | tf_op jit(solution)/shard_map/ppermute | solution.py:19
  74.9 2.8 %collective-permute-start.6 = (bf16[48,2176]{1,0:T(8,128)(2,1)S(1)}, bf16[48,2176]{1,0:T(8,128)(2,1)}, u32[]{:S(2)}, u32[]{:S(2)}) collective-permute-start(bf16[48,2176]{1,0:T(8,128)(2,1)S(1)} %get-tuple-element.11), channel_id=1, source_target_pairs={{0,3},{1,0},{2,1},{3,2},{4,7},{5,4},{6,5},{7,6},{8,11},{9,8},{10,9... | collective-permute-start | bytes 626696 | tf_op jit(solution)/shard_map/ppermute | solution.py:19
  79.1 3.7 %all-to-all-start.1 = ((bf16[8,192,256]{2,1,0:T(8,128)(2,1)}), bf16[8,192,256]{2,1,0:T(8,128)(2,1)S(1)}, u32[]{:S(2)}, u32[]{:S(2)}) async-start(bf16[8,192,256]{2,1,0:T(8,128)(2,1)} %bitcast.75), calls=%async_computation.1 | async-start | bytes 1572864 | tf_op jit(solution)/shard_map/all_to_all | solution.py:68
  82.9 7.5 %collective-permute-done.7 = bf16[48,2176]{1,0:T(8,128)(2,1)S(1)} collective-permute-done((bf16[48,2176]{1,0:T(8,128)(2,1)S(1)}, bf16[48,2176]{1,0:T(8,128)(2,1)S(1)}, u32[]{:S(2)}, u32[]{:S(2)}) %collective-permute-start.7) | collective-permute-done | bytes 208928 | tf_op jit(solution)/shard_map/ppermute | solution.py:19
  90.3 1.4 %convolution_convert_fusion.1 = bf16[128,2176]{1,0:T(8,128)(2,1)S(1)} fusion(bf16[48,2176]{1,0:T(8,128)(2,1)S(1)} %collective-permute-done.8, bf16[48,2176]{1,0:T(8,128)(2,1)S(1)} %collective-permute-done.7, bf16[48,2176]{1,0:T(8,128)(2,1)} %collective-permute-done.6, bf16[48,2176]{1,0:T(8,128)(2,1)S(1)} %get-tuple-element.10, ...), kind=kOutput, calls=%fused_computation.11 | convolution fusion | flops 110649344 | bytes 1395200 | tf_op jit(solution)/shard_map/dot_general | solution.py:93
  93.2 15.5 %all-gather.2.cloned.1.call-done = bf16[3,1536,512]{2,1,0:T(8,128)(2,1)} async-done(((bf16[3,192,512]{2,1,0:T(8,128)(2,1)}), bf16[3,1536,512]{2,1,0:T(8,128)(2,1)}) %all-gather.2.cloned.1.call-update) | async-done | bytes 4718608 | tf_op jit(solution)/shard_map/all_gather | solution.py:79
  108.7 2.8 %fusion.19 = f32[1,256,512]{2,1,0:T(8,128)} fusion(bf16[1536,256]{1,0:T(8,128)(2,1)S(1)} %bitcast.81, bf16[3,1536,512]{2,1,0:T(8,128)(2,1)} %all-gather.2.cloned.1.call-done), kind=kOutput, calls=%fused_computation.24 | convolution fusion | flops 402653184 | bytes 2883584 | tf_op jit(solution)/shard_map/dot_general | solution.py:101
  111.5 2.8 %fusion.20 = f32[1,256,512]{2,1,0:T(8,128)} fusion(bf16[1536,256]{1,0:T(8,128)(2,1)S(1)} %bitcast.82, bf16[3,1536,512]{2,1,0:T(8,128)(2,1)} %all-gather.2.cloned.1.call-done), kind=kOutput, calls=%fused_computation.25 | convolution fusion | flops 402653184 | bytes 2883584 | tf_op jit(solution)/shard_map/dot_general | solution.py:101
  114.3 2.8 %fusion.21 = f32[1,256,512]{2,1,0:T(8,128)} fusion(bf16[1536,256]{1,0:T(8,128)(2,1)S(1)} %bitcast.83, bf16[3,1536,512]{2,1,0:T(8,128)(2,1)} %all-gather.2.cloned.1.call-done), kind=kOutput, calls=%fused_computation.26 | convolution fusion | flops 402653184 | bytes 2883584 | tf_op jit(solution)/shard_map/dot_general | solution.py:101
  (50 shorter events, 7.9 us)
Async XLA Ops:
  7.2 1.9 %copy-start = (bf16[128,2048]{1,0:T(8,128)(2,1)S(1)}, bf16[128,2048]{1,0:T(8,128)(2,1)}, u32[]{:S(2)}) copy-start(bf16[128,2048]{1,0:T(8,128)(2,1)} %param.7) | copy-start | bytes 1572868
  7.2 101.5 %all-gather.2.cloned.1.call-start = ((), (), s32[]{:S(2)}) async-start(), calls=%async_computation.2 | async-start | bytes 5308416 | tf_op jit(solution)/shard_map/all_gather | solution.py:79
  7.2 9.1 %copy-start.8 = (bf16[128]{0:T(256)(128)(2,1)S(1)}, bf16[128]{0:T(256)(128)(2,1)}, u32[]{:S(2)}) copy-start(bf16[128]{0:T(256)(128)(2,1)} %param.10) | copy-start | bytes 772
  8.0 8.4 %copy-start.5 = (bf16[128,2048]{1,0:T(8,128)(2,1)S(1)}, bf16[128,2048]{1,0:T(8,128)(2,1)}, u32[]{:S(2)}) copy-start(bf16[128,2048]{1,0:T(8,128)(2,1)} %param.8) | copy-start | bytes 1572868
  8.0 8.4 %copy-start.7 = (s32[128,1]{0,1:T(1,128)S(1)}, s32[128,1]{0,1:T(1,128)}, u32[]{:S(2)}) copy-start(s32[128,1]{0,1:T(1,128)} %param.9) | copy-start | bytes 1540
  10.2 23.6 %copy-start.1 = (f32[1,2048,512]{2,1,0:T(8,128)S(1)}, f32[1,2048,512]{2,1,0:T(8,128)}, u32[]{:S(2)}) copy-start(f32[1,2048,512]{2,1,0:T(8,128)} %param.11) | copy-start | bytes 12582916
  10.2 10.7 %collective-permute-start.5 = (bf16[48,2048]{1,0:T(8,128)(2,1)S(1)}, bf16[48,2048]{1,0:T(8,128)(2,1)S(1)}, u32[]{:S(2)}, u32[]{:S(2)}) collective-permute-start(bf16[48,2048]{1,0:T(8,128)(2,1)S(1)} %get-tuple-element.21), channel_id=1, source_target_pairs={{0,3},{1,0},{2,1},{3,2},{4,7},{5,4},{6,5},{7,6},{8,11},{9,8},{10,9... | collective-permute-start | bytes 589832 | tf_op jit(solution)/shard_map/ppermute | solution.py:19
  15.3 18.4 %collective-permute-start.4 = (bf16[48,2048]{1,0:T(8,128)(2,1)S(1)}, bf16[48,2048]{1,0:T(8,128)(2,1)S(1)}, u32[]{:S(2)}, u32[]{:S(2)}) collective-permute-start(bf16[48,2048]{1,0:T(8,128)(2,1)S(1)} %get-tuple-element.22), channel_id=1, source_target_pairs={{0,2},{1,3},{2,0},{3,1},{4,6},{5,7},{6,4},{7,5},{8,10},{9,11},{10,... | collective-permute-start | bytes 589832 | tf_op jit(solution)/shard_map/ppermute | solution.py:19
  15.3 18.4 %collective-permute-start.3 = (bf16[48,2048]{1,0:T(8,128)(2,1)S(1)}, bf16[48,2048]{1,0:T(8,128)(2,1)S(1)}, u32[]{:S(2)}, u32[]{:S(2)}) collective-permute-start(bf16[48,2048]{1,0:T(8,128)(2,1)S(1)} %get-tuple-element.23), channel_id=1, source_target_pairs={{0,1},{1,2},{2,3},{3,0},{4,5},{5,6},{6,7},{7,4},{8,9},{9,10},{10,1... | collective-permute-start | bytes 589832 | tf_op jit(solution)/shard_map/ppermute | solution.py:19
  17.0 18.7 %collective-permute-start.2 = (bf16[48,2176]{1,0:T(8,128)(2,1)S(1)}, bf16[48,2176]{1,0:T(8,128)(2,1)S(1)}, u32[]{:S(2)}, u32[]{:S(2)}) collective-permute-start(bf16[48,2176]{1,0:T(8,128)(2,1)S(1)} %get-tuple-element.15), channel_id=1, source_target_pairs={{0,3},{1,0},{2,1},{3,2},{4,7},{5,4},{6,5},{7,6},{8,11},{9,8},{10,9... | collective-permute-start | bytes 626696 | tf_op jit(solution)/shard_map/ppermute | solution.py:19
  19.8 30.1 %collective-permute-start.1 = (bf16[48,2176]{1,0:T(8,128)(2,1)S(1)}, bf16[48,2176]{1,0:T(8,128)(2,1)S(1)}, u32[]{:S(2)}, u32[]{:S(2)}) collective-permute-start(bf16[48,2176]{1,0:T(8,128)(2,1)S(1)} %get-tuple-element.16), channel_id=1, source_target_pairs={{0,2},{1,3},{2,0},{3,1},{4,6},{5,7},{6,4},{7,5},{8,10},{9,11},{10,... | collective-permute-start | bytes 626696 | tf_op jit(solution)/shard_map/ppermute | solution.py:19
  21.0 29.0 %collective-permute-start = (bf16[48,2176]{1,0:T(8,128)(2,1)S(1)}, bf16[48,2176]{1,0:T(8,128)(2,1)S(1)}, u32[]{:S(2)}, u32[]{:S(2)}) collective-permute-start(bf16[48,2176]{1,0:T(8,128)(2,1)S(1)} %get-tuple-element.17), channel_id=1, source_target_pairs={{0,1},{1,2},{2,3},{3,0},{4,5},{5,6},{6,7},{7,4},{8,9},{9,10},{10,1... | collective-permute-start | bytes 626696 | tf_op jit(solution)/shard_map/ppermute | solution.py:19
  33.7 16.3 %copy-start.2 = (f32[1,2048,512]{2,1,0:T(8,128)S(1)}, f32[1,2048,512]{2,1,0:T(8,128)}, u32[]{:S(2)}) copy-start(f32[1,2048,512]{2,1,0:T(8,128)} %param.13) | copy-start | bytes 12582916
  50.0 2.2 %copy-start.3 = (f32[1,2048,512]{2,1,0:T(8,128)S(1)}, f32[1,2048,512]{2,1,0:T(8,128)}, u32[]{:S(2)}) copy-start(f32[1,2048,512]{2,1,0:T(8,128)} %param.12) | copy-start | bytes 12582916
  56.0 4.7 %copy-start.6 = (f32[192,512]{1,0:T(8,128)S(1)}, f32[192,512]{1,0:T(8,128)}, u32[]{:S(2)}) copy-start(f32[192,512]{1,0:T(8,128)} %get-tuple-element.8) | copy-start | bytes 1179652
  57.0 22.1 %all-to-all-start = ((bf16[8,192,256]{2,1,0:T(8,128)(2,1)}), bf16[8,192,256]{2,1,0:T(8,128)(2,1)S(1)}, u32[]{:S(2)}, u32[]{:S(2)}) async-start(bf16[8,192,256]{2,1,0:T(8,128)(2,1)} %maximum_bitcast_fusion), calls=%async_computation | async-start | bytes 1572864 | tf_op jit(solution)/shard_map/all_to_all | solution.py:63
  60.7 6.4 %copy-start.4 = (f32[1,2048,512]{2,1,0:T(8,128)S(1)}, f32[1,2048,512]{2,1,0:T(8,128)}, u32[]{:S(2)}) copy-start(f32[1,2048,512]{2,1,0:T(8,128)} %param.12) | copy-start | bytes 12582916
  71.9 11.0 %collective-permute-start.8 = (bf16[48,2176]{1,0:T(8,128)(2,1)S(1)}, bf16[48,2176]{1,0:T(8,128)(2,1)S(1)}, u32[]{:S(2)}, u32[]{:S(2)}) collective-permute-start(bf16[48,2176]{1,0:T(8,128)(2,1)S(1)} %get-tuple-element.12), channel_id=1, source_target_pairs={{0,1},{1,2},{2,3},{3,0},{4,5},{5,6},{6,7},{7,4},{8,9},{9,10},{10,1... | collective-permute-start | bytes 626696 | tf_op jit(solution)/shard_map/ppermute | solution.py:19
  72.9 17.5 %collective-permute-start.7 = (bf16[48,2176]{1,0:T(8,128)(2,1)S(1)}, bf16[48,2176]{1,0:T(8,128)(2,1)S(1)}, u32[]{:S(2)}, u32[]{:S(2)}) collective-permute-start(bf16[48,2176]{1,0:T(8,128)(2,1)S(1)} %get-tuple-element.13), channel_id=1, source_target_pairs={{0,2},{1,3},{2,0},{3,1},{4,6},{5,7},{6,4},{7,5},{8,10},{9,11},{10,... | collective-permute-start | bytes 626696 | tf_op jit(solution)/shard_map/ppermute | solution.py:19
  74.9 15.5 %collective-permute-start.6 = (bf16[48,2176]{1,0:T(8,128)(2,1)S(1)}, bf16[48,2176]{1,0:T(8,128)(2,1)}, u32[]{:S(2)}, u32[]{:S(2)}) collective-permute-start(bf16[48,2176]{1,0:T(8,128)(2,1)S(1)} %get-tuple-element.11), channel_id=1, source_target_pairs={{0,3},{1,0},{2,1},{3,2},{4,7},{5,4},{6,5},{7,6},{8,11},{9,8},{10,9... | collective-permute-start | bytes 626696 | tf_op jit(solution)/shard_map/ppermute | solution.py:19
  79.1 35.2 %all-to-all-start.1 = ((bf16[8,192,256]{2,1,0:T(8,128)(2,1)}), bf16[8,192,256]{2,1,0:T(8,128)(2,1)S(1)}, u32[]{:S(2)}, u32[]{:S(2)}) async-start(bf16[8,192,256]{2,1,0:T(8,128)(2,1)} %bitcast.75), calls=%async_computation.1 | async-start | bytes 1572864 | tf_op jit(solution)/shard_map/all_to_all | solution.py:68
Sparse Core Ops, SparseCore 0:
  56.1 52.5 all-gather.1

commit v2 on v1

v2 whole, which is shorter than its diff:
```python
import math

import jax
import jax.numpy as jnp
from jax import lax
from jax.sharding import PartitionSpec as P

HOT = 4
CAP = 48
LANES = 128
CHUNKS = 2

highest = lax.Precision.HIGHEST
f32 = jnp.float32
bf16 = jnp.bfloat16


def shifted(values, axis, by):
    size = lax.axis_size(axis)
    return lax.ppermute(values, axis, [(i, (i + by) % size) for i in range(size)])


def placing_matrix(route_column, me, n_expert):
    quarters = n_expert // HOT
    onehot = (route_column[:, None] == jnp.arange(HOT, dtype=jnp.int32)[None, :]).astype(jnp.int32)
    earlier = jnp.cumsum(onehot, axis=0) - onehot
    rank = jnp.sum(earlier * onehot, axis=1)
    slots = jnp.arange(n_expert * CAP, dtype=jnp.int32)
    owner = lax.rem(me + slots // CAP, n_expert) // quarters
    wanted = (owner[:, None] == route_column[None, :]) & ((slots % CAP)[:, None] == rank[None, :])
    return wanted.astype(bf16)


def gathered(values, axis):
    size = lax.axis_size(axis)
    chips = [values] + [
        lax.ppermute(values, axis, [(i, i ^ (2 * k)) for i in range(size)]) for k in range(1, size // 2)
    ]
    own = jnp.concatenate(chips, axis=1)
    other = lax.ppermute(own, axis, [(i, i ^ 1) for i in range(size)])
    return own, other


def column_slices(values, axis):
    size = lax.axis_size(axis)
    share = values.shape[2] // size
    at = lax.axis_index(axis)

    def part(to):
        return lax.dynamic_slice_in_dim(values, to * share, share, axis=2)

    chips = range(size // 2)
    mine = [part(at ^ (2 * k)) for k in chips]
    theirs = jnp.stack([part((at ^ 1) ^ (2 * k)) for k in chips])
    theirs = lax.ppermute(theirs, axis, [(i, i ^ 1) for i in range(size)])
    both = [jnp.stack([mine[k], theirs[k]], axis=1) for k in chips]
    got = [both[0]] + [
        lax.ppermute(both[k], axis, [(i, i ^ (2 * k)) for i in range(size)]) for k in chips[1:]
    ]
    return jnp.stack(got, axis=1).reshape(values.shape[0], -1, share)


def expert_chunk(row, w_gate, w_up, w_down, scale, back_type):
    width = w_gate.shape[0]
    row_tok = row[:, :width]
    row_cot = row[:, width : 2 * width]
    row_prob = row[:, 2 * width : 2 * width + 1].astype(f32)
    gate_pre = jnp.dot(row_tok, w_gate, precision=highest, preferred_element_type=f32)
    up_pre = jnp.dot(row_tok, w_up, precision=highest, preferred_element_type=f32)
    backward = jnp.dot(row_cot, w_down, precision=highest, preferred_element_type=f32)
    sig = jax.nn.sigmoid(gate_pre)
    act = gate_pre * sig
    hidden = act * up_pre
    prob_part = jnp.sum(hidden * backward, axis=1)
    d_hidden = row_prob * backward
    d_up = d_hidden * act
    d_gate = d_hidden * up_pre * sig * (1.0 + gate_pre * (1.0 - sig))
    terms = jnp.stack(
        [
            (d_gate * scale).astype(bf16),
            (d_up * scale).astype(bf16),
            (row_prob * scale * hidden).astype(bf16),
        ]
    )
    input_part = jnp.dot(d_gate, w_gate.T, precision=highest) + jnp.dot(
        d_up, w_up.T, precision=highest
    )
    back = jnp.concatenate(
        [
            input_part.astype(back_type),
            jnp.broadcast_to(prob_part.astype(back_type)[:, None], (row.shape[0], LANES)),
        ],
        axis=1,
    )
    return terms, back


def shards(tokens, cotangent, route, prob, w_gate, w_up, w_down):
    n_expert = lax.axis_size("expert")
    n_dp = lax.axis_size("dp")
    quarters = n_expert // HOT
    width = tokens.shape[1]
    scale = 1.0 / math.sqrt(tokens.shape[0] * n_dp * n_expert)
    back_type = bf16 if quarters == 1 else f32
    me = lax.axis_index("expert")
    placing = placing_matrix(route[:, 0], me, n_expert)
    prob_lanes = jnp.broadcast_to(prob[:, None], (prob.shape[0], LANES))
    full_rows = jnp.concatenate([tokens, cotangent, prob_lanes], axis=1)
    part = CAP // CHUNKS
    by_shift = placing.reshape(n_expert, CHUNKS, part, -1)

    def send(chunk):
        slots = jnp.dot(
            by_shift[:, chunk].reshape(n_expert * part, -1), full_rows, preferred_element_type=f32
        ).astype(bf16).reshape(n_expert, part, -1)
        return jnp.concatenate(
            [slots[0]] + [shifted(slots[k], "expert", k) for k in range(1, n_expert)]
        )

    rows = [send(chunk) for chunk in range(CHUNKS)]
    sums = [None, None, None]
    taken = None
    for chunk in range(CHUNKS):
        row = rows[chunk]
        cols = column_slices(jnp.stack([row[:, :width], row[:, width : 2 * width]]), "dp")
        terms, back = expert_chunk(
            rows[chunk], w_gate[0], w_up[0], w_down[0], scale, back_type
        )
        back = back.reshape(n_expert, part, -1)
        home = jnp.concatenate(
            [back[0]] + [shifted(back[k], "expert", n_expert - k) for k in range(1, n_expert)]
        )
        mine = lax.dot_general(
            by_shift[:, chunk].reshape(n_expert * part, -1).astype(back_type), home,
            (((0,), (0,)), ((), ())),
            precision=None if quarters == 1 else highest, preferred_element_type=f32,
        )
        taken = mine if taken is None else taken + mine
        own, other = gathered(terms, "dp")
        count = row.shape[0]
        all_terms = jnp.stack(
            [own.reshape(3, n_dp // 2, count, -1), other.reshape(3, n_dp // 2, count, -1)], axis=2
        ).reshape(3, n_dp * count, -1)
        for which, side in enumerate((0, 0, 1)):
            got = lax.dot_general(
                cols[side], all_terms[which], (((0,), (0,)), ((), ())), preferred_element_type=f32
            )
            sums[which] = got if sums[which] is None else sums[which] + got
    taken = taken.astype(bf16)
    return (
        taken[:, :width],
        taken[:, width],
        sums[0][None],
        sums[1][None],
        sums[2][None],
    )


def solution(mesh):
    placed = (
        P(("dp", "expert"), None),
        P(("dp", "expert"), None),
        P(("dp", "expert"), None),
        P(("dp", "expert")),
        P("expert", None, None),
        P("expert", None, None),
        P("expert", None, None),
    )
    return jax.shard_map(
        shards,
        mesh=mesh,
        in_specs=placed,
        out_specs=(
            P(("dp", "expert"), None),
            P(("dp", "expert")),
            P("expert", "dp", None),
            P("expert", "dp", None),
            P("expert", "dp", None),
        ),
        check_vma=False,
    )
```

time: 124 us -> 128 us (1.032)
  starting transfers between devices: 24.4 us -> 38.9 us
  between operations: 14.3 us -> 1.07 us
  matrix products: 28.7 us -> 36.8 us
  waiting for transfers between devices: 49.6 us -> 44.5 us
    ppermute x0 -> x16, waiting for transfers between devices: none -> 23.7 us  [the longest x6 13.2 us: column_slices(): lax.ppermute(both[k], axis, [(i, i ^ 2 * k) for i in range(size)])]
    ppermute x0 -> x16, starting transfers between devices: none -> 16.8 us  [the longest x6 8.1 us: gathered(): lax.ppermute(values, axis, [(i, i ^ 2 * k) for i in range(size)])]
    all_gather x1 -> x0, waiting for transfers between devices: 15.5 us -> none  [shards(): all_terms = lax.all_gather(terms, 'dp', axis=1, tiled=True)]
    ppermute x9 -> x12, waiting for transfers between devices: 33.6 us -> 20.7 us  [shifted(): lax.ppermute(values, axis, [(i, (i + by) % size) for i in range(size)])]
    dot_general x11 -> x20, matrix products: 28.7 us -> 36.8 us  [the longest x2 8.48 us: expert_chunk(): jnp.dot(d_gate, w_gate.T, precision=highest)]
    all_to_all x2 -> x0, starting transfers between devices: 7.45 us -> none  [the longest x1 3.73 us: shards(): lax.all_to_all(row_tok.reshape(rows, n_dp, width // n_dp).transpose(1, 0,...]
    ppermute x9 -> x12, starting transfers between devices: 16.9 us -> 22 us  [shifted(): lax.ppermute(values, axis, [(i, (i + by) % size) for i in range(size)])]
  transfers between devices with their start and end apart: 12 -> 28, of which waited for: 5 -> 10; matrix products, arithmetic and copies ran while one was open for 19% -> 27% of each run, Pallas kernels for 0% -> 0%
where the time goes in v2:
time: 128 us
  waiting for transfers between devices  44.5 us (35%)
  starting transfers between devices  38.9 us (30%)
  matrix products  36.8 us (29%)
  other arithmetic  3.84 us (3%)
  local copies, waits for them, and re-layouts  3.1 us (2%)
    ppermute x12, starting transfers between devices, shifted(): lax.ppermute(values, axis, [(i, (i + by) % size) for i in range(size)])  22 us
    ppermute x12, waiting for transfers between devices, shifted(): lax.ppermute(values, axis, [(i, (i + by) % size) for i in range(size)])  20.7 us
    ppermute x6, waiting for transfers between devices, column_slices(): lax.ppermute(both[k], axis, [(i, i ^ 2 * k) for i in range(size)])  13.2 us
    ppermute x6, waiting for transfers between devices, gathered(): lax.ppermute(values, axis, [(i, i ^ 2 * k) for i in range(size)])  10.5 us
    dot_general x2, matrix products, expert_chunk(): jnp.dot(d_gate, w_gate.T, precision=highest)  8.48 us
    dot_general x2, matrix products, expert_chunk(): jnp.dot(d_up, w_up.T, precision=highest)  8.38 us
    ppermute x6, starting transfers between devices, gathered(): lax.ppermute(values, axis, [(i, i ^ 2 * k) for i in range(size)])  8.1 us
    ppermute x6, starting transfers between devices, column_slices(): lax.ppermute(both[k], axis, [(i, i ^ 2 * k) for i in range(size)])  8.06 us
  transfers between devices with their start and end apart: 28, of which 10 were waited for; matrix products, arithmetic and copies ran while one was open for 27% of the time, Pallas kernels for 0%

profile of v2, /device:TPU:0, one launch (start us, length us, event | category | flops | bytes accessed | tf_op | source)
XLA Modules:
  0.0 128.2 jit_solution(11227574648057022597)
XLA Ops:
  4.0 1.7 %convolution_convert_fusion.1 = bf16[96,4224]{1,0:T(8,128)(2,1)S(1)} fusion(pred[96,128]{1,0:T(8,128)(4,1)S(1)} %bitcast.244, bf16[128,128]{1,0:T(8,128)(2,1)S(1)} %broadcast_in_dim.12, bf16[128,2048]{1,0:T(8,128)(2,1)} %param.8, bf16[128,2048]{1,0:T(8,128)(2,1)} %param.7), kind=kOutput, calls=%fused_computation.1 | convolution fusion | flops 107458560 | bytes 1904640 | tf_op jit(solution)/shard_map/dot_general | solution.py:113
  5.7 5.1 %collective-permute-start.2 = (bf16[24,4224]{1,0:T(8,128)(2,1)S(1)}, bf16[24,4224]{1,0:T(8,128)(2,1)S(1)}, u32[]{:S(2)}, u32[]{:S(2)}) collective-permute-start(bf16[24,4224]{1,0:T(8,128)(2,1)S(1)} %get-tuple-element.18), channel_id=1, source_target_pairs={{0,3},{1,0},{2,1},{3,2},{4,7},{5,4},{6,5},{7,6},{8,11},{9,8},{10,9... | collective-permute-start | bytes 608264 | tf_op jit(solution)/shard_map/ppermute | solution.py:20
  12.3 2.9 %collective-permute-start.8 = (bf16[24,4224]{1,0:T(8,128)(2,1)S(1)}, bf16[24,4224]{1,0:T(8,128)(2,1)S(1)}, u32[]{:S(2)}, u32[]{:S(2)}) collective-permute-start(bf16[24,4224]{1,0:T(8,128)(2,1)S(1)} %get-tuple-element.22), channel_id=1, source_target_pairs={{0,3},{1,0},{2,1},{3,2},{4,7},{5,4},{6,5},{7,6},{8,11},{9,8},{10,9... | collective-permute-start | bytes 608264 | tf_op jit(solution)/shard_map/ppermute | solution.py:20
  17.8 12.5 %collective-permute-done.1 = bf16[24,4224]{1,0:T(8,128)(2,1)S(1)} collective-permute-done((bf16[24,4224]{1,0:T(8,128)(2,1)S(1)}, bf16[24,4224]{1,0:T(8,128)(2,1)S(1)}, u32[]{:S(2)}, u32[]{:S(2)}) %collective-permute-start.1) | collective-permute-done | bytes 202784 | tf_op jit(solution)/shard_map/ppermute | solution.py:20
  30.4 4.0 %fusion.6 = f32[96,512]{1,0:T(8,128)S(1)} fusion(bf16[96,2048]{1,0:T(8,128)(2,1)S(1)} %get-tuple-element.14, f32[1,2048,512]{2,1,0:T(8,128)} %param.11), kind=kOutput, calls=%fused_computation.8 | convolution fusion | flops 1207959552 | bytes 4784128 | tf_op jit(solution)/shard_map/dot_general | solution.py:68
  34.5 1.6 %fusion.18 = f32[96,512]{1,0:T(8,128)S(1)} fusion(f32[1,2048,512]{2,1,0:T(8,128)S(1)} %copy-done.2, bf16[24,4224]{1,0:T(8,128)(2,1)S(1)} %collective-permute-done.2, bf16[24,4224]{1,0:T(8,128)(2,1)S(1)} %collective-permute-done.1, bf16[24,4224]{1,0:T(8,128)(2,1)S(1)} %collective-permute-done, bf16[24,4224]{1,0:T(8,128)(2,1)S(1)} %get-tuple-element.17), kind=kOutput, calls=%fused_computation.20 | convolution fusion | flops 1209532416 | bytes 5201920 | tf_op jit(solution)/shard_map/dot_general | solution.py:70
  36.6 1.8 %fusion.96 = (bf16[1,96,512]{2,1,0:T(8,128)(2,1)S(1)}, f32[96,512]{1,0:T(8,128)S(1)}, bf16[96]{0:T(256)(128)(2,1)S(1)}, bf16[1,96,512]{2,1,0:T(8,128)(2,1)S(1)}, bf16[1,96,512]{2,1,0:T(8,128)(2,1)S(1)}) fusion(f32[96,512]{1,0:T(8,128)S(1)} %fusion.6, f32[96,512]{1,0:T(8,128)S(1)} %fusion.18, f32[96]{0:T(128)S(1)} %get-tuple-element.6, ...), kind=kOutput, calls=%fused_computation.190 | convolution fusion | flops 1208991616 | bytes 5473216 | tf_op jit(solution)/shard_map/dot_general | solution.py:69
  38.5 2.5 %collective-permute-start.18 = (bf16[3,96,512]{2,1,0:T(8,128)(2,1)S(1)}, bf16[3,96,512]{2,1,0:T(8,128)(2,1)S(1)}, u32[]{:S(2)}, u32[]{:S(2)}) collective-permute-start(bf16[3,96,512]{2,1,0:T(8,128)(2,1)S(1)} %pad_maximum_fusion.19), channel_id=1, source_target_pairs={{0,24},{4,28},{8,16},{12,20},{16,8},{20,12},{24,0},{28,4},{1,25},{... | collective-permute-start | bytes 884744 | tf_op jit(solution)/shard_map/ppermute | solution.py:37
  41.5 3.9 %collective-permute-done.7 = bf16[24,4224]{1,0:T(8,128)(2,1)S(1)} collective-permute-done((bf16[24,4224]{1,0:T(8,128)(2,1)S(1)}, bf16[24,4224]{1,0:T(8,128)(2,1)S(1)}, u32[]{:S(2)}, u32[]{:S(2)}) %collective-permute-start.7) | collective-permute-done | bytes 202784 | tf_op jit(solution)/shard_map/ppermute | solution.py:20
  45.5 1.6 %fusion.2 = f32[96,512]{1,0:T(8,128)S(1)} fusion(bf16[96,2048]{1,0:T(8,128)(2,1)S(1)} %get-tuple-element.16, f32[1,2048,512]{2,1,0:T(8,128)S(1)} %copy-done), kind=kOutput, calls=%fused_computation.4 | convolution fusion | flops 1207959552 | bytes 4784128 | tf_op jit(solution)/shard_map/dot_general | solution.py:68
  48.9 1.8 %fusion.99 = (bf16[1,96,512]{2,1,0:T(8,128)(2,1)S(1)}, f32[96,512]{1,0:T(8,128)S(1)}, bf16[96]{0:T(256)(128)(2,1)S(1)}, bf16[1,96,512]{2,1,0:T(8,128)(2,1)S(1)}, bf16[1,96,512]{2,1,0:T(8,128)(2,1)S(1)}) fusion(f32[96,512]{1,0:T(8,128)S(1)} %fusion.2, f32[96,512]{1,0:T(8,128)S(1)} %fusion.16, f32[96]{0:T(128)S(1)} %get-tuple-element.8, ...), kind=kOutput, calls=%fused_computation.193 | convolution fusion | flops 1208991616 | bytes 5473216 | tf_op jit(solution)/shard_map/dot_general | solution.py:69
  50.7 4.3 %fusion = f32[96,2048]{1,0:T(8,128)S(1)} fusion(f32[96,512]{1,0:T(8,128)S(1)} %get-tuple-element.12, f32[1,2048,512]{2,1,0:T(8,128)S(1)} %copy-done), kind=kOutput, calls=%fused_computation.2 | convolution fusion | flops 1207959552 | bytes 5177344 | tf_op jit(solution)/shard_map/dot_general | solution.py:85
  55.1 4.2 %fusion.27 = bf16[96,2048]{1,0:T(8,128)(2,1)S(1)} fusion(f32[96,2048]{1,0:T(8,128)S(1)} %fusion, f32[1,2048,512]{2,1,0:T(8,128)S(1)} %copy-done.1, f32[96,512]{1,0:T(8,128)S(1)} %fusion.16, f32[96]{0:T(128)S(1)} %get-tuple-element.8, f32[96,512]{1,0:T(8,128)S(1)} %fusion.2), kind=kOutput, calls=%fused_computation.34 | convolution fusion | flops 1208647680 | bytes 5767552 | tf_op jit(solution)/shard_map/dot_general | solution.py:85
  59.4 1.9 %collective-permute-start.9 = (bf16[24,2176]{1,0:T(8,128)(2,1)S(1)}, bf16[24,2176]{1,0:T(8,128)(2,1)S(1)}, u32[]{:S(2)}, u32[]{:S(2)}) collective-permute-start(bf16[24,2176]{1,0:T(8,128)(2,1)S(1)} %get-tuple-element.48), channel_id=1, source_target_pairs={{0,3},{1,0},{2,1},{3,2},{4,7},{5,4},{6,5},{7,6},{8,11},{9,8},{10,9... | collective-permute-start | bytes 313352 | tf_op jit(solution)/shard_map/ppermute | solution.py:20
  61.3 2.6 %collective-permute-start.11 = (bf16[24,2176]{1,0:T(8,128)(2,1)S(1)}, bf16[24,2176]{1,0:T(8,128)(2,1)S(1)}, u32[]{:S(2)}, u32[]{:S(2)}) collective-permute-start(bf16[24,2176]{1,0:T(8,128)(2,1)S(1)} %get-tuple-element.49), channel_id=1, source_target_pairs={{0,1},{1,2},{2,3},{3,0},{4,5},{5,6},{6,7},{7,4},{8,9},{9,10},{10,1... | collective-permute-start | bytes 313352 | tf_op jit(solution)/shard_map/ppermute | solution.py:20
  63.9 3.9 %collective-permute-start.10 = (bf16[24,2176]{1,0:T(8,128)(2,1)S(1)}, bf16[24,2176]{1,0:T(8,128)(2,1)S(1)}, u32[]{:S(2)}, u32[]{:S(2)}) collective-permute-start(bf16[24,2176]{1,0:T(8,128)(2,1)S(1)} %get-tuple-element.50), channel_id=1, source_target_pairs={{0,2},{1,3},{2,0},{3,1},{4,6},{5,7},{6,4},{7,5},{8,10},{9,11},{10,... | collective-permute-start | bytes 313352 | tf_op jit(solution)/shard_map/ppermute | solution.py:20
  67.7 4.1 %fusion.4 = f32[96,2048]{1,0:T(8,128)S(1)} fusion(f32[96,512]{1,0:T(8,128)S(1)} %get-tuple-element.10, f32[1,2048,512]{2,1,0:T(8,128)S(1)} %copy-done), kind=kOutput, calls=%fused_computation.6 | convolution fusion | flops 1207959552 | bytes 5177344 | tf_op jit(solution)/shard_map/dot_general | solution.py:85
  71.9 4.2 %fusion.30 = bf16[96,2048]{1,0:T(8,128)(2,1)S(1)} fusion(f32[96,2048]{1,0:T(8,128)S(1)} %fusion.4, f32[1,2048,512]{2,1,0:T(8,128)S(1)} %copy-done.1, f32[96,512]{1,0:T(8,128)S(1)} %fusion.18, f32[96]{0:T(128)S(1)} %get-tuple-element.6, f32[96,512]{1,0:T(8,128)S(1)} %fusion.6), kind=kOutput, calls=%fused_computation.35 | convolution fusion | flops 1208647680 | bytes 5767552 | tf_op jit(solution)/shard_map/dot_general | solution.py:85
  79.1 2.9 %collective-permute-done.3 = bf16[24,2176]{1,0:T(8,128)(2,1)S(1)} collective-permute-done((bf16[24,2176]{1,0:T(8,128)(2,1)S(1)}, bf16[24,2176]{1,0:T(8,128)(2,1)S(1)}, u32[]{:S(2)}, u32[]{:S(2)}) %collective-permute-start.3) | collective-permute-done | bytes 104480 | tf_op jit(solution)/shard_map/ppermute | solution.py:20
  90.4 10.5 %collective-permute-done.16 = bf16[3,96,512]{2,1,0:T(8,128)(2,1)S(1)} collective-permute-done((bf16[3,96,512]{2,1,0:T(8,128)(2,1)S(1)}, bf16[3,96,512]{2,1,0:T(8,128)(2,1)S(1)}, u32[]{:S(2)}, u32[]{:S(2)}) %collective-permute-start.16) | collective-permute-done | bytes 294944 | tf_op jit(solution)/shard_map/ppermute | solution.py:37
  105.6 3.9 %collective-permute-done.21 = bf16[2,2,96,256]{3,2,0,1:T(8,128)(2,1)S(1)} collective-permute-done((bf16[2,2,96,256]{3,2,0,1:T(8,128)(2,1)S(1)}, bf16[2,2,96,256]{3,2,0,1:T(8,128)(2,1)S(1)}, u32[]{:S(2)}, u32[]{:S(2)}) %collective-permute-start.21) | collective-permute-done | bytes 196640 | tf_op jit(solution)/shard_map/ppermute | solution.py:58
  110.1 2.6 %collective-permute-done.22 = bf16[2,2,96,256]{3,2,0,1:T(8,128)(2,1)S(1)} collective-permute-done((bf16[2,2,96,256]{3,2,0,1:T(8,128)(2,1)S(1)}, bf16[2,2,96,256]{3,2,0,1:T(8,128)(2,1)S(1)}, u32[]{:S(2)}, u32[]{:S(2)}) %collective-permute-start.22) | collective-permute-done | bytes 196640 | tf_op jit(solution)/shard_map/ppermute | solution.py:58
  112.6 2.8 %collective-permute-start.14 = (bf16[2,2,96,256]{3,2,0,1:T(8,128)(2,1)S(1)}, bf16[2,2,96,256]{3,2,0,1:T(8,128)(2,1)S(1)}, u32[]{:S(2)}, u32[]{:S(2)}) collective-permute-start(bf16[2,2,96,256]{3,2,0,1:T(8,128)(2,1)S(1)} %pad_maximum_fusion.22), channel_id=1, source_target_pairs={{0,16},{4,20},{8,24},{12,28},{16,0},{20,4},{24,8},{28,12},{1,17},{... | collective-permute-start | bytes 589832 | tf_op jit(solution)/shard_map/ppermute | solution.py:58
  118.0 5.3 %collective-permute-done.14 = bf16[2,2,96,256]{3,2,0,1:T(8,128)(2,1)S(1)} collective-permute-done((bf16[2,2,96,256]{3,2,0,1:T(8,128)(2,1)S(1)}, bf16[2,2,96,256]{3,2,0,1:T(8,128)(2,1)S(1)}, u32[]{:S(2)}, u32[]{:S(2)}) %collective-permute-start.14) | collective-permute-done | bytes 196640 | tf_op jit(solution)/shard_map/ppermute | solution.py:58
  (101 shorter events, 34.6 us)
Async XLA Ops:
  5.7 10.6 %collective-permute-start.2 = (bf16[24,4224]{1,0:T(8,128)(2,1)S(1)}, bf16[24,4224]{1,0:T(8,128)(2,1)S(1)}, u32[]{:S(2)}, u32[]{:S(2)}) collective-permute-start(bf16[24,4224]{1,0:T(8,128)(2,1)S(1)} %get-tuple-element.18), channel_id=1, source_target_pairs={{0,3},{1,0},{2,1},{3,2},{4,7},{5,4},{6,5},{7,6},{8,11},{9,8},{10,9... | collective-permute-start | bytes 608264 | tf_op jit(solution)/shard_map/ppermute | solution.py:20
  10.8 19.4 %collective-permute-start.1 = (bf16[24,4224]{1,0:T(8,128)(2,1)S(1)}, bf16[24,4224]{1,0:T(8,128)(2,1)S(1)}, u32[]{:S(2)}, u32[]{:S(2)}) collective-permute-start(bf16[24,4224]{1,0:T(8,128)(2,1)S(1)} %get-tuple-element.19), channel_id=1, source_target_pairs={{0,2},{1,3},{2,0},{3,1},{4,6},{5,7},{6,4},{7,5},{8,10},{9,11},{10,... | collective-permute-start | bytes 608264 | tf_op jit(solution)/shard_map/ppermute | solution.py:20
  10.8 19.4 %collective-permute-start = (bf16[24,4224]{1,0:T(8,128)(2,1)S(1)}, bf16[24,4224]{1,0:T(8,128)(2,1)S(1)}, u32[]{:S(2)}, u32[]{:S(2)}) collective-permute-start(bf16[24,4224]{1,0:T(8,128)(2,1)S(1)} %get-tuple-element.20), channel_id=1, source_target_pairs={{0,1},{1,2},{2,3},{3,0},{4,5},{5,6},{6,7},{7,4},{8,9},{9,10},{10,1... | collective-permute-start | bytes 608264 | tf_op jit(solution)/shard_map/ppermute | solution.py:20
  12.3 29.2 %collective-permute-start.8 = (bf16[24,4224]{1,0:T(8,128)(2,1)S(1)}, bf16[24,4224]{1,0:T(8,128)(2,1)S(1)}, u32[]{:S(2)}, u32[]{:S(2)}) collective-permute-start(bf16[24,4224]{1,0:T(8,128)(2,1)S(1)} %get-tuple-element.22), channel_id=1, source_target_pairs={{0,3},{1,0},{2,1},{3,2},{4,7},{5,4},{6,5},{7,6},{8,11},{9,8},{10,9... | collective-permute-start | bytes 608264 | tf_op jit(solution)/shard_map/ppermute | solution.py:20
  15.1 30.3 %collective-permute-start.7 = (bf16[24,4224]{1,0:T(8,128)(2,1)S(1)}, bf16[24,4224]{1,0:T(8,128)(2,1)S(1)}, u32[]{:S(2)}, u32[]{:S(2)}) collective-permute-start(bf16[24,4224]{1,0:T(8,128)(2,1)S(1)} %get-tuple-element.23), channel_id=1, source_target_pairs={{0,2},{1,3},{2,0},{3,1},{4,6},{5,7},{6,4},{7,5},{8,10},{9,11},{10,... | collective-permute-start | bytes 608264 | tf_op jit(solution)/shard_map/ppermute | solution.py:20
  16.3 29.1 %collective-permute-start.6 = (bf16[24,4224]{1,0:T(8,128)(2,1)S(1)}, bf16[24,4224]{1,0:T(8,128)(2,1)S(1)}, u32[]{:S(2)}, u32[]{:S(2)}) collective-permute-start(bf16[24,4224]{1,0:T(8,128)(2,1)S(1)} %get-tuple-element.24), channel_id=1, source_target_pairs={{0,1},{1,2},{2,3},{3,0},{4,5},{5,6},{6,7},{7,4},{8,9},{9,10},{10,1... | collective-permute-start | bytes 608264 | tf_op jit(solution)/shard_map/ppermute | solution.py:20
  38.5 48.6 %collective-permute-start.18 = (bf16[3,96,512]{2,1,0:T(8,128)(2,1)S(1)}, bf16[3,96,512]{2,1,0:T(8,128)(2,1)S(1)}, u32[]{:S(2)}, u32[]{:S(2)}) collective-permute-start(bf16[3,96,512]{2,1,0:T(8,128)(2,1)S(1)} %pad_maximum_fusion.19), channel_id=1, source_target_pairs={{0,24},{4,28},{8,16},{12,20},{16,8},{20,12},{24,0},{28,4},{1,25},{... | collective-permute-start | bytes 884744 | tf_op jit(solution)/shard_map/ppermute | solution.py:37
  41.0 48.7 %collective-permute-start.17 = (bf16[3,96,512]{2,1,0:T(8,128)(2,1)S(1)}, bf16[3,96,512]{2,1,0:T(8,128)(2,1)S(1)}, u32[]{:S(2)}, u32[]{:S(2)}) collective-permute-start(bf16[3,96,512]{2,1,0:T(8,128)(2,1)S(1)} %pad_maximum_fusion.19), channel_id=1, source_target_pairs={{0,16},{4,20},{8,24},{12,28},{16,0},{20,4},{24,8},{28,12},{1,17},{... | collective-permute-start | bytes 884744 | tf_op jit(solution)/shard_map/ppermute | solution.py:37
  59.4 17.3 %collective-permute-start.9 = (bf16[24,2176]{1,0:T(8,128)(2,1)S(1)}, bf16[24,2176]{1,0:T(8,128)(2,1)S(1)}, u32[]{:S(2)}, u32[]{:S(2)}) collective-permute-start(bf16[24,2176]{1,0:T(8,128)(2,1)S(1)} %get-tuple-element.48), channel_id=1, source_target_pairs={{0,3},{1,0},{2,1},{3,2},{4,7},{5,4},{6,5},{7,6},{8,11},{9,8},{10,9... | collective-permute-start | bytes 313352 | tf_op jit(solution)/shard_map/ppermute | solution.py:20
  61.3 16.4 %collective-permute-start.11 = (bf16[24,2176]{1,0:T(8,128)(2,1)S(1)}, bf16[24,2176]{1,0:T(8,128)(2,1)S(1)}, u32[]{:S(2)}, u32[]{:S(2)}) collective-permute-start(bf16[24,2176]{1,0:T(8,128)(2,1)S(1)} %get-tuple-element.49), channel_id=1, source_target_pairs={{0,1},{1,2},{2,3},{3,0},{4,5},{5,6},{6,7},{7,4},{8,9},{9,10},{10,1... | collective-permute-start | bytes 313352 | tf_op jit(solution)/shard_map/ppermute | solution.py:20
  63.9 14.9 %collective-permute-start.10 = (bf16[24,2176]{1,0:T(8,128)(2,1)S(1)}, bf16[24,2176]{1,0:T(8,128)(2,1)S(1)}, u32[]{:S(2)}, u32[]{:S(2)}) collective-permute-start(bf16[24,2176]{1,0:T(8,128)(2,1)S(1)} %get-tuple-element.50), channel_id=1, source_target_pairs={{0,2},{1,3},{2,0},{3,1},{4,6},{5,7},{6,4},{7,5},{8,10},{9,11},{10,... | collective-permute-start | bytes 313352 | tf_op jit(solution)/shard_map/ppermute | solution.py:20
  82.0 18.9 %collective-permute-start.26 = (bf16[3,96,512]{2,1,0:T(8,128)(2,1)S(1)}, bf16[3,96,512]{2,1,0:T(8,128)(2,1)S(1)}, u32[]{:S(2)}, u32[]{:S(2)}) collective-permute-start(bf16[3,96,512]{2,1,0:T(8,128)(2,1)S(1)} %pad_maximum_fusion.20), channel_id=1, source_target_pairs={{0,24},{4,28},{8,16},{12,20},{16,8},{20,12},{24,0},{28,4},{1,25},{... | collective-permute-start | bytes 884744 | tf_op jit(solution)/shard_map/ppermute | solution.py:37
  84.3 17.2 %collective-permute-start.25 = (bf16[3,96,512]{2,1,0:T(8,128)(2,1)S(1)}, bf16[3,96,512]{2,1,0:T(8,128)(2,1)S(1)}, u32[]{:S(2)}, u32[]{:S(2)}) collective-permute-start(bf16[3,96,512]{2,1,0:T(8,128)(2,1)S(1)} %pad_maximum_fusion.20), channel_id=1, source_target_pairs={{0,16},{4,20},{8,24},{12,28},{16,0},{20,4},{24,8},{28,12},{1,17},{... | collective-permute-start | bytes 884744 | tf_op jit(solution)/shard_map/ppermute | solution.py:37
  86.5 15.0 %collective-permute-start.24 = (bf16[3,96,512]{2,1,0:T(8,128)(2,1)S(1)}, bf16[3,96,512]{2,1,0:T(8,128)(2,1)S(1)}, u32[]{:S(2)}, u32[]{:S(2)}) collective-permute-start(bf16[3,96,512]{2,1,0:T(8,128)(2,1)S(1)} %pad_maximum_fusion.20), channel_id=1, source_target_pairs={{0,8},{4,12},{8,0},{12,4},{16,24},{20,28},{24,16},{28,20},{1,9},{5... | collective-permute-start | bytes 884744 | tf_op jit(solution)/shard_map/ppermute | solution.py:37
  87.0 13.8 %collective-permute-start.16 = (bf16[3,96,512]{2,1,0:T(8,128)(2,1)S(1)}, bf16[3,96,512]{2,1,0:T(8,128)(2,1)S(1)}, u32[]{:S(2)}, u32[]{:S(2)}) collective-permute-start(bf16[3,96,512]{2,1,0:T(8,128)(2,1)S(1)} %pad_maximum_fusion.19), channel_id=1, source_target_pairs={{0,8},{4,12},{8,0},{12,4},{16,24},{20,28},{24,16},{28,20},{1,9},{5... | collective-permute-start | bytes 884744 | tf_op jit(solution)/shard_map/ppermute | solution.py:37
  89.7 12.0 %collective-permute-start.20 = (bf16[4,2,96,256]{3,2,1,0:T(8,128)(2,1)S(1)}, bf16[4,2,96,256]{3,2,1,0:T(8,128)(2,1)S(1)}, u32[]{:S(2)}, u32[]{:S(2)}) collective-permute-start(bf16[4,2,96,256]{3,2,1,0:T(8,128)(2,1)S(1)} %pad_maximum_fusion.18), channel_id=1, source_target_pairs={{0,4},{4,0},{8,12},{12,8},{16,20},{20,16},{24,28},{28,24},{1,5},{5... | collective-permute-start | bytes 1179656 | tf_op jit(solution)/shard_map/ppermute | solution.py:55
  100.9 23.6 %collective-permute-start.19 = (bf16[3,384,512]{2,1,0:T(8,128)(2,1)S(1)}, bf16[3,384,512]{2,1,0:T(8,128)(2,1)S(1)}, u32[]{:S(2)}, u32[]{:S(2)}) collective-permute-start(bf16[3,384,512]{2,1,0:T(8,128)(2,1)S(1)} %pad_maximum_fusion), channel_id=1, source_target_pairs={{0,4},{4,0},{8,12},{12,8},{16,20},{20,16},{24,28},{28,24},{1,5},{5... | collective-permute-start | bytes 3538952 | tf_op jit(solution)/shard_map/ppermute | solution.py:40
  101.6 21.8 %collective-permute-start.27 = (bf16[3,384,512]{2,1,0:T(8,128)(2,1)S(1)}, bf16[3,384,512]{2,1,0:T(8,128)(2,1)S(1)}, u32[]{:S(2)}, u32[]{:S(2)}) collective-permute-start(bf16[3,384,512]{2,1,0:T(8,128)(2,1)S(1)} %pad_maximum_fusion.1), channel_id=1, source_target_pairs={{0,4},{4,0},{8,12},{12,8},{16,20},{20,16},{24,28},{28,24},{1,5},{5... | collective-permute-start | bytes 3538952 | tf_op jit(solution)/shard_map/ppermute | solution.py:40
  101.8 7.8 %collective-permute-start.21 = (bf16[2,2,96,256]{3,2,0,1:T(8,128)(2,1)S(1)}, bf16[2,2,96,256]{3,2,0,1:T(8,128)(2,1)S(1)}, u32[]{:S(2)}, u32[]{:S(2)}) collective-permute-start(bf16[2,2,96,256]{3,2,0,1:T(8,128)(2,1)S(1)} %pad_maximum_fusion.24), channel_id=1, source_target_pairs={{0,8},{4,12},{8,0},{12,4},{16,24},{20,28},{24,16},{28,20},{1,9},{5... | collective-permute-start | bytes 589832 | tf_op jit(solution)/shard_map/ppermute | solution.py:58
  102.4 10.3 %collective-permute-start.22 = (bf16[2,2,96,256]{3,2,0,1:T(8,128)(2,1)S(1)}, bf16[2,2,96,256]{3,2,0,1:T(8,128)(2,1)S(1)}, u32[]{:S(2)}, u32[]{:S(2)}) collective-permute-start(bf16[2,2,96,256]{3,2,0,1:T(8,128)(2,1)S(1)} %pad_maximum_fusion.25), channel_id=1, source_target_pairs={{0,16},{4,20},{8,24},{12,28},{16,0},{20,4},{24,8},{28,12},{1,17},{... | collective-permute-start | bytes 589832 | tf_op jit(solution)/shard_map/ppermute | solution.py:58
  104.0 11.4 %collective-permute-start.23 = (bf16[2,2,96,256]{3,2,1,0:T(8,128)(2,1)S(1)}, bf16[2,2,96,256]{3,2,1,0:T(8,128)(2,1)S(1)}, u32[]{:S(2)}, u32[]{:S(2)}) collective-permute-start(bf16[2,2,96,256]{3,2,1,0:T(8,128)(2,1)S(1)} %pad_maximum_fusion.26), channel_id=1, source_target_pairs={{0,24},{4,28},{8,16},{12,20},{16,8},{20,12},{24,0},{28,4},{1,25},{... | collective-permute-start | bytes 589832 | tf_op jit(solution)/shard_map/ppermute | solution.py:58
  109.5 8.5 %collective-permute-start.13 = (bf16[2,2,96,256]{3,2,0,1:T(8,128)(2,1)S(1)}, bf16[2,2,96,256]{3,2,0,1:T(8,128)(2,1)S(1)}, u32[]{:S(2)}, u32[]{:S(2)}) collective-permute-start(bf16[2,2,96,256]{3,2,0,1:T(8,128)(2,1)S(1)} %pad_maximum_fusion.21), channel_id=1, source_target_pairs={{0,8},{4,12},{8,0},{12,4},{16,24},{20,28},{24,16},{28,20},{1,9},{5... | collective-permute-start | bytes 589832 | tf_op jit(solution)/shard_map/ppermute | solution.py:58
  112.6 10.7 %collective-permute-start.14 = (bf16[2,2,96,256]{3,2,0,1:T(8,128)(2,1)S(1)}, bf16[2,2,96,256]{3,2,0,1:T(8,128)(2,1)S(1)}, u32[]{:S(2)}, u32[]{:S(2)}) collective-permute-start(bf16[2,2,96,256]{3,2,0,1:T(8,128)(2,1)S(1)} %pad_maximum_fusion.22), channel_id=1, source_target_pairs={{0,16},{4,20},{8,24},{12,28},{16,0},{20,4},{24,8},{28,12},{1,17},{... | collective-permute-start | bytes 589832 | tf_op jit(solution)/shard_map/ppermute | solution.py:58
  115.4 7.9 %collective-permute-start.15 = (bf16[2,2,96,256]{3,2,1,0:T(8,128)(2,1)S(1)}, bf16[2,2,96,256]{3,2,1,0:T(8,128)(2,1)S(1)}, u32[]{:S(2)}, u32[]{:S(2)}) collective-permute-start(bf16[2,2,96,256]{3,2,1,0:T(8,128)(2,1)S(1)} %pad_maximum_fusion.23), channel_id=1, source_target_pairs={{0,24},{4,28},{8,16},{12,20},{16,8},{20,12},{24,0},{28,4},{1,25},{... | collective-permute-start | bytes 589832 | tf_op jit(solution)/shard_map/ppermute | solution.py:58
  (9 other events, 53.7 us)

commit v3 on v1

v3 whole, which is shorter than its diff:
```python
import functools
import math

import jax
import jax.numpy as jnp
from jax import lax
from jax.experimental import pallas as pl
from jax.experimental.pallas import tpu as pltpu
from jax.sharding import PartitionSpec as P

HOT = 4
CAP = 48
LANES = 128
BLOCK = 256
MIB = 1 << 20

highest = lax.Precision.HIGHEST
f32 = jnp.float32
bf16 = jnp.bfloat16
i32 = jnp.int32
VMEM = pl.BlockSpec(memory_space=pltpu.VMEM)
SMEM = pl.BlockSpec(memory_space=pltpu.SMEM)


def shifted(values, axis, by):
    size = lax.axis_size(axis)
    return lax.ppermute(values, axis, [(i, (i + by) % size) for i in range(size)])


def flipped(values, axis, mask):
    size = lax.axis_size(axis)
    return lax.ppermute(values, axis, [(i, i ^ mask) for i in range(size)])


def cost(flops, moved):
    return pl.CostEstimate(flops=int(flops), bytes_accessed=int(moved), transcendentals=0)


def place_kernel(n_expert, me_ref, route_ref, prob_ref, tok_ref, placing_ref, *pieces):
    quarters = n_expert // HOT
    count, width = tok_ref.shape
    route = route_ref[...]
    hot = (route == lax.broadcasted_iota(i32, (16, count), 0)).astype(f32)
    before = lax.broadcasted_iota(i32, (count, count), 0) < lax.broadcasted_iota(i32, (count, count), 1)
    earlier = jnp.dot(hot.astype(bf16), before.astype(f32).astype(bf16), preferred_element_type=f32)
    rank = jnp.sum(earlier * hot, axis=0, keepdims=True).astype(i32)
    slot = lax.broadcasted_iota(i32, (CAP, count), 0)
    prob = prob_ref[...].astype(f32)
    for k in range(n_expert):
        owner = lax.rem(me_ref[0] + k, n_expert) // quarters
        block = jnp.where((route == owner) & (rank == slot), 1.0, 0.0)
        placing_ref[k * CAP : (k + 1) * CAP, :] = block.astype(bf16)
        slot_prob = jnp.sum(block * prob, axis=1, keepdims=True)
        pieces[k][:, width:] = jnp.broadcast_to(slot_prob, (CAP, LANES)).astype(bf16)
    for at in range(0, width, 512):
        part = jnp.dot(placing_ref[...], tok_ref[:, at : at + 512], preferred_element_type=f32)
        part = part.astype(bf16)
        for k in range(n_expert):
            pieces[k][:, at : at + 512] = part[k * CAP : (k + 1) * CAP]


def place(me, route, prob, tokens, n_expert):
    count, width = tokens.shape
    piece = jax.ShapeDtypeStruct((CAP, width + LANES), bf16)
    outs = pl.pallas_call(
        functools.partial(place_kernel, n_expert),
        out_shape=[jax.ShapeDtypeStruct((n_expert * CAP, count), bf16)] + [piece] * n_expert,
        in_specs=[SMEM, VMEM, VMEM, VMEM],
        out_specs=[VMEM] * (n_expert + 1),
        cost_estimate=cost(2 * n_expert * CAP * count * width, 2 * MIB),
    )(me.reshape(1), route.reshape(1, count), prob.reshape(1, count), tokens)
    return outs[0], outs[1:]


def split_kernel(*refs):
    half = len(refs) // 3
    for i in range(half):
        whole = refs[i][...]
        high = whole.astype(bf16)
        refs[half + 2 * i][...] = high
        refs[half + 2 * i + 1][...] = (whole - high.astype(f32)).astype(bf16)


def split_weights(*weights):
    depth, units = weights[0].shape
    spec = pl.BlockSpec((BLOCK, units), lambda i: (i, 0))
    return pl.pallas_call(
        split_kernel,
        grid=(depth // BLOCK,),
        out_shape=[jax.ShapeDtypeStruct((depth, units), bf16)] * (2 * len(weights)),
        in_specs=[spec] * len(weights),
        out_specs=[spec] * (2 * len(weights)),
        cost_estimate=cost(0, 8 * depth * units * len(weights)),
    )(*weights)


def forward_kernel(n_expert, *refs):
    pieces = refs[:n_expert]
    gate_hi, gate_lo, up_hi, up_lo = refs[n_expert : n_expert + 4]
    act_ref, slope_ref, hidden_ref, share_ref = refs[n_expert + 4 : n_expert + 8]
    rows, gate_sum, up_sum = refs[n_expert + 8 :]
    step = pl.program_id(0)
    width = pieces[0].shape[1] - LANES

    @pl.when(step == 0)
    def _():
        gate_sum[...] = jnp.zeros_like(gate_sum)
        up_sum[...] = jnp.zeros_like(up_sum)

    for k in range(n_expert):
        rows[k * CAP : (k + 1) * CAP, :] = pieces[k][:, pl.ds(pl.multiple_of(step * BLOCK, BLOCK), BLOCK)]
    row = rows[...]
    gate_sum[...] += jnp.dot(row, gate_hi[...], preferred_element_type=f32) + jnp.dot(
        row, gate_lo[...], preferred_element_type=f32
    )
    up_sum[...] += jnp.dot(row, up_hi[...], preferred_element_type=f32) + jnp.dot(
        row, up_lo[...], preferred_element_type=f32
    )

    @pl.when(step == pl.num_programs(0) - 1)
    def _():
        for k in range(n_expert):
            part = slice(k * CAP, (k + 1) * CAP)
            prob = pieces[k][:, width:].astype(f32)[:, :1]
            gate = gate_sum[part, :]
            up = up_sum[part, :]
            sig = jax.nn.sigmoid(gate)
            act = gate * sig
            hidden = act * up
            act_ref[part, :] = prob * act
            slope_ref[part, :] = prob * (up * sig * (1.0 + gate * (1.0 - sig)))
            hidden_ref[part, :] = hidden
            share_ref[part, :] = (prob * hidden).astype(bf16)


def forward(pieces, weights):
    n_expert = len(pieces)
    depth, units = weights[0].shape
    count = n_expert * CAP
    whole = pl.BlockSpec((CAP, depth + LANES), lambda i: (0, 0))
    block = pl.BlockSpec((BLOCK, units), lambda i: (i, 0))
    out = pl.BlockSpec((count, units), lambda i: (0, 0))
    shape = jax.ShapeDtypeStruct((count, units), f32)
    return pl.pallas_call(
        functools.partial(forward_kernel, n_expert),
        grid=(depth // BLOCK,),
        out_shape=[shape] * 3 + [jax.ShapeDtypeStruct((count, units), bf16)],
        in_specs=[whole] * n_expert + [block] * 4,
        out_specs=[out] * 4,
        scratch_shapes=[
            pltpu.VMEM((count, BLOCK), bf16),
            pltpu.VMEM((count, units), f32),
            pltpu.VMEM((count, units), f32),
        ],
        compiler_params=pltpu.CompilerParams(vmem_limit_bytes=24 * MIB),
        cost_estimate=cost(8 * count * depth * units, 8 * depth * units),
    )(*pieces, *weights)


def backward_kernel(n_expert, *refs):
    pieces = refs[:n_expert]
    down_hi, down_lo, act_ref, slope_ref, hidden_ref = refs[n_expert : n_expert + 5]
    high_ref, low_ref, prob_ref = refs[n_expert + 5 : n_expert + 8]
    rows, back_sum = refs[n_expert + 8 :]
    step = pl.program_id(0)
    units = down_hi.shape[1]

    @pl.when(step == 0)
    def _():
        back_sum[...] = jnp.zeros_like(back_sum)

    for k in range(n_expert):
        rows[k * CAP : (k + 1) * CAP, :] = pieces[k][:, pl.ds(pl.multiple_of(step * BLOCK, BLOCK), BLOCK)]
    row = rows[...]
    back_sum[...] += jnp.dot(row, down_hi[...], preferred_element_type=f32) + jnp.dot(
        row, down_lo[...], preferred_element_type=f32
    )

    @pl.when(step == pl.num_programs(0) - 1)
    def _():
        for k in range(n_expert):
            part = slice(k * CAP, (k + 1) * CAP)
            back = back_sum[part, :]
            total = jnp.sum(hidden_ref[part, :] * back, axis=1, keepdims=True)
            prob_ref[part, :] = jnp.broadcast_to(total, (CAP, LANES))
            for at, factor in ((0, slope_ref), (units, act_ref)):
                grad = factor[part, :] * back
                high = grad.astype(bf16)
                high_ref[part, at : at + units] = high
                low_ref[part, at : at + units] = (grad - high.astype(f32)).astype(bf16)


def backward(pieces, weights, act, slope, hidden):
    n_expert = len(pieces)
    depth, units = weights[0].shape
    count = n_expert * CAP
    whole = pl.BlockSpec((CAP, depth), lambda i: (0, 0))
    block = pl.BlockSpec((BLOCK, units), lambda i: (i, 0))

    def full(width):
        return pl.BlockSpec((count, width), lambda i: (0, 0))

    return pl.pallas_call(
        functools.partial(backward_kernel, n_expert),
        grid=(depth // BLOCK,),
        out_shape=[jax.ShapeDtypeStruct((count, 2 * units), bf16)] * 2
        + [jax.ShapeDtypeStruct((count, LANES), f32)],
        in_specs=[whole] * n_expert + [block] * 2 + [full(units)] * 3,
        out_specs=[full(2 * units)] * 2 + [full(LANES)],
        scratch_shapes=[pltpu.VMEM((count, BLOCK), bf16), pltpu.VMEM((count, units), f32)],
        compiler_params=pltpu.CompilerParams(vmem_limit_bytes=24 * MIB),
        cost_estimate=cost(4 * count * depth * units, 4 * depth * units),
    )(*pieces, *weights, act, slope, hidden)


def input_kernel(n_expert, *refs):
    high_ref, low_ref, prob_ref, gate_hi, gate_lo, up_hi, up_lo = refs[:7]
    pieces = refs[7:]
    step = pl.program_id(0)
    units = gate_hi.shape[1]
    width = pieces[0].shape[1] - LANES

    def against(left, right):
        return lax.dot_general(left, right, (((1,), (1,)), ((), ())), preferred_element_type=f32)

    grad_hi, grad_lo = high_ref[:, :units], low_ref[:, :units]
    total = against(grad_hi, gate_hi[...]) + against(grad_lo, gate_hi[...])
    total += against(grad_hi, gate_lo[...])
    grad_hi, grad_lo = high_ref[:, units:], low_ref[:, units:]
    total += against(grad_hi, up_hi[...]) + against(grad_lo, up_hi[...])
    total += against(grad_hi, up_lo[...])
    for k in range(n_expert):
        part = slice(k * CAP, (k + 1) * CAP)
        here = pl.ds(pl.multiple_of(step * BLOCK, BLOCK), BLOCK)
        pieces[k][:, here] = total[part].astype(pieces[k].dtype)

    @pl.when(step == 0)
    def _():
        for k in range(n_expert):
            pieces[k][:, width:] = prob_ref[k * CAP : (k + 1) * CAP, :].astype(pieces[k].dtype)


def input_gradient(high, low, prob_part, weights, n_expert, back_type):
    depth, units = weights[0].shape
    count = n_expert * CAP
    block = pl.BlockSpec((BLOCK, units), lambda i: (i, 0))

    def full(rows, width):
        return pl.BlockSpec((rows, width), lambda i: (0, 0))

    return pl.pallas_call(
        functools.partial(input_kernel, n_expert),
        grid=(depth // BLOCK,),
        out_shape=[jax.ShapeDtypeStruct((CAP, depth + LANES), back_type)] * n_expert,
        in_specs=[full(count, 2 * units)] * 2 + [full(count, LANES)] + [block] * 4,
        out_specs=[full(CAP, depth + LANES)] * n_expert,
        compiler_params=pltpu.CompilerParams(vmem_limit_bytes=24 * MIB),
        cost_estimate=cost(12 * count * depth * units, 8 * depth * units),
    )(high, low, prob_part, *weights)


def take_kernel(n_expert, placing_ref, *refs):
    pieces = refs[:n_expert]
    out_ref, prob_ref, rows = refs[n_expert:]
    count, width = out_ref.shape
    exact = rows.dtype != bf16
    for k in range(n_expert):
        rows[k * CAP : (k + 1) * CAP, :] = pieces[k][...]
    placing = placing_ref[...].astype(rows.dtype)
    for at in range(0, width, 512):
        part = lax.dot_general(
            placing, rows[:, at : at + 512], (((0,), (0,)), ((), ())),
            precision=highest if exact else None, preferred_element_type=f32,
        )
        out_ref[:, at : at + 512] = part.astype(bf16)
    column = rows[:, width:].astype(f32)[:, :1]
    prob_ref[...] = jnp.sum(placing_ref[...].astype(f32) * column, axis=0, keepdims=True).astype(bf16)


def take(placing, pieces):
    n_expert = len(pieces)
    count = placing.shape[1]
    width = pieces[0].shape[1] - LANES
    grad, prob = pl.pallas_call(
        functools.partial(take_kernel, n_expert),
        out_shape=[
            jax.ShapeDtypeStruct((count, width), bf16),
            jax.ShapeDtypeStruct((1, count), bf16),
        ],
        in_specs=[VMEM] * (n_expert + 1),
        out_specs=[VMEM] * 2,
        scratch_shapes=[pltpu.VMEM((n_expert * CAP, width + LANES), pieces[0].dtype)],
        compiler_params=pltpu.CompilerParams(vmem_limit_bytes=32 * MIB),
        cost_estimate=cost(2 * n_expert * CAP * count * width, 2 * MIB),
    )(placing, *pieces)
    return grad, prob.reshape(count)


def in_plane(rows, terms):
    size = lax.axis_size("dp")
    share = rows.shape[1] // size
    units = terms.shape[1]
    at = lax.axis_index("dp")
    chips = range(size // 2)

    def part(to):
        return lax.dynamic_slice_in_dim(rows, to * share, share, axis=1)

    theirs = flipped(jnp.stack([part((at ^ 1) ^ (2 * k)) for k in chips]), "dp", 1)
    payload = [
        jnp.concatenate([part(at ^ (2 * k)), theirs[k], terms], axis=1) for k in chips
    ]
    got = [payload[0]] + [flipped(payload[k], "dp", 2 * k) for k in chips[1:]]
    own_cols = jnp.concatenate([g[:, :share] for g in got])
    other_cols = jnp.concatenate([g[:, share : 2 * share] for g in got])
    own_terms = jnp.concatenate([g[:, 2 * share :] for g in got])
    other_terms = flipped(own_terms, "dp", 1)
    return own_cols, other_cols, own_terms, other_terms


def over_rows(own_cols, other_cols, own_terms, other_terms, scale):
    def dot(cols, term):
        return lax.dot_general(cols, term, (((0,), (0,)), ((), ())), preferred_element_type=f32)

    return ((dot(own_cols, own_terms) + dot(other_cols, other_terms)) * scale)[None]


def shards(tokens, cotangent, route, prob, w_gate, w_up, w_down):
    n_expert = lax.axis_size("expert")
    n_dp = lax.axis_size("dp")
    width = tokens.shape[1]
    units = w_gate.shape[2]
    scale = 1.0 / math.sqrt(tokens.shape[0] * n_dp * n_expert)
    back_type = bf16 if n_expert == HOT else f32
    me = lax.axis_index("expert").astype(i32)

    placing, slot_tok = place(me, route, prob, tokens, n_expert)
    tok_pieces = [slot_tok[0]] + [shifted(slot_tok[k], "expert", k) for k in range(1, n_expert)]

    weights, _ = lax.optimization_barrier(((w_gate[0], w_up[0], w_down[0]), slot_tok[0]))
    gate_hi, gate_lo, up_hi, up_lo, down_hi, down_lo = split_weights(*weights)
    (late_cot, _) = lax.optimization_barrier((cotangent, down_lo))
    slot_cot = jnp.dot(placing, late_cot, preferred_element_type=f32).astype(bf16)
    slot_cot = slot_cot.reshape(n_expert, CAP, width)
    cot_pieces = [slot_cot[0]] + [shifted(slot_cot[k], "expert", k) for k in range(1, n_expert)]

    act, slope, hidden, weighted = forward(tok_pieces, (gate_hi, gate_lo, up_hi, up_lo))
    row_tok = jnp.concatenate([p[:, :width] for p in tok_pieces])
    tok_own, tok_other, weighted_own, weighted_other = in_plane(row_tok, weighted)

    cot_pieces, act = lax.optimization_barrier((cot_pieces, act))
    high, low, prob_part = backward(cot_pieces, (down_hi, down_lo), act, slope, hidden)
    row_cot = jnp.concatenate(cot_pieces)
    cot_own, cot_other, grads_own, grads_other = in_plane(row_cot, high)
    back = input_gradient(
        high, low, prob_part, (gate_hi, gate_lo, up_hi, up_lo), n_expert, back_type
    )
    home = [back[0]] + [shifted(back[k], "expert", n_expert - k) for k in range(1, n_expert)]
    grad_input, grad_prob = take(placing, home)

    return (
        grad_input,
        grad_prob,
        over_rows(tok_own, tok_other, grads_own[:, :units], grads_other[:, :units], scale),
        over_rows(tok_own, tok_other, grads_own[:, units:], grads_other[:, units:], scale),
        over_rows(cot_own, cot_other, weighted_own, weighted_other, scale),
    )


def solution(mesh):
    placed = (
        P(("dp", "expert"), None),
        P(("dp", "expert"), None),
        P(("dp", "expert"), None),
        P(("dp", "expert")),
        P("expert", None, None),
        P("expert", None, None),
        P("expert", None, None),
    )
    return jax.shard_map(
        shards,
        mesh=mesh,
        in_specs=placed,
        out_specs=(
            P(("dp", "expert"), None),
            P(("dp", "expert")),
            P("expert", "dp", None),
            P("expert", "dp", None),
            P("expert", "dp", None),
        ),
        check_vma=False,
    )
```

time: 124 us -> 114 us (0.919)
  Pallas kernels: 0 us -> 27 us
  matrix products: 28.7 us -> 5.11 us
  between operations: 14.3 us -> 1.05 us
  local copies, waits for them, and re-layouts: 2.98 us -> 12.8 us
  waiting for transfers between devices: 49.6 us -> 41.3 us
  other arithmetic: 3.91 us -> 0.6 us
  starting transfers between devices: 24.4 us -> 26 us
    pallas_call x0 -> x6, Pallas kernels: none -> 27 us  [the longest x1 10.9 us: split_weights(): pl.pallas_call(split_kernel, grid=(depth // BLOCK,), out_shape=[jax.Shape...]
    ppermute x0 -> x10, waiting for transfers between devices: none -> 24.8 us  [flipped(): return lax.ppermute(values, axis, [(i, i ^ mask) for i in range(size)])]
    dot_general x11 -> x7, matrix products: 28.7 us -> 5.11 us  [the longest x6 4.75 us: dot(): lax.dot_general(cols, term, (((0,), (0,)), ((), ())), preferred_element_t...]
    ppermute x9, waiting for transfers between devices: 33.6 us -> 16.5 us  [shifted(): lax.ppermute(values, axis, [(i, (i + by) % size) for i in range(size)])]
    all_gather x1 -> x0, waiting for transfers between devices: 15.5 us -> none  [shards(): all_terms = lax.all_gather(terms, 'dp', axis=1, tiled=True)]
    ppermute x0 -> x10, starting transfers between devices: none -> 8.75 us  [flipped(): return lax.ppermute(values, axis, [(i, i ^ mask) for i in range(size)])]
    unnamed x18 -> x29, local copies, waits for them, and re-layouts: 0.21 us -> 8.85 us
    all_to_all x2 -> x0, starting transfers between devices: 7.45 us -> none  [the longest x1 3.73 us: shards(): lax.all_to_all(row_tok.reshape(rows, n_dp, width // n_dp).transpose(1, 0,...]
  transfers between devices with their start and end apart: 12 -> 19, of which waited for: 5 -> 6; matrix products, arithmetic and copies ran while one was open for 19% -> 5% of each run, Pallas kernels for 0% -> 22%
where the time goes in v3:
time: 114 us
  waiting for transfers between devices  41.3 us (36%)
  Pallas kernels  27 us (24%)
  starting transfers between devices  26 us (23%)
  local copies, waits for them, and re-layouts  12.8 us (11%)
  matrix products  5.11 us (4%)
    ppermute x10, waiting for transfers between devices, flipped(): return lax.ppermute(values, axis, [(i, i ^ mask) for i in range(size)])  24.8 us
    ppermute x9, starting transfers between devices, shifted(): lax.ppermute(values, axis, [(i, (i + by) % size) for i in range(size)])  17.2 us
    ppermute x9, waiting for transfers between devices, shifted(): lax.ppermute(values, axis, [(i, (i + by) % size) for i in range(size)])  16.5 us
    pallas_call x1, Pallas kernels, split_weights(): pl.pallas_call(split_kernel, grid=(depth // BLOCK,), out_shape=[jax.Shape...  10.9 us
    unnamed x29, local copies, waits for them, and re-layouts  8.85 us
    ppermute x10, starting transfers between devices, flipped(): return lax.ppermute(values, axis, [(i, i ^ mask) for i in range(size)])  8.75 us
    pallas_call x1, Pallas kernels, input_gradient(): pl.pallas_call(functools.partial(input_kernel, n_expert), grid=(depth //...  5.42 us
    dot_general x6, matrix products, dot(): lax.dot_general(cols, term, (((0,), (0,)), ((), ())), preferred_element_t...  4.75 us
  transfers between devices with their start and end apart: 19, of which 6 were waited for; matrix products, arithmetic and copies ran while one was open for 5% of the time, Pallas kernels for 22%

profile of v3, /device:TPU:0, one launch (start us, length us, event | category | flops | bytes accessed | tf_op | source)
XLA Modules:
  0.0 113.9 jit_solution(1992989496513690494)
XLA Ops:
  0.7 2.5 %shard_map.110 = (bf16[192,128]{1,0:T(8,128)(2,1)}, bf16[48,2176]{1,0:T(8,128)(2,1)}, bf16[48,2176]{1,0:T(8,128)(2,1)}, bf16[48,2176]{1,0:T(8,128)(2,1)}, bf16[48,2176]{1,0:T(8,128)(2,1)}) custom-call(s32[1]{0:T(128)} %bitcast.me_ref, s32[1,128]{1,0:T(1,128)} %bitcast.51, bf16[1,128]{1,0:T(2,128)(2,1)} %bitcast.52, bf16[128,2048]{1,0:T(8,128)(2,1)} %tok_ref.1), custom_call_target="tpu_custom_call" | custom-call | flops 100663296 | bytes 2097152 | tf_op jit(solution)/shard_map/pallas_call | solution.py:65
  3.1 3.0 %collective-permute-start.3 = (bf16[48,2176]{1,0:T(8,128)(2,1)}, bf16[48,2176]{1,0:T(8,128)(2,1)S(1)}, u32[]{:S(2)}, u32[]{:S(2)}) collective-permute-start(bf16[48,2176]{1,0:T(8,128)(2,1)} %get-tuple-element.45), channel_id=1, source_target_pairs={{0,1},{1,2},{2,3},{3,0},{4,5},{5,6},{6,7},{7,4},{8,9},{9,10},{10,1... | collective-permute-start | bytes 626696 | tf_op jit(solution)/shard_map/ppermute | solution.py:27
  6.1 2.6 %collective-permute-start.4 = (bf16[48,2176]{1,0:T(8,128)(2,1)}, bf16[48,2176]{1,0:T(8,128)(2,1)S(1)}, u32[]{:S(2)}, u32[]{:S(2)}) collective-permute-start(bf16[48,2176]{1,0:T(8,128)(2,1)} %get-tuple-element.46), channel_id=1, source_target_pairs={{0,2},{1,3},{2,0},{3,1},{4,6},{5,7},{6,4},{7,5},{8,10},{9,11},{10,... | collective-permute-start | bytes 626696 | tf_op jit(solution)/shard_map/ppermute | solution.py:27
  8.7 1.3 %collective-permute-start.5 = (bf16[48,2176]{1,0:T(8,128)(2,1)}, bf16[48,2176]{1,0:T(8,128)(2,1)S(1)}, u32[]{:S(2)}, u32[]{:S(2)}) collective-permute-start(bf16[48,2176]{1,0:T(8,128)(2,1)} %get-tuple-element.47), channel_id=1, source_target_pairs={{0,3},{1,0},{2,1},{3,2},{4,7},{5,4},{6,5},{7,6},{8,11},{9,8},{10,9... | collective-permute-start | bytes 626696 | tf_op jit(solution)/shard_map/ppermute | solution.py:27
  10.1 10.9 %shard_map.111 = (bf16[2048,512]{1,0:T(8,128)(2,1)}, bf16[2048,512]{1,0:T(8,128)(2,1)}, bf16[2048,512]{1,0:T(8,128)(2,1)}, bf16[2048,512]{1,0:T(8,128)(2,1)}, bf...) custom-call(f32[2048,512]{1,0:T(8,128)} %bitcast.48, f32[2048,512]{1,0:T(8,128)} %bitcast.49, f32[2048,512]{1,0:T(8,128)} %bitcast.50), custom_call_target="tpu_custom_call" | custom-call | bytes 25165824 | tf_op jit(solution)/shard_map/pallas_call | solution.py:87
  23.2 2.8 %collective-permute-start.2 = (bf16[48,2048]{1,0:T(8,128)(2,1)}, bf16[48,2048]{1,0:T(8,128)(2,1)}, u32[]{:S(2)}, u32[]{:S(2)}) collective-permute-start(bf16[48,2048]{1,0:T(8,128)(2,1)} %get-tuple-element.87), channel_id=1, source_target_pairs={{0,3},{1,0},{2,1},{3,2},{4,7},{5,4},{6,5},{7,6},{8,11},{9,8},{10,9... | collective-permute-start | bytes 589832 | tf_op jit(solution)/shard_map/ppermute | solution.py:27
  26.0 1.6 %slice.122 = bf16[48,2048]{1,0:T(8,128)(2,1)} slice(bf16[48,2176]{1,0:T(8,128)(2,1)} %get-tuple-element.39.refs_0_), slice={[0:48], [0:2048]} | slice | bytes 393216 | tf_op jit(solution)/shard_map/slice | solution.py:348
  27.7 1.6 %copy-done.2 = bf16[2048,512]{1,0:T(8,128)(2,1)S(1)} copy-done((bf16[2048,512]{1,0:T(8,128)(2,1)S(1)}, bf16[2048,512]{1,0:T(8,128)(2,1)}, u32[]{:S(2)}) %copy-start.2) | copy-done | bytes 2097176
  29.2 1.6 %copy-done.4 = bf16[2048,512]{1,0:T(8,128)(2,1)S(1)} copy-done((bf16[2048,512]{1,0:T(8,128)(2,1)S(1)}, bf16[2048,512]{1,0:T(8,128)(2,1)}, u32[]{:S(2)}) %copy-start.4) | copy-done | bytes 2097176
  30.8 1.6 %copy-done.6 = bf16[2048,512]{1,0:T(8,128)(2,1)S(1)} copy-done((bf16[2048,512]{1,0:T(8,128)(2,1)S(1)}, bf16[2048,512]{1,0:T(8,128)(2,1)}, u32[]{:S(2)}) %copy-start.6) | copy-done | bytes 2097176
  33.4 3.4 %shard_map.112 = (f32[192,512]{1,0:T(8,128)S(1)}, f32[192,512]{1,0:T(8,128)S(1)}, f32[192,512]{1,0:T(8,128)S(1)}, bf16[192,512]{1,0:T(8,128)(2,1)S(1)}) custom-call(bf16[48,2176]{1,0:T(8,128)(2,1)S(1)} %copy-done.10, bf16[48,2176]{1,0:T(8,128)(2,1)S(1)} %collective-permute-done.3.refs_1_, bf16[48,2176]{1,0:T(8,128)(2,1)S(1)} %collective-permute-done.4.refs_2_, ...), custom_call_target="tpu_custom_call" | custom-call | flops 1610612736 | bytes 8388608 | tf_op jit(solution)/shard_map/pallas_call | solution.py:144
  36.8 3.1 %collective-permute-done.1.refs_2_ = bf16[48,2048]{1,0:T(8,128)(2,1)} collective-permute-done((bf16[48,2048]{1,0:T(8,128)(2,1)}, bf16[48,2048]{1,0:T(8,128)(2,1)}, u32[]{:S(2)}, u32[]{:S(2)}) %collective-permute-start.1) | collective-permute-done | bytes 196640 | tf_op jit(solution)/shard_map/ppermute | solution.py:27
  45.1 3.7 %shard_map.113 = (bf16[192,1024]{1,0:T(8,128)(2,1)S(1)}, bf16[192,1024]{1,0:T(8,128)(2,1)S(1)}, f32[192,128]{1,0:T(8,128)S(1)}) custom-call(bf16[48,2048]{1,0:T(8,128)(2,1)S(1)} %get-tuple-element.53.refs_0_, bf16[48,2048]{1,0:T(8,128)(2,1)} %collective-permute-done.refs_1_, bf16[48,2048]{1,0:T(8,128)(2,1)} %collective-permute-done.1.refs_2_, ...), custom_call_target="tpu_custom_call" | custom-call | flops 805306368 | bytes 4194304 | tf_op jit(solution)/shard_map/pallas_call | solution.py:203
  48.9 5.4 %shard_map.114 = (bf16[48,2176]{1,0:T(8,128)(2,1)S(1)}, bf16[48,2176]{1,0:T(8,128)(2,1)S(1)}, bf16[48,2176]{1,0:T(8,128)(2,1)S(1)}, bf16[48,2176]{1,0:T(8,128)(2,1)S(1)}) custom-call(bf16[192,1024]{1,0:T(8,128)(2,1)S(1)} %get-tuple-element.61.refs_0_, bf16[192,1024]{1,0:T(8,128)(2,1)S(1)} %get-tuple-element.62.refs_1_, ...), custom_call_target="tpu_custom_call" | custom-call | flops 2415919104 | bytes 8388608 | tf_op jit(solution)/shard_map/pallas_call | solution.py:251
  54.3 5.8 %collective-permute-start.6 = (bf16[48,2176]{1,0:T(8,128)(2,1)S(1)}, bf16[48,2176]{1,0:T(8,128)(2,1)S(1)}, u32[]{:S(2)}, u32[]{:S(2)}) collective-permute-start(bf16[48,2176]{1,0:T(8,128)(2,1)S(1)} %get-tuple-element.65), channel_id=1, source_target_pairs={{0,3},{1,0},{2,1},{3,2},{4,7},{5,4},{6,5},{7,6},{8,11},{9,8},{10,9... | collective-permute-start | bytes 626696 | tf_op jit(solution)/shard_map/ppermute | solution.py:27
  60.9 2.5 %collective-permute-start.12 = (bf16[192,1024]{1,0:T(8,128)(2,1)S(1)}, bf16[192,1024]{1,0:T(8,128)(2,1)S(1)}, u32[]{:S(2)}, u32[]{:S(2)}) collective-permute-start(bf16[192,1024]{1,0:T(8,128)(2,1)S(1)} %get-tuple-element.116), channel_id=1, source_target_pairs={{0,24},{4,28},{8,16},{12,20},{16,8},{20,12},{24,0},{28,4},{1,25},{... | collective-permute-start | bytes 1179656 | tf_op jit(solution)/shard_map/ppermute | solution.py:32
  64.0 1.8 %collective-permute-done.6.refs_1_ = bf16[48,2176]{1,0:T(8,128)(2,1)S(1)} collective-permute-done((bf16[48,2176]{1,0:T(8,128)(2,1)S(1)}, bf16[48,2176]{1,0:T(8,128)(2,1)S(1)}, u32[]{:S(2)}, u32[]{:S(2)}) %collective-permute-start.6) | collective-permute-done | bytes 208928 | tf_op jit(solution)/shard_map/ppermute | solution.py:27
  65.8 1.5 %collective-permute-start.10 = (bf16[192,1024]{1,0:T(8,128)(2,1)S(1)}, bf16[192,1024]{1,0:T(8,128)(2,1)S(1)}, u32[]{:S(2)}, u32[]{:S(2)}) collective-permute-start(bf16[192,1024]{1,0:T(8,128)(2,1)S(1)} %get-tuple-element.114), channel_id=1, source_target_pairs={{0,8},{4,12},{8,0},{12,4},{16,24},{20,28},{24,16},{28,20},{1,9},{5... | collective-permute-start | bytes 1179656 | tf_op jit(solution)/shard_map/ppermute | solution.py:32
  67.4 11.6 %collective-permute-done.7.refs_2_ = bf16[48,2176]{1,0:T(8,128)(2,1)S(1)} collective-permute-done((bf16[48,2176]{1,0:T(8,128)(2,1)S(1)}, bf16[48,2176]{1,0:T(8,128)(2,1)S(1)}, u32[]{:S(2)}, u32[]{:S(2)}) %collective-permute-start.7) | collective-permute-done | bytes 208928 | tf_op jit(solution)/shard_map/ppermute | solution.py:27
  79.0 2.4 %collective-permute-start.16 = (bf16[192,1536]{1,0:T(8,128)(2,1)S(1)}, bf16[192,1536]{1,0:T(8,128)(2,1)S(1)}, u32[]{:S(2)}, u32[]{:S(2)}) collective-permute-start(bf16[192,1536]{1,0:T(8,128)(2,1)S(1)} %get-tuple-element.113), channel_id=1, source_target_pairs={{0,24},{4,28},{8,16},{12,20},{16,8},{20,12},{24,0},{28,4},{1,25},{... | collective-permute-start | bytes 1769480 | tf_op jit(solution)/shard_map/ppermute | solution.py:32
  83.9 12.3 %collective-permute-done.16 = bf16[192,1536]{1,0:T(8,128)(2,1)S(1)} collective-permute-done((bf16[192,1536]{1,0:T(8,128)(2,1)S(1)}, bf16[192,1536]{1,0:T(8,128)(2,1)S(1)}, u32[]{:S(2)}, u32[]{:S(2)}) %collective-permute-start.16) | collective-permute-done | bytes 589856 | tf_op jit(solution)/shard_map/ppermute | solution.py:32
  96.2 10.7 %collective-permute-done.15 = bf16[192,1536]{1,0:T(8,128)(2,1)S(1)} collective-permute-done((bf16[192,1536]{1,0:T(8,128)(2,1)S(1)}, bf16[192,1536]{1,0:T(8,128)(2,1)S(1)}, u32[]{:S(2)}, u32[]{:S(2)}) %collective-permute-start.15) | collective-permute-done | bytes 589856 | tf_op jit(solution)/shard_map/ppermute | solution.py:32
  109.0 1.7 %collective-permute-done.17 = bf16[768,1024]{1,0:T(8,128)(2,1)S(1)} collective-permute-done((bf16[768,1024]{1,0:T(8,128)(2,1)S(1)}, bf16[768,1024]{1,0:T(8,128)(2,1)S(1)}, u32[]{:S(2)}, u32[]{:S(2)}) %collective-permute-start.17) | collective-permute-done | bytes 1572896 | tf_op jit(solution)/shard_map/ppermute | solution.py:32
  112.7 1.2 %fusion.3 = f32[1,256,512]{2,1,0:T(8,128)} fusion(f32[256,512]{1,0:T(8,128)S(1)} %fusion.6, bf16[768,1024]{1,0:T(8,128)(2,1)S(1)} %pad_maximum_fusion, bf16[192,256]{1,0:T(8,128)(2,1)S(1)} %get-tuple-element.105, bf16[192,256]{1,0:T(8,128)(2,1)S(1)} %get-tuple-element.103, bf16[192,256]{1,0:T(8,128)(2,1)S(1)} %get-tuple-element.101, ...), kind=kOutput, calls=%fused_computation.8 | convolution fusion | flops 203161600 | bytes 2228224 | tf_op jit(solution)/shard_map/dot_general | solution.py:323
  (85 shorter events, 16.2 us)
Async XLA Ops:
  0.6 20.3 %copy-start = (bf16[128,2048]{1,0:T(8,128)(2,1)S(1)}, bf16[128,2048]{1,0:T(8,128)(2,1)}, u32[]{:S(2)}) copy-start(bf16[128,2048]{1,0:T(8,128)(2,1)} %param.8) | copy-start | bytes 1572868
  3.1 20.1 %collective-permute-start.3 = (bf16[48,2176]{1,0:T(8,128)(2,1)}, bf16[48,2176]{1,0:T(8,128)(2,1)S(1)}, u32[]{:S(2)}, u32[]{:S(2)}) collective-permute-start(bf16[48,2176]{1,0:T(8,128)(2,1)} %get-tuple-element.45), channel_id=1, source_target_pairs={{0,1},{1,2},{2,3},{3,0},{4,5},{5,6},{6,7},{7,4},{8,9},{9,10},{10,1... | collective-permute-start | bytes 626696 | tf_op jit(solution)/shard_map/ppermute | solution.py:27
  6.1 21.5 %collective-permute-start.4 = (bf16[48,2176]{1,0:T(8,128)(2,1)}, bf16[48,2176]{1,0:T(8,128)(2,1)S(1)}, u32[]{:S(2)}, u32[]{:S(2)}) collective-permute-start(bf16[48,2176]{1,0:T(8,128)(2,1)} %get-tuple-element.46), channel_id=1, source_target_pairs={{0,2},{1,3},{2,0},{3,1},{4,6},{5,7},{6,4},{7,5},{8,10},{9,11},{10,... | collective-permute-start | bytes 626696 | tf_op jit(solution)/shard_map/ppermute | solution.py:27
  8.7 18.9 %collective-permute-start.5 = (bf16[48,2176]{1,0:T(8,128)(2,1)}, bf16[48,2176]{1,0:T(8,128)(2,1)S(1)}, u32[]{:S(2)}, u32[]{:S(2)}) collective-permute-start(bf16[48,2176]{1,0:T(8,128)(2,1)} %get-tuple-element.47), channel_id=1, source_target_pairs={{0,3},{1,0},{2,1},{3,2},{4,7},{5,4},{6,5},{7,6},{8,11},{9,8},{10,9... | collective-permute-start | bytes 626696 | tf_op jit(solution)/shard_map/ppermute | solution.py:27
  10.1 10.9 %copy-start.11 = (bf16[192,128]{1,0:T(8,128)(2,1)S(1)}, bf16[192,128]{1,0:T(8,128)(2,1)}, u32[]{:S(2)}) copy-start(bf16[192,128]{1,0:T(8,128)(2,1)} %get-tuple-element.38.placing_ref) | copy-start | bytes 147460
  21.0 6.7 %copy-start.1 = (bf16[2048,512]{1,0:T(8,128)(2,1)S(1)}, bf16[2048,512]{1,0:T(8,128)(2,1)}, u32[]{:S(2)}) copy-start(bf16[2048,512]{1,0:T(8,128)(2,1)} %get-tuple-element.48.refs_4_.refs_3_) | copy-start | bytes 6291460
  22.2 14.6 %collective-permute-start = (bf16[48,2048]{1,0:T(8,128)(2,1)}, bf16[48,2048]{1,0:T(8,128)(2,1)}, u32[]{:S(2)}, u32[]{:S(2)}) collective-permute-start(bf16[48,2048]{1,0:T(8,128)(2,1)} %get-tuple-element.89), channel_id=1, source_target_pairs={{0,1},{1,2},{2,3},{3,0},{4,5},{5,6},{6,7},{7,4},{8,9},{9,10},{10,1... | collective-permute-start | bytes 589832 | tf_op jit(solution)/shard_map/ppermute | solution.py:27
  22.9 17.0 %collective-permute-start.1 = (bf16[48,2048]{1,0:T(8,128)(2,1)}, bf16[48,2048]{1,0:T(8,128)(2,1)}, u32[]{:S(2)}, u32[]{:S(2)}) collective-permute-start(bf16[48,2048]{1,0:T(8,128)(2,1)} %get-tuple-element.88), channel_id=1, source_target_pairs={{0,2},{1,3},{2,0},{3,1},{4,6},{5,7},{6,4},{7,5},{8,10},{9,11},{10,... | collective-permute-start | bytes 589832 | tf_op jit(solution)/shard_map/ppermute | solution.py:27
  23.2 16.6 %collective-permute-start.2 = (bf16[48,2048]{1,0:T(8,128)(2,1)}, bf16[48,2048]{1,0:T(8,128)(2,1)}, u32[]{:S(2)}, u32[]{:S(2)}) collective-permute-start(bf16[48,2048]{1,0:T(8,128)(2,1)} %get-tuple-element.87), channel_id=1, source_target_pairs={{0,3},{1,0},{2,1},{3,2},{4,7},{5,4},{6,5},{7,6},{8,11},{9,8},{10,9... | collective-permute-start | bytes 589832 | tf_op jit(solution)/shard_map/ppermute | solution.py:27
  36.8 6.0 %copy-start.12 = (bf16[48,2048]{1,0:T(8,128)(2,1)S(1)}, bf16[48,2048]{1,0:T(8,128)(2,1)}, u32[]{:S(2)}) copy-start(bf16[48,2048]{1,0:T(8,128)(2,1)} %slice.122) | copy-start | bytes 589828
  43.2 17.5 %collective-permute-start.9 = (bf16[4,192,256]{2,1,0:T(8,128)(2,1)S(1)}, bf16[4,192,256]{2,1,0:T(8,128)(2,1)S(1)}, u32[]{:S(2)}, u32[]{:S(2)}) collective-permute-start(bf16[4,192,256]{2,1,0:T(8,128)(2,1)S(1)} %pad_maximum_fusion.9), channel_id=1, source_target_pairs={{0,4},{4,0},{8,12},{12,8},{16,20},{20,16},{24,28},{28,24},{1,5},{5... | collective-permute-start | bytes 1179656 | tf_op jit(solution)/shard_map/ppermute | solution.py:32
  43.3 5.6 %copy-start.7 = (bf16[2048,512]{1,0:T(8,128)(2,1)S(1)}, bf16[2048,512]{1,0:T(8,128)(2,1)}, u32[]{:S(2)}) copy-start(bf16[2048,512]{1,0:T(8,128)(2,1)} %get-tuple-element.51.refs_7_.refs_6_) | copy-start | bytes 6291460
  43.3 20.1 %collective-permute-start.13 = (bf16[4,192,256]{2,1,0:T(8,128)(2,1)S(1)}, bf16[4,192,256]{2,1,0:T(8,128)(2,1)S(1)}, u32[]{:S(2)}, u32[]{:S(2)}) collective-permute-start(bf16[4,192,256]{2,1,0:T(8,128)(2,1)S(1)} %pad_maximum_fusion.11), channel_id=1, source_target_pairs={{0,4},{4,0},{8,12},{12,8},{16,20},{20,16},{24,28},{28,24},{1,5},{5... | collective-permute-start | bytes 1179656 | tf_op jit(solution)/shard_map/ppermute | solution.py:32
  54.3 11.5 %collective-permute-start.6 = (bf16[48,2176]{1,0:T(8,128)(2,1)S(1)}, bf16[48,2176]{1,0:T(8,128)(2,1)S(1)}, u32[]{:S(2)}, u32[]{:S(2)}) collective-permute-start(bf16[48,2176]{1,0:T(8,128)(2,1)S(1)} %get-tuple-element.65), channel_id=1, source_target_pairs={{0,3},{1,0},{2,1},{3,2},{4,7},{5,4},{6,5},{7,6},{8,11},{9,8},{10,9... | collective-permute-start | bytes 626696 | tf_op jit(solution)/shard_map/ppermute | solution.py:27
  60.1 18.9 %collective-permute-start.7 = (bf16[48,2176]{1,0:T(8,128)(2,1)S(1)}, bf16[48,2176]{1,0:T(8,128)(2,1)S(1)}, u32[]{:S(2)}, u32[]{:S(2)}) collective-permute-start(bf16[48,2176]{1,0:T(8,128)(2,1)S(1)} %get-tuple-element.66), channel_id=1, source_target_pairs={{0,2},{1,3},{2,0},{3,1},{4,6},{5,7},{6,4},{7,5},{8,10},{9,11},{10,... | collective-permute-start | bytes 626696 | tf_op jit(solution)/shard_map/ppermute | solution.py:27
  60.5 20.9 %collective-permute-start.8 = (bf16[48,2176]{1,0:T(8,128)(2,1)S(1)}, bf16[48,2176]{1,0:T(8,128)(2,1)S(1)}, u32[]{:S(2)}, u32[]{:S(2)}) collective-permute-start(bf16[48,2176]{1,0:T(8,128)(2,1)S(1)} %get-tuple-element.67), channel_id=1, source_target_pairs={{0,1},{1,2},{2,3},{3,0},{4,5},{5,6},{6,7},{7,4},{8,9},{9,10},{10,1... | collective-permute-start | bytes 626696 | tf_op jit(solution)/shard_map/ppermute | solution.py:27
  60.9 21.0 %collective-permute-start.12 = (bf16[192,1024]{1,0:T(8,128)(2,1)S(1)}, bf16[192,1024]{1,0:T(8,128)(2,1)S(1)}, u32[]{:S(2)}, u32[]{:S(2)}) collective-permute-start(bf16[192,1024]{1,0:T(8,128)(2,1)S(1)} %get-tuple-element.116), channel_id=1, source_target_pairs={{0,24},{4,28},{8,16},{12,20},{16,8},{20,12},{24,0},{28,4},{1,25},{... | collective-permute-start | bytes 1179656 | tf_op jit(solution)/shard_map/ppermute | solution.py:32
  63.4 20.2 %collective-permute-start.11 = (bf16[192,1024]{1,0:T(8,128)(2,1)S(1)}, bf16[192,1024]{1,0:T(8,128)(2,1)S(1)}, u32[]{:S(2)}, u32[]{:S(2)}) collective-permute-start(bf16[192,1024]{1,0:T(8,128)(2,1)S(1)} %get-tuple-element.115), channel_id=1, source_target_pairs={{0,16},{4,20},{8,24},{12,28},{16,0},{20,4},{24,8},{28,12},{1,17},{... | collective-permute-start | bytes 1179656 | tf_op jit(solution)/shard_map/ppermute | solution.py:32
  65.8 17.9 %collective-permute-start.10 = (bf16[192,1024]{1,0:T(8,128)(2,1)S(1)}, bf16[192,1024]{1,0:T(8,128)(2,1)S(1)}, u32[]{:S(2)}, u32[]{:S(2)}) collective-permute-start(bf16[192,1024]{1,0:T(8,128)(2,1)S(1)} %get-tuple-element.114), channel_id=1, source_target_pairs={{0,8},{4,12},{8,0},{12,4},{16,24},{20,28},{24,16},{28,20},{1,9},{5... | collective-permute-start | bytes 1179656 | tf_op jit(solution)/shard_map/ppermute | solution.py:32
  79.0 17.2 %collective-permute-start.16 = (bf16[192,1536]{1,0:T(8,128)(2,1)S(1)}, bf16[192,1536]{1,0:T(8,128)(2,1)S(1)}, u32[]{:S(2)}, u32[]{:S(2)}) collective-permute-start(bf16[192,1536]{1,0:T(8,128)(2,1)S(1)} %get-tuple-element.113), channel_id=1, source_target_pairs={{0,24},{4,28},{8,16},{12,20},{16,8},{20,12},{24,0},{28,4},{1,25},{... | collective-permute-start | bytes 1769480 | tf_op jit(solution)/shard_map/ppermute | solution.py:32
  81.4 25.5 %collective-permute-start.15 = (bf16[192,1536]{1,0:T(8,128)(2,1)S(1)}, bf16[192,1536]{1,0:T(8,128)(2,1)S(1)}, u32[]{:S(2)}, u32[]{:S(2)}) collective-permute-start(bf16[192,1536]{1,0:T(8,128)(2,1)S(1)} %get-tuple-element.112), channel_id=1, source_target_pairs={{0,16},{4,20},{8,24},{12,28},{16,0},{20,4},{24,8},{28,12},{1,17},{... | collective-permute-start | bytes 1769480 | tf_op jit(solution)/shard_map/ppermute | solution.py:32
  81.9 25.1 %collective-permute-start.14 = (bf16[192,1536]{1,0:T(8,128)(2,1)S(1)}, bf16[192,1536]{1,0:T(8,128)(2,1)S(1)}, u32[]{:S(2)}, u32[]{:S(2)}) collective-permute-start(bf16[192,1536]{1,0:T(8,128)(2,1)S(1)} %get-tuple-element.111), channel_id=1, source_target_pairs={{0,8},{4,12},{8,0},{12,4},{16,24},{20,28},{24,16},{28,20},{1,9},{5... | collective-permute-start | bytes 1769480 | tf_op jit(solution)/shard_map/ppermute | solution.py:32
  83.8 23.6 %collective-permute-start.18 = (bf16[768,512]{1,0:T(8,128)(2,1)S(1)}, bf16[768,512]{1,0:T(8,128)(2,1)S(1)}, u32[]{:S(2)}, u32[]{:S(2)}) collective-permute-start(bf16[768,512]{1,0:T(8,128)(2,1)S(1)} %pad_maximum_fusion.2), channel_id=1, source_target_pairs={{0,4},{4,0},{8,12},{12,8},{16,20},{20,16},{24,28},{28,24},{1,5},{5... | collective-permute-start | bytes 2359304 | tf_op jit(solution)/shard_map/ppermute | solution.py:32
  107.2 3.5 %collective-permute-start.17 = (bf16[768,1024]{1,0:T(8,128)(2,1)S(1)}, bf16[768,1024]{1,0:T(8,128)(2,1)S(1)}, u32[]{:S(2)}, u32[]{:S(2)}) collective-permute-start(bf16[768,1024]{1,0:T(8,128)(2,1)S(1)} %pad_maximum_fusion), channel_id=1, source_target_pairs={{0,4},{4,0},{8,12},{12,8},{16,20},{20,16},{24,28},{28,24},{1,5},{5... | collective-permute-start | bytes 4718600 | tf_op jit(solution)/shard_map/ppermute | solution.py:32
  (8 other events, 16.9 us)

commit v4 on v1

v4 whole, which is shorter than its diff:
```python
import functools
import math

import jax
import jax.numpy as jnp
from jax import lax
from jax.experimental import pallas as pl
from jax.experimental.pallas import tpu as pltpu
from jax.sharding import PartitionSpec as P

HOT = 4
CAP = 48
LANES = 128
BLOCK = 256
MIB = 1 << 20

highest = lax.Precision.HIGHEST
f32 = jnp.float32
bf16 = jnp.bfloat16
i32 = jnp.int32
VMEM = pl.BlockSpec(memory_space=pltpu.VMEM)
SMEM = pl.BlockSpec(memory_space=pltpu.SMEM)
PARAMS = pltpu.CompilerParams(vmem_limit_bytes=14 * MIB)
SMALL = pl.CostEstimate(flops=0, bytes_accessed=1024, transcendentals=0)


def shifted(values, axis, by):
    size = lax.axis_size(axis)
    return lax.ppermute(values, axis, [(i, (i + by) % size) for i in range(size)])


def flipped(values, axis, mask):
    size = lax.axis_size(axis)
    return lax.ppermute(values, axis, [(i, i ^ mask) for i in range(size)])


def cut_kernel(count, at_ref, *refs):
    pieces, (mine, theirs) = refs[:count], refs[count:]
    chips, _, share = mine.shape
    for k in range(chips):
        for target, core in ((mine, at_ref[0]), (theirs, 1 - at_ref[0])):
            start = pl.multiple_of((2 * k + core) * share, share)
            for i in range(count):
                target[k, i * CAP : (i + 1) * CAP, :] = pieces[i][:, pl.ds(start, share)]


def cut(pieces, width):
    size = lax.axis_size("dp")
    share = width // size
    core = lax.axis_index("dp").astype(i32) % 2
    chips = size // 2
    if share % LANES:
        rows = jnp.concatenate([p[:, :width] for p in pieces])

        def part(which):
            return lax.dynamic_slice_in_dim(rows, which * share, share, axis=1)

        return (
            jnp.stack([part(2 * k + core) for k in range(chips)]),
            jnp.stack([part(2 * k + 1 - core) for k in range(chips)]),
        )
    shape = jax.ShapeDtypeStruct((chips, len(pieces) * CAP, share), bf16)
    return pl.pallas_call(
        functools.partial(cut_kernel, len(pieces)),
        out_shape=[shape, shape],
        in_specs=[SMEM] + [VMEM] * len(pieces),
        out_specs=[VMEM] * 2,
        compiler_params=PARAMS,
        cost_estimate=SMALL,
    )(core.reshape(1), *pieces)


def place_kernel(n_expert, me_ref, route_ref, prob_ref, tok_ref, cot_ref, placing_ref, *refs):
    quarters = n_expert // HOT
    count, width = tok_ref.shape
    pieces, cot_pieces = refs[:n_expert], refs[n_expert:]
    route = route_ref[...]
    hot = (route == lax.broadcasted_iota(i32, (16, count), 0)).astype(f32)
    before = lax.broadcasted_iota(i32, (count, count), 0) < lax.broadcasted_iota(i32, (count, count), 1)
    earlier = jnp.dot(hot.astype(bf16), before.astype(f32).astype(bf16), preferred_element_type=f32)
    rank = jnp.sum(earlier * hot, axis=0, keepdims=True).astype(i32)
    slot = lax.broadcasted_iota(i32, (CAP, count), 0)
    prob = prob_ref[...].astype(f32)
    for k in range(n_expert):
        owner = lax.rem(me_ref[0] + k, n_expert) // quarters
        block = jnp.where((route == owner) & (rank == slot), 1.0, 0.0)
        placing_ref[k * CAP : (k + 1) * CAP, :] = block.astype(bf16)
        slot_prob = jnp.sum(block * prob, axis=1, keepdims=True)
        pieces[k][:, width:] = jnp.broadcast_to(slot_prob, (CAP, LANES)).astype(bf16)
    for source, targets in ((tok_ref, pieces), (cot_ref, cot_pieces)):
        for at in range(0, width, 512):
            part = jnp.dot(placing_ref[...], source[:, at : at + 512], preferred_element_type=f32)
            part = part.astype(bf16)
            for k in range(n_expert):
                targets[k][:, at : at + 512] = part[k * CAP : (k + 1) * CAP]


def place(me, route, prob, tokens, cotangent, n_expert):
    count, width = tokens.shape
    outs = pl.pallas_call(
        functools.partial(place_kernel, n_expert),
        out_shape=[jax.ShapeDtypeStruct((n_expert * CAP, count), bf16)]
        + [jax.ShapeDtypeStruct((CAP, width + LANES), bf16)] * n_expert
        + [jax.ShapeDtypeStruct((CAP, width), bf16)] * n_expert,
        in_specs=[SMEM] + [VMEM] * 4,
        out_specs=[VMEM] * (2 * n_expert + 1),
        compiler_params=PARAMS,
        cost_estimate=SMALL,
    )(me.reshape(1), route.reshape(1, count), prob.reshape(1, count), tokens, cotangent)
    return outs[0], outs[1 : n_expert + 1], outs[n_expert + 1 :]


def halves(whole):
    high = whole.astype(bf16)
    return high, (whole - high.astype(f32)).astype(bf16)


def fill(rows, pieces, width):
    for k, piece in enumerate(pieces):
        rows[k * CAP : (k + 1) * CAP, :] = piece[:, :width]


def times_weight(rows, weight, total):
    depth = weight.shape[0]
    for at in range(0, depth, BLOCK):
        high, low = halves(weight[at : at + BLOCK, :])
        row = rows[:, at : at + BLOCK]
        part = jnp.dot(row, high, preferred_element_type=f32)
        part += jnp.dot(row, low, preferred_element_type=f32)
        if at == 0:
            total[...] = part
        else:
            total[...] += part


def gate_factors(gate, up, prob):
    sig = jax.nn.sigmoid(gate)
    act = gate * sig
    hidden = act * up
    return prob * act, prob * (up * sig * (1.0 + gate * (1.0 - sig))), hidden


def forward_kernel(count, *refs):
    pieces, (w_gate, w_up, act_ref, slope_ref, hidden_ref, share_ref, rows, gate_sum, up_sum) = (
        refs[:count], refs[count:]
    )
    fill(rows, pieces, rows.shape[1])
    times_weight(rows, w_gate, gate_sum)
    times_weight(rows, w_up, up_sum)
    for k in range(count):
        part = slice(k * CAP, (k + 1) * CAP)
        prob = pieces[k][:, rows.shape[1] :].astype(f32)[:, :1]
        act, slope, hidden = gate_factors(gate_sum[part, :], up_sum[part, :], prob)
        act_ref[part, :] = act
        slope_ref[part, :] = slope
        hidden_ref[part, :] = hidden
        share_ref[part, :] = (prob * hidden).astype(bf16)


def forward(pieces, w_gate, w_up):
    count = len(pieces)
    depth, units = w_gate.shape
    shape = jax.ShapeDtypeStruct((count * CAP, units), f32)
    return pl.pallas_call(
        functools.partial(forward_kernel, count),
        out_shape=[shape] * 3 + [jax.ShapeDtypeStruct((count * CAP, units), bf16)],
        in_specs=[VMEM] * (count + 2),
        out_specs=[VMEM] * 4,
        scratch_shapes=[
            pltpu.VMEM((count * CAP, depth), bf16),
            pltpu.VMEM((count * CAP, units), f32),
            pltpu.VMEM((count * CAP, units), f32),
        ],
        compiler_params=PARAMS,
        cost_estimate=SMALL,
    )(*pieces, w_gate, w_up)


def backward_kernel(count, *refs):
    pieces, (w_down, act_ref, slope_ref, hidden_ref, high_ref, low_ref, prob_ref, rows, back_sum) = (
        refs[:count], refs[count:]
    )
    units = w_down.shape[1]
    fill(rows, pieces, rows.shape[1])
    times_weight(rows, w_down, back_sum)
    for k in range(count):
        part = slice(k * CAP, (k + 1) * CAP)
        back = back_sum[part, :]
        total = jnp.sum(hidden_ref[part, :] * back, axis=1, keepdims=True)
        prob_ref[part, :] = jnp.broadcast_to(total, (CAP, LANES))
        for at, factor in ((0, slope_ref), (units, act_ref)):
            high, low = halves(factor[part, :] * back)
            high_ref[part, at : at + units] = high
            low_ref[part, at : at + units] = low


def backward(pieces, w_down, act, slope, hidden):
    count = len(pieces)
    depth, units = w_down.shape
    rows = count * CAP
    return pl.pallas_call(
        functools.partial(backward_kernel, count),
        out_shape=[jax.ShapeDtypeStruct((rows, 2 * units), bf16)] * 2
        + [jax.ShapeDtypeStruct((rows, LANES), f32)],
        in_specs=[VMEM] * (count + 4),
        out_specs=[VMEM] * 3,
        scratch_shapes=[pltpu.VMEM((rows, depth), bf16), pltpu.VMEM((rows, units), f32)],
        compiler_params=PARAMS,
        cost_estimate=SMALL,
    )(*pieces, w_down, act, slope, hidden)


def against(left, right):
    return lax.dot_general(left, right, (((1,), (1,)), ((), ())), preferred_element_type=f32)


def write_input(high_ref, low_ref, prob_ref, w_gate, w_up, pieces):
    depth, units = w_gate.shape
    for at in range(0, depth, BLOCK):
        total = None
        for start, weight in ((0, w_gate), (units, w_up)):
            weight_hi, weight_lo = halves(weight[at : at + BLOCK, :])
            grad_hi = high_ref[:, start : start + units]
            grad_lo = low_ref[:, start : start + units]
            part = against(grad_hi, weight_hi) + against(grad_lo, weight_hi)
            part += against(grad_hi, weight_lo)
            total = part if total is None else total + part
        for k, piece in enumerate(pieces):
            piece[:, at : at + BLOCK] = total[k * CAP : (k + 1) * CAP].astype(piece.dtype)
    for k, piece in enumerate(pieces):
        piece[:, depth:] = prob_ref[k * CAP : (k + 1) * CAP, :].astype(piece.dtype)


def input_kernel(high_ref, low_ref, prob_ref, w_gate, w_up, *pieces):
    write_input(high_ref, low_ref, prob_ref, w_gate, w_up, pieces)


def input_gradient(high, low, prob_part, w_gate, w_up, back_type):
    depth = w_gate.shape[0]
    count = high.shape[0] // CAP
    return pl.pallas_call(
        input_kernel,
        out_shape=[jax.ShapeDtypeStruct((CAP, depth + LANES), back_type)] * count,
        in_specs=[VMEM] * 5,
        out_specs=[VMEM] * count,
        compiler_params=PARAMS,
        cost_estimate=SMALL,
    )(high, low, prob_part, w_gate, w_up)


def local_kernel(
    tok_ref, cot_ref, w_gate, w_up, w_down, terms_ref, piece_ref,
    rows, gate_sum, up_sum, back_sum, low_ref, prob_ref,
):
    units = w_gate.shape[1]
    width = rows.shape[1]
    fill(rows, (tok_ref,), width)
    times_weight(rows, w_gate, gate_sum)
    times_weight(rows, w_up, up_sum)
    times_weight(cot_ref, w_down, back_sum)
    prob = tok_ref[:, width:].astype(f32)[:, :1]
    act, slope, hidden = gate_factors(gate_sum[...], up_sum[...], prob)
    back = back_sum[...]
    total = jnp.sum(hidden * back, axis=1, keepdims=True)
    prob_ref[...] = jnp.broadcast_to(total, prob_ref.shape)
    for at, factor in ((0, slope), (units, act)):
        high, low = halves(factor * back)
        terms_ref[:, at : at + units] = high
        low_ref[:, at : at + units] = low
    terms_ref[:, 2 * units :] = (prob * hidden).astype(bf16)
    write_input(terms_ref, low_ref, prob_ref, w_gate, w_up, (piece_ref,))


def local_rows(tok, cot, w_gate, w_up, w_down, back_type):
    depth, units = w_gate.shape
    return pl.pallas_call(
        local_kernel,
        out_shape=[
            jax.ShapeDtypeStruct((CAP, 3 * units), bf16),
            jax.ShapeDtypeStruct((CAP, depth + LANES), back_type),
        ],
        in_specs=[VMEM] * 5,
        out_specs=[VMEM] * 2,
        scratch_shapes=[pltpu.VMEM((CAP, depth), bf16)]
        + [pltpu.VMEM((CAP, units), f32)] * 3
        + [pltpu.VMEM((CAP, 2 * units), bf16), pltpu.VMEM((CAP, LANES), f32)],
        compiler_params=PARAMS,
        cost_estimate=SMALL,
    )(tok, cot, w_gate, w_up, w_down)


def take_kernel(n_expert, placing_ref, *refs):
    pieces = refs[:n_expert]
    out_ref, prob_ref, rows = refs[n_expert:]
    count, width = out_ref.shape
    exact = rows.dtype != bf16
    for k in range(n_expert):
        rows[k * CAP : (k + 1) * CAP, :] = pieces[k][...]
    placing = placing_ref[...].astype(rows.dtype)
    for at in range(0, width, 512):
        part = lax.dot_general(
            placing, rows[:, at : at + 512], (((0,), (0,)), ((), ())),
            precision=highest if exact else None, preferred_element_type=f32,
        )
        out_ref[:, at : at + 512] = part.astype(bf16)
    column = rows[:, width:].astype(f32)[:, :1]
    prob_ref[...] = jnp.sum(placing_ref[...].astype(f32) * column, axis=0, keepdims=True).astype(bf16)


def take(placing, pieces):
    n_expert = len(pieces)
    count = placing.shape[1]
    width = pieces[0].shape[1] - LANES
    grad, prob = pl.pallas_call(
        functools.partial(take_kernel, n_expert),
        out_shape=[
            jax.ShapeDtypeStruct((count, width), bf16),
            jax.ShapeDtypeStruct((1, count), bf16),
        ],
        in_specs=[VMEM] * (n_expert + 1),
        out_specs=[VMEM] * 2,
        scratch_shapes=[pltpu.VMEM((n_expert * CAP, width + LANES), pieces[0].dtype)],
        compiler_params=pltpu.CompilerParams(vmem_limit_bytes=32 * MIB) if pieces[0].dtype != bf16 else PARAMS,
        cost_estimate=SMALL,
    )(placing, *pieces)
    return grad, prob.reshape(count)


def over_chips(mine, theirs, terms):
    chips, rows, share = mine.shape
    payload = jnp.concatenate(
        [mine, theirs, jnp.broadcast_to(terms[None], (chips,) + terms.shape)], axis=2
    )
    groups = [[2 * k + core for k in range(chips)] for core in range(2)]
    got = lax.all_to_all(
        payload, "dp", split_axis=0, concat_axis=0, tiled=True, axis_index_groups=groups
    ).reshape(chips * rows, -1)
    return got[:, :share], got[:, share : 2 * share], got[:, 2 * share :]


def shards(tokens, cotangent, route, prob, w_gate, w_up, w_down):
    n_expert = lax.axis_size("expert")
    n_dp = lax.axis_size("dp")
    width = tokens.shape[1]
    units = w_gate.shape[2]
    share = width // n_dp
    scale = 1.0 / math.sqrt(tokens.shape[0] * n_dp * n_expert)
    back_type = bf16 if n_expert == HOT else f32
    me = lax.axis_index("expert").astype(i32)
    gate, up, down = w_gate[0], w_up[0], w_down[0]
    ahead = range(1, n_expert)

    placing, slot_tok, slot_cot = place(me, route, prob, tokens, cotangent, n_expert)
    tok = [shifted(slot_tok[k], "expert", k) for k in ahead]

    local_cut = [cut((piece,), width) for piece in (slot_tok[0], slot_cot[0])]
    local_theirs = flipped(jnp.concatenate([c[1] for c in local_cut], axis=2), "dp", 1)
    own_cot, local_theirs = lax.optimization_barrier((slot_cot[0], local_theirs))
    local_terms, local_back = local_rows(slot_tok[0], own_cot, gate, up, down, back_type)
    cot = []
    for k in ahead:
        late, tok[k - 1], local_terms = lax.optimization_barrier(
            (slot_cot[k], tok[k - 1], local_terms)
        )
        cot.append(shifted(late, "expert", k))
    local_mine = jnp.concatenate([c[0] for c in local_cut], axis=2)
    local_own_cols, local_other_cols, local_own = over_chips(local_mine, local_theirs, local_terms)
    local_other = flipped(local_own, "dp", 1)

    mine, theirs = cut(tok, width)
    theirs = flipped(theirs, "dp", 1)
    tok, theirs, local_own = lax.optimization_barrier((tok, theirs, local_own))
    act, slope, hidden, weighted = forward(tok, gate, up)
    tok_own, tok_other, weighted_own = over_chips(mine, theirs, weighted)

    cot, act, local_other = lax.optimization_barrier((cot, act, local_other))
    mine, theirs = cut(cot, width)
    theirs = flipped(theirs, "dp", 1)
    high, low, prob_part = backward(cot, down, act, slope, hidden)
    high, theirs = lax.optimization_barrier((high, theirs))
    back = list(input_gradient(high, low, prob_part, gate, up, back_type))
    back[-1], weighted_own = lax.optimization_barrier((back[-1], weighted_own))
    home = [local_back] + [shifted(back[k - 1], "expert", n_expert - k) for k in ahead]
    weighted_other = flipped(weighted_own, "dp", 1)
    cot_own, cot_other, grads_own = over_chips(mine, theirs, high)
    grads_other = flipped(grads_own, "dp", 1)
    grad_input, grad_prob = take(placing, home)

    def dot(cols, term):
        return lax.dot_general(cols, term, (((0,), (0,)), ((), ())), preferred_element_type=f32)

    def over_rows(first, local, remote):
        local_cols = slice(first * share, (first + 1) * share)
        total = dot(local_own_cols[:, local_cols], local[0])
        total += dot(local_other_cols[:, local_cols], local[1])
        for cols, term in remote:
            total += dot(cols, term)
        return (total * scale)[None]

    def part(values, at):
        return values[:, at * units : (at + 1) * units]

    results = [
        over_rows(
            0,
            (part(local_own, at), part(local_other, at)),
            ((tok_own, part(grads_own, at)), (tok_other, part(grads_other, at))),
        )
        for at in range(2)
    ]
    results.append(
        over_rows(
            1,
            (part(local_own, 2), part(local_other, 2)),
            ((cot_own, weighted_own), (cot_other, weighted_other)),
        )
    )
    return (grad_input, grad_prob, *results)


def solution(mesh):
    placed = (
        P(("dp", "expert"), None),
        P(("dp", "expert"), None),
        P(("dp", "expert"), None),
        P(("dp", "expert")),
        P("expert", None, None),
        P("expert", None, None),
        P("expert", None, None),
    )
    return jax.shard_map(
        shards,
        mesh=mesh,
        in_specs=placed,
        out_specs=(
            P(("dp", "expert"), None),
            P(("dp", "expert")),
            P("expert", "dp", None),
            P("expert", "dp", None),
            P("expert", "dp", None),
        ),
        check_vma=False,
    )
```

time: 124 us -> 140 us (1.13)
  local copies, waits for them, and re-layouts: 2.98 us -> 22.6 us
  Pallas kernels: 0 us -> 15.7 us
  between operations: 14.3 us -> 0.97 us
  matrix products: 28.7 us -> 20.8 us
  starting transfers between devices: 24.4 us -> 32.2 us
  waiting for transfers between devices: 49.6 us -> 42.8 us
    unnamed x18 -> x30, local copies, waits for them, and re-layouts: 0.21 us -> 18.7 us
    pallas_call x0 -> x10, Pallas kernels: none -> 15.7 us  [the longest x1 6.52 us: local_rows(): pl.pallas_call(local_kernel, out_shape=[jax.ShapeDtypeStruct((CAP, 3 * un...]
    all_gather x1 -> x0, waiting for transfers between devices: 15.5 us -> none  [shards(): all_terms = lax.all_gather(terms, 'dp', axis=1, tiled=True)]
    all_to_all x2 -> x3, waiting for transfers between devices: 0.48 us -> 13.3 us  [over_chips(): lax.all_to_all(payload, 'dp', split_axis=0, concat_axis=0, tiled=True, ax...]
    dot_general x11 -> x12, matrix products: 28.7 us -> 20.8 us  [dot(): lax.dot_general(cols, term, (((0,), (0,)), ((), ())), preferred_element_t...]
    all_to_all x2 -> x3, starting transfers between devices: 7.45 us -> 13.1 us  [over_chips(): lax.all_to_all(payload, 'dp', split_axis=0, concat_axis=0, tiled=True, ax...]
    ppermute x9, waiting for transfers between devices: 33.6 us -> 28 us  [shifted(): lax.ppermute(values, axis, [(i, (i + by) % size) for i in range(size)])]
    concatenate x2 -> x4, other arithmetic: 0.15 us -> 3.6 us  [the longest x3 3.58 us: over_chips(): jnp.concatenate([mine, theirs, jnp.broadcast_to(terms[None], (chips,) + t...]
  transfers between devices with their start and end apart: 12 -> 18, of which waited for: 5 -> 7; matrix products, arithmetic and copies ran while one was open for 19% -> 16% of each run, Pallas kernels for 0% -> 11%
where the time goes in v4:
time: 140 us; the launch traced here: 139 us
  waiting for transfers between devices  42.8 us (31%)
  starting transfers between devices  32.2 us (23%)
  local copies, waits for them, and re-layouts  22.6 us (16%)
  matrix products  20.8 us (15%)
  Pallas kernels  15.7 us (11%)
  other arithmetic  3.6 us (3%)
    ppermute x9, waiting for transfers between devices, shifted(): lax.ppermute(values, axis, [(i, (i + by) % size) for i in range(size)])  28 us
    dot_general x12, matrix products, dot(): lax.dot_general(cols, term, (((0,), (0,)), ((), ())), preferred_element_t...  20.8 us
    unnamed x30, local copies, waits for them, and re-layouts  18.7 us
    ppermute x9, starting transfers between devices, shifted(): lax.ppermute(values, axis, [(i, (i + by) % size) for i in range(size)])  18.1 us
    all_to_all x3, waiting for transfers between devices, over_chips(): lax.all_to_all(payload, 'dp', split_axis=0, concat_axis=0, tiled=True, ax...  13.3 us
    all_to_all x3, starting transfers between devices, over_chips(): lax.all_to_all(payload, 'dp', split_axis=0, concat_axis=0, tiled=True, ax...  13.1 us
    pallas_call x1, Pallas kernels, local_rows(): pl.pallas_call(local_kernel, out_shape=[jax.ShapeDtypeStruct((CAP, 3 * un...  6.52 us
    pallas_call x1, Pallas kernels, input_gradient(): pl.pallas_call(input_kernel, out_shape=[jax.ShapeDtypeStruct((CAP, depth...  4.37 us
  transfers between devices with their start and end apart: 18, of which 7 were waited for; matrix products, arithmetic and copies ran while one was open for 16% of the time, Pallas kernels for 11%

profile of v4, /device:TPU:0, one launch (start us, length us, event | category | flops | bytes accessed | tf_op | source)
XLA Modules:
  0.0 138.7 jit_solution(3827693068130620145)
XLA Ops:
  4.7 3.1 %collective-permute-start.1 = (bf16[48,2176]{1,0:T(8,128)(2,1)S(1)}, bf16[48,2176]{1,0:T(8,128)(2,1)S(1)}, u32[]{:S(2)}, u32[]{:S(2)}) collective-permute-start(bf16[48,2176]{1,0:T(8,128)(2,1)S(1)} %get-tuple-element.69), channel_id=1, source_target_pairs={{0,1},{1,2},{2,3},{3,0},{4,5},{5,6},{6,7},{7,4},{8,9},{9,10},{10,1... | collective-permute-start | bytes 626696 | tf_op jit(solution)/shard_map/ppermute | solution.py:29
  7.8 2.6 %collective-permute-start.3 = (bf16[48,2176]{1,0:T(8,128)(2,1)S(1)}, bf16[48,2176]{1,0:T(8,128)(2,1)S(1)}, u32[]{:S(2)}, u32[]{:S(2)}) collective-permute-start(bf16[48,2176]{1,0:T(8,128)(2,1)S(1)} %get-tuple-element.73), channel_id=1, source_target_pairs={{0,2},{1,3},{2,0},{3,1},{4,6},{5,7},{6,4},{7,5},{8,10},{9,11},{10,... | collective-permute-start | bytes 626696 | tf_op jit(solution)/shard_map/ppermute | solution.py:29
  13.3 2.2 %copy-done = f32[1,2048,512]{2,1,0:T(8,128)S(1)} copy-done((f32[1,2048,512]{2,1,0:T(8,128)S(1)}, f32[1,2048,512]{2,1,0:T(8,128)}, u32[]{:S(2)}) %copy-start) | copy-done | bytes 4194328
  15.5 2.2 %copy-done.3 = f32[1,2048,512]{2,1,0:T(8,128)S(1)} copy-done((f32[1,2048,512]{2,1,0:T(8,128)S(1)}, f32[1,2048,512]{2,1,0:T(8,128)}, u32[]{:S(2)}) %copy-start.3) | copy-done | bytes 4194328
  17.7 2.2 %copy-done.6 = f32[1,2048,512]{2,1,0:T(8,128)S(1)} copy-done((f32[1,2048,512]{2,1,0:T(8,128)S(1)}, f32[1,2048,512]{2,1,0:T(8,128)}, u32[]{:S(2)}) %copy-start.6) | copy-done | bytes 4194328
  19.9 6.5 %shard_map.113 = (bf16[48,1536]{1,0:T(8,128)(2,1)S(1)}, bf16[48,2176]{1,0:T(8,128)(2,1)S(1)}) custom-call(bf16[48,2176]{1,0:T(8,128)(2,1)S(1)} %get-tuple-element.62.refs_0_.tok_ref, bf16[48,2048]{1,0:T(8,128)(2,1)S(1)} %get-tuple-element.66.refs_0_.cot_ref, f32[2048,512]{1,0:T(8,128)S(1)} %bitcast.19, f32[2048,512]{1,0:T(8,128)S(1)} %bitcast.22, ...), custom_call_target="tpu_custom_call" | custom-call | bytes 1024 | tf_op jit(solution)/shard_map/pallas_call | solution.py:276
  27.6 4.2 %all-to-all-start = ((bf16[4,48,2560]{2,1,0:T(8,128)(2,1)}), bf16[4,48,2560]{2,1,0:T(8,128)(2,1)}, u32[]{:S(2)}, u32[]{:S(2)}) async-start(bf16[4,48,2560]{2,1,0:T(8,128)(2,1)} %pad_maximum_fusion.2), calls=%async_computation | async-start | bytes 1966080 | tf_op jit(solution)/shard_map/all_to_all | solution.py:335
  32.1 13.3 %all-to-all-done = bf16[4,48,2560]{2,1,0:T(8,128)(2,1)} async-done(((bf16[4,48,2560]{2,1,0:T(8,128)(2,1)}), bf16[4,48,2560]{2,1,0:T(8,128)(2,1)}, u32[]{:S(2)}, u32[]{:S(2)}) %all-to-all-start) | async-done | bytes 983072 | tf_op jit(solution)/shard_map/all_to_all | solution.py:335
  46.6 2.2 %copy-done.1 = f32[1,2048,512]{2,1,0:T(8,128)S(1)} copy-done((f32[1,2048,512]{2,1,0:T(8,128)S(1)}, f32[1,2048,512]{2,1,0:T(8,128)}, u32[]{:S(2)}) %copy-start.1) | copy-done | bytes 4194328
  48.8 2.2 %copy-done.4 = f32[1,2048,512]{2,1,0:T(8,128)S(1)} copy-done((f32[1,2048,512]{2,1,0:T(8,128)S(1)}, f32[1,2048,512]{2,1,0:T(8,128)}, u32[]{:S(2)}) %copy-start.4) | copy-done | bytes 4194328
  54.0 4.3 %all-to-all-start.1 = ((bf16[4,144,1024]{2,1,0:T(8,128)(2,1)}), bf16[4,144,1024]{2,1,0:T(8,128)(2,1)}, u32[]{:S(2)}, u32[]{:S(2)}) async-start(bf16[4,144,1024]{2,1,0:T(8,128)(2,1)} %pad_maximum_fusion.1), calls=%async_computation.1 | async-start | bytes 2359296 | tf_op jit(solution)/shard_map/all_to_all | solution.py:335
  58.2 2.5 %collective-permute-start.2 = (bf16[48,2048]{1,0:T(8,128)(2,1)S(1)}, bf16[48,2048]{1,0:T(8,128)(2,1)S(1)}, u32[]{:S(2)}, u32[]{:S(2)}) collective-permute-start(bf16[48,2048]{1,0:T(8,128)(2,1)S(1)} %get-tuple-element.71), channel_id=1, source_target_pairs={{0,1},{1,2},{2,3},{3,0},{4,5},{5,6},{6,7},{7,4},{8,9},{9,10},{10,1... | collective-permute-start | bytes 589832 | tf_op jit(solution)/shard_map/ppermute | solution.py:29
  63.2 4.8 %collective-permute-done.2.refs_0_ = bf16[48,2048]{1,0:T(8,128)(2,1)S(1)} collective-permute-done((bf16[48,2048]{1,0:T(8,128)(2,1)S(1)}, bf16[48,2048]{1,0:T(8,128)(2,1)S(1)}, u32[]{:S(2)}, u32[]{:S(2)}) %collective-permute-start.2) | collective-permute-done | bytes 196640 | tf_op jit(solution)/shard_map/ppermute | solution.py:29
  67.9 8.0 %collective-permute-done.4.refs_1_ = bf16[48,2048]{1,0:T(8,128)(2,1)S(1)} collective-permute-done((bf16[48,2048]{1,0:T(8,128)(2,1)S(1)}, bf16[48,2048]{1,0:T(8,128)(2,1)S(1)}, u32[]{:S(2)}, u32[]{:S(2)}) %collective-permute-start.4) | collective-permute-done | bytes 196640 | tf_op jit(solution)/shard_map/ppermute | solution.py:29
  76.1 2.2 %copy-done.7 = f32[1,2048,512]{2,1,0:T(8,128)S(1)} copy-done((f32[1,2048,512]{2,1,0:T(8,128)S(1)}, f32[1,2048,512]{2,1,0:T(8,128)}, u32[]{:S(2)}) %copy-start.7) | copy-done | bytes 4194328
  80.8 4.6 %all-to-all-start.2 = ((bf16[4,144,1536]{2,1,0:T(8,128)(2,1)}), bf16[4,144,1536]{2,1,0:T(8,128)(2,1)}, u32[]{:S(2)}, u32[]{:S(2)}) async-start(bf16[4,144,1536]{2,1,0:T(8,128)(2,1)} %pad_maximum_fusion), calls=%async_computation.2 | async-start | bytes 3538944 | tf_op jit(solution)/shard_map/all_to_all | solution.py:335
  93.0 2.2 %copy-done.5 = f32[1,2048,512]{2,1,0:T(8,128)S(1)} copy-done((f32[1,2048,512]{2,1,0:T(8,128)S(1)}, f32[1,2048,512]{2,1,0:T(8,128)}, u32[]{:S(2)}) %copy-start.5) | copy-done | bytes 4194328
  95.2 4.4 %shard_map.118 = (bf16[48,2176]{1,0:T(8,128)(2,1)S(1)}, bf16[48,2176]{1,0:T(8,128)(2,1)S(1)}, bf16[48,2176]{1,0:T(8,128)(2,1)S(1)}) custom-call(bf16[144,1024]{1,0:T(8,128)(2,1)S(1)} %get-tuple-element.100.high_ref, bf16[144,1024]{1,0:T(8,128)(2,1)S(1)} %get-tuple-element.101.low_ref, f32[144,128]{1,0:T(8,128)S(1)} %get-tuple-element.102.prob_ref, ...), custom_call_target="tpu_custom_call" | custom-call | bytes 1024 | tf_op jit(solution)/shard_map/pallas_call | solution.py:241
  102.2 4.7 %collective-permute-start.12 = (bf16[48,2176]{1,0:T(8,128)(2,1)S(1)}, bf16[48,2176]{1,0:T(8,128)(2,1)S(1)}, u32[]{:S(2)}, u32[]{:S(2)}) collective-permute-start(bf16[48,2176]{1,0:T(8,128)(2,1)S(1)} %get-tuple-element.109), channel_id=1, source_target_pairs={{0,1},{1,2},{2,3},{3,0},{4,5},{5,6},{6,7},{7,4},{8,9},{9,10},{10,1... | collective-permute-start | bytes 626696 | tf_op jit(solution)/shard_map/ppermute | solution.py:29
  111.0 2.5 %collective-permute-done.12.refs_3_ = bf16[48,2176]{1,0:T(8,128)(2,1)S(1)} collective-permute-done((bf16[48,2176]{1,0:T(8,128)(2,1)S(1)}, bf16[48,2176]{1,0:T(8,128)(2,1)S(1)}, u32[]{:S(2)}, u32[]{:S(2)}) %collective-permute-start.12) | collective-permute-done | bytes 208928 | tf_op jit(solution)/shard_map/ppermute | solution.py:29
  113.5 3.8 %collective-permute-done.10.refs_1_ = bf16[48,2176]{1,0:T(8,128)(2,1)S(1)} collective-permute-done((bf16[48,2176]{1,0:T(8,128)(2,1)S(1)}, bf16[48,2176]{1,0:T(8,128)(2,1)S(1)}, u32[]{:S(2)}, u32[]{:S(2)}) %collective-permute-start.10) | collective-permute-done | bytes 208928 | tf_op jit(solution)/shard_map/ppermute | solution.py:29
  117.4 8.9 %collective-permute-done.11.refs_2_ = bf16[48,2176]{1,0:T(8,128)(2,1)S(1)} collective-permute-done((bf16[48,2176]{1,0:T(8,128)(2,1)S(1)}, bf16[48,2176]{1,0:T(8,128)(2,1)S(1)}, u32[]{:S(2)}, u32[]{:S(2)}) %collective-permute-start.11) | collective-permute-done | bytes 208928 | tf_op jit(solution)/shard_map/ppermute | solution.py:29
  128.8 2.4 %fusion.1 = f32[1,256,512]{2,1,0:T(8,128)} fusion(f32[256,512]{1,0:T(8,128)S(1)} %convolution_add_fusion.1, bf16[576,512]{1,0:T(8,128)(2,1)} %collective-permute-done.14, bf16[576,1536]{1,0:T(8,128)(2,1)} %bitcast.10), kind=kOutput, calls=%fused_computation.3 | convolution fusion | flops 151257088 | bytes 1933312 | tf_op jit(solution)/shard_map/dot_general | solution.py:390
  134.3 2.2 %fusion.3 = f32[1,256,512]{2,1,0:T(8,128)} fusion(f32[256,512]{1,0:T(8,128)S(1)} %convolution_add_fusion.4, bf16[576,1024]{1,0:T(8,128)(2,1)S(1)} %collective-permute-done.13, bf16[576,1024]{1,0:T(8,128)(2,1)} %bitcast.8), kind=kOutput, calls=%fused_computation.8 | convolution fusion | flops 151257088 | bytes 1933312 | tf_op jit(solution)/shard_map/dot_general | solution.py:390
  (74 shorter events, 39.7 us)
Async XLA Ops:
  4.7 21.7 %collective-permute-start.1 = (bf16[48,2176]{1,0:T(8,128)(2,1)S(1)}, bf16[48,2176]{1,0:T(8,128)(2,1)S(1)}, u32[]{:S(2)}, u32[]{:S(2)}) collective-permute-start(bf16[48,2176]{1,0:T(8,128)(2,1)S(1)} %get-tuple-element.69), channel_id=1, source_target_pairs={{0,1},{1,2},{2,3},{3,0},{4,5},{5,6},{6,7},{7,4},{8,9},{9,10},{10,1... | collective-permute-start | bytes 626696 | tf_op jit(solution)/shard_map/ppermute | solution.py:29
  7.8 18.6 %collective-permute-start.3 = (bf16[48,2176]{1,0:T(8,128)(2,1)S(1)}, bf16[48,2176]{1,0:T(8,128)(2,1)S(1)}, u32[]{:S(2)}, u32[]{:S(2)}) collective-permute-start(bf16[48,2176]{1,0:T(8,128)(2,1)S(1)} %get-tuple-element.73), channel_id=1, source_target_pairs={{0,2},{1,3},{2,0},{3,1},{4,6},{5,7},{6,4},{7,5},{8,10},{9,11},{10,... | collective-permute-start | bytes 626696 | tf_op jit(solution)/shard_map/ppermute | solution.py:29
  10.4 16.1 %collective-permute-start.5 = (bf16[48,2176]{1,0:T(8,128)(2,1)S(1)}, bf16[48,2176]{1,0:T(8,128)(2,1)S(1)}, u32[]{:S(2)}, u32[]{:S(2)}) collective-permute-start(bf16[48,2176]{1,0:T(8,128)(2,1)S(1)} %get-tuple-element.77), channel_id=1, source_target_pairs={{0,3},{1,0},{2,1},{3,2},{4,7},{5,4},{6,5},{7,6},{8,11},{9,8},{10,9... | collective-permute-start | bytes 626696 | tf_op jit(solution)/shard_map/ppermute | solution.py:29
  11.8 1.5 %collective-permute-start = (bf16[4,48,512]{2,1,0:T(8,128)(2,1)S(1)}, bf16[4,48,512]{2,1,0:T(8,128)(2,1)S(1)}, u32[]{:S(2)}, u32[]{:S(2)}) collective-permute-start(bf16[4,48,512]{2,1,0:T(8,128)(2,1)S(1)} %pad_maximum_fusion.3), channel_id=1, source_target_pairs={{0,4},{4,0},{8,12},{12,8},{16,20},{20,16},{24,28},{28,24},{1,5},{5... | collective-permute-start | bytes 589832 | tf_op jit(solution)/shard_map/ppermute | solution.py:34
  27.6 17.8 %all-to-all-start = ((bf16[4,48,2560]{2,1,0:T(8,128)(2,1)}), bf16[4,48,2560]{2,1,0:T(8,128)(2,1)}, u32[]{:S(2)}, u32[]{:S(2)}) async-start(bf16[4,48,2560]{2,1,0:T(8,128)(2,1)} %pad_maximum_fusion.2), calls=%async_computation | async-start | bytes 1966080 | tf_op jit(solution)/shard_map/all_to_all | solution.py:335
  31.9 14.7 %collective-permute-start.7 = (bf16[4,144,256]{2,1,0:T(8,128)(2,1)S(1)}, bf16[4,144,256]{2,1,0:T(8,128)(2,1)S(1)}, u32[]{:S(2)}, u32[]{:S(2)}) collective-permute-start(bf16[4,144,256]{2,1,0:T(8,128)(2,1)S(1)} %get-tuple-element.83), channel_id=1, source_target_pairs={{0,4},{4,0},{8,12},{12,8},{16,20},{20,16},{24,28},{28,24},{1,5},{5... | collective-permute-start | bytes 884744 | tf_op jit(solution)/shard_map/ppermute | solution.py:34
  46.5 29.4 %collective-permute-start.8 = (bf16[192,1536]{1,0:T(8,128)(2,1)S(1)}, bf16[192,1536]{1,0:T(8,128)(2,1)}, u32[]{:S(2)}, u32[]{:S(2)}) collective-permute-start(bf16[192,1536]{1,0:T(8,128)(2,1)S(1)} %slice.94), channel_id=1, source_target_pairs={{0,4},{4,0},{8,12},{12,8},{16,20},{20,16},{24,28},{28,24},{1,5},{5... | collective-permute-start | bytes 1769480 | tf_op jit(solution)/shard_map/ppermute | solution.py:34
  46.6 2.2 %copy-start.1 = (f32[1,2048,512]{2,1,0:T(8,128)S(1)}, f32[1,2048,512]{2,1,0:T(8,128)}, u32[]{:S(2)}) copy-start(f32[1,2048,512]{2,1,0:T(8,128)} %param.11) | copy-start | bytes 12582916
  54.0 26.9 %all-to-all-start.1 = ((bf16[4,144,1024]{2,1,0:T(8,128)(2,1)}), bf16[4,144,1024]{2,1,0:T(8,128)(2,1)}, u32[]{:S(2)}, u32[]{:S(2)}) async-start(bf16[4,144,1024]{2,1,0:T(8,128)(2,1)} %pad_maximum_fusion.1), calls=%async_computation.1 | async-start | bytes 2359296 | tf_op jit(solution)/shard_map/all_to_all | solution.py:335
  58.2 9.7 %collective-permute-start.2 = (bf16[48,2048]{1,0:T(8,128)(2,1)S(1)}, bf16[48,2048]{1,0:T(8,128)(2,1)S(1)}, u32[]{:S(2)}, u32[]{:S(2)}) collective-permute-start(bf16[48,2048]{1,0:T(8,128)(2,1)S(1)} %get-tuple-element.71), channel_id=1, source_target_pairs={{0,1},{1,2},{2,3},{3,0},{4,5},{5,6},{6,7},{7,4},{8,9},{9,10},{10,1... | collective-permute-start | bytes 589832 | tf_op jit(solution)/shard_map/ppermute | solution.py:29
  60.7 15.2 %collective-permute-start.4 = (bf16[48,2048]{1,0:T(8,128)(2,1)S(1)}, bf16[48,2048]{1,0:T(8,128)(2,1)S(1)}, u32[]{:S(2)}, u32[]{:S(2)}) collective-permute-start(bf16[48,2048]{1,0:T(8,128)(2,1)S(1)} %get-tuple-element.75), channel_id=1, source_target_pairs={{0,2},{1,3},{2,0},{3,1},{4,6},{5,7},{6,4},{7,5},{8,10},{9,11},{10,... | collective-permute-start | bytes 589832 | tf_op jit(solution)/shard_map/ppermute | solution.py:29
  61.3 14.6 %collective-permute-start.6 = (bf16[48,2048]{1,0:T(8,128)(2,1)S(1)}, bf16[48,2048]{1,0:T(8,128)(2,1)S(1)}, u32[]{:S(2)}, u32[]{:S(2)}) collective-permute-start(bf16[48,2048]{1,0:T(8,128)(2,1)S(1)} %get-tuple-element.79), channel_id=1, source_target_pairs={{0,3},{1,0},{2,1},{3,2},{4,7},{5,4},{6,5},{7,6},{8,11},{9,8},{10,9... | collective-permute-start | bytes 589832 | tf_op jit(solution)/shard_map/ppermute | solution.py:29
  76.0 3.3 %collective-permute-start.9 = (bf16[4,144,256]{2,1,0:T(8,128)(2,1)S(1)}, bf16[4,144,256]{2,1,0:T(8,128)(2,1)S(1)}, u32[]{:S(2)}, u32[]{:S(2)}) collective-permute-start(bf16[4,144,256]{2,1,0:T(8,128)(2,1)S(1)} %get-tuple-element.99), channel_id=1, source_target_pairs={{0,4},{4,0},{8,12},{12,8},{16,20},{20,16},{24,28},{28,24},{1,5},{5... | collective-permute-start | bytes 884744 | tf_op jit(solution)/shard_map/ppermute | solution.py:34
  76.1 2.2 %copy-start.7 = (f32[1,2048,512]{2,1,0:T(8,128)S(1)}, f32[1,2048,512]{2,1,0:T(8,128)}, u32[]{:S(2)}) copy-start(f32[1,2048,512]{2,1,0:T(8,128)} %param.13) | copy-start | bytes 12582916
  80.8 27.5 %all-to-all-start.2 = ((bf16[4,144,1536]{2,1,0:T(8,128)(2,1)}), bf16[4,144,1536]{2,1,0:T(8,128)(2,1)}, u32[]{:S(2)}, u32[]{:S(2)}) async-start(bf16[4,144,1536]{2,1,0:T(8,128)(2,1)} %pad_maximum_fusion), calls=%async_computation.2 | async-start | bytes 3538944 | tf_op jit(solution)/shard_map/all_to_all | solution.py:335
  86.6 6.4 %copy-start.2 = (f32[1,2048,512]{2,1,0:T(8,128)S(1)}, f32[1,2048,512]{2,1,0:T(8,128)}, u32[]{:S(2)}) copy-start(f32[1,2048,512]{2,1,0:T(8,128)} %param.11) | copy-start | bytes 12582916
  93.0 2.2 %copy-start.5 = (f32[1,2048,512]{2,1,0:T(8,128)S(1)}, f32[1,2048,512]{2,1,0:T(8,128)}, u32[]{:S(2)}) copy-start(f32[1,2048,512]{2,1,0:T(8,128)} %param.12) | copy-start | bytes 12582916
  99.6 29.2 %collective-permute-start.14 = (bf16[576,512]{1,0:T(8,128)(2,1)S(1)}, bf16[576,512]{1,0:T(8,128)(2,1)}, u32[]{:S(2)}, u32[]{:S(2)}) collective-permute-start(bf16[576,512]{1,0:T(8,128)(2,1)S(1)} %slice.95), channel_id=1, source_target_pairs={{0,4},{4,0},{8,12},{12,8},{16,20},{20,16},{24,28},{28,24},{1,5},{5... | collective-permute-start | bytes 1769480 | tf_op jit(solution)/shard_map/ppermute | solution.py:34
  102.2 11.4 %collective-permute-start.12 = (bf16[48,2176]{1,0:T(8,128)(2,1)S(1)}, bf16[48,2176]{1,0:T(8,128)(2,1)S(1)}, u32[]{:S(2)}, u32[]{:S(2)}) collective-permute-start(bf16[48,2176]{1,0:T(8,128)(2,1)S(1)} %get-tuple-element.109), channel_id=1, source_target_pairs={{0,1},{1,2},{2,3},{3,0},{4,5},{5,6},{6,7},{7,4},{8,9},{9,10},{10,1... | collective-permute-start | bytes 626696 | tf_op jit(solution)/shard_map/ppermute | solution.py:29
  106.9 10.5 %collective-permute-start.10 = (bf16[48,2176]{1,0:T(8,128)(2,1)S(1)}, bf16[48,2176]{1,0:T(8,128)(2,1)S(1)}, u32[]{:S(2)}, u32[]{:S(2)}) collective-permute-start(bf16[48,2176]{1,0:T(8,128)(2,1)S(1)} %get-tuple-element.103), channel_id=1, source_target_pairs={{0,3},{1,0},{2,1},{3,2},{4,7},{5,4},{6,5},{7,6},{8,11},{9,8},{10,9... | collective-permute-start | bytes 626696 | tf_op jit(solution)/shard_map/ppermute | solution.py:29
  107.5 18.8 %collective-permute-start.11 = (bf16[48,2176]{1,0:T(8,128)(2,1)S(1)}, bf16[48,2176]{1,0:T(8,128)(2,1)S(1)}, u32[]{:S(2)}, u32[]{:S(2)}) collective-permute-start(bf16[48,2176]{1,0:T(8,128)(2,1)S(1)} %get-tuple-element.104), channel_id=1, source_target_pairs={{0,2},{1,3},{2,0},{3,1},{4,6},{5,7},{6,4},{7,5},{8,10},{9,11},{10,... | collective-permute-start | bytes 626696 | tf_op jit(solution)/shard_map/ppermute | solution.py:29
  108.3 19.1 %copy-start.14 = (f32[256,512]{1,0:T(8,128)S(1)}, f32[256,512]{1,0:T(8,128)}, u32[]{:S(2)}) copy-start(f32[256,512]{1,0:T(8,128)} %convolution_add_fusion.2) | copy-start | bytes 1572868
  109.8 24.6 %collective-permute-start.13 = (bf16[576,1024]{1,0:T(8,128)(2,1)S(1)}, bf16[576,1024]{1,0:T(8,128)(2,1)S(1)}, u32[]{:S(2)}, u32[]{:S(2)}) collective-permute-start(bf16[576,1024]{1,0:T(8,128)(2,1)S(1)} %slice.101), channel_id=1, source_target_pairs={{0,4},{4,0},{8,12},{12,8},{16,20},{20,16},{24,28},{28,24},{1,5},{5... | collective-permute-start | bytes 3538952 | tf_op jit(solution)/shard_map/ppermute | solution.py:34
  128.8 4.0 %copy-start.13 = (f32[256,512]{1,0:T(8,128)S(1)}, f32[256,512]{1,0:T(8,128)}, u32[]{:S(2)}) copy-start(f32[256,512]{1,0:T(8,128)} %convolution_add_fusion.8) | copy-start | bytes 1572868
  (9 other events, 13.7 us)

commit v5 on v1

v5 whole, which is shorter than its diff:
```python
import functools
import math

import jax
import jax.numpy as jnp
from jax import lax
from jax.experimental import pallas as pl
from jax.experimental.pallas import tpu as pltpu
from jax.sharding import PartitionSpec as P

HOT = 4
CAP = 48
LANES = 128
BLOCK = 256
MIB = 1 << 20

highest = lax.Precision.HIGHEST
f32 = jnp.float32
bf16 = jnp.bfloat16
i32 = jnp.int32
VMEM = pl.BlockSpec(memory_space=pltpu.VMEM)
SMEM = pl.BlockSpec(memory_space=pltpu.SMEM)
HBM = pl.BlockSpec(memory_space=pltpu.HBM)
PARAMS = pltpu.CompilerParams(vmem_limit_bytes=14 * MIB)
ALONE = pltpu.CompilerParams(vmem_limit_bytes=52 * MIB)
SMALL = pl.CostEstimate(flops=0, bytes_accessed=1024, transcendentals=0)


def shifted(values, axis, by):
    size = lax.axis_size(axis)
    return lax.ppermute(values, axis, [(i, (i + by) % size) for i in range(size)])


def flipped(values, axis, mask):
    size = lax.axis_size(axis)
    return lax.ppermute(values, axis, [(i, i ^ mask) for i in range(size)])


def cut_kernel(count, at_ref, *refs):
    pieces, theirs = refs[:count], refs[count]
    chips, _, double = theirs.shape
    share = double // 2
    width = 2 * chips * share
    for k in range(chips):
        start = pl.multiple_of((at_ref[0] ^ (2 * k + 1)) * share, share)
        for i in range(count):
            part = slice(i * CAP, (i + 1) * CAP)
            theirs[k, part, :share] = pieces[i][:, pl.ds(start, share)]
            theirs[k, part, share:] = pieces[i][:, pl.ds(width + start, share)]


def pack_kernel(count, at_ref, *refs):
    pieces, theirs, terms, payload = refs[:count], refs[count], refs[count + 1], refs[count + 2 :]
    chips, _, double = theirs.shape
    share = double // 2
    width = 2 * chips * share
    for k in range(chips):
        start = pl.multiple_of((at_ref[0] ^ (2 * k)) * share, share)
        for i in range(count):
            part = slice(i * CAP, (i + 1) * CAP)
            payload[k][part, :share] = pieces[i][:, pl.ds(start, share)]
            payload[k][part, share:double] = pieces[i][:, pl.ds(width + start, share)]
        payload[k][:, double : 2 * double] = theirs[k]
        payload[k][:, 2 * double :] = terms[...]


def slices_of(pieces, width, share, flips):
    at = lax.axis_index("dp").astype(i32)
    rows = jnp.concatenate(pieces)
    return [
        jnp.concatenate(
            [
                lax.dynamic_slice_in_dim(rows, base + (at ^ flip) * share, share, axis=1)
                for base in (0, width)
            ],
            axis=1,
        )
        for flip in flips
    ]


def cut(pieces, width):
    size = lax.axis_size("dp")
    share = width // size
    if share % LANES:
        return jnp.stack(slices_of(pieces, width, share, range(1, size, 2)))
    return pl.pallas_call(
        functools.partial(cut_kernel, len(pieces)),
        out_shape=jax.ShapeDtypeStruct((size // 2, len(pieces) * CAP, 2 * share), bf16),
        in_specs=[SMEM] + [VMEM] * len(pieces),
        out_specs=VMEM,
        compiler_params=PARAMS,
        cost_estimate=SMALL,
    )(lax.axis_index("dp").astype(i32).reshape(1), *pieces)


def pack(pieces, theirs, terms, width):
    size = lax.axis_size("dp")
    share = width // size
    if share % LANES:
        own = slices_of(pieces, width, share, range(0, size, 2))
        return [jnp.concatenate([own[k], theirs[k], terms], axis=1) for k in range(size // 2)]
    shape = jax.ShapeDtypeStruct((terms.shape[0], 4 * share + terms.shape[1]), bf16)
    return pl.pallas_call(
        functools.partial(pack_kernel, len(pieces)),
        out_shape=[shape] * (size // 2),
        in_specs=[SMEM] + [VMEM] * (len(pieces) + 2),
        out_specs=[VMEM] * (size // 2),
        compiler_params=PARAMS,
        cost_estimate=SMALL,
    )(lax.axis_index("dp").astype(i32).reshape(1), *pieces, theirs, terms)


def sum_kernel(chips, share, units, scale, first, *refs):
    got, others = refs[:chips], refs[chips]
    past = () if first else refs[chips + 1 : chips + 4]
    outs = refs[-5:-2]
    cols, terms = refs[-2:]
    rows = got[0].shape[0]
    for k in range(chips):
        for core in range(2):
            part = slice((2 * k + core) * rows, (2 * k + core + 1) * rows)
            cols[part, :] = got[k][:, 2 * core * share : 2 * (core + 1) * share]
        terms[2 * k * rows : (2 * k + 1) * rows, :] = got[k][:, 4 * share :]
        terms[(2 * k + 1) * rows : (2 * k + 2) * rows, :] = others[k * rows : (k + 1) * rows, :]
    for i in range(3):
        column = share if i == 2 else 0
        total = lax.dot_general(
            cols[:, column : column + share], terms[:, i * units : (i + 1) * units],
            (((0,), (0,)), ((), ())), preferred_element_type=f32,
        )
        if not first:
            total += past[i][...]
        outs[i][...] = total if scale is None else total * scale


def weight_sums(got, others, past, share, scale):
    chips = len(got)
    rows = got[0].shape[0]
    units = others.shape[1] // 3
    if share % LANES:
        wide = [jnp.concatenate([g[:, 2 * c * share : 2 * (c + 1) * share] for g in got]) for c in range(2)]
        near = jnp.concatenate([g[:, 4 * share :] for g in got])
        sums = []
        for i in range(3):
            total = 0.0 if past is None else past[i]
            for cols, terms in zip(wide, (near, others)):
                column = share if i == 2 else 0
                total += lax.dot_general(
                    cols[:, column : column + share], terms[:, i * units : (i + 1) * units],
                    (((0,), (0,)), ((), ())), preferred_element_type=f32,
                )
            sums.append(total if scale is None else total * scale)
        return sums
    past = [] if past is None else list(past)
    return pl.pallas_call(
        functools.partial(sum_kernel, chips, share, units, scale, not past),
        out_shape=[jax.ShapeDtypeStruct((share, units), f32)] * 3,
        in_specs=[VMEM] * (chips + 1 + len(past)),
        out_specs=[VMEM] * 3,
        scratch_shapes=[
            pltpu.VMEM((2 * chips * rows, 2 * share), bf16),
            pltpu.VMEM((2 * chips * rows, 3 * units), bf16),
        ],
        compiler_params=PARAMS,
        cost_estimate=SMALL,
    )(*got, others, *past)


def place_kernel(n_expert, me_ref, route_ref, prob_ref, tok_ref, cot_ref, placing_ref, *pieces):
    quarters = n_expert // HOT
    count, width = tok_ref.shape
    route = route_ref[...]
    hot = (route == lax.broadcasted_iota(i32, (16, count), 0)).astype(f32)
    before = lax.broadcasted_iota(i32, (count, count), 0) < lax.broadcasted_iota(i32, (count, count), 1)
    earlier = jnp.dot(hot.astype(bf16), before.astype(f32).astype(bf16), preferred_element_type=f32)
    rank = jnp.sum(earlier * hot, axis=0, keepdims=True).astype(i32)
    slot = lax.broadcasted_iota(i32, (CAP, count), 0)
    prob = prob_ref[...].astype(f32)
    for k in range(n_expert):
        owner = lax.rem(me_ref[0] + k, n_expert) // quarters
        block = jnp.where((route == owner) & (rank == slot), 1.0, 0.0)
        placing_ref[k * CAP : (k + 1) * CAP, :] = block.astype(bf16)
        slot_prob = jnp.sum(block * prob, axis=1, keepdims=True)
        pieces[k][:, 2 * width :] = jnp.broadcast_to(slot_prob, (CAP, LANES)).astype(bf16)
    for start, source in ((0, tok_ref), (width, cot_ref)):
        for at in range(0, width, 512):
            part = jnp.dot(placing_ref[...], source[:, at : at + 512], preferred_element_type=f32)
            part = part.astype(bf16)
            for k in range(n_expert):
                pieces[k][:, start + at : start + at + 512] = part[k * CAP : (k + 1) * CAP]


def place(me, route, prob, tokens, cotangent, n_expert):
    count, width = tokens.shape
    outs = pl.pallas_call(
        functools.partial(place_kernel, n_expert),
        out_shape=[jax.ShapeDtypeStruct((n_expert * CAP, count), bf16)]
        + [jax.ShapeDtypeStruct((CAP, 2 * width + LANES), bf16)] * n_expert,
        in_specs=[SMEM] + [VMEM] * 4,
        out_specs=[VMEM] * (n_expert + 1),
        compiler_params=PARAMS,
        cost_estimate=SMALL,
    )(me.reshape(1), route.reshape(1, count), prob.reshape(1, count), tokens, cotangent)
    return outs[0], outs[1:]


def halves(whole):
    high = whole.astype(bf16)
    return high, (whole - high.astype(f32)).astype(bf16)


def weight_scratch(count, depth, units):
    return [
        pltpu.VMEM((count, depth, units), f32),
        pltpu.SemaphoreType.DMA((count, depth // BLOCK)),
    ]


def fetch(weights, buffer, arrived):
    copies = []
    for at in range(weights[0].shape[0] // BLOCK):
        here = slice(at * BLOCK, (at + 1) * BLOCK)
        for i, weight in enumerate(weights):
            copy = pltpu.make_async_copy(weight.at[here, :], buffer.at[i, here, :], arrived.at[i, at])
            copy.start()
            copies.append(copy)
    return copies


def times_weights(factors, buffer, copies):
    depth = buffer.shape[1]
    for at in range(depth // BLOCK):
        here = slice(at * BLOCK, (at + 1) * BLOCK)
        for i, (rows, total) in enumerate(factors):
            copies[at * len(factors) + i].wait()
            high, low = halves(buffer[i, here, :])
            row = rows[:, here]
            part = jnp.dot(row, high, preferred_element_type=f32)
            part += jnp.dot(row, low, preferred_element_type=f32)
            if at == 0:
                total[...] = part
            else:
                total[...] += part


def gate_factors(gate, up, prob):
    sig = jax.nn.sigmoid(gate)
    act = gate * sig
    hidden = act * up
    return prob * act, prob * (up * sig * (1.0 + gate * (1.0 - sig))), hidden


def against(left, right):
    return lax.dot_general(left, right, (((1,), (1,)), ((), ())), preferred_element_type=f32)


def chunk_kernel(count, *refs):
    pieces, weights, terms_ref = refs[:count], refs[count : count + 3], refs[count + 3]
    outs = refs[count + 4 : 2 * count + 4]
    tok, cot, gate_sum, up_sum, back_sum, low_ref, buffer, arrived = refs[2 * count + 4 :]
    depth, units = weights[0].shape
    copies = fetch(weights, buffer, arrived)
    for k, piece in enumerate(pieces):
        part = slice(k * CAP, (k + 1) * CAP)
        tok[part, :] = piece[:, :depth]
        cot[part, :] = piece[:, depth : 2 * depth]
    times_weights(((tok, gate_sum), (tok, up_sum), (cot, back_sum)), buffer, copies)
    for k, piece in enumerate(pieces):
        part = slice(k * CAP, (k + 1) * CAP)
        prob = piece[:, 2 * depth :].astype(f32)[:, :1]
        act, slope, hidden = gate_factors(gate_sum[part, :], up_sum[part, :], prob)
        back = back_sum[part, :]
        total = jnp.sum(hidden * back, axis=1, keepdims=True)
        outs[k][:, depth:] = jnp.broadcast_to(total, (CAP, LANES)).astype(outs[k].dtype)
        for at, factor in ((0, slope), (units, act)):
            high, low = halves(factor * back)
            terms_ref[part, at : at + units] = high
            low_ref[part, at : at + units] = low
        terms_ref[part, 2 * units :] = (prob * hidden).astype(bf16)
    for at in range(0, depth, BLOCK):
        total = None
        for i in range(2):
            high, low = halves(buffer[i, at : at + BLOCK, :])
            grad_hi = terms_ref[:, i * units : (i + 1) * units]
            grad_lo = low_ref[:, i * units : (i + 1) * units]
            part = against(grad_hi, high) + against(grad_lo, high) + against(grad_hi, low)
            total = part if total is None else total + part
        for k, out in enumerate(outs):
            out[:, at : at + BLOCK] = total[k * CAP : (k + 1) * CAP].astype(out.dtype)


def chunk_rows(pieces, weights, back_type):
    count = len(pieces)
    depth, units = weights[0].shape
    rows = count * CAP
    outs = pl.pallas_call(
        functools.partial(chunk_kernel, count),
        out_shape=[jax.ShapeDtypeStruct((rows, 3 * units), bf16)]
        + [jax.ShapeDtypeStruct((CAP, depth + LANES), back_type)] * count,
        in_specs=[VMEM] * count + [HBM] * 3,
        out_specs=[VMEM] * (count + 1),
        scratch_shapes=[pltpu.VMEM((rows, depth), bf16)] * 2
        + [pltpu.VMEM((rows, units), f32)] * 3
        + [pltpu.VMEM((rows, 2 * units), bf16)]
        + weight_scratch(3, depth, units),
        compiler_params=ALONE,
        cost_estimate=pl.CostEstimate(flops=36 * 192 * depth * units, bytes_accessed=MIB, transcendentals=0),
    )(*pieces, *weights)
    return outs[0], outs[1:]


def take_kernel(n_expert, placing_ref, *refs):
    pieces = refs[:n_expert]
    out_ref, prob_ref, rows = refs[n_expert:]
    count, width = out_ref.shape
    exact = rows.dtype != bf16
    for k in range(n_expert):
        rows[k * CAP : (k + 1) * CAP, :] = pieces[k][...]
    placing = placing_ref[...].astype(rows.dtype)
    for at in range(0, width, 512):
        part = lax.dot_general(
            placing, rows[:, at : at + 512], (((0,), (0,)), ((), ())),
            precision=highest if exact else None, preferred_element_type=f32,
        )
        out_ref[:, at : at + 512] = part.astype(bf16)
    column = rows[:, width:].astype(f32)[:, :1]
    prob_ref[...] = jnp.sum(placing_ref[...].astype(f32) * column, axis=0, keepdims=True).astype(bf16)


def take(placing, pieces):
    n_expert = len(pieces)
    count = placing.shape[1]
    width = pieces[0].shape[1] - LANES
    grad, prob = pl.pallas_call(
        functools.partial(take_kernel, n_expert),
        out_shape=[
            jax.ShapeDtypeStruct((count, width), bf16),
            jax.ShapeDtypeStruct((1, count), bf16),
        ],
        in_specs=[VMEM] * (n_expert + 1),
        out_specs=[VMEM] * 2,
        scratch_shapes=[pltpu.VMEM((n_expert * CAP, width + LANES), pieces[0].dtype)],
        compiler_params=pltpu.CompilerParams(vmem_limit_bytes=32 * MIB) if pieces[0].dtype != bf16 else PARAMS,
        cost_estimate=SMALL,
    )(placing, *pieces)
    return grad, prob.reshape(count)


def shards(tokens, cotangent, route, prob, w_gate, w_up, w_down):
    n_expert = lax.axis_size("expert")
    n_dp = lax.axis_size("dp")
    width = tokens.shape[1]
    share = width // n_dp
    scale = 1.0 / math.sqrt(tokens.shape[0] * n_dp * n_expert)
    back_type = bf16 if n_expert == HOT else f32
    me = lax.axis_index("expert").astype(i32)
    weights = (w_gate[0], w_up[0], w_down[0])
    chips = range(n_dp // 2)
    home = [None] * n_expert

    def exchange(payload):
        return [payload[0]] + [flipped(payload[k], "dp", 2 * k) for k in chips[1:]]

    def swap(got):
        return flipped(jnp.concatenate([g[:, 4 * share :] for g in got]), "dp", 1)

    def give_back(home, shifts, back):
        home = list(home)
        for i, k in enumerate(shifts):
            home[k] = shifted(back[i], "expert", n_expert - k)
        return home

    placing, pieces = place(me, route, prob, tokens, cotangent, n_expert)
    odd = list(range(1, n_expert, 2))
    even = list(range(2, n_expert, 2))
    first = [shifted(pieces[k], "expert", k) for k in odd]

    theirs = flipped(cut(pieces[:1], width), "dp", 1)
    terms, back = chunk_rows(pieces[:1], weights, back_type)
    home[0] = back[0]
    payload = pack(pieces[:1], theirs, terms, width)
    got_local = exchange(payload)
    late, first, got_local = lax.optimization_barrier(
        ([pieces[k] for k in even], first, got_local)
    )
    second = [shifted(piece, "expert", k) for piece, k in zip(late, even)]

    theirs = flipped(cut(first, width), "dp", 1)
    terms, back = chunk_rows(first, weights, back_type)
    got_first = exchange(pack(first, theirs, terms, width))
    home = give_back(home, odd[:-1], back[:-1])
    last = back[-1]
    sums = weight_sums(got_local, swap(got_local), None, share, None)

    second, sums, home, last = lax.optimization_barrier((second, sums, home, last))
    home = give_back(home, odd[-1:], [last])
    theirs = flipped(cut(second, width), "dp", 1)
    terms, back = chunk_rows(second, weights, back_type)
    home = give_back(home, even, back)
    payload, got_first = lax.optimization_barrier((pack(second, theirs, terms, width), got_first))
    sums = weight_sums(got_first, swap(got_first), sums, share, None)
    got_second, home, sums = lax.optimization_barrier((exchange(payload), home, sums))
    sums = weight_sums(got_second, swap(got_second), sums, share, scale)

    grad_input, grad_prob = take(placing, home)
    return (grad_input, grad_prob, *[total[None] for total in sums])


def solution(mesh):
    placed = (
        P(("dp", "expert"), None),
        P(("dp", "expert"), None),
        P(("dp", "expert"), None),
        P(("dp", "expert")),
        P("expert", None, None),
        P("expert", None, None),
        P("expert", None, None),
    )
    return jax.shard_map(
        shards,
        mesh=mesh,
        in_specs=placed,
        out_specs=(
            P(("dp", "expert"), None),
            P(("dp", "expert")),
            P("expert", "dp", None),
            P("expert", "dp", None),
            P("expert", "dp", None),
        ),
        check_vma=False,
    )
```

time: 124 us -> 95.3 us (0.77)
  Pallas kernels: 0 us -> 32.3 us
  matrix products: 28.7 us -> 0 us
  between operations: 14.3 us -> 0.9 us
  waiting for transfers between devices: 49.6 us -> 36.4 us
  other arithmetic: 3.91 us -> 0.16 us
  starting transfers between devices: 24.4 us -> 21.7 us
    pallas_call x0 -> x14, Pallas kernels: none -> 32.3 us  [the longest x3 27.2 us: chunk_rows(): pl.pallas_call(functools.partial(chunk_kernel, count), out_shape=[jax.Sha...]
    dot_general x11 -> x0, matrix products: 28.7 us -> none  [the longest x3 8.38 us: over_rows(): lax.dot_general(cols, term, (((0,), (0,)), ((), ())), preferred_element_t...]
    all_gather x1 -> x0, waiting for transfers between devices: 15.5 us -> none  [shards(): all_terms = lax.all_gather(terms, 'dp', axis=1, tiled=True)]
    ppermute x0 -> x15, starting transfers between devices: none -> 11.8 us  [flipped(): return lax.ppermute(values, axis, [(i, i ^ mask) for i in range(size)])]
    ppermute x0 -> x15, waiting for transfers between devices: none -> 8.98 us  [flipped(): return lax.ppermute(values, axis, [(i, i ^ mask) for i in range(size)])]
    all_to_all x2 -> x0, starting transfers between devices: 7.45 us -> none  [the longest x1 3.73 us: shards(): lax.all_to_all(row_tok.reshape(rows, n_dp, width // n_dp).transpose(1, 0,...]
    ppermute x9 -> x6, starting transfers between devices: 16.9 us -> 9.99 us  [shifted(): lax.ppermute(values, axis, [(i, (i + by) % size) for i in range(size)])]
    ppermute x9 -> x6, waiting for transfers between devices: 33.6 us -> 27.4 us  [shifted(): lax.ppermute(values, axis, [(i, (i + by) % size) for i in range(size)])]
  transfers between devices with their start and end apart: 12 -> 21, of which waited for: 5 -> 8; matrix products, arithmetic and copies ran while one was open for 19% -> 0% of each run, Pallas kernels for 0% -> 32%
where the time goes in v5:
time: 95.3 us; the launch traced here: 95 us
  waiting for transfers between devices  36.4 us (38%)
  Pallas kernels  32.3 us (34%)
  starting transfers between devices  21.7 us (23%)
  local copies, waits for them, and re-layouts  3.56 us (4%)
    ppermute x6, waiting for transfers between devices, shifted(): lax.ppermute(values, axis, [(i, (i + by) % size) for i in range(size)])  27.4 us
    pallas_call x3, Pallas kernels, chunk_rows(): pl.pallas_call(functools.partial(chunk_kernel, count), out_shape=[jax.Sha...  27.2 us
    ppermute x15, starting transfers between devices, flipped(): return lax.ppermute(values, axis, [(i, i ^ mask) for i in range(size)])  11.8 us
    ppermute x6, starting transfers between devices, shifted(): lax.ppermute(values, axis, [(i, (i + by) % size) for i in range(size)])  9.99 us
    ppermute x15, waiting for transfers between devices, flipped(): return lax.ppermute(values, axis, [(i, i ^ mask) for i in range(size)])  8.98 us
    unnamed x8, local copies, waits for them, and re-layouts  3.39 us
    pallas_call x3, Pallas kernels, weight_sums(): pl.pallas_call(functools.partial(sum_kernel, chips, share, units, scale,...  2.91 us
  transfers between devices with their start and end apart: 21, of which 8 were waited for; matrix products, arithmetic and copies ran while one was open for 0% of the time, Pallas kernels for 32%

profile of v5, /device:TPU:0, one launch (start us, length us, event | category | flops | bytes accessed | tf_op | source)
XLA Modules:
  0.0 95.0 jit_solution(4252437017341539292)
XLA Ops:
  0.6 1.0 %copy-done = bf16[128,2048]{1,0:T(8,128)(2,1)S(1)} copy-done((bf16[128,2048]{1,0:T(8,128)(2,1)S(1)}, bf16[128,2048]{1,0:T(8,128)(2,1)}, u32[]{:S(2)}) %copy-start) | copy-done | bytes 524312
  1.7 1.0 %copy-done.1 = bf16[128,2048]{1,0:T(8,128)(2,1)S(1)} copy-done((bf16[128,2048]{1,0:T(8,128)(2,1)S(1)}, bf16[128,2048]{1,0:T(8,128)(2,1)}, u32[]{:S(2)}) %copy-start.1) | copy-done | bytes 524312
  5.3 2.6 %collective-permute-start = (bf16[48,4224]{1,0:T(8,128)(2,1)S(1)}, bf16[48,4224]{1,0:T(8,128)(2,1)S(1)}, u32[]{:S(2)}, u32[]{:S(2)}) collective-permute-start(bf16[48,4224]{1,0:T(8,128)(2,1)S(1)} %get-tuple-element.75), channel_id=1, source_target_pairs={{0,1},{1,2},{2,3},{3,0},{4,5},{5,6},{6,7},{7,4},{8,9},{9,10},{10,1... | collective-permute-start | bytes 1216520 | tf_op jit(solution)/shard_map/ppermute | solution.py:31
  7.9 2.1 %collective-permute-start.1 = (bf16[48,4224]{1,0:T(8,128)(2,1)S(1)}, bf16[48,4224]{1,0:T(8,128)(2,1)S(1)}, u32[]{:S(2)}, u32[]{:S(2)}) collective-permute-start(bf16[48,4224]{1,0:T(8,128)(2,1)S(1)} %get-tuple-element.76), channel_id=1, source_target_pairs={{0,3},{1,0},{2,1},{3,2},{4,7},{5,4},{6,5},{7,6},{8,11},{9,8},{10,9... | collective-permute-start | bytes 1216520 | tf_op jit(solution)/shard_map/ppermute | solution.py:31
  10.0 9.0 %shard_map.112 = (bf16[48,1536]{1,0:T(8,128)(2,1)S(1)}, bf16[48,2176]{1,0:T(8,128)(2,1)S(1)}) custom-call(bf16[48,4224]{1,0:T(8,128)(2,1)S(1)} %get-tuple-element.77.refs_0_, f32[2048,512]{1,0:T(8,128)} %bitcast.13, f32[2048,512]{1,0:T(8,128)} %bitcast.16, f32[2048,512]{1,0:T(8,128)} %bitcast.19), custom_call_target="tpu_custom_call" | custom-call | flops 7247757312 | bytes 1048576 | tf_op jit(solution)/shard_map/pallas_call | solution.py:297
  19.1 1.7 %collective-permute-start.3 = (bf16[48,2560]{1,0:T(8,128)(2,1)S(1)}, bf16[48,2560]{1,0:T(8,128)(2,1)S(1)}, u32[]{:S(2)}, u32[]{:S(2)}) collective-permute-start(bf16[48,2560]{1,0:T(8,128)(2,1)S(1)} %get-tuple-element.80), channel_id=1, source_target_pairs={{0,8},{4,12},{8,0},{12,4},{16,24},{20,28},{24,16},{28,20},{1,9},{5... | collective-permute-start | bytes 737288 | tf_op jit(solution)/shard_map/ppermute | solution.py:36
  20.8 1.5 %collective-permute-start.4 = (bf16[48,2560]{1,0:T(8,128)(2,1)S(1)}, bf16[48,2560]{1,0:T(8,128)(2,1)S(1)}, u32[]{:S(2)}, u32[]{:S(2)}) collective-permute-start(bf16[48,2560]{1,0:T(8,128)(2,1)S(1)} %get-tuple-element.81), channel_id=1, source_target_pairs={{0,16},{4,20},{8,24},{12,28},{16,0},{20,4},{24,8},{28,12},{1,17},{... | collective-permute-start | bytes 737288 | tf_op jit(solution)/shard_map/ppermute | solution.py:36
  22.7 5.3 %collective-permute-done.1.refs_1_ = bf16[48,4224]{1,0:T(8,128)(2,1)S(1)} collective-permute-done((bf16[48,4224]{1,0:T(8,128)(2,1)S(1)}, bf16[48,4224]{1,0:T(8,128)(2,1)S(1)}, u32[]{:S(2)}, u32[]{:S(2)}) %collective-permute-start.1) | collective-permute-done | bytes 405536 | tf_op jit(solution)/shard_map/ppermute | solution.py:31
  28.1 5.6 %collective-permute-done.4.refs_2_ = bf16[48,2560]{1,0:T(8,128)(2,1)S(1)} collective-permute-done((bf16[48,2560]{1,0:T(8,128)(2,1)S(1)}, bf16[48,2560]{1,0:T(8,128)(2,1)S(1)}, u32[]{:S(2)}, u32[]{:S(2)}) %collective-permute-start.4) | collective-permute-done | bytes 245792 | tf_op jit(solution)/shard_map/ppermute | solution.py:36
  34.9 9.2 %shard_map.115 = (bf16[96,1536]{1,0:T(8,128)(2,1)S(1)}, bf16[48,2176]{1,0:T(8,128)(2,1)S(1)}, bf16[48,2176]{1,0:T(8,128)(2,1)S(1)}) custom-call(bf16[48,4224]{1,0:T(8,128)(2,1)S(1)} %collective-permute-done.refs_0_, bf16[48,4224]{1,0:T(8,128)(2,1)S(1)} %collective-permute-done.1.refs_1_, f32[2048,512]{1,0:T(8,128)} %bitcast.14, f32[2048,512]{1,0:T(8,128)} %bitcast.17, ...), custom_call_target="tpu_custom_call" | custom-call | flops 7247757312 | bytes 1048576 | tf_op jit(solution)/shard_map/pallas_call | solution.py:297
  44.1 1.6 %collective-permute-start.8 = (bf16[48,2176]{1,0:T(8,128)(2,1)S(1)}, bf16[48,2176]{1,0:T(8,128)(2,1)S(1)}, u32[]{:S(2)}, u32[]{:S(2)}) collective-permute-start(bf16[48,2176]{1,0:T(8,128)(2,1)S(1)} %get-tuple-element.94), channel_id=1, source_target_pairs={{0,3},{1,0},{2,1},{3,2},{4,7},{5,4},{6,5},{7,6},{8,11},{9,8},{10,9... | collective-permute-start | bytes 626696 | tf_op jit(solution)/shard_map/ppermute | solution.py:31
  45.8 1.3 %collective-permute-start.11 = (bf16[96,2560]{1,0:T(8,128)(2,1)S(1)}, bf16[96,2560]{1,0:T(8,128)(2,1)S(1)}, u32[]{:S(2)}, u32[]{:S(2)}) collective-permute-start(bf16[96,2560]{1,0:T(8,128)(2,1)S(1)} %get-tuple-element.104), channel_id=1, source_target_pairs={{0,8},{4,12},{8,0},{12,4},{16,24},{20,28},{24,16},{28,20},{1,9},{5... | collective-permute-start | bytes 1474568 | tf_op jit(solution)/shard_map/ppermute | solution.py:36
  48.0 1.4 %collective-permute-start.13 = (bf16[96,2560]{1,0:T(8,128)(2,1)S(1)}, bf16[96,2560]{1,0:T(8,128)(2,1)S(1)}, u32[]{:S(2)}, u32[]{:S(2)}) collective-permute-start(bf16[96,2560]{1,0:T(8,128)(2,1)S(1)} %get-tuple-element.106), channel_id=1, source_target_pairs={{0,24},{4,28},{8,16},{12,20},{16,8},{20,12},{24,0},{28,4},{1,25},{... | collective-permute-start | bytes 1474568 | tf_op jit(solution)/shard_map/ppermute | solution.py:36
  50.0 8.8 %collective-permute-done.8.refs_1_ = bf16[48,2176]{1,0:T(8,128)(2,1)S(1)} collective-permute-done((bf16[48,2176]{1,0:T(8,128)(2,1)S(1)}, bf16[48,2176]{1,0:T(8,128)(2,1)S(1)}, u32[]{:S(2)}, u32[]{:S(2)}) %collective-permute-start.8) | collective-permute-done | bytes 208928 | tf_op jit(solution)/shard_map/ppermute | solution.py:31
  59.0 9.0 %shard_map.117 = (bf16[48,1536]{1,0:T(8,128)(2,1)S(1)}, bf16[48,2176]{1,0:T(8,128)(2,1)S(1)}) custom-call(bf16[48,4224]{1,0:T(8,128)(2,1)S(1)} %collective-permute-done.6.refs_0_, f32[2048,512]{1,0:T(8,128)} %bitcast.15, f32[2048,512]{1,0:T(8,128)} %bitcast.18, f32[2048,512]{1,0:T(8,128)} %bitcast.21), custom_call_target="tpu_custom_call" | custom-call | flops 7247757312 | bytes 1048576 | tf_op jit(solution)/shard_map/pallas_call | solution.py:297
  68.1 0.9 collective-permute-done.12.refs_2_
  69.0 1.6 %collective-permute-done.13.refs_3_ = bf16[96,2560]{1,0:T(8,128)(2,1)S(1)} collective-permute-done((bf16[96,2560]{1,0:T(8,128)(2,1)S(1)}, bf16[96,2560]{1,0:T(8,128)(2,1)S(1)}, u32[]{:S(2)}, u32[]{:S(2)}) %collective-permute-start.13) | collective-permute-done | bytes 491552 | tf_op jit(solution)/shard_map/ppermute | solution.py:36
  71.7 1.5 %collective-permute-start.15 = (bf16[48,2560]{1,0:T(8,128)(2,1)S(1)}, bf16[48,2560]{1,0:T(8,128)(2,1)S(1)}, u32[]{:S(2)}, u32[]{:S(2)}) collective-permute-start(bf16[48,2560]{1,0:T(8,128)(2,1)S(1)} %get-tuple-element.109), channel_id=1, source_target_pairs={{0,16},{4,20},{8,24},{12,28},{16,0},{20,4},{24,8},{28,12},{1,17},{... | collective-permute-start | bytes 737288 | tf_op jit(solution)/shard_map/ppermute | solution.py:36
  73.2 1.2 %collective-permute-start.16 = (bf16[48,2560]{1,0:T(8,128)(2,1)S(1)}, bf16[48,2560]{1,0:T(8,128)(2,1)S(1)}, u32[]{:S(2)}, u32[]{:S(2)}) collective-permute-start(bf16[48,2560]{1,0:T(8,128)(2,1)S(1)} %get-tuple-element.110), channel_id=1, source_target_pairs={{0,24},{4,28},{8,16},{12,20},{16,8},{20,12},{24,0},{28,4},{1,25},{... | collective-permute-start | bytes 737288 | tf_op jit(solution)/shard_map/ppermute | solution.py:36
  75.1 2.2 %collective-permute-start.17 = (bf16[48,2176]{1,0:T(8,128)(2,1)S(1)}, bf16[48,2176]{1,0:T(8,128)(2,1)S(1)}, u32[]{:S(2)}, u32[]{:S(2)}) collective-permute-start(bf16[48,2176]{1,0:T(8,128)(2,1)S(1)} %get-tuple-element.113), channel_id=1, source_target_pairs={{0,2},{1,3},{2,0},{3,1},{4,6},{5,7},{6,4},{7,5},{8,10},{9,11},{10,... | collective-permute-start | bytes 626696 | tf_op jit(solution)/shard_map/ppermute | solution.py:31
  78.1 6.2 %collective-permute-done.18.refs_3_ = bf16[48,2176]{1,0:T(8,128)(2,1)S(1)} collective-permute-done((bf16[48,2176]{1,0:T(8,128)(2,1)S(1)}, bf16[48,2176]{1,0:T(8,128)(2,1)S(1)}, u32[]{:S(2)}, u32[]{:S(2)}) %collective-permute-start.18) | collective-permute-done | bytes 208928 | tf_op jit(solution)/shard_map/ppermute | solution.py:31
  84.4 7.0 %collective-permute-done.17.refs_2_ = bf16[48,2176]{1,0:T(8,128)(2,1)S(1)} collective-permute-done((bf16[48,2176]{1,0:T(8,128)(2,1)S(1)}, bf16[48,2176]{1,0:T(8,128)(2,1)S(1)}, u32[]{:S(2)}, u32[]{:S(2)}) %collective-permute-start.17) | collective-permute-done | bytes 208928 | tf_op jit(solution)/shard_map/ppermute | solution.py:31
  91.6 1.1 %shard_map.122 = (bf16[128,2048]{1,0:T(8,128)(2,1)}, bf16[1,128]{1,0:T(2,128)(2,1)}) custom-call(bf16[192,128]{1,0:T(8,128)(2,1)S(1)} %get-tuple-element.73.placing_ref, bf16[48,2176]{1,0:T(8,128)(2,1)S(1)} %get-tuple-element.125.refs_0_, bf16[48,2176]{1,0:T(8,128)(2,1)S(1)} %collective-permute-done.8.refs_1_, ...), custom_call_target="tpu_custom_call" | custom-call | bytes 1024 | tf_op jit(solution)/shard_map/pallas_call | solution.py:335
  93.6 1.5 %shard_map.123 = (f32[256,512]{1,0:T(8,128)}, f32[256,512]{1,0:T(8,128)}, f32[256,512]{1,0:T(8,128)}) custom-call(bf16[48,2560]{1,0:T(8,128)(2,1)S(1)} %get-tuple-element.131.refs_0_, bf16[48,2560]{1,0:T(8,128)(2,1)S(1)} %collective-permute-done.14.refs_1_, bf16[48,2560]{1,0:T(8,128)(2,1)S(1)} %collective-permute-done.15.refs_2_, ...), custom_call_target="tpu_custom_call" | custom-call | bytes 1024 | tf_op jit(solution)/shard_map/pallas_call | solution.py:156
  (55 shorter events, 9.6 us)
Async XLA Ops:
  0.6 1.0 %copy-start = (bf16[128,2048]{1,0:T(8,128)(2,1)S(1)}, bf16[128,2048]{1,0:T(8,128)(2,1)}, u32[]{:S(2)}) copy-start(bf16[128,2048]{1,0:T(8,128)(2,1)} %tok_ref.1) | copy-start | bytes 1572868
  1.7 1.0 %copy-start.1 = (bf16[128,2048]{1,0:T(8,128)(2,1)S(1)}, bf16[128,2048]{1,0:T(8,128)(2,1)}, u32[]{:S(2)}) copy-start(bf16[128,2048]{1,0:T(8,128)(2,1)} %cot_ref.1) | copy-start | bytes 1572868
  2.7 0.7 copy-start.2
  4.8 14.3 %collective-permute-start.2 = (bf16[4,48,512]{2,1,0:T(8,128)(2,1)S(1)}, bf16[4,48,512]{2,1,0:T(8,128)(2,1)S(1)}, u32[]{:S(2)}, u32[]{:S(2)}) collective-permute-start(bf16[4,48,512]{2,1,0:T(8,128)(2,1)S(1)} %shard_map.111), channel_id=1, source_target_pairs={{0,4},{4,0},{8,12},{12,8},{16,20},{20,16},{24,28},{28,24},{1,5},{5... | collective-permute-start | bytes 589832 | tf_op jit(solution)/shard_map/ppermute | solution.py:36
  5.3 17.4 %collective-permute-start = (bf16[48,4224]{1,0:T(8,128)(2,1)S(1)}, bf16[48,4224]{1,0:T(8,128)(2,1)S(1)}, u32[]{:S(2)}, u32[]{:S(2)}) collective-permute-start(bf16[48,4224]{1,0:T(8,128)(2,1)S(1)} %get-tuple-element.75), channel_id=1, source_target_pairs={{0,1},{1,2},{2,3},{3,0},{4,5},{5,6},{6,7},{7,4},{8,9},{9,10},{10,1... | collective-permute-start | bytes 1216520 | tf_op jit(solution)/shard_map/ppermute | solution.py:31
  7.9 20.1 %collective-permute-start.1 = (bf16[48,4224]{1,0:T(8,128)(2,1)S(1)}, bf16[48,4224]{1,0:T(8,128)(2,1)S(1)}, u32[]{:S(2)}, u32[]{:S(2)}) collective-permute-start(bf16[48,4224]{1,0:T(8,128)(2,1)S(1)} %get-tuple-element.76), channel_id=1, source_target_pairs={{0,3},{1,0},{2,1},{3,2},{4,7},{5,4},{6,5},{7,6},{8,11},{9,8},{10,9... | collective-permute-start | bytes 1216520 | tf_op jit(solution)/shard_map/ppermute | solution.py:31
  19.1 8.9 %collective-permute-start.3 = (bf16[48,2560]{1,0:T(8,128)(2,1)S(1)}, bf16[48,2560]{1,0:T(8,128)(2,1)S(1)}, u32[]{:S(2)}, u32[]{:S(2)}) collective-permute-start(bf16[48,2560]{1,0:T(8,128)(2,1)S(1)} %get-tuple-element.80), channel_id=1, source_target_pairs={{0,8},{4,12},{8,0},{12,4},{16,24},{20,28},{24,16},{28,20},{1,9},{5... | collective-permute-start | bytes 737288 | tf_op jit(solution)/shard_map/ppermute | solution.py:36
  20.8 12.8 %collective-permute-start.4 = (bf16[48,2560]{1,0:T(8,128)(2,1)S(1)}, bf16[48,2560]{1,0:T(8,128)(2,1)S(1)}, u32[]{:S(2)}, u32[]{:S(2)}) collective-permute-start(bf16[48,2560]{1,0:T(8,128)(2,1)S(1)} %get-tuple-element.81), channel_id=1, source_target_pairs={{0,16},{4,20},{8,24},{12,28},{16,0},{20,4},{24,8},{28,12},{1,17},{... | collective-permute-start | bytes 737288 | tf_op jit(solution)/shard_map/ppermute | solution.py:36
  22.4 11.3 %collective-permute-start.5 = (bf16[48,2560]{1,0:T(8,128)(2,1)S(1)}, bf16[48,2560]{1,0:T(8,128)(2,1)S(1)}, u32[]{:S(2)}, u32[]{:S(2)}) collective-permute-start(bf16[48,2560]{1,0:T(8,128)(2,1)S(1)} %get-tuple-element.82), channel_id=1, source_target_pairs={{0,24},{4,28},{8,16},{12,20},{16,8},{20,12},{24,0},{28,4},{1,25},{... | collective-permute-start | bytes 737288 | tf_op jit(solution)/shard_map/ppermute | solution.py:36
  33.7 12.0 %collective-permute-start.10 = (bf16[4,96,512]{2,1,0:T(8,128)(2,1)S(1)}, bf16[4,96,512]{2,1,0:T(8,128)(2,1)S(1)}, u32[]{:S(2)}, u32[]{:S(2)}) collective-permute-start(bf16[4,96,512]{2,1,0:T(8,128)(2,1)S(1)} %shard_map.119), channel_id=1, source_target_pairs={{0,4},{4,0},{8,12},{12,8},{16,20},{20,16},{24,28},{28,24},{1,5},{5... | collective-permute-start | bytes 1179656 | tf_op jit(solution)/shard_map/ppermute | solution.py:36
  33.8 25.0 %collective-permute-start.6 = (bf16[48,4224]{1,0:T(8,128)(2,1)S(1)}, bf16[48,4224]{1,0:T(8,128)(2,1)S(1)}, u32[]{:S(2)}, u32[]{:S(2)}) collective-permute-start(bf16[48,4224]{1,0:T(8,128)(2,1)S(1)} %get-tuple-element.83), channel_id=1, source_target_pairs={{0,2},{1,3},{2,0},{3,1},{4,6},{5,7},{6,4},{7,5},{8,10},{9,11},{10,... | collective-permute-start | bytes 1216520 | tf_op jit(solution)/shard_map/ppermute | solution.py:31
  34.7 13.3 %collective-permute-start.7 = (bf16[192,1536]{1,0:T(8,128)(2,1)S(1)}, bf16[192,1536]{1,0:T(8,128)(2,1)S(1)}, u32[]{:S(2)}, u32[]{:S(2)}) collective-permute-start(bf16[192,1536]{1,0:T(8,128)(2,1)S(1)} %pad_maximum_fusion.1), channel_id=1, source_target_pairs={{0,4},{4,0},{8,12},{12,8},{16,20},{20,16},{24,28},{28,24},{1,5},{5... | collective-permute-start | bytes 1769480 | tf_op jit(solution)/shard_map/ppermute | solution.py:36
  44.1 14.7 %collective-permute-start.8 = (bf16[48,2176]{1,0:T(8,128)(2,1)S(1)}, bf16[48,2176]{1,0:T(8,128)(2,1)S(1)}, u32[]{:S(2)}, u32[]{:S(2)}) collective-permute-start(bf16[48,2176]{1,0:T(8,128)(2,1)S(1)} %get-tuple-element.94), channel_id=1, source_target_pairs={{0,3},{1,0},{2,1},{3,2},{4,7},{5,4},{6,5},{7,6},{8,11},{9,8},{10,9... | collective-permute-start | bytes 626696 | tf_op jit(solution)/shard_map/ppermute | solution.py:31
  45.8 22.2 %collective-permute-start.11 = (bf16[96,2560]{1,0:T(8,128)(2,1)S(1)}, bf16[96,2560]{1,0:T(8,128)(2,1)S(1)}, u32[]{:S(2)}, u32[]{:S(2)}) collective-permute-start(bf16[96,2560]{1,0:T(8,128)(2,1)S(1)} %get-tuple-element.104), channel_id=1, source_target_pairs={{0,8},{4,12},{8,0},{12,4},{16,24},{20,28},{24,16},{28,20},{1,9},{5... | collective-permute-start | bytes 1474568 | tf_op jit(solution)/shard_map/ppermute | solution.py:36
  47.1 21.8 %collective-permute-start.12 = (bf16[96,2560]{1,0:T(8,128)(2,1)S(1)}, bf16[96,2560]{1,0:T(8,128)(2,1)S(1)}, u32[]{:S(2)}, u32[]{:S(2)}) collective-permute-start(bf16[96,2560]{1,0:T(8,128)(2,1)S(1)} %get-tuple-element.105), channel_id=1, source_target_pairs={{0,16},{4,20},{8,24},{12,28},{16,0},{20,4},{24,8},{28,12},{1,17},{... | collective-permute-start | bytes 1474568 | tf_op jit(solution)/shard_map/ppermute | solution.py:36
  48.0 22.6 %collective-permute-start.13 = (bf16[96,2560]{1,0:T(8,128)(2,1)S(1)}, bf16[96,2560]{1,0:T(8,128)(2,1)S(1)}, u32[]{:S(2)}, u32[]{:S(2)}) collective-permute-start(bf16[96,2560]{1,0:T(8,128)(2,1)S(1)} %get-tuple-element.106), channel_id=1, source_target_pairs={{0,24},{4,28},{8,16},{12,20},{16,8},{20,12},{24,0},{28,4},{1,25},{... | collective-permute-start | bytes 1474568 | tf_op jit(solution)/shard_map/ppermute | solution.py:36
  58.9 9.1 %collective-permute-start.9 = (bf16[4,48,512]{2,1,0:T(8,128)(2,1)S(1)}, bf16[4,48,512]{2,1,0:T(8,128)(2,1)S(1)}, u32[]{:S(2)}, u32[]{:S(2)}) collective-permute-start(bf16[4,48,512]{2,1,0:T(8,128)(2,1)S(1)} %shard_map.116), channel_id=1, source_target_pairs={{0,4},{4,0},{8,12},{12,8},{16,20},{20,16},{24,28},{28,24},{1,5},{5... | collective-permute-start | bytes 589832 | tf_op jit(solution)/shard_map/ppermute | solution.py:36
  70.8 4.3 %collective-permute-start.19 = (bf16[384,1536]{1,0:T(8,128)(2,1)S(1)}, bf16[384,1536]{1,0:T(8,128)(2,1)S(1)}, u32[]{:S(2)}, u32[]{:S(2)}) collective-permute-start(bf16[384,1536]{1,0:T(8,128)(2,1)S(1)} %pad_maximum_fusion), channel_id=1, source_target_pairs={{0,4},{4,0},{8,12},{12,8},{16,20},{20,16},{24,28},{28,24},{1,5},{5... | collective-permute-start | bytes 3538952 | tf_op jit(solution)/shard_map/ppermute | solution.py:36
  70.9 20.5 %collective-permute-start.14 = (bf16[48,2560]{1,0:T(8,128)(2,1)S(1)}, bf16[48,2560]{1,0:T(8,128)(2,1)S(1)}, u32[]{:S(2)}, u32[]{:S(2)}) collective-permute-start(bf16[48,2560]{1,0:T(8,128)(2,1)S(1)} %get-tuple-element.108), channel_id=1, source_target_pairs={{0,8},{4,12},{8,0},{12,4},{16,24},{20,28},{24,16},{28,20},{1,9},{5... | collective-permute-start | bytes 737288 | tf_op jit(solution)/shard_map/ppermute | solution.py:36
  71.7 19.6 %collective-permute-start.15 = (bf16[48,2560]{1,0:T(8,128)(2,1)S(1)}, bf16[48,2560]{1,0:T(8,128)(2,1)S(1)}, u32[]{:S(2)}, u32[]{:S(2)}) collective-permute-start(bf16[48,2560]{1,0:T(8,128)(2,1)S(1)} %get-tuple-element.109), channel_id=1, source_target_pairs={{0,16},{4,20},{8,24},{12,28},{16,0},{20,4},{24,8},{28,12},{1,17},{... | collective-permute-start | bytes 737288 | tf_op jit(solution)/shard_map/ppermute | solution.py:36
  73.2 18.1 %collective-permute-start.16 = (bf16[48,2560]{1,0:T(8,128)(2,1)S(1)}, bf16[48,2560]{1,0:T(8,128)(2,1)S(1)}, u32[]{:S(2)}, u32[]{:S(2)}) collective-permute-start(bf16[48,2560]{1,0:T(8,128)(2,1)S(1)} %get-tuple-element.110), channel_id=1, source_target_pairs={{0,24},{4,28},{8,16},{12,20},{16,8},{20,12},{24,0},{28,4},{1,25},{... | collective-permute-start | bytes 737288 | tf_op jit(solution)/shard_map/ppermute | solution.py:36
  74.4 9.9 %collective-permute-start.18 = (bf16[48,2176]{1,0:T(8,128)(2,1)S(1)}, bf16[48,2176]{1,0:T(8,128)(2,1)S(1)}, u32[]{:S(2)}, u32[]{:S(2)}) collective-permute-start(bf16[48,2176]{1,0:T(8,128)(2,1)S(1)} %get-tuple-element.114), channel_id=1, source_target_pairs={{0,1},{1,2},{2,3},{3,0},{4,5},{5,6},{6,7},{7,4},{8,9},{9,10},{10,1... | collective-permute-start | bytes 626696 | tf_op jit(solution)/shard_map/ppermute | solution.py:31
  75.1 16.2 %collective-permute-start.17 = (bf16[48,2176]{1,0:T(8,128)(2,1)S(1)}, bf16[48,2176]{1,0:T(8,128)(2,1)S(1)}, u32[]{:S(2)}, u32[]{:S(2)}) collective-permute-start(bf16[48,2176]{1,0:T(8,128)(2,1)S(1)} %get-tuple-element.113), channel_id=1, source_target_pairs={{0,2},{1,3},{2,0},{3,1},{4,6},{5,7},{6,4},{7,5},{8,10},{9,11},{10,... | collective-permute-start | bytes 626696 | tf_op jit(solution)/shard_map/ppermute | solution.py:31
  91.5 2.1 %collective-permute-start.20 = (bf16[192,1536]{1,0:T(8,128)(2,1)S(1)}, bf16[192,1536]{1,0:T(8,128)(2,1)S(1)}, u32[]{:S(2)}, u32[]{:S(2)}) collective-permute-start(bf16[192,1536]{1,0:T(8,128)(2,1)S(1)} %pad_maximum_fusion.2), channel_id=1, source_target_pairs={{0,4},{4,0},{8,12},{12,8},{16,20},{20,16},{24,28},{28,24},{1,5},{5... | collective-permute-start | bytes 1769480 | tf_op jit(solution)/shard_map/ppermute | solution.py:36
  (1 other events, 0.7 us)

commit v6 on v5

--- a/solution.py
+++ b/solution.py
@@ -95,6 +95,10 @@
 
 
 def pack(pieces, theirs, terms, width):
+    return list(packed(pieces, theirs, terms, width))
+
+
+def packed(pieces, theirs, terms, width):
     size = lax.axis_size("dp")
     share = width // size
     if share % LANES:
@@ -199,7 +203,6 @@
         + [jax.ShapeDtypeStruct((CAP, 2 * width + LANES), bf16)] * n_expert,
         in_specs=[SMEM] + [VMEM] * 4,
         out_specs=[VMEM] * (n_expert + 1),
-        compiler_params=PARAMS,
         cost_estimate=SMALL,
     )(me.reshape(1), route.reshape(1, count), prob.reshape(1, count), tokens, cotangent)
     return outs[0], outs[1:]
@@ -284,8 +287,9 @@
             high, low = halves(buffer[i, at : at + BLOCK, :])
             grad_hi = terms_ref[:, i * units : (i + 1) * units]
             grad_lo = low_ref[:, i * units : (i + 1) * units]
-            part = against(grad_hi, high) + against(grad_lo, high) + against(grad_hi, low)
+            part = against(high, grad_hi) + against(high, grad_lo) + against(low, grad_hi)
             total = part if total is None else total + part
+        total = total.T
         for k, out in enumerate(outs):
             out[:, at : at + BLOCK] = total[k * CAP : (k + 1) * CAP].astype(out.dtype)
 
@@ -380,27 +384,28 @@
     terms, back = chunk_rows(pieces[:1], weights, back_type)
     home[0] = back[0]
     payload = pack(pieces[:1], theirs, terms, width)
+    late, _ = lax.optimization_barrier(([pieces[k] for k in even], payload[0]))
+    second = [shifted(piece, "expert", k) for piece, k in zip(late, even)]
+    payload[-1], first = lax.optimization_barrier((payload[-1], first))
     got_local = exchange(payload)
-    late, first, got_local = lax.optimization_barrier(
-        ([pieces[k] for k in even], first, got_local)
-    )
-    second = [shifted(piece, "expert", k) for piece, k in zip(late, even)]
 
     theirs = flipped(cut(first, width), "dp", 1)
     terms, back = chunk_rows(first, weights, back_type)
-    got_first = exchange(pack(first, theirs, terms, width))
-    home = give_back(home, odd[:-1], back[:-1])
-    last = back[-1]
-    sums = weight_sums(got_local, swap(got_local), None, share, None)
-
-    second, sums, home, last = lax.optimization_barrier((second, sums, home, last))
-    home = give_back(home, odd[-1:], [last])
+    payload = pack(first, theirs, terms, width)
+    got_first = exchange(payload)
+
+    second, back, got_local, _ = lax.optimization_barrier((second, back, got_local, payload))
+    home = give_back(home, odd, back)
     theirs = flipped(cut(second, width), "dp", 1)
     terms, back = chunk_rows(second, weights, back_type)
+    sums = weight_sums(got_local, swap(got_local), None, share, None)
+    payload, got_first, sums, back, home = lax.optimization_barrier(
+        (pack(second, theirs, terms, width), got_first, sums, back, home)
+    )
     home = give_back(home, even, back)
-    payload, got_first = lax.optimization_barrier((pack(second, theirs, terms, width), got_first))
+    got_second = exchange(payload)
     sums = weight_sums(got_first, swap(got_first), sums, share, None)
-    got_second, home, sums = lax.optimization_barrier((exchange(payload), home, sums))
+    got_second, home, sums = lax.optimization_barrier((got_second, home, sums))
     sums = weight_sums(got_second, swap(got_second), sums, share, scale)
 
     grad_input, grad_prob = take(placing, home)

time: 95.3 us -> 90.7 us (0.952)
  waiting for transfers between devices: 36.4 us -> 28.5 us
  starting transfers between devices: 21.7 us -> 24.7 us
  Pallas kernels: 32.3 us -> 33.4 us
    ppermute x6, waiting for transfers between devices: 27.4 us -> 20.9 us  [shifted(): lax.ppermute(values, axis, [(i, (i + by) % size) for i in range(size)])]
    pallas_call x1, Pallas kernels: 0.69 us -> 3.03 us  [place(): pl.pallas_call(functools.partial(place_kernel, n_expert), out_shape=[jax....]
    ppermute x15, starting transfers between devices: 11.8 us -> 14.1 us  [flipped(): return lax.ppermute(values, axis, [(i, i ^ mask) for i in range(size)])]
    ppermute x15, waiting for transfers between devices: 8.98 us -> 7.56 us  [flipped(): return lax.ppermute(values, axis, [(i, i ^ mask) for i in range(size)])]
    pallas_call x3, Pallas kernels: 27.2 us -> 26 us  [chunk_rows(): pl.pallas_call(functools.partial(chunk_kernel, count), out_shape=[jax.Sha...]
  transfers between devices with their start and end apart: 21 -> 21, of which waited for: 8 -> 6; matrix products, arithmetic and copies ran while one was open for 0% -> 0% of each run, Pallas kernels for 32% -> 32%
where the time goes in v6:
time: 90.7 us; the launch traced here: 90.4 us
  Pallas kernels  33.4 us (37%)
  waiting for transfers between devices  28.5 us (31%)
  starting transfers between devices  24.7 us (27%)
  local copies, waits for them, and re-layouts  2.76 us (3%)
    pallas_call x3, Pallas kernels, chunk_rows(): pl.pallas_call(functools.partial(chunk_kernel, count), out_shape=[jax.Sha...  26 us
    ppermute x6, waiting for transfers between devices, shifted(): lax.ppermute(values, axis, [(i, (i + by) % size) for i in range(size)])  20.9 us
    ppermute x15, starting transfers between devices, flipped(): return lax.ppermute(values, axis, [(i, i ^ mask) for i in range(size)])  14.1 us
    ppermute x6, starting transfers between devices, shifted(): lax.ppermute(values, axis, [(i, (i + by) % size) for i in range(size)])  10.6 us
    ppermute x15, waiting for transfers between devices, flipped(): return lax.ppermute(values, axis, [(i, i ^ mask) for i in range(size)])  7.56 us
    pallas_call x1, Pallas kernels, place(): pl.pallas_call(functools.partial(place_kernel, n_expert), out_shape=[jax....  3.03 us
    pallas_call x3, Pallas kernels, weight_sums(): pl.pallas_call(functools.partial(sum_kernel, chips, share, units, scale,...  2.89 us
    unnamed x8, local copies, waits for them, and re-layouts  2.59 us
  transfers between devices with their start and end apart: 21, of which 6 were waited for; matrix products, arithmetic and copies ran while one was open for 0% of the time, Pallas kernels for 32%

profile of v6, /device:TPU:0, one launch (start us, length us, event | category | flops | bytes accessed | tf_op | source)
XLA Modules:
  0.0 90.4 jit_solution(9870507259876576807)
XLA Ops:
  0.6 3.0 %shard_map.110 = (bf16[192,128]{1,0:T(8,128)(2,1)}, bf16[48,4224]{1,0:T(8,128)(2,1)}, bf16[48,4224]{1,0:T(8,128)(2,1)}, bf16[48,4224]{1,0:T(8,128)(2,1)}, bf16[48,4224]{1,0:T(8,128)(2,1)}) custom-call(s32[1]{0:T(128)} %bitcast.me_ref, s32[1,128]{1,0:T(1,128)} %bitcast.11, bf16[1,128]{1,0:T(2,128)(2,1)} %bitcast.12, bf16[128,2048]{1,0:T(8,128)(2,1)} %tok_ref.1, ...), custom_call_target="tpu_custom_call" | custom-call | bytes 1024 | tf_op jit(solution)/shard_map/pallas_call | solution.py:200
  3.7 1.0 %copy-done = bf16[48,4224]{1,0:T(8,128)(2,1)S(1)} copy-done((bf16[48,4224]{1,0:T(8,128)(2,1)S(1)}, bf16[48,4224]{1,0:T(8,128)(2,1)}, u32[]{:S(2)}) %copy-start) | copy-done | bytes 405528
  5.2 2.6 %collective-permute-start.2 = (bf16[48,4224]{1,0:T(8,128)(2,1)}, bf16[48,4224]{1,0:T(8,128)(2,1)S(1)}, u32[]{:S(2)}, u32[]{:S(2)}) collective-permute-start(bf16[48,4224]{1,0:T(8,128)(2,1)} %get-tuple-element.84), channel_id=1, source_target_pairs={{0,1},{1,2},{2,3},{3,0},{4,5},{5,6},{6,7},{7,4},{8,9},{9,10},{10,1... | collective-permute-start | bytes 1216520 | tf_op jit(solution)/shard_map/ppermute | solution.py:31
  7.8 2.1 %collective-permute-start.3 = (bf16[48,4224]{1,0:T(8,128)(2,1)}, bf16[48,4224]{1,0:T(8,128)(2,1)S(1)}, u32[]{:S(2)}, u32[]{:S(2)}) collective-permute-start(bf16[48,4224]{1,0:T(8,128)(2,1)} %get-tuple-element.85), channel_id=1, source_target_pairs={{0,3},{1,0},{2,1},{3,2},{4,7},{5,4},{6,5},{7,6},{8,11},{9,8},{10,9... | collective-permute-start | bytes 1216520 | tf_op jit(solution)/shard_map/ppermute | solution.py:31
  10.0 1.0 %copy-done.1 = bf16[48,4224]{1,0:T(8,128)(2,1)S(1)} copy-done((bf16[48,4224]{1,0:T(8,128)(2,1)S(1)}, bf16[48,4224]{1,0:T(8,128)(2,1)}, u32[]{:S(2)}) %copy-start.1) | copy-done | bytes 405528
  11.0 8.7 %shard_map.112 = (bf16[48,1536]{1,0:T(8,128)(2,1)S(1)}, bf16[48,2176]{1,0:T(8,128)(2,1)S(1)}) custom-call(bf16[48,4224]{1,0:T(8,128)(2,1)S(1)} %copy-done.1, f32[2048,512]{1,0:T(8,128)} %bitcast.13, f32[2048,512]{1,0:T(8,128)} %bitcast.16, f32[2048,512]{1,0:T(8,128)} %bitcast.19), custom_call_target="tpu_custom_call" | custom-call | flops 7247757312 | bytes 1048576 | tf_op jit(solution)/shard_map/pallas_call | solution.py:301
  19.7 1.7 %collective-permute-start.4 = (bf16[48,2560]{1,0:T(8,128)(2,1)S(1)}, bf16[48,2560]{1,0:T(8,128)(2,1)S(1)}, u32[]{:S(2)}, u32[]{:S(2)}) collective-permute-start(bf16[48,2560]{1,0:T(8,128)(2,1)S(1)} %get-tuple-element.90), channel_id=1, source_target_pairs={{0,8},{4,12},{8,0},{12,4},{16,24},{20,28},{24,16},{28,20},{1,9},{5... | collective-permute-start | bytes 737288 | tf_op jit(solution)/shard_map/ppermute | solution.py:36
  21.4 1.5 %collective-permute-start.5 = (bf16[48,2560]{1,0:T(8,128)(2,1)S(1)}, bf16[48,2560]{1,0:T(8,128)(2,1)S(1)}, u32[]{:S(2)}, u32[]{:S(2)}) collective-permute-start(bf16[48,2560]{1,0:T(8,128)(2,1)S(1)} %get-tuple-element.91), channel_id=1, source_target_pairs={{0,16},{4,20},{8,24},{12,28},{16,0},{20,4},{24,8},{28,12},{1,17},{... | collective-permute-start | bytes 737288 | tf_op jit(solution)/shard_map/ppermute | solution.py:36
  23.7 4.5 %collective-permute-done.3.refs_1_ = bf16[48,4224]{1,0:T(8,128)(2,1)S(1)} collective-permute-done((bf16[48,4224]{1,0:T(8,128)(2,1)}, bf16[48,4224]{1,0:T(8,128)(2,1)S(1)}, u32[]{:S(2)}, u32[]{:S(2)}) %collective-permute-start.3) | collective-permute-done | bytes 405536 | tf_op jit(solution)/shard_map/ppermute | solution.py:31
  28.2 2.4 %collective-permute-start.6 = (bf16[48,2560]{1,0:T(8,128)(2,1)S(1)}, bf16[48,2560]{1,0:T(8,128)(2,1)S(1)}, u32[]{:S(2)}, u32[]{:S(2)}) collective-permute-start(bf16[48,2560]{1,0:T(8,128)(2,1)S(1)} %get-tuple-element.92), channel_id=1, source_target_pairs={{0,24},{4,28},{8,16},{12,20},{16,8},{20,12},{24,0},{28,4},{1,25},{... | collective-permute-start | bytes 737288 | tf_op jit(solution)/shard_map/ppermute | solution.py:36
  30.8 8.7 %shard_map.114 = (bf16[96,1536]{1,0:T(8,128)(2,1)S(1)}, bf16[48,2176]{1,0:T(8,128)(2,1)S(1)}, bf16[48,2176]{1,0:T(8,128)(2,1)S(1)}) custom-call(bf16[48,4224]{1,0:T(8,128)(2,1)S(1)} %collective-permute-done.2.refs_0_, bf16[48,4224]{1,0:T(8,128)(2,1)S(1)} %collective-permute-done.3.refs_1_, f32[2048,512]{1,0:T(8,128)} %bitcast.14, f32[2048,512]{1,0:T(8,128)} %bitcast.17, ...), custom_call_target="tpu_custom_call" | custom-call | flops 7247757312 | bytes 1048576 | tf_op jit(solution)/shard_map/pallas_call | solution.py:301
  39.7 6.5 %collective-permute-done.1.refs_0_ = bf16[48,4224]{1,0:T(8,128)(2,1)S(1)} collective-permute-done((bf16[48,4224]{1,0:T(8,128)(2,1)S(1)}, bf16[48,4224]{1,0:T(8,128)(2,1)S(1)}, u32[]{:S(2)}, u32[]{:S(2)}) %collective-permute-start.1) | collective-permute-done | bytes 405536 | tf_op jit(solution)/shard_map/ppermute | solution.py:31
  46.9 1.5 %collective-permute-start.9 = (bf16[96,2560]{1,0:T(8,128)(2,1)S(1)}, bf16[96,2560]{1,0:T(8,128)(2,1)S(1)}, u32[]{:S(2)}, u32[]{:S(2)}) collective-permute-start(bf16[96,2560]{1,0:T(8,128)(2,1)S(1)} %get-tuple-element.95), channel_id=1, source_target_pairs={{0,8},{4,12},{8,0},{12,4},{16,24},{20,28},{24,16},{28,20},{1,9},{5... | collective-permute-start | bytes 1474568 | tf_op jit(solution)/shard_map/ppermute | solution.py:36
  48.4 1.5 %collective-permute-start.10 = (bf16[96,2560]{1,0:T(8,128)(2,1)S(1)}, bf16[96,2560]{1,0:T(8,128)(2,1)S(1)}, u32[]{:S(2)}, u32[]{:S(2)}) collective-permute-start(bf16[96,2560]{1,0:T(8,128)(2,1)S(1)} %get-tuple-element.96), channel_id=1, source_target_pairs={{0,16},{4,20},{8,24},{12,28},{16,0},{20,4},{24,8},{28,12},{1,17},{... | collective-permute-start | bytes 1474568 | tf_op jit(solution)/shard_map/ppermute | solution.py:36
  50.4 1.6 %collective-permute-start.13 = (bf16[48,2176]{1,0:T(8,128)(2,1)S(1)}, bf16[48,2176]{1,0:T(8,128)(2,1)S(1)}, u32[]{:S(2)}, u32[]{:S(2)}) collective-permute-start(bf16[48,2176]{1,0:T(8,128)(2,1)S(1)} %get-tuple-element.113), channel_id=1, source_target_pairs={{0,3},{1,0},{2,1},{3,2},{4,7},{5,4},{6,5},{7,6},{8,11},{9,8},{10,9... | collective-permute-start | bytes 626696 | tf_op jit(solution)/shard_map/ppermute | solution.py:31
  52.5 8.6 %shard_map.118 = (bf16[48,1536]{1,0:T(8,128)(2,1)S(1)}, bf16[48,2176]{1,0:T(8,128)(2,1)S(1)}) custom-call(bf16[48,4224]{1,0:T(8,128)(2,1)S(1)} %collective-permute-done.1.refs_0_, f32[2048,512]{1,0:T(8,128)} %bitcast.15, f32[2048,512]{1,0:T(8,128)} %bitcast.18, f32[2048,512]{1,0:T(8,128)} %bitcast.21), custom_call_target="tpu_custom_call" | custom-call | flops 7247757312 | bytes 1048576 | tf_op jit(solution)/shard_map/pallas_call | solution.py:301
  61.8 2.8 %collective-permute-done.14.refs_3_ = bf16[48,2176]{1,0:T(8,128)(2,1)S(1)} collective-permute-done((bf16[48,2176]{1,0:T(8,128)(2,1)S(1)}, bf16[48,2176]{1,0:T(8,128)(2,1)S(1)}, u32[]{:S(2)}, u32[]{:S(2)}) %collective-permute-start.14) | collective-permute-done | bytes 208928 | tf_op jit(solution)/shard_map/ppermute | solution.py:31
  64.6 7.3 %collective-permute-done.10.refs_2_ = bf16[96,2560]{1,0:T(8,128)(2,1)S(1)} collective-permute-done((bf16[96,2560]{1,0:T(8,128)(2,1)S(1)}, bf16[96,2560]{1,0:T(8,128)(2,1)S(1)}, u32[]{:S(2)}, u32[]{:S(2)}) %collective-permute-start.10) | collective-permute-done | bytes 491552 | tf_op jit(solution)/shard_map/ppermute | solution.py:36
  72.2 1.3 %collective-permute-start.15 = (bf16[48,2560]{1,0:T(8,128)(2,1)S(1)}, bf16[48,2560]{1,0:T(8,128)(2,1)S(1)}, u32[]{:S(2)}, u32[]{:S(2)}) collective-permute-start(bf16[48,2560]{1,0:T(8,128)(2,1)S(1)} %get-tuple-element.116), channel_id=1, source_target_pairs={{0,8},{4,12},{8,0},{12,4},{16,24},{20,28},{24,16},{28,20},{1,9},{5... | collective-permute-start | bytes 737288 | tf_op jit(solution)/shard_map/ppermute | solution.py:36
  74.3 1.4 %collective-permute-start.17 = (bf16[48,2560]{1,0:T(8,128)(2,1)S(1)}, bf16[48,2560]{1,0:T(8,128)(2,1)S(1)}, u32[]{:S(2)}, u32[]{:S(2)}) collective-permute-start(bf16[48,2560]{1,0:T(8,128)(2,1)S(1)} %get-tuple-element.118), channel_id=1, source_target_pairs={{0,24},{4,28},{8,16},{12,20},{16,8},{20,12},{24,0},{28,4},{1,25},{... | collective-permute-start | bytes 737288 | tf_op jit(solution)/shard_map/ppermute | solution.py:36
  75.7 3.0 %collective-permute-start.18 = (bf16[48,2176]{1,0:T(8,128)(2,1)S(1)}, bf16[48,2176]{1,0:T(8,128)(2,1)S(1)}, u32[]{:S(2)}, u32[]{:S(2)}) collective-permute-start(bf16[48,2176]{1,0:T(8,128)(2,1)S(1)} %get-tuple-element.121), channel_id=1, source_target_pairs={{0,2},{1,3},{2,0},{3,1},{4,6},{5,7},{6,4},{7,5},{8,10},{9,11},{10,... | collective-permute-start | bytes 626696 | tf_op jit(solution)/shard_map/ppermute | solution.py:31
  79.6 7.2 %collective-permute-done.18.refs_2_ = bf16[48,2176]{1,0:T(8,128)(2,1)S(1)} collective-permute-done((bf16[48,2176]{1,0:T(8,128)(2,1)S(1)}, bf16[48,2176]{1,0:T(8,128)(2,1)S(1)}, u32[]{:S(2)}, u32[]{:S(2)}) %collective-permute-start.18) | collective-permute-done | bytes 208928 | tf_op jit(solution)/shard_map/ppermute | solution.py:31
  87.5 1.1 %shard_map.122 = (bf16[128,2048]{1,0:T(8,128)(2,1)}, bf16[1,128]{1,0:T(2,128)(2,1)}) custom-call(bf16[192,128]{1,0:T(8,128)(2,1)S(1)} %copy-done.2, bf16[48,2176]{1,0:T(8,128)(2,1)S(1)} %get-tuple-element.133.refs_0_, bf16[48,2176]{1,0:T(8,128)(2,1)S(1)} %collective-permute-done.13.refs_1_, bf16[48,2176]{1,0:T(8,128)(2,1)S(1)} %collective-permute-done.18.refs_2_, ...), custom_call_target="tpu_custom_call" | custom-call | bytes 1024 | tf_op jit(solution)/shard_map/pallas_call | solution.py:339
  88.9 1.5 %shard_map.123 = (f32[256,512]{1,0:T(8,128)}, f32[256,512]{1,0:T(8,128)}, f32[256,512]{1,0:T(8,128)}) custom-call(bf16[48,2560]{1,0:T(8,128)(2,1)S(1)} %get-tuple-element.139.refs_0_, bf16[48,2560]{1,0:T(8,128)(2,1)S(1)} %collective-permute-done.15.refs_1_, bf16[48,2560]{1,0:T(8,128)(2,1)S(1)} %collective-permute-done.16.refs_2_, ...), custom_call_target="tpu_custom_call" | custom-call | bytes 1024 | tf_op jit(solution)/shard_map/pallas_call | solution.py:160
  (55 shorter events, 6.9 us)
Async XLA Ops:
  3.7 1.0 %copy-start = (bf16[48,4224]{1,0:T(8,128)(2,1)S(1)}, bf16[48,4224]{1,0:T(8,128)(2,1)}, u32[]{:S(2)}) copy-start(bf16[48,4224]{1,0:T(8,128)(2,1)} %get-tuple-element.79.refs_0_) | copy-start | bytes 1216516
  4.7 14.9 %collective-permute-start = (bf16[4,48,512]{2,1,0:T(8,128)(2,1)S(1)}, bf16[4,48,512]{2,1,0:T(8,128)(2,1)S(1)}, u32[]{:S(2)}, u32[]{:S(2)}) collective-permute-start(bf16[4,48,512]{2,1,0:T(8,128)(2,1)S(1)} %shard_map.111), channel_id=1, source_target_pairs={{0,4},{4,0},{8,12},{12,8},{16,20},{20,16},{24,28},{28,24},{1,5},{5... | collective-permute-start | bytes 589832 | tf_op jit(solution)/shard_map/ppermute | solution.py:36
  5.2 18.5 %collective-permute-start.2 = (bf16[48,4224]{1,0:T(8,128)(2,1)}, bf16[48,4224]{1,0:T(8,128)(2,1)S(1)}, u32[]{:S(2)}, u32[]{:S(2)}) collective-permute-start(bf16[48,4224]{1,0:T(8,128)(2,1)} %get-tuple-element.84), channel_id=1, source_target_pairs={{0,1},{1,2},{2,3},{3,0},{4,5},{5,6},{6,7},{7,4},{8,9},{9,10},{10,1... | collective-permute-start | bytes 1216520 | tf_op jit(solution)/shard_map/ppermute | solution.py:31
  7.8 20.3 %collective-permute-start.3 = (bf16[48,4224]{1,0:T(8,128)(2,1)}, bf16[48,4224]{1,0:T(8,128)(2,1)S(1)}, u32[]{:S(2)}, u32[]{:S(2)}) collective-permute-start(bf16[48,4224]{1,0:T(8,128)(2,1)} %get-tuple-element.85), channel_id=1, source_target_pairs={{0,3},{1,0},{2,1},{3,2},{4,7},{5,4},{6,5},{7,6},{8,11},{9,8},{10,9... | collective-permute-start | bytes 1216520 | tf_op jit(solution)/shard_map/ppermute | solution.py:31
  10.0 1.0 %copy-start.1 = (bf16[48,4224]{1,0:T(8,128)(2,1)S(1)}, bf16[48,4224]{1,0:T(8,128)(2,1)}, u32[]{:S(2)}) copy-start(bf16[48,4224]{1,0:T(8,128)(2,1)} %get-tuple-element.79.refs_0_) | copy-start | bytes 1216516
  11.0 12.0 %copy-start.3 = (bf16[48,4224]{1,0:T(8,128)(2,1)S(1)}, bf16[48,4224]{1,0:T(8,128)(2,1)}, u32[]{:S(2)}) copy-start(bf16[48,4224]{1,0:T(8,128)(2,1)} %get-tuple-element.82) | copy-start | bytes 1216516
  19.7 19.9 %collective-permute-start.4 = (bf16[48,2560]{1,0:T(8,128)(2,1)S(1)}, bf16[48,2560]{1,0:T(8,128)(2,1)S(1)}, u32[]{:S(2)}, u32[]{:S(2)}) collective-permute-start(bf16[48,2560]{1,0:T(8,128)(2,1)S(1)} %get-tuple-element.90), channel_id=1, source_target_pairs={{0,8},{4,12},{8,0},{12,4},{16,24},{20,28},{24,16},{28,20},{1,9},{5... | collective-permute-start | bytes 737288 | tf_op jit(solution)/shard_map/ppermute | solution.py:36
  21.4 18.3 %collective-permute-start.5 = (bf16[48,2560]{1,0:T(8,128)(2,1)S(1)}, bf16[48,2560]{1,0:T(8,128)(2,1)S(1)}, u32[]{:S(2)}, u32[]{:S(2)}) collective-permute-start(bf16[48,2560]{1,0:T(8,128)(2,1)S(1)} %get-tuple-element.91), channel_id=1, source_target_pairs={{0,16},{4,20},{8,24},{12,28},{16,0},{20,4},{24,8},{28,12},{1,17},{... | collective-permute-start | bytes 737288 | tf_op jit(solution)/shard_map/ppermute | solution.py:36
  22.9 23.2 %collective-permute-start.1 = (bf16[48,4224]{1,0:T(8,128)(2,1)S(1)}, bf16[48,4224]{1,0:T(8,128)(2,1)S(1)}, u32[]{:S(2)}, u32[]{:S(2)}) collective-permute-start(bf16[48,4224]{1,0:T(8,128)(2,1)S(1)} %copy-done.3), channel_id=1, source_target_pairs={{0,2},{1,3},{2,0},{3,1},{4,6},{5,7},{6,4},{7,5},{8,10},{9,11},{10,... | collective-permute-start | bytes 1216520 | tf_op jit(solution)/shard_map/ppermute | solution.py:31
  28.2 18.0 %collective-permute-start.6 = (bf16[48,2560]{1,0:T(8,128)(2,1)S(1)}, bf16[48,2560]{1,0:T(8,128)(2,1)S(1)}, u32[]{:S(2)}, u32[]{:S(2)}) collective-permute-start(bf16[48,2560]{1,0:T(8,128)(2,1)S(1)} %get-tuple-element.92), channel_id=1, source_target_pairs={{0,24},{4,28},{8,16},{12,20},{16,8},{20,12},{24,0},{28,4},{1,25},{... | collective-permute-start | bytes 737288 | tf_op jit(solution)/shard_map/ppermute | solution.py:36
  30.7 8.8 %collective-permute-start.7 = (bf16[4,96,512]{2,1,0:T(8,128)(2,1)S(1)}, bf16[4,96,512]{2,1,0:T(8,128)(2,1)S(1)}, u32[]{:S(2)}, u32[]{:S(2)}) collective-permute-start(bf16[4,96,512]{2,1,0:T(8,128)(2,1)S(1)} %shard_map.115), channel_id=1, source_target_pairs={{0,4},{4,0},{8,12},{12,8},{16,20},{20,16},{24,28},{28,24},{1,5},{5... | collective-permute-start | bytes 1179656 | tf_op jit(solution)/shard_map/ppermute | solution.py:36
  46.3 5.7 %collective-permute-start.12 = (bf16[192,1536]{1,0:T(8,128)(2,1)S(1)}, bf16[192,1536]{1,0:T(8,128)(2,1)S(1)}, u32[]{:S(2)}, u32[]{:S(2)}) collective-permute-start(bf16[192,1536]{1,0:T(8,128)(2,1)S(1)} %pad_maximum_fusion.1), channel_id=1, source_target_pairs={{0,4},{4,0},{8,12},{12,8},{16,20},{20,16},{24,28},{28,24},{1,5},{5... | collective-permute-start | bytes 1769480 | tf_op jit(solution)/shard_map/ppermute | solution.py:36
  46.4 4.0 %collective-permute-start.8 = (bf16[4,48,512]{2,1,0:T(8,128)(2,1)S(1)}, bf16[4,48,512]{2,1,0:T(8,128)(2,1)S(1)}, u32[]{:S(2)}, u32[]{:S(2)}) collective-permute-start(bf16[4,48,512]{2,1,0:T(8,128)(2,1)S(1)} %shard_map.117), channel_id=1, source_target_pairs={{0,4},{4,0},{8,12},{12,8},{16,20},{20,16},{24,28},{28,24},{1,5},{5... | collective-permute-start | bytes 589832 | tf_op jit(solution)/shard_map/ppermute | solution.py:36
  46.9 17.7 %collective-permute-start.9 = (bf16[96,2560]{1,0:T(8,128)(2,1)S(1)}, bf16[96,2560]{1,0:T(8,128)(2,1)S(1)}, u32[]{:S(2)}, u32[]{:S(2)}) collective-permute-start(bf16[96,2560]{1,0:T(8,128)(2,1)S(1)} %get-tuple-element.95), channel_id=1, source_target_pairs={{0,8},{4,12},{8,0},{12,4},{16,24},{20,28},{24,16},{28,20},{1,9},{5... | collective-permute-start | bytes 1474568 | tf_op jit(solution)/shard_map/ppermute | solution.py:36
  48.4 23.5 %collective-permute-start.10 = (bf16[96,2560]{1,0:T(8,128)(2,1)S(1)}, bf16[96,2560]{1,0:T(8,128)(2,1)S(1)}, u32[]{:S(2)}, u32[]{:S(2)}) collective-permute-start(bf16[96,2560]{1,0:T(8,128)(2,1)S(1)} %get-tuple-element.96), channel_id=1, source_target_pairs={{0,16},{4,20},{8,24},{12,28},{16,0},{20,4},{24,8},{28,12},{1,17},{... | collective-permute-start | bytes 1474568 | tf_op jit(solution)/shard_map/ppermute | solution.py:36
  49.9 21.9 %collective-permute-start.11 = (bf16[96,2560]{1,0:T(8,128)(2,1)S(1)}, bf16[96,2560]{1,0:T(8,128)(2,1)S(1)}, u32[]{:S(2)}, u32[]{:S(2)}) collective-permute-start(bf16[96,2560]{1,0:T(8,128)(2,1)S(1)} %get-tuple-element.97), channel_id=1, source_target_pairs={{0,24},{4,28},{8,16},{12,20},{16,8},{20,12},{24,0},{28,4},{1,25},{... | collective-permute-start | bytes 1474568 | tf_op jit(solution)/shard_map/ppermute | solution.py:36
  50.4 11.3 %collective-permute-start.13 = (bf16[48,2176]{1,0:T(8,128)(2,1)S(1)}, bf16[48,2176]{1,0:T(8,128)(2,1)S(1)}, u32[]{:S(2)}, u32[]{:S(2)}) collective-permute-start(bf16[48,2176]{1,0:T(8,128)(2,1)S(1)} %get-tuple-element.113), channel_id=1, source_target_pairs={{0,3},{1,0},{2,1},{3,2},{4,7},{5,4},{6,5},{7,6},{8,11},{9,8},{10,9... | collective-permute-start | bytes 626696 | tf_op jit(solution)/shard_map/ppermute | solution.py:31
  52.0 12.6 %collective-permute-start.14 = (bf16[48,2176]{1,0:T(8,128)(2,1)S(1)}, bf16[48,2176]{1,0:T(8,128)(2,1)S(1)}, u32[]{:S(2)}, u32[]{:S(2)}) collective-permute-start(bf16[48,2176]{1,0:T(8,128)(2,1)S(1)} %get-tuple-element.114), channel_id=1, source_target_pairs={{0,1},{1,2},{2,3},{3,0},{4,5},{5,6},{6,7},{7,4},{8,9},{9,10},{10,1... | collective-permute-start | bytes 626696 | tf_op jit(solution)/shard_map/ppermute | solution.py:31
  72.1 6.7 %collective-permute-start.19 = (bf16[384,1536]{1,0:T(8,128)(2,1)S(1)}, bf16[384,1536]{1,0:T(8,128)(2,1)S(1)}, u32[]{:S(2)}, u32[]{:S(2)}) collective-permute-start(bf16[384,1536]{1,0:T(8,128)(2,1)S(1)} %pad_maximum_fusion), channel_id=1, source_target_pairs={{0,4},{4,0},{8,12},{12,8},{16,20},{20,16},{24,28},{28,24},{1,5},{5... | collective-permute-start | bytes 3538952 | tf_op jit(solution)/shard_map/ppermute | solution.py:36
  72.2 14.6 %collective-permute-start.15 = (bf16[48,2560]{1,0:T(8,128)(2,1)S(1)}, bf16[48,2560]{1,0:T(8,128)(2,1)S(1)}, u32[]{:S(2)}, u32[]{:S(2)}) collective-permute-start(bf16[48,2560]{1,0:T(8,128)(2,1)S(1)} %get-tuple-element.116), channel_id=1, source_target_pairs={{0,8},{4,12},{8,0},{12,4},{16,24},{20,28},{24,16},{28,20},{1,9},{5... | collective-permute-start | bytes 737288 | tf_op jit(solution)/shard_map/ppermute | solution.py:36
  73.4 13.3 %collective-permute-start.16 = (bf16[48,2560]{1,0:T(8,128)(2,1)S(1)}, bf16[48,2560]{1,0:T(8,128)(2,1)S(1)}, u32[]{:S(2)}, u32[]{:S(2)}) collective-permute-start(bf16[48,2560]{1,0:T(8,128)(2,1)S(1)} %get-tuple-element.117), channel_id=1, source_target_pairs={{0,16},{4,20},{8,24},{12,28},{16,0},{20,4},{24,8},{28,12},{1,17},{... | collective-permute-start | bytes 737288 | tf_op jit(solution)/shard_map/ppermute | solution.py:36
  74.3 12.5 %collective-permute-start.17 = (bf16[48,2560]{1,0:T(8,128)(2,1)S(1)}, bf16[48,2560]{1,0:T(8,128)(2,1)S(1)}, u32[]{:S(2)}, u32[]{:S(2)}) collective-permute-start(bf16[48,2560]{1,0:T(8,128)(2,1)S(1)} %get-tuple-element.118), channel_id=1, source_target_pairs={{0,24},{4,28},{8,16},{12,20},{16,8},{20,12},{24,0},{28,4},{1,25},{... | collective-permute-start | bytes 737288 | tf_op jit(solution)/shard_map/ppermute | solution.py:36
  75.7 11.0 %collective-permute-start.18 = (bf16[48,2176]{1,0:T(8,128)(2,1)S(1)}, bf16[48,2176]{1,0:T(8,128)(2,1)S(1)}, u32[]{:S(2)}, u32[]{:S(2)}) collective-permute-start(bf16[48,2176]{1,0:T(8,128)(2,1)S(1)} %get-tuple-element.121), channel_id=1, source_target_pairs={{0,2},{1,3},{2,0},{3,1},{4,6},{5,7},{6,4},{7,5},{8,10},{9,11},{10,... | collective-permute-start | bytes 626696 | tf_op jit(solution)/shard_map/ppermute | solution.py:31
  86.9 2.1 %collective-permute-start.20 = (bf16[192,1536]{1,0:T(8,128)(2,1)S(1)}, bf16[192,1536]{1,0:T(8,128)(2,1)S(1)}, u32[]{:S(2)}, u32[]{:S(2)}) collective-permute-start(bf16[192,1536]{1,0:T(8,128)(2,1)S(1)} %pad_maximum_fusion.2), channel_id=1, source_target_pairs={{0,4},{4,0},{8,12},{12,8},{16,20},{20,16},{24,28},{28,24},{1,5},{5... | collective-permute-start | bytes 1769480 | tf_op jit(solution)/shard_map/ppermute | solution.py:36
  (1 other events, 0.8 us)

commit v7 on v6

--- a/solution.py
+++ b/solution.py
@@ -287,14 +287,14 @@
             high, low = halves(buffer[i, at : at + BLOCK, :])
             grad_hi = terms_ref[:, i * units : (i + 1) * units]
             grad_lo = low_ref[:, i * units : (i + 1) * units]
-            part = against(high, grad_hi) + against(high, grad_lo) + against(low, grad_hi)
+            both = against(high, jnp.concatenate([grad_hi, grad_lo], axis=0)).T
+            part = both[: count * CAP] + both[count * CAP :] + against(low, grad_hi).T
             total = part if total is None else total + part
-        total = total.T
         for k, out in enumerate(outs):
             out[:, at : at + BLOCK] = total[k * CAP : (k + 1) * CAP].astype(out.dtype)
 
 
-def chunk_rows(pieces, weights, back_type):
+def chunk_rows(pieces, weights, back_type, passes):
     count = len(pieces)
     depth, units = weights[0].shape
     rows = count * CAP
@@ -309,7 +309,7 @@
         + [pltpu.VMEM((rows, 2 * units), bf16)]
         + weight_scratch(3, depth, units),
         compiler_params=ALONE,
-        cost_estimate=pl.CostEstimate(flops=36 * 192 * depth * units, bytes_accessed=MIB, transcendentals=0),
+        cost_estimate=pl.CostEstimate(flops=passes * 192 * depth * units, bytes_accessed=MIB, transcendentals=0),
     )(*pieces, *weights)
     return outs[0], outs[1:]
 
@@ -366,8 +366,15 @@
     def exchange(payload):
         return [payload[0]] + [flipped(payload[k], "dp", 2 * k) for k in chips[1:]]
 
-    def swap(got):
-        return flipped(jnp.concatenate([g[:, 4 * share :] for g in got]), "dp", 1)
+    def swap(*groups):
+        terms = [g[:, 4 * share :] for got in groups for g in got]
+        other = flipped(jnp.concatenate(terms), "dp", 1)
+        cuts, at = [], 0
+        for got in groups:
+            count = len(got) * got[0].shape[0]
+            cuts.append(other[at : at + count])
+            at += count
+        return cuts
 
     def give_back(home, shifts, back):
         home = list(home)
@@ -381,7 +388,7 @@
     first = [shifted(pieces[k], "expert", k) for k in odd]
 
     theirs = flipped(cut(pieces[:1], width), "dp", 1)
-    terms, back = chunk_rows(pieces[:1], weights, back_type)
+    terms, back = chunk_rows(pieces[:1], weights, back_type, 36)
     home[0] = back[0]
     payload = pack(pieces[:1], theirs, terms, width)
     late, _ = lax.optimization_barrier(([pieces[k] for k in even], payload[0]))
@@ -390,23 +397,25 @@
     got_local = exchange(payload)
 
     theirs = flipped(cut(first, width), "dp", 1)
-    terms, back = chunk_rows(first, weights, back_type)
+    terms, back = chunk_rows(first, weights, back_type, 36)
     payload = pack(first, theirs, terms, width)
+    payload, got_local = lax.optimization_barrier((payload, got_local))
     got_first = exchange(payload)
 
-    second, back, got_local, _ = lax.optimization_barrier((second, back, got_local, payload))
+    second, back, _ = lax.optimization_barrier((second, back, payload))
     home = give_back(home, odd, back)
     theirs = flipped(cut(second, width), "dp", 1)
-    terms, back = chunk_rows(second, weights, back_type)
-    sums = weight_sums(got_local, swap(got_local), None, share, None)
-    payload, got_first, sums, back, home = lax.optimization_barrier(
-        (pack(second, theirs, terms, width), got_first, sums, back, home)
+    terms, back = chunk_rows(second, weights, back_type, 12)
+    payload, got_first, back, home = lax.optimization_barrier(
+        (pack(second, theirs, terms, width), got_first, back, home)
     )
     home = give_back(home, even, back)
     got_second = exchange(payload)
-    sums = weight_sums(got_first, swap(got_first), sums, share, None)
+    local_other, first_other = swap(got_local, got_first)
+    sums = weight_sums(got_local, local_other, None, share, None)
+    sums = weight_sums(got_first, first_other, sums, share, None)
     got_second, home, sums = lax.optimization_barrier((got_second, home, sums))
-    sums = weight_sums(got_second, swap(got_second), sums, share, scale)
+    sums = weight_sums(got_second, swap(got_second)[0], sums, share, scale)
 
     grad_input, grad_prob = take(placing, home)
     return (grad_input, grad_prob, *[total[None] for total in sums])

time: 90.7 us -> 88.3 us (0.974)
  the two profiles are of different devices: /device:TPU:0 before, /device:TPU:17 now
where the time goes in v7:
time: 88.3 us; the launch traced here: 88.1 us
  Pallas kernels  30.4 us (34%)
  starting transfers between devices  28.2 us (32%)
  waiting for transfers between devices  26.3 us (30%)
  local copies, waits for them, and re-layouts  2.3 us (3%)
  between operations  0.91 us (1%)
    ppermute x14, starting transfers between devices, flipped(): return lax.ppermute(values, axis, [(i, i ^ mask) for i in range(size)])  24.1 us
    pallas_call x3, Pallas kernels, chunk_rows(): pl.pallas_call(functools.partial(chunk_kernel, count), out_shape=[jax.Sha...  22.9 us
    ppermute x14, waiting for transfers between devices, flipped(): return lax.ppermute(values, axis, [(i, i ^ mask) for i in range(size)])  16.6 us
    ppermute x6, waiting for transfers between devices, shifted(): lax.ppermute(values, axis, [(i, (i + by) % size) for i in range(size)])  9.74 us
    ppermute x6, starting transfers between devices, shifted(): lax.ppermute(values, axis, [(i, (i + by) % size) for i in range(size)])  4.1 us
    pallas_call x1, Pallas kernels, place(): pl.pallas_call(functools.partial(place_kernel, n_expert), out_shape=[jax....  3.05 us
    pallas_call x3, Pallas kernels, weight_sums(): pl.pallas_call(functools.partial(sum_kernel, chips, share, units, scale,...  2.91 us
    unnamed x15, local copies, waits for them, and re-layouts  2.12 us
  transfers between devices with their start and end apart: 20, of which 7 were waited for; matrix products, arithmetic and copies ran while one was open for 0% of the time, Pallas kernels for 29%

profile of v7, /device:TPU:17, one launch (start us, length us, event | category | flops | bytes accessed | tf_op | source)
XLA Modules:
  0.0 88.1 jit_solution(14161988743289441711)
XLA Ops:
  0.6 3.0 %shard_map.110 = (bf16[192,128]{1,0:T(8,128)(2,1)}, bf16[48,4224]{1,0:T(8,128)(2,1)}, bf16[48,4224]{1,0:T(8,128)(2,1)}, bf16[48,4224]{1,0:T(8,128)(2,1)}, bf16[48,4224]{1,0:T(8,128)(2,1)}) custom-call(s32[1]{0:T(128)} %bitcast.me_ref, s32[1,128]{1,0:T(1,128)} %bitcast.20, bf16[1,128]{1,0:T(2,128)(2,1)} %bitcast.21, bf16[128,2048]{1,0:T(8,128)(2,1)} %tok_ref.1, ...), custom_call_target="tpu_custom_call" | custom-call | bytes 1024 | tf_op jit(solution)/shard_map/pallas_call | solution.py:200
  3.7 1.0 %copy-done = bf16[48,4224]{1,0:T(8,128)(2,1)S(1)} copy-done((bf16[48,4224]{1,0:T(8,128)(2,1)S(1)}, bf16[48,4224]{1,0:T(8,128)(2,1)}, u32[]{:S(2)}) %copy-start) | copy-done | bytes 405528
  5.4 1.3 %collective-permute-start.2 = (bf16[48,4224]{1,0:T(8,128)(2,1)}, bf16[48,4224]{1,0:T(8,128)(2,1)S(1)}, u32[]{:S(2)}, u32[]{:S(2)}) collective-permute-start(bf16[48,4224]{1,0:T(8,128)(2,1)} %get-tuple-element.85), channel_id=1, source_target_pairs={{0,1},{1,2},{2,3},{3,0},{4,5},{5,6},{6,7},{7,4},{8,9},{9,10},{10,1... | collective-permute-start | bytes 1216520 | tf_op jit(solution)/shard_map/ppermute | solution.py:31
  6.9 1.0 %copy-done.1 = bf16[48,4224]{1,0:T(8,128)(2,1)S(1)} copy-done((bf16[48,4224]{1,0:T(8,128)(2,1)S(1)}, bf16[48,4224]{1,0:T(8,128)(2,1)}, u32[]{:S(2)}) %copy-start.1) | copy-done | bytes 405528
  7.9 7.6 %shard_map.112 = (bf16[48,1536]{1,0:T(8,128)(2,1)S(1)}, bf16[48,2176]{1,0:T(8,128)(2,1)S(1)}) custom-call(bf16[48,4224]{1,0:T(8,128)(2,1)S(1)} %copy-done.1, f32[2048,512]{1,0:T(8,128)} %bitcast.11, f32[2048,512]{1,0:T(8,128)} %bitcast.14, f32[2048,512]{1,0:T(8,128)} %bitcast.17), custom_call_target="tpu_custom_call" | custom-call | flops 7247757312 | bytes 1048576 | tf_op jit(solution)/shard_map/pallas_call | solution.py:301
  15.6 1.3 %collective-permute-start.5 = (bf16[48,2560]{1,0:T(8,128)(2,1)S(1)}, bf16[48,2560]{1,0:T(8,128)(2,1)S(1)}, u32[]{:S(2)}, u32[]{:S(2)}) collective-permute-start(bf16[48,2560]{1,0:T(8,128)(2,1)S(1)} %get-tuple-element.96), channel_id=1, source_target_pairs={{0,8},{4,12},{8,0},{12,4},{16,24},{20,28},{24,16},{28,20},{1,9},{5... | collective-permute-start | bytes 737288 | tf_op jit(solution)/shard_map/ppermute | solution.py:36
  16.9 1.2 %collective-permute-start.6 = (bf16[48,2560]{1,0:T(8,128)(2,1)S(1)}, bf16[48,2560]{1,0:T(8,128)(2,1)S(1)}, u32[]{:S(2)}, u32[]{:S(2)}) collective-permute-start(bf16[48,2560]{1,0:T(8,128)(2,1)S(1)} %get-tuple-element.97), channel_id=1, source_target_pairs={{0,16},{4,20},{8,24},{12,28},{16,0},{20,4},{24,8},{28,12},{1,17},{... | collective-permute-start | bytes 737288 | tf_op jit(solution)/shard_map/ppermute | solution.py:36
  18.1 1.9 %collective-permute-start.1 = (bf16[48,4224]{1,0:T(8,128)(2,1)S(1)}, bf16[48,4224]{1,0:T(8,128)(2,1)S(1)}, u32[]{:S(2)}, u32[]{:S(2)}) collective-permute-start(bf16[48,4224]{1,0:T(8,128)(2,1)S(1)} %copy-done.3), channel_id=1, source_target_pairs={{0,2},{1,3},{2,0},{3,1},{4,6},{5,7},{6,4},{7,5},{8,10},{9,11},{10,... | collective-permute-start | bytes 1216520 | tf_op jit(solution)/shard_map/ppermute | solution.py:31
  20.1 5.3 %collective-permute-done.3.refs_1_ = bf16[48,4224]{1,0:T(8,128)(2,1)S(1)} collective-permute-done((bf16[48,4224]{1,0:T(8,128)(2,1)}, bf16[48,4224]{1,0:T(8,128)(2,1)S(1)}, u32[]{:S(2)}, u32[]{:S(2)}) %collective-permute-start.3) | collective-permute-done | bytes 405536 | tf_op jit(solution)/shard_map/ppermute | solution.py:31
  25.4 2.0 %collective-permute-start.7 = (bf16[48,2560]{1,0:T(8,128)(2,1)S(1)}, bf16[48,2560]{1,0:T(8,128)(2,1)S(1)}, u32[]{:S(2)}, u32[]{:S(2)}) collective-permute-start(bf16[48,2560]{1,0:T(8,128)(2,1)S(1)} %get-tuple-element.98), channel_id=1, source_target_pairs={{0,24},{4,28},{8,16},{12,20},{16,8},{20,12},{24,0},{28,4},{1,25},{... | collective-permute-start | bytes 737288 | tf_op jit(solution)/shard_map/ppermute | solution.py:36
  27.4 10.0 %collective-permute-start.4 = (bf16[4,96,512]{2,1,0:T(8,128)(2,1)S(1)}, bf16[4,96,512]{2,1,0:T(8,128)(2,1)S(1)}, u32[]{:S(2)}, u32[]{:S(2)}) collective-permute-start(bf16[4,96,512]{2,1,0:T(8,128)(2,1)S(1)} %shard_map.115), channel_id=1, source_target_pairs={{0,4},{4,0},{8,12},{12,8},{16,20},{20,16},{24,28},{28,24},{1,5},{5... | collective-permute-start | bytes 1179656 | tf_op jit(solution)/shard_map/ppermute | solution.py:36
  37.4 7.7 %shard_map.114 = (bf16[96,1536]{1,0:T(8,128)(2,1)S(1)}, bf16[48,2176]{1,0:T(8,128)(2,1)S(1)}, bf16[48,2176]{1,0:T(8,128)(2,1)S(1)}) custom-call(bf16[48,4224]{1,0:T(8,128)(2,1)S(1)} %collective-permute-done.2.refs_0_, bf16[48,4224]{1,0:T(8,128)(2,1)S(1)} %collective-permute-done.3.refs_1_, f32[2048,512]{1,0:T(8,128)} %bitcast.12, f32[2048,512]{1,0:T(8,128)} %bitcast.15, ...), custom_call_target="tpu_custom_call" | custom-call | flops 7247757312 | bytes 1048576 | tf_op jit(solution)/shard_map/pallas_call | solution.py:301
  45.8 2.2 %collective-permute-start.11 = (bf16[96,2560]{1,0:T(8,128)(2,1)S(1)}, bf16[96,2560]{1,0:T(8,128)(2,1)S(1)}, u32[]{:S(2)}, u32[]{:S(2)}) collective-permute-start(bf16[96,2560]{1,0:T(8,128)(2,1)S(1)} %get-tuple-element.102), channel_id=1, source_target_pairs={{0,24},{4,28},{8,16},{12,20},{16,8},{20,12},{24,0},{28,4},{1,25},{... | collective-permute-start | bytes 1474568 | tf_op jit(solution)/shard_map/ppermute | solution.py:36
  49.0 1.0 %collective-permute-done.8.refs_1_ = bf16[4,48,512]{2,1,0:T(8,128)(2,1)S(1)} collective-permute-done((bf16[4,48,512]{2,1,0:T(8,128)(2,1)S(1)}, bf16[4,48,512]{2,1,0:T(8,128)(2,1)S(1)}, u32[]{:S(2)}, u32[]{:S(2)}) %collective-permute-start.8) | collective-permute-done | bytes 196640 | tf_op jit(solution)/shard_map/ppermute | solution.py:36
  50.7 7.6 %shard_map.118 = (bf16[48,1536]{1,0:T(8,128)(2,1)S(1)}, bf16[48,2176]{1,0:T(8,128)(2,1)S(1)}) custom-call(bf16[48,4224]{1,0:T(8,128)(2,1)S(1)} %collective-permute-done.1.refs_0_, f32[2048,512]{1,0:T(8,128)} %bitcast.13, f32[2048,512]{1,0:T(8,128)} %bitcast.16, f32[2048,512]{1,0:T(8,128)} %bitcast.19), custom_call_target="tpu_custom_call" | custom-call | flops 2415919104 | bytes 1048576 | tf_op jit(solution)/shard_map/pallas_call | solution.py:301
  58.4 10.3 %collective-permute-done.11.refs_3_ = bf16[96,2560]{1,0:T(8,128)(2,1)S(1)} collective-permute-done((bf16[96,2560]{1,0:T(8,128)(2,1)S(1)}, bf16[96,2560]{1,0:T(8,128)(2,1)S(1)}, u32[]{:S(2)}, u32[]{:S(2)}) %collective-permute-start.11) | collective-permute-done | bytes 491552 | tf_op jit(solution)/shard_map/ppermute | solution.py:36
  68.8 1.1 %collective-permute-start.18 = (bf16[576,1536]{1,0:T(8,128)(2,1)S(1)}, bf16[576,1536]{1,0:T(8,128)(2,1)S(1)}, u32[]{:S(2)}, u32[]{:S(2)}) collective-permute-start(bf16[576,1536]{1,0:T(8,128)(2,1)S(1)} %slice_dynamic-update-slice_fusion), channel_id=1, source_target_pairs={{0,4},{4,0},{8,12},{12,8},{16,20},{20,16},{24,28},{28,24},{1,5},{5... | collective-permute-start | bytes 5308424 | tf_op jit(solution)/shard_map/ppermute | solution.py:36
  70.0 1.2 %collective-permute-start.14 = (bf16[48,2560]{1,0:T(8,128)(2,1)S(1)}, bf16[48,2560]{1,0:T(8,128)(2,1)S(1)}, u32[]{:S(2)}, u32[]{:S(2)}) collective-permute-start(bf16[48,2560]{1,0:T(8,128)(2,1)S(1)} %get-tuple-element.114), channel_id=1, source_target_pairs={{0,8},{4,12},{8,0},{12,4},{16,24},{20,28},{24,16},{28,20},{1,9},{5... | collective-permute-start | bytes 737288 | tf_op jit(solution)/shard_map/ppermute | solution.py:36
  71.4 1.2 %collective-permute-start.16 = (bf16[48,2560]{1,0:T(8,128)(2,1)S(1)}, bf16[48,2560]{1,0:T(8,128)(2,1)S(1)}, u32[]{:S(2)}, u32[]{:S(2)}) collective-permute-start(bf16[48,2560]{1,0:T(8,128)(2,1)S(1)} %get-tuple-element.116), channel_id=1, source_target_pairs={{0,24},{4,28},{8,16},{12,20},{16,8},{20,12},{24,0},{28,4},{1,25},{... | collective-permute-start | bytes 737288 | tf_op jit(solution)/shard_map/ppermute | solution.py:36
  74.9 4.4 %collective-permute-done.17.refs_2_ = bf16[48,2176]{1,0:T(8,128)(2,1)S(1)} collective-permute-done((bf16[48,2176]{1,0:T(8,128)(2,1)S(1)}, bf16[48,2176]{1,0:T(8,128)(2,1)S(1)}, u32[]{:S(2)}, u32[]{:S(2)}) %collective-permute-start.17) | collective-permute-done | bytes 208928 | tf_op jit(solution)/shard_map/ppermute | solution.py:31
  79.3 4.1 %collective-permute-done.16.refs_3_ = bf16[48,2560]{1,0:T(8,128)(2,1)S(1)} collective-permute-done((bf16[48,2560]{1,0:T(8,128)(2,1)S(1)}, bf16[48,2560]{1,0:T(8,128)(2,1)S(1)}, u32[]{:S(2)}, u32[]{:S(2)}) %collective-permute-start.16) | collective-permute-done | bytes 245792 | tf_op jit(solution)/shard_map/ppermute | solution.py:36
  83.6 1.4 %collective-permute-start.19 = (bf16[192,1536]{1,0:T(8,128)(2,1)S(1)}, bf16[192,1536]{1,0:T(8,128)(2,1)S(1)}, u32[]{:S(2)}, u32[]{:S(2)}) collective-permute-start(bf16[192,1536]{1,0:T(8,128)(2,1)S(1)} %pad_maximum_fusion), channel_id=1, source_target_pairs={{0,4},{4,0},{8,12},{12,8},{16,20},{20,16},{24,28},{28,24},{1,5},{5... | collective-permute-start | bytes 1769480 | tf_op jit(solution)/shard_map/ppermute | solution.py:36
  85.0 1.1 %shard_map.122 = (bf16[128,2048]{1,0:T(8,128)(2,1)}, bf16[1,128]{1,0:T(2,128)(2,1)}) custom-call(bf16[192,128]{1,0:T(8,128)(2,1)S(1)} %copy-done.2, bf16[48,2176]{1,0:T(8,128)(2,1)S(1)} %get-tuple-element.135.refs_0_, bf16[48,2176]{1,0:T(8,128)(2,1)S(1)} %collective-permute-done.12.refs_1_, bf16[48,2176]{1,0:T(8,128)(2,1)S(1)} %collective-permute-done.17.refs_2_, ...), custom_call_target="tpu_custom_call" | custom-call | bytes 1024 | tf_op jit(solution)/shard_map/pallas_call | solution.py:339
  86.7 1.5 %shard_map.123 = (f32[256,512]{1,0:T(8,128)}, f32[256,512]{1,0:T(8,128)}, f32[256,512]{1,0:T(8,128)}) custom-call(bf16[48,2560]{1,0:T(8,128)(2,1)S(1)} %get-tuple-element.141.refs_0_, bf16[48,2560]{1,0:T(8,128)(2,1)S(1)} %collective-permute-done.14.refs_1_, bf16[48,2560]{1,0:T(8,128)(2,1)S(1)} %collective-permute-done.15.refs_2_, ...), custom_call_target="tpu_custom_call" | custom-call | bytes 1024 | tf_op jit(solution)/shard_map/pallas_call | solution.py:160
  (53 shorter events, 6.6 us)
Async XLA Ops:
  3.7 1.0 %copy-start = (bf16[48,4224]{1,0:T(8,128)(2,1)S(1)}, bf16[48,4224]{1,0:T(8,128)(2,1)}, u32[]{:S(2)}) copy-start(bf16[48,4224]{1,0:T(8,128)(2,1)} %get-tuple-element.80.refs_0_) | copy-start | bytes 1216516
  4.7 10.8 %collective-permute-start = (bf16[4,48,512]{2,1,0:T(8,128)(2,1)S(1)}, bf16[4,48,512]{2,1,0:T(8,128)(2,1)S(1)}, u32[]{:S(2)}, u32[]{:S(2)}) collective-permute-start(bf16[4,48,512]{2,1,0:T(8,128)(2,1)S(1)} %shard_map.111), channel_id=1, source_target_pairs={{0,4},{4,0},{8,12},{12,8},{16,20},{20,16},{24,28},{28,24},{1,5},{5... | collective-permute-start | bytes 589832 | tf_op jit(solution)/shard_map/ppermute | solution.py:36
  5.4 14.6 %collective-permute-start.2 = (bf16[48,4224]{1,0:T(8,128)(2,1)}, bf16[48,4224]{1,0:T(8,128)(2,1)S(1)}, u32[]{:S(2)}, u32[]{:S(2)}) collective-permute-start(bf16[48,4224]{1,0:T(8,128)(2,1)} %get-tuple-element.85), channel_id=1, source_target_pairs={{0,1},{1,2},{2,3},{3,0},{4,5},{5,6},{6,7},{7,4},{8,9},{9,10},{10,1... | collective-permute-start | bytes 1216520 | tf_op jit(solution)/shard_map/ppermute | solution.py:31
  6.7 18.6 %collective-permute-start.3 = (bf16[48,4224]{1,0:T(8,128)(2,1)}, bf16[48,4224]{1,0:T(8,128)(2,1)S(1)}, u32[]{:S(2)}, u32[]{:S(2)}) collective-permute-start(bf16[48,4224]{1,0:T(8,128)(2,1)} %get-tuple-element.86), channel_id=1, source_target_pairs={{0,3},{1,0},{2,1},{3,2},{4,7},{5,4},{6,5},{7,6},{8,11},{9,8},{10,9... | collective-permute-start | bytes 1216520 | tf_op jit(solution)/shard_map/ppermute | solution.py:31
  6.9 1.0 %copy-start.1 = (bf16[48,4224]{1,0:T(8,128)(2,1)S(1)}, bf16[48,4224]{1,0:T(8,128)(2,1)}, u32[]{:S(2)}) copy-start(bf16[48,4224]{1,0:T(8,128)(2,1)} %get-tuple-element.80.refs_0_) | copy-start | bytes 1216516
  7.9 10.2 %copy-start.3 = (bf16[48,4224]{1,0:T(8,128)(2,1)S(1)}, bf16[48,4224]{1,0:T(8,128)(2,1)}, u32[]{:S(2)}) copy-start(bf16[48,4224]{1,0:T(8,128)(2,1)} %get-tuple-element.83) | copy-start | bytes 1216516
  15.6 29.6 %collective-permute-start.5 = (bf16[48,2560]{1,0:T(8,128)(2,1)S(1)}, bf16[48,2560]{1,0:T(8,128)(2,1)S(1)}, u32[]{:S(2)}, u32[]{:S(2)}) collective-permute-start(bf16[48,2560]{1,0:T(8,128)(2,1)S(1)} %get-tuple-element.96), channel_id=1, source_target_pairs={{0,8},{4,12},{8,0},{12,4},{16,24},{20,28},{24,16},{28,20},{1,9},{5... | collective-permute-start | bytes 737288 | tf_op jit(solution)/shard_map/ppermute | solution.py:36
  16.9 28.4 %collective-permute-start.6 = (bf16[48,2560]{1,0:T(8,128)(2,1)S(1)}, bf16[48,2560]{1,0:T(8,128)(2,1)S(1)}, u32[]{:S(2)}, u32[]{:S(2)}) collective-permute-start(bf16[48,2560]{1,0:T(8,128)(2,1)S(1)} %get-tuple-element.97), channel_id=1, source_target_pairs={{0,16},{4,20},{8,24},{12,28},{16,0},{20,4},{24,8},{28,12},{1,17},{... | collective-permute-start | bytes 737288 | tf_op jit(solution)/shard_map/ppermute | solution.py:36
  18.1 29.9 %collective-permute-start.1 = (bf16[48,4224]{1,0:T(8,128)(2,1)S(1)}, bf16[48,4224]{1,0:T(8,128)(2,1)S(1)}, u32[]{:S(2)}, u32[]{:S(2)}) collective-permute-start(bf16[48,4224]{1,0:T(8,128)(2,1)S(1)} %copy-done.3), channel_id=1, source_target_pairs={{0,2},{1,3},{2,0},{3,1},{4,6},{5,7},{6,4},{7,5},{8,10},{9,11},{10,... | collective-permute-start | bytes 1216520 | tf_op jit(solution)/shard_map/ppermute | solution.py:31
  25.4 19.9 %collective-permute-start.7 = (bf16[48,2560]{1,0:T(8,128)(2,1)S(1)}, bf16[48,2560]{1,0:T(8,128)(2,1)S(1)}, u32[]{:S(2)}, u32[]{:S(2)}) collective-permute-start(bf16[48,2560]{1,0:T(8,128)(2,1)S(1)} %get-tuple-element.98), channel_id=1, source_target_pairs={{0,24},{4,28},{8,16},{12,20},{16,8},{20,12},{24,0},{28,4},{1,25},{... | collective-permute-start | bytes 737288 | tf_op jit(solution)/shard_map/ppermute | solution.py:36
  27.4 17.7 %collective-permute-start.4 = (bf16[4,96,512]{2,1,0:T(8,128)(2,1)S(1)}, bf16[4,96,512]{2,1,0:T(8,128)(2,1)S(1)}, u32[]{:S(2)}, u32[]{:S(2)}) collective-permute-start(bf16[4,96,512]{2,1,0:T(8,128)(2,1)S(1)} %shard_map.115), channel_id=1, source_target_pairs={{0,4},{4,0},{8,12},{12,8},{16,20},{20,16},{24,28},{28,24},{1,5},{5... | collective-permute-start | bytes 1179656 | tf_op jit(solution)/shard_map/ppermute | solution.py:36
  45.3 13.1 %collective-permute-start.9 = (bf16[96,2560]{1,0:T(8,128)(2,1)S(1)}, bf16[96,2560]{1,0:T(8,128)(2,1)S(1)}, u32[]{:S(2)}, u32[]{:S(2)}) collective-permute-start(bf16[96,2560]{1,0:T(8,128)(2,1)S(1)} %get-tuple-element.100), channel_id=1, source_target_pairs={{0,8},{4,12},{8,0},{12,4},{16,24},{20,28},{24,16},{28,20},{1,9},{5... | collective-permute-start | bytes 1474568 | tf_op jit(solution)/shard_map/ppermute | solution.py:36
  45.6 12.8 %collective-permute-start.10 = (bf16[96,2560]{1,0:T(8,128)(2,1)S(1)}, bf16[96,2560]{1,0:T(8,128)(2,1)S(1)}, u32[]{:S(2)}, u32[]{:S(2)}) collective-permute-start(bf16[96,2560]{1,0:T(8,128)(2,1)S(1)} %get-tuple-element.101), channel_id=1, source_target_pairs={{0,16},{4,20},{8,24},{12,28},{16,0},{20,4},{24,8},{28,12},{1,17},{... | collective-permute-start | bytes 1474568 | tf_op jit(solution)/shard_map/ppermute | solution.py:36
  45.8 22.9 %collective-permute-start.11 = (bf16[96,2560]{1,0:T(8,128)(2,1)S(1)}, bf16[96,2560]{1,0:T(8,128)(2,1)S(1)}, u32[]{:S(2)}, u32[]{:S(2)}) collective-permute-start(bf16[96,2560]{1,0:T(8,128)(2,1)S(1)} %get-tuple-element.102), channel_id=1, source_target_pairs={{0,24},{4,28},{8,16},{12,20},{16,8},{20,12},{24,0},{28,4},{1,25},{... | collective-permute-start | bytes 1474568 | tf_op jit(solution)/shard_map/ppermute | solution.py:36
  48.0 2.0 %collective-permute-start.8 = (bf16[4,48,512]{2,1,0:T(8,128)(2,1)S(1)}, bf16[4,48,512]{2,1,0:T(8,128)(2,1)S(1)}, u32[]{:S(2)}, u32[]{:S(2)}) collective-permute-start(bf16[4,48,512]{2,1,0:T(8,128)(2,1)S(1)} %shard_map.117), channel_id=1, source_target_pairs={{0,4},{4,0},{8,12},{12,8},{16,20},{20,16},{24,28},{28,24},{1,5},{5... | collective-permute-start | bytes 589832 | tf_op jit(solution)/shard_map/ppermute | solution.py:36
  49.0 9.4 %collective-permute-start.12 = (bf16[48,2176]{1,0:T(8,128)(2,1)S(1)}, bf16[48,2176]{1,0:T(8,128)(2,1)S(1)}, u32[]{:S(2)}, u32[]{:S(2)}) collective-permute-start(bf16[48,2176]{1,0:T(8,128)(2,1)S(1)} %get-tuple-element.111), channel_id=1, source_target_pairs={{0,3},{1,0},{2,1},{3,2},{4,7},{5,4},{6,5},{7,6},{8,11},{9,8},{10,9... | collective-permute-start | bytes 626696 | tf_op jit(solution)/shard_map/ppermute | solution.py:31
  50.0 8.4 %collective-permute-start.13 = (bf16[48,2176]{1,0:T(8,128)(2,1)S(1)}, bf16[48,2176]{1,0:T(8,128)(2,1)S(1)}, u32[]{:S(2)}, u32[]{:S(2)}) collective-permute-start(bf16[48,2176]{1,0:T(8,128)(2,1)S(1)} %get-tuple-element.112), channel_id=1, source_target_pairs={{0,1},{1,2},{2,3},{3,0},{4,5},{5,6},{6,7},{7,4},{8,9},{9,10},{10,1... | collective-permute-start | bytes 626696 | tf_op jit(solution)/shard_map/ppermute | solution.py:31
  68.8 4.5 %collective-permute-start.18 = (bf16[576,1536]{1,0:T(8,128)(2,1)S(1)}, bf16[576,1536]{1,0:T(8,128)(2,1)S(1)}, u32[]{:S(2)}, u32[]{:S(2)}) collective-permute-start(bf16[576,1536]{1,0:T(8,128)(2,1)S(1)} %slice_dynamic-update-slice_fusion), channel_id=1, source_target_pairs={{0,4},{4,0},{8,12},{12,8},{16,20},{20,16},{24,28},{28,24},{1,5},{5... | collective-permute-start | bytes 5308424 | tf_op jit(solution)/shard_map/ppermute | solution.py:36
  70.0 9.3 %collective-permute-start.14 = (bf16[48,2560]{1,0:T(8,128)(2,1)S(1)}, bf16[48,2560]{1,0:T(8,128)(2,1)S(1)}, u32[]{:S(2)}, u32[]{:S(2)}) collective-permute-start(bf16[48,2560]{1,0:T(8,128)(2,1)S(1)} %get-tuple-element.114), channel_id=1, source_target_pairs={{0,8},{4,12},{8,0},{12,4},{16,24},{20,28},{24,16},{28,20},{1,9},{5... | collective-permute-start | bytes 737288 | tf_op jit(solution)/shard_map/ppermute | solution.py:36
  71.2 8.1 %collective-permute-start.15 = (bf16[48,2560]{1,0:T(8,128)(2,1)S(1)}, bf16[48,2560]{1,0:T(8,128)(2,1)S(1)}, u32[]{:S(2)}, u32[]{:S(2)}) collective-permute-start(bf16[48,2560]{1,0:T(8,128)(2,1)S(1)} %get-tuple-element.115), channel_id=1, source_target_pairs={{0,16},{4,20},{8,24},{12,28},{16,0},{20,4},{24,8},{28,12},{1,17},{... | collective-permute-start | bytes 737288 | tf_op jit(solution)/shard_map/ppermute | solution.py:36
  71.4 12.0 %collective-permute-start.16 = (bf16[48,2560]{1,0:T(8,128)(2,1)S(1)}, bf16[48,2560]{1,0:T(8,128)(2,1)S(1)}, u32[]{:S(2)}, u32[]{:S(2)}) collective-permute-start(bf16[48,2560]{1,0:T(8,128)(2,1)S(1)} %get-tuple-element.116), channel_id=1, source_target_pairs={{0,24},{4,28},{8,16},{12,20},{16,8},{20,12},{24,0},{28,4},{1,25},{... | collective-permute-start | bytes 737288 | tf_op jit(solution)/shard_map/ppermute | solution.py:36
  72.6 6.7 %collective-permute-start.17 = (bf16[48,2176]{1,0:T(8,128)(2,1)S(1)}, bf16[48,2176]{1,0:T(8,128)(2,1)S(1)}, u32[]{:S(2)}, u32[]{:S(2)}) collective-permute-start(bf16[48,2176]{1,0:T(8,128)(2,1)S(1)} %get-tuple-element.119), channel_id=1, source_target_pairs={{0,2},{1,3},{2,0},{3,1},{4,6},{5,7},{6,4},{7,5},{8,10},{9,11},{10,... | collective-permute-start | bytes 626696 | tf_op jit(solution)/shard_map/ppermute | solution.py:31
  74.9 10.2 %copy-start.2 = (bf16[192,128]{1,0:T(8,128)(2,1)S(1)}, bf16[192,128]{1,0:T(8,128)(2,1)}, u32[]{:S(2)}) copy-start(bf16[192,128]{1,0:T(8,128)(2,1)} %get-tuple-element.78.placing_ref) | copy-start | bytes 147460
  83.6 3.1 %collective-permute-start.19 = (bf16[192,1536]{1,0:T(8,128)(2,1)S(1)}, bf16[192,1536]{1,0:T(8,128)(2,1)S(1)}, u32[]{:S(2)}, u32[]{:S(2)}) collective-permute-start(bf16[192,1536]{1,0:T(8,128)(2,1)S(1)} %pad_maximum_fusion), channel_id=1, source_target_pairs={{0,4},{4,0},{8,12},{12,8},{16,20},{20,16},{24,28},{28,24},{1,5},{5... | collective-permute-start | bytes 1769480 | tf_op jit(solution)/shard_map/ppermute | solution.py:36

commit v8 on v7

--- a/solution.py
+++ b/solution.py
@@ -391,13 +391,14 @@
     terms, back = chunk_rows(pieces[:1], weights, back_type, 36)
     home[0] = back[0]
     payload = pack(pieces[:1], theirs, terms, width)
-    late, _ = lax.optimization_barrier(([pieces[k] for k in even], payload[0]))
+    late, payload[-1], first, _ = lax.optimization_barrier(
+        ([pieces[k] for k in even], payload[-1], first, payload[0])
+    )
     second = [shifted(piece, "expert", k) for piece, k in zip(late, even)]
-    payload[-1], first = lax.optimization_barrier((payload[-1], first))
     got_local = exchange(payload)
 
     theirs = flipped(cut(first, width), "dp", 1)
-    terms, back = chunk_rows(first, weights, back_type, 36)
+    terms, back = chunk_rows(first, weights, back_type, 24)
     payload = pack(first, theirs, terms, width)
     payload, got_local = lax.optimization_barrier((payload, got_local))
     got_first = exchange(payload)

time: 88.3 us -> 84.5 us (0.957)
  the two profiles are of different devices: /device:TPU:17 before, /device:TPU:0 now
where the time goes in v8:
time: 84.5 us; the launch traced here: 84.3 us
  Pallas kernels  30.3 us (36%)
  waiting for transfers between devices  27.7 us (33%)
  starting transfers between devices  23 us (27%)
  local copies, waits for them, and re-layouts  2.31 us (3%)
  between operations  0.95 us (1%)
    ppermute x6, waiting for transfers between devices, shifted(): lax.ppermute(values, axis, [(i, (i + by) % size) for i in range(size)])  26.8 us
    pallas_call x3, Pallas kernels, chunk_rows(): pl.pallas_call(functools.partial(chunk_kernel, count), out_shape=[jax.Sha...  22.9 us
    ppermute x14, starting transfers between devices, flipped(): return lax.ppermute(values, axis, [(i, i ^ mask) for i in range(size)])  13.6 us
    ppermute x6, starting transfers between devices, shifted(): lax.ppermute(values, axis, [(i, (i + by) % size) for i in range(size)])  9.43 us
    pallas_call x1, Pallas kernels, place(): pl.pallas_call(functools.partial(place_kernel, n_expert), out_shape=[jax....  3.03 us
    pallas_call x3, Pallas kernels, weight_sums(): pl.pallas_call(functools.partial(sum_kernel, chips, share, units, scale,...  2.91 us
    unnamed x15, local copies, waits for them, and re-layouts  2.12 us
  transfers between devices with their start and end apart: 20, of which 5 were waited for; matrix products, arithmetic and copies ran while one was open for 0% of the time, Pallas kernels for 31%

profile of v8, /device:TPU:0, one launch (start us, length us, event | category | flops | bytes accessed | tf_op | source)
XLA Modules:
  0.0 84.3 jit_solution(4294604951768234170)
XLA Ops:
  0.6 3.0 %shard_map.110 = (bf16[192,128]{1,0:T(8,128)(2,1)}, bf16[48,4224]{1,0:T(8,128)(2,1)}, bf16[48,4224]{1,0:T(8,128)(2,1)}, bf16[48,4224]{1,0:T(8,128)(2,1)}, bf16[48,4224]{1,0:T(8,128)(2,1)}) custom-call(s32[1]{0:T(128)} %bitcast.me_ref, s32[1,128]{1,0:T(1,128)} %bitcast.20, bf16[1,128]{1,0:T(2,128)(2,1)} %bitcast.21, bf16[128,2048]{1,0:T(8,128)(2,1)} %tok_ref.1, ...), custom_call_target="tpu_custom_call" | custom-call | bytes 1024 | tf_op jit(solution)/shard_map/pallas_call | solution.py:200
  3.7 1.0 %copy-done = bf16[48,4224]{1,0:T(8,128)(2,1)S(1)} copy-done((bf16[48,4224]{1,0:T(8,128)(2,1)S(1)}, bf16[48,4224]{1,0:T(8,128)(2,1)}, u32[]{:S(2)}) %copy-start) | copy-done | bytes 405528
  5.2 2.6 %collective-permute-start.1 = (bf16[48,4224]{1,0:T(8,128)(2,1)}, bf16[48,4224]{1,0:T(8,128)(2,1)S(1)}, u32[]{:S(2)}, u32[]{:S(2)}) collective-permute-start(bf16[48,4224]{1,0:T(8,128)(2,1)} %get-tuple-element.83), channel_id=1, source_target_pairs={{0,1},{1,2},{2,3},{3,0},{4,5},{5,6},{6,7},{7,4},{8,9},{9,10},{10,1... | collective-permute-start | bytes 1216520 | tf_op jit(solution)/shard_map/ppermute | solution.py:31
  7.8 2.1 %collective-permute-start.2 = (bf16[48,4224]{1,0:T(8,128)(2,1)}, bf16[48,4224]{1,0:T(8,128)(2,1)S(1)}, u32[]{:S(2)}, u32[]{:S(2)}) collective-permute-start(bf16[48,4224]{1,0:T(8,128)(2,1)} %get-tuple-element.84), channel_id=1, source_target_pairs={{0,3},{1,0},{2,1},{3,2},{4,7},{5,4},{6,5},{7,6},{8,11},{9,8},{10,9... | collective-permute-start | bytes 1216520 | tf_op jit(solution)/shard_map/ppermute | solution.py:31
  10.0 1.0 %copy-done.1 = bf16[48,4224]{1,0:T(8,128)(2,1)S(1)} copy-done((bf16[48,4224]{1,0:T(8,128)(2,1)S(1)}, bf16[48,4224]{1,0:T(8,128)(2,1)}, u32[]{:S(2)}) %copy-start.1) | copy-done | bytes 405528
  11.0 7.6 %shard_map.112 = (bf16[48,1536]{1,0:T(8,128)(2,1)S(1)}, bf16[48,2176]{1,0:T(8,128)(2,1)S(1)}) custom-call(bf16[48,4224]{1,0:T(8,128)(2,1)S(1)} %copy-done.1, f32[2048,512]{1,0:T(8,128)} %bitcast.11, f32[2048,512]{1,0:T(8,128)} %bitcast.14, f32[2048,512]{1,0:T(8,128)} %bitcast.17), custom_call_target="tpu_custom_call" | custom-call | flops 7247757312 | bytes 1048576 | tf_op jit(solution)/shard_map/pallas_call | solution.py:301
  18.7 1.7 %collective-permute-start.5 = (bf16[48,2560]{1,0:T(8,128)(2,1)S(1)}, bf16[48,2560]{1,0:T(8,128)(2,1)S(1)}, u32[]{:S(2)}, u32[]{:S(2)}) collective-permute-start(bf16[48,2560]{1,0:T(8,128)(2,1)S(1)} %get-tuple-element.96), channel_id=1, source_target_pairs={{0,8},{4,12},{8,0},{12,4},{16,24},{20,28},{24,16},{28,20},{1,9},{5... | collective-permute-start | bytes 737288 | tf_op jit(solution)/shard_map/ppermute | solution.py:36
  20.3 1.5 %collective-permute-start.6 = (bf16[48,2560]{1,0:T(8,128)(2,1)S(1)}, bf16[48,2560]{1,0:T(8,128)(2,1)S(1)}, u32[]{:S(2)}, u32[]{:S(2)}) collective-permute-start(bf16[48,2560]{1,0:T(8,128)(2,1)S(1)} %get-tuple-element.97), channel_id=1, source_target_pairs={{0,16},{4,20},{8,24},{12,28},{16,0},{20,4},{24,8},{28,12},{1,17},{... | collective-permute-start | bytes 737288 | tf_op jit(solution)/shard_map/ppermute | solution.py:36
  21.9 6.3 %collective-permute-done.2.refs_1_ = bf16[48,4224]{1,0:T(8,128)(2,1)S(1)} collective-permute-done((bf16[48,4224]{1,0:T(8,128)(2,1)}, bf16[48,4224]{1,0:T(8,128)(2,1)S(1)}, u32[]{:S(2)}, u32[]{:S(2)}) %collective-permute-start.2) | collective-permute-done | bytes 405536 | tf_op jit(solution)/shard_map/ppermute | solution.py:31
  28.2 2.4 %collective-permute-start.7 = (bf16[48,2560]{1,0:T(8,128)(2,1)S(1)}, bf16[48,2560]{1,0:T(8,128)(2,1)S(1)}, u32[]{:S(2)}, u32[]{:S(2)}) collective-permute-start(bf16[48,2560]{1,0:T(8,128)(2,1)S(1)} %get-tuple-element.98), channel_id=1, source_target_pairs={{0,24},{4,28},{8,16},{12,20},{16,8},{20,12},{24,0},{28,4},{1,25},{... | collective-permute-start | bytes 737288 | tf_op jit(solution)/shard_map/ppermute | solution.py:36
  30.8 1.4 %collective-permute-start.3 = (bf16[48,4224]{1,0:T(8,128)(2,1)S(1)}, bf16[48,4224]{1,0:T(8,128)(2,1)S(1)}, u32[]{:S(2)}, u32[]{:S(2)}) collective-permute-start(bf16[48,4224]{1,0:T(8,128)(2,1)S(1)} %copy-done.3), channel_id=1, source_target_pairs={{0,2},{1,3},{2,0},{3,1},{4,6},{5,7},{6,4},{7,5},{8,10},{9,11},{10,... | collective-permute-start | bytes 1216520 | tf_op jit(solution)/shard_map/ppermute | solution.py:31
  32.1 7.7 %shard_map.114 = (bf16[96,1536]{1,0:T(8,128)(2,1)S(1)}, bf16[48,2176]{1,0:T(8,128)(2,1)S(1)}, bf16[48,2176]{1,0:T(8,128)(2,1)S(1)}) custom-call(bf16[48,4224]{1,0:T(8,128)(2,1)S(1)} %collective-permute-done.1.refs_0_, bf16[48,4224]{1,0:T(8,128)(2,1)S(1)} %collective-permute-done.2.refs_1_, f32[2048,512]{1,0:T(8,128)} %bitcast.12, f32[2048,512]{1,0:T(8,128)} %bitcast.15, ...), custom_call_target="tpu_custom_call" | custom-call | flops 4831838208 | bytes 1048576 | tf_op jit(solution)/shard_map/pallas_call | solution.py:301
  41.2 2.4 %collective-permute-start.11 = (bf16[96,2560]{1,0:T(8,128)(2,1)S(1)}, bf16[96,2560]{1,0:T(8,128)(2,1)S(1)}, u32[]{:S(2)}, u32[]{:S(2)}) collective-permute-start(bf16[96,2560]{1,0:T(8,128)(2,1)S(1)} %get-tuple-element.102), channel_id=1, source_target_pairs={{0,24},{4,28},{8,16},{12,20},{16,8},{20,12},{24,0},{28,4},{1,25},{... | collective-permute-start | bytes 1474568 | tf_op jit(solution)/shard_map/ppermute | solution.py:36
  43.7 8.5 %collective-permute-done.3.refs_0_ = bf16[48,4224]{1,0:T(8,128)(2,1)S(1)} collective-permute-done((bf16[48,4224]{1,0:T(8,128)(2,1)S(1)}, bf16[48,4224]{1,0:T(8,128)(2,1)S(1)}, u32[]{:S(2)}, u32[]{:S(2)}) %collective-permute-start.3) | collective-permute-done | bytes 405536 | tf_op jit(solution)/shard_map/ppermute | solution.py:31
  52.3 2.3 %collective-permute-start.12 = (bf16[48,2176]{1,0:T(8,128)(2,1)S(1)}, bf16[48,2176]{1,0:T(8,128)(2,1)S(1)}, u32[]{:S(2)}, u32[]{:S(2)}) collective-permute-start(bf16[48,2176]{1,0:T(8,128)(2,1)S(1)} %get-tuple-element.111), channel_id=1, source_target_pairs={{0,3},{1,0},{2,1},{3,2},{4,7},{5,4},{6,5},{7,6},{8,11},{9,8},{10,9... | collective-permute-start | bytes 626696 | tf_op jit(solution)/shard_map/ppermute | solution.py:31
  54.6 7.6 %shard_map.118 = (bf16[48,1536]{1,0:T(8,128)(2,1)S(1)}, bf16[48,2176]{1,0:T(8,128)(2,1)S(1)}) custom-call(bf16[48,4224]{1,0:T(8,128)(2,1)S(1)} %collective-permute-done.3.refs_0_, f32[2048,512]{1,0:T(8,128)} %bitcast.13, f32[2048,512]{1,0:T(8,128)} %bitcast.16, f32[2048,512]{1,0:T(8,128)} %bitcast.19), custom_call_target="tpu_custom_call" | custom-call | flops 2415919104 | bytes 1048576 | tf_op jit(solution)/shard_map/pallas_call | solution.py:301
  62.2 2.6 %collective-permute-done.13.refs_3_ = bf16[48,2176]{1,0:T(8,128)(2,1)S(1)} collective-permute-done((bf16[48,2176]{1,0:T(8,128)(2,1)S(1)}, bf16[48,2176]{1,0:T(8,128)(2,1)S(1)}, u32[]{:S(2)}, u32[]{:S(2)}) %collective-permute-start.13) | collective-permute-done | bytes 208928 | tf_op jit(solution)/shard_map/ppermute | solution.py:31
  65.0 0.9 %collective-permute-start.14 = (bf16[48,2560]{1,0:T(8,128)(2,1)S(1)}, bf16[48,2560]{1,0:T(8,128)(2,1)S(1)}, u32[]{:S(2)}, u32[]{:S(2)}) collective-permute-start(bf16[48,2560]{1,0:T(8,128)(2,1)S(1)} %get-tuple-element.114), channel_id=1, source_target_pairs={{0,8},{4,12},{8,0},{12,4},{16,24},{20,28},{24,16},{28,20},{1,9},{5... | collective-permute-start | bytes 737288 | tf_op jit(solution)/shard_map/ppermute | solution.py:36
  66.5 2.1 %collective-permute-start.16 = (bf16[48,2560]{1,0:T(8,128)(2,1)S(1)}, bf16[48,2560]{1,0:T(8,128)(2,1)S(1)}, u32[]{:S(2)}, u32[]{:S(2)}) collective-permute-start(bf16[48,2560]{1,0:T(8,128)(2,1)S(1)} %get-tuple-element.116), channel_id=1, source_target_pairs={{0,24},{4,28},{8,16},{12,20},{16,8},{20,12},{24,0},{28,4},{1,25},{... | collective-permute-start | bytes 737288 | tf_op jit(solution)/shard_map/ppermute | solution.py:36
  68.6 1.0 %collective-permute-start.17 = (bf16[48,2176]{1,0:T(8,128)(2,1)S(1)}, bf16[48,2176]{1,0:T(8,128)(2,1)S(1)}, u32[]{:S(2)}, u32[]{:S(2)}) collective-permute-start(bf16[48,2176]{1,0:T(8,128)(2,1)S(1)} %get-tuple-element.119), channel_id=1, source_target_pairs={{0,2},{1,3},{2,0},{3,1},{4,6},{5,7},{6,4},{7,5},{8,10},{9,11},{10,... | collective-permute-start | bytes 626696 | tf_op jit(solution)/shard_map/ppermute | solution.py:31
  71.2 9.4 %collective-permute-done.17.refs_2_ = bf16[48,2176]{1,0:T(8,128)(2,1)S(1)} collective-permute-done((bf16[48,2176]{1,0:T(8,128)(2,1)S(1)}, bf16[48,2176]{1,0:T(8,128)(2,1)S(1)}, u32[]{:S(2)}, u32[]{:S(2)}) %collective-permute-start.17) | collective-permute-done | bytes 208928 | tf_op jit(solution)/shard_map/ppermute | solution.py:31
  80.8 1.1 %shard_map.122 = (bf16[128,2048]{1,0:T(8,128)(2,1)}, bf16[1,128]{1,0:T(2,128)(2,1)}) custom-call(bf16[192,128]{1,0:T(8,128)(2,1)S(1)} %copy-done.2, bf16[48,2176]{1,0:T(8,128)(2,1)S(1)} %get-tuple-element.135.refs_0_, bf16[48,2176]{1,0:T(8,128)(2,1)S(1)} %collective-permute-done.12.refs_1_, bf16[48,2176]{1,0:T(8,128)(2,1)S(1)} %collective-permute-done.17.refs_2_, ...), custom_call_target="tpu_custom_call" | custom-call | bytes 1024 | tf_op jit(solution)/shard_map/pallas_call | solution.py:339
  82.0 0.8 %collective-permute-done.19.refs_4_ = bf16[192,1536]{1,0:T(8,128)(2,1)S(1)} collective-permute-done((bf16[192,1536]{1,0:T(8,128)(2,1)S(1)}, bf16[192,1536]{1,0:T(8,128)(2,1)S(1)}, u32[]{:S(2)}, u32[]{:S(2)}) %collective-permute-start.19) | collective-permute-done | bytes 589856 | tf_op jit(solution)/shard_map/ppermute | solution.py:36
  82.8 1.5 %shard_map.123 = (f32[256,512]{1,0:T(8,128)}, f32[256,512]{1,0:T(8,128)}, f32[256,512]{1,0:T(8,128)}) custom-call(bf16[48,2560]{1,0:T(8,128)(2,1)S(1)} %get-tuple-element.141.refs_0_, bf16[48,2560]{1,0:T(8,128)(2,1)S(1)} %collective-permute-done.14.refs_1_, bf16[48,2560]{1,0:T(8,128)(2,1)S(1)} %collective-permute-done.15.refs_2_, ...), custom_call_target="tpu_custom_call" | custom-call | bytes 1024 | tf_op jit(solution)/shard_map/pallas_call | solution.py:160
  (53 shorter events, 4.6 us)
Async XLA Ops:
  3.7 1.0 %copy-start = (bf16[48,4224]{1,0:T(8,128)(2,1)S(1)}, bf16[48,4224]{1,0:T(8,128)(2,1)}, u32[]{:S(2)}) copy-start(bf16[48,4224]{1,0:T(8,128)(2,1)} %get-tuple-element.80.refs_0_) | copy-start | bytes 1216516
  4.7 13.9 %collective-permute-start = (bf16[4,48,512]{2,1,0:T(8,128)(2,1)S(1)}, bf16[4,48,512]{2,1,0:T(8,128)(2,1)S(1)}, u32[]{:S(2)}, u32[]{:S(2)}) collective-permute-start(bf16[4,48,512]{2,1,0:T(8,128)(2,1)S(1)} %shard_map.111), channel_id=1, source_target_pairs={{0,4},{4,0},{8,12},{12,8},{16,20},{20,16},{24,28},{28,24},{1,5},{5... | collective-permute-start | bytes 589832 | tf_op jit(solution)/shard_map/ppermute | solution.py:36
  5.2 16.7 %collective-permute-start.1 = (bf16[48,4224]{1,0:T(8,128)(2,1)}, bf16[48,4224]{1,0:T(8,128)(2,1)S(1)}, u32[]{:S(2)}, u32[]{:S(2)}) collective-permute-start(bf16[48,4224]{1,0:T(8,128)(2,1)} %get-tuple-element.83), channel_id=1, source_target_pairs={{0,1},{1,2},{2,3},{3,0},{4,5},{5,6},{6,7},{7,4},{8,9},{9,10},{10,1... | collective-permute-start | bytes 1216520 | tf_op jit(solution)/shard_map/ppermute | solution.py:31
  7.8 20.3 %collective-permute-start.2 = (bf16[48,4224]{1,0:T(8,128)(2,1)}, bf16[48,4224]{1,0:T(8,128)(2,1)S(1)}, u32[]{:S(2)}, u32[]{:S(2)}) collective-permute-start(bf16[48,4224]{1,0:T(8,128)(2,1)} %get-tuple-element.84), channel_id=1, source_target_pairs={{0,3},{1,0},{2,1},{3,2},{4,7},{5,4},{6,5},{7,6},{8,11},{9,8},{10,9... | collective-permute-start | bytes 1216520 | tf_op jit(solution)/shard_map/ppermute | solution.py:31
  10.0 1.0 %copy-start.1 = (bf16[48,4224]{1,0:T(8,128)(2,1)S(1)}, bf16[48,4224]{1,0:T(8,128)(2,1)}, u32[]{:S(2)}) copy-start(bf16[48,4224]{1,0:T(8,128)(2,1)} %get-tuple-element.80.refs_0_) | copy-start | bytes 1216516
  18.6 12.2 %copy-start.3 = (bf16[48,4224]{1,0:T(8,128)(2,1)S(1)}, bf16[48,4224]{1,0:T(8,128)(2,1)}, u32[]{:S(2)}) copy-start(bf16[48,4224]{1,0:T(8,128)(2,1)} %get-tuple-element.86) | copy-start | bytes 1216516
  18.7 21.4 %collective-permute-start.5 = (bf16[48,2560]{1,0:T(8,128)(2,1)S(1)}, bf16[48,2560]{1,0:T(8,128)(2,1)S(1)}, u32[]{:S(2)}, u32[]{:S(2)}) collective-permute-start(bf16[48,2560]{1,0:T(8,128)(2,1)S(1)} %get-tuple-element.96), channel_id=1, source_target_pairs={{0,8},{4,12},{8,0},{12,4},{16,24},{20,28},{24,16},{28,20},{1,9},{5... | collective-permute-start | bytes 737288 | tf_op jit(solution)/shard_map/ppermute | solution.py:36
  20.3 19.7 %collective-permute-start.6 = (bf16[48,2560]{1,0:T(8,128)(2,1)S(1)}, bf16[48,2560]{1,0:T(8,128)(2,1)S(1)}, u32[]{:S(2)}, u32[]{:S(2)}) collective-permute-start(bf16[48,2560]{1,0:T(8,128)(2,1)S(1)} %get-tuple-element.97), channel_id=1, source_target_pairs={{0,16},{4,20},{8,24},{12,28},{16,0},{20,4},{24,8},{28,12},{1,17},{... | collective-permute-start | bytes 737288 | tf_op jit(solution)/shard_map/ppermute | solution.py:36
  28.2 11.9 %collective-permute-start.7 = (bf16[48,2560]{1,0:T(8,128)(2,1)S(1)}, bf16[48,2560]{1,0:T(8,128)(2,1)S(1)}, u32[]{:S(2)}, u32[]{:S(2)}) collective-permute-start(bf16[48,2560]{1,0:T(8,128)(2,1)S(1)} %get-tuple-element.98), channel_id=1, source_target_pairs={{0,24},{4,28},{8,16},{12,20},{16,8},{20,12},{24,0},{28,4},{1,25},{... | collective-permute-start | bytes 737288 | tf_op jit(solution)/shard_map/ppermute | solution.py:36
  30.7 9.2 %collective-permute-start.4 = (bf16[4,96,512]{2,1,0:T(8,128)(2,1)S(1)}, bf16[4,96,512]{2,1,0:T(8,128)(2,1)S(1)}, u32[]{:S(2)}, u32[]{:S(2)}) collective-permute-start(bf16[4,96,512]{2,1,0:T(8,128)(2,1)S(1)} %shard_map.115), channel_id=1, source_target_pairs={{0,4},{4,0},{8,12},{12,8},{16,20},{20,16},{24,28},{28,24},{1,5},{5... | collective-permute-start | bytes 1179656 | tf_op jit(solution)/shard_map/ppermute | solution.py:36
  30.8 21.4 %collective-permute-start.3 = (bf16[48,4224]{1,0:T(8,128)(2,1)S(1)}, bf16[48,4224]{1,0:T(8,128)(2,1)S(1)}, u32[]{:S(2)}, u32[]{:S(2)}) collective-permute-start(bf16[48,4224]{1,0:T(8,128)(2,1)S(1)} %copy-done.3), channel_id=1, source_target_pairs={{0,2},{1,3},{2,0},{3,1},{4,6},{5,7},{6,4},{7,5},{8,10},{9,11},{10,... | collective-permute-start | bytes 1216520 | tf_op jit(solution)/shard_map/ppermute | solution.py:31
  40.1 24.7 %collective-permute-start.9 = (bf16[96,2560]{1,0:T(8,128)(2,1)S(1)}, bf16[96,2560]{1,0:T(8,128)(2,1)S(1)}, u32[]{:S(2)}, u32[]{:S(2)}) collective-permute-start(bf16[96,2560]{1,0:T(8,128)(2,1)S(1)} %get-tuple-element.100), channel_id=1, source_target_pairs={{0,8},{4,12},{8,0},{12,4},{16,24},{20,28},{24,16},{28,20},{1,9},{5... | collective-permute-start | bytes 1474568 | tf_op jit(solution)/shard_map/ppermute | solution.py:36
  40.7 24.1 %collective-permute-start.10 = (bf16[96,2560]{1,0:T(8,128)(2,1)S(1)}, bf16[96,2560]{1,0:T(8,128)(2,1)S(1)}, u32[]{:S(2)}, u32[]{:S(2)}) collective-permute-start(bf16[96,2560]{1,0:T(8,128)(2,1)S(1)} %get-tuple-element.101), channel_id=1, source_target_pairs={{0,16},{4,20},{8,24},{12,28},{16,0},{20,4},{24,8},{28,12},{1,17},{... | collective-permute-start | bytes 1474568 | tf_op jit(solution)/shard_map/ppermute | solution.py:36
  41.2 23.6 %collective-permute-start.11 = (bf16[96,2560]{1,0:T(8,128)(2,1)S(1)}, bf16[96,2560]{1,0:T(8,128)(2,1)S(1)}, u32[]{:S(2)}, u32[]{:S(2)}) collective-permute-start(bf16[96,2560]{1,0:T(8,128)(2,1)S(1)} %get-tuple-element.102), channel_id=1, source_target_pairs={{0,24},{4,28},{8,16},{12,20},{16,8},{20,12},{24,0},{28,4},{1,25},{... | collective-permute-start | bytes 1474568 | tf_op jit(solution)/shard_map/ppermute | solution.py:36
  52.2 2.4 %collective-permute-start.8 = (bf16[4,48,512]{2,1,0:T(8,128)(2,1)S(1)}, bf16[4,48,512]{2,1,0:T(8,128)(2,1)S(1)}, u32[]{:S(2)}, u32[]{:S(2)}) collective-permute-start(bf16[4,48,512]{2,1,0:T(8,128)(2,1)S(1)} %shard_map.117), channel_id=1, source_target_pairs={{0,4},{4,0},{8,12},{12,8},{16,20},{20,16},{24,28},{28,24},{1,5},{5... | collective-permute-start | bytes 589832 | tf_op jit(solution)/shard_map/ppermute | solution.py:36
  52.3 10.0 %collective-permute-start.12 = (bf16[48,2176]{1,0:T(8,128)(2,1)S(1)}, bf16[48,2176]{1,0:T(8,128)(2,1)S(1)}, u32[]{:S(2)}, u32[]{:S(2)}) collective-permute-start(bf16[48,2176]{1,0:T(8,128)(2,1)S(1)} %get-tuple-element.111), channel_id=1, source_target_pairs={{0,3},{1,0},{2,1},{3,2},{4,7},{5,4},{6,5},{7,6},{8,11},{9,8},{10,9... | collective-permute-start | bytes 626696 | tf_op jit(solution)/shard_map/ppermute | solution.py:31
  54.6 10.2 %collective-permute-start.13 = (bf16[48,2176]{1,0:T(8,128)(2,1)S(1)}, bf16[48,2176]{1,0:T(8,128)(2,1)S(1)}, u32[]{:S(2)}, u32[]{:S(2)}) collective-permute-start(bf16[48,2176]{1,0:T(8,128)(2,1)S(1)} %get-tuple-element.112), channel_id=1, source_target_pairs={{0,1},{1,2},{2,3},{3,0},{4,5},{5,6},{6,7},{7,4},{8,9},{9,10},{10,1... | collective-permute-start | bytes 626696 | tf_op jit(solution)/shard_map/ppermute | solution.py:31
  64.9 4.7 %collective-permute-start.18 = (bf16[576,1536]{1,0:T(8,128)(2,1)S(1)}, bf16[576,1536]{1,0:T(8,128)(2,1)S(1)}, u32[]{:S(2)}, u32[]{:S(2)}) collective-permute-start(bf16[576,1536]{1,0:T(8,128)(2,1)S(1)} %slice_dynamic-update-slice_fusion), channel_id=1, source_target_pairs={{0,4},{4,0},{8,12},{12,8},{16,20},{20,16},{24,28},{28,24},{1,5},{5... | collective-permute-start | bytes 5308424 | tf_op jit(solution)/shard_map/ppermute | solution.py:36
  65.0 15.6 %collective-permute-start.14 = (bf16[48,2560]{1,0:T(8,128)(2,1)S(1)}, bf16[48,2560]{1,0:T(8,128)(2,1)S(1)}, u32[]{:S(2)}, u32[]{:S(2)}) collective-permute-start(bf16[48,2560]{1,0:T(8,128)(2,1)S(1)} %get-tuple-element.114), channel_id=1, source_target_pairs={{0,8},{4,12},{8,0},{12,4},{16,24},{20,28},{24,16},{28,20},{1,9},{5... | collective-permute-start | bytes 737288 | tf_op jit(solution)/shard_map/ppermute | solution.py:36
  65.9 14.7 %collective-permute-start.15 = (bf16[48,2560]{1,0:T(8,128)(2,1)S(1)}, bf16[48,2560]{1,0:T(8,128)(2,1)S(1)}, u32[]{:S(2)}, u32[]{:S(2)}) collective-permute-start(bf16[48,2560]{1,0:T(8,128)(2,1)S(1)} %get-tuple-element.115), channel_id=1, source_target_pairs={{0,16},{4,20},{8,24},{12,28},{16,0},{20,4},{24,8},{28,12},{1,17},{... | collective-permute-start | bytes 737288 | tf_op jit(solution)/shard_map/ppermute | solution.py:36
  66.5 14.2 %collective-permute-start.16 = (bf16[48,2560]{1,0:T(8,128)(2,1)S(1)}, bf16[48,2560]{1,0:T(8,128)(2,1)S(1)}, u32[]{:S(2)}, u32[]{:S(2)}) collective-permute-start(bf16[48,2560]{1,0:T(8,128)(2,1)S(1)} %get-tuple-element.116), channel_id=1, source_target_pairs={{0,24},{4,28},{8,16},{12,20},{16,8},{20,12},{24,0},{28,4},{1,25},{... | collective-permute-start | bytes 737288 | tf_op jit(solution)/shard_map/ppermute | solution.py:36
  68.6 12.1 %collective-permute-start.17 = (bf16[48,2176]{1,0:T(8,128)(2,1)S(1)}, bf16[48,2176]{1,0:T(8,128)(2,1)S(1)}, u32[]{:S(2)}, u32[]{:S(2)}) collective-permute-start(bf16[48,2176]{1,0:T(8,128)(2,1)S(1)} %get-tuple-element.119), channel_id=1, source_target_pairs={{0,2},{1,3},{2,0},{3,1},{4,6},{5,7},{6,4},{7,5},{8,10},{9,11},{10,... | collective-permute-start | bytes 626696 | tf_op jit(solution)/shard_map/ppermute | solution.py:31
  71.2 9.7 %copy-start.2 = (bf16[192,128]{1,0:T(8,128)(2,1)S(1)}, bf16[192,128]{1,0:T(8,128)(2,1)}, u32[]{:S(2)}) copy-start(bf16[192,128]{1,0:T(8,128)(2,1)} %get-tuple-element.78.placing_ref) | copy-start | bytes 147460
  80.8 2.1 %collective-permute-start.19 = (bf16[192,1536]{1,0:T(8,128)(2,1)S(1)}, bf16[192,1536]{1,0:T(8,128)(2,1)S(1)}, u32[]{:S(2)}, u32[]{:S(2)}) collective-permute-start(bf16[192,1536]{1,0:T(8,128)(2,1)S(1)} %pad_maximum_fusion), channel_id=1, source_target_pairs={{0,4},{4,0},{8,12},{12,8},{16,20},{20,16},{24,28},{28,24},{1,5},{5... | collective-permute-start | bytes 1769480 | tf_op jit(solution)/shard_map/ppermute | solution.py:36

commit v9 on v8

--- a/solution.py
+++ b/solution.py
@@ -50,8 +50,9 @@
 
 
 def pack_kernel(count, at_ref, *refs):
-    pieces, theirs, terms, payload = refs[:count], refs[count], refs[count + 1], refs[count + 2 :]
+    pieces, theirs = refs[:count], refs[count]
     chips, _, double = theirs.shape
+    payload, terms = refs[-chips:], refs[count + 1 : -chips]
     share = double // 2
     width = 2 * chips * share
     for k in range(chips):
@@ -61,7 +62,8 @@
             payload[k][part, :share] = pieces[i][:, pl.ds(start, share)]
             payload[k][part, share:double] = pieces[i][:, pl.ds(width + start, share)]
         payload[k][:, double : 2 * double] = theirs[k]
-        payload[k][:, 2 * double :] = terms[...]
+        for term in terms:
+            payload[k][:, 2 * double :] = term[...]
 
 
 def slices_of(pieces, width, share, flips):
@@ -94,38 +96,38 @@
     )(lax.axis_index("dp").astype(i32).reshape(1), *pieces)
 
 
-def pack(pieces, theirs, terms, width):
-    return list(packed(pieces, theirs, terms, width))
-
-
-def packed(pieces, theirs, terms, width):
+def pack(pieces, theirs, width, *terms):
     size = lax.axis_size("dp")
     share = width // size
     if share % LANES:
         own = slices_of(pieces, width, share, range(0, size, 2))
-        return [jnp.concatenate([own[k], theirs[k], terms], axis=1) for k in range(size // 2)]
-    shape = jax.ShapeDtypeStruct((terms.shape[0], 4 * share + terms.shape[1]), bf16)
-    return pl.pallas_call(
-        functools.partial(pack_kernel, len(pieces)),
-        out_shape=[shape] * (size // 2),
-        in_specs=[SMEM] + [VMEM] * (len(pieces) + 2),
-        out_specs=[VMEM] * (size // 2),
-        compiler_params=PARAMS,
-        cost_estimate=SMALL,
-    )(lax.axis_index("dp").astype(i32).reshape(1), *pieces, theirs, terms)
+        return [jnp.concatenate([own[k], theirs[k], *terms], axis=1) for k in range(size // 2)]
+    wide = 4 * share + sum(term.shape[1] for term in terms)
+    shape = jax.ShapeDtypeStruct((theirs.shape[1], wide), bf16)
+    return list(
+        pl.pallas_call(
+            functools.partial(pack_kernel, len(pieces)),
+            out_shape=[shape] * (size // 2),
+            in_specs=[SMEM] + [VMEM] * (len(pieces) + 1 + len(terms)),
+            out_specs=[VMEM] * (size // 2),
+            compiler_params=PARAMS,
+            cost_estimate=SMALL,
+        )(lax.axis_index("dp").astype(i32).reshape(1), *pieces, theirs, *terms)
+    )
 
 
 def sum_kernel(chips, share, units, scale, first, *refs):
-    got, others = refs[:chips], refs[chips]
-    past = () if first else refs[chips + 1 : chips + 4]
+    got, near, others = refs[:chips], refs[chips : 2 * chips], refs[2 * chips]
+    past = () if first else refs[2 * chips + 1 : 2 * chips + 4]
     outs = refs[-5:-2]
     cols, terms = refs[-2:]
     rows = got[0].shape[0]
+    start = near[0].shape[1] - 3 * units
     for k in range(chips):
         for core in range(2):
             part = slice((2 * k + core) * rows, (2 * k + core + 1) * rows)
             cols[part, :] = got[k][:, 2 * core * share : 2 * (core + 1) * share]
-        terms[2 * k * rows : (2 * k + 1) * rows, :] = got[k][:, 4 * share :]
+        terms[2 * k * rows : (2 * k + 1) * rows, :] = near[k][:, start:]
         terms[(2 * k + 1) * rows : (2 * k + 2) * rows, :] = others[k * rows : (k + 1) * rows, :]
     for i in range(3):
         column = share if i == 2 else 0
@@ -138,17 +140,17 @@
         outs[i][...] = total if scale is None else total * scale
 
 
-def weight_sums(got, others, past, share, scale):
+def weight_sums(got, near, others, past, share, scale):
     chips = len(got)
     rows = got[0].shape[0]
     units = others.shape[1] // 3
     if share % LANES:
         wide = [jnp.concatenate([g[:, 2 * c * share : 2 * (c + 1) * share] for g in got]) for c in range(2)]
-        near = jnp.concatenate([g[:, 4 * share :] for g in got])
+        own = jnp.concatenate([n[:, -3 * units :] for n in near])
         sums = []
         for i in range(3):
             total = 0.0 if past is None else past[i]
-            for cols, terms in zip(wide, (near, others)):
+            for cols, terms in zip(wide, (own, others)):
                 column = share if i == 2 else 0
                 total += lax.dot_general(
                     cols[:, column : column + share], terms[:, i * units : (i + 1) * units],
@@ -160,7 +162,7 @@
     return pl.pallas_call(
         functools.partial(sum_kernel, chips, share, units, scale, not past),
         out_shape=[jax.ShapeDtypeStruct((share, units), f32)] * 3,
-        in_specs=[VMEM] * (chips + 1 + len(past)),
+        in_specs=[VMEM] * (2 * chips + 1 + len(past)),
         out_specs=[VMEM] * 3,
         scratch_shapes=[
             pltpu.VMEM((2 * chips * rows, 2 * share), bf16),
@@ -168,7 +170,7 @@
         ],
         compiler_params=PARAMS,
         cost_estimate=SMALL,
-    )(*got, others, *past)
+    )(*got, *near, others, *past)
 
 
 def place_kernel(n_expert, me_ref, route_ref, prob_ref, tok_ref, cot_ref, placing_ref, *pieces):
@@ -355,6 +357,7 @@
     n_expert = lax.axis_size("expert")
     n_dp = lax.axis_size("dp")
     width = tokens.shape[1]
+    units = w_gate.shape[2]
     share = width // n_dp
     scale = 1.0 / math.sqrt(tokens.shape[0] * n_dp * n_expert)
     back_type = bf16 if n_expert == HOT else f32
@@ -367,11 +370,11 @@
         return [payload[0]] + [flipped(payload[k], "dp", 2 * k) for k in chips[1:]]
 
     def swap(*groups):
-        terms = [g[:, 4 * share :] for got in groups for g in got]
+        terms = [near[:, -3 * units :] for group in groups for near in group]
         other = flipped(jnp.concatenate(terms), "dp", 1)
         cuts, at = [], 0
-        for got in groups:
-            count = len(got) * got[0].shape[0]
+        for group in groups:
+            count = len(group) * group[0].shape[0]
             cuts.append(other[at : at + count])
             at += count
         return cuts
@@ -390,33 +393,34 @@
     theirs = flipped(cut(pieces[:1], width), "dp", 1)
     terms, back = chunk_rows(pieces[:1], weights, back_type, 36)
     home[0] = back[0]
-    payload = pack(pieces[:1], theirs, terms, width)
-    late, payload[-1], first, _ = lax.optimization_barrier(
-        ([pieces[k] for k in even], payload[-1], first, payload[0])
+    payload = pack(pieces[:1], theirs, width, terms)
+    got_local = exchange(payload)
+    late, first, got_local[1:] = lax.optimization_barrier(
+        ([pieces[k] for k in even], first, got_local[1:])
     )
     second = [shifted(piece, "expert", k) for piece, k in zip(late, even)]
-    got_local = exchange(payload)
 
     theirs = flipped(cut(first, width), "dp", 1)
+    got_first = exchange(pack(first, theirs, width))
     terms, back = chunk_rows(first, weights, back_type, 24)
-    payload = pack(first, theirs, terms, width)
-    payload, got_local = lax.optimization_barrier((payload, got_local))
-    got_first = exchange(payload)
-
-    second, back, _ = lax.optimization_barrier((second, back, payload))
-    home = give_back(home, odd, back)
+    terms, got_first, got_local = lax.optimization_barrier((terms, got_first, got_local))
+    near_first = exchange([terms] * len(chips))
+
+    second, back, _ = lax.optimization_barrier((second, back, terms))
+    home = give_back(home, odd[:-1], back[:-1])
     theirs = flipped(cut(second, width), "dp", 1)
-    terms, back = chunk_rows(second, weights, back_type, 12)
-    payload, got_first, back, home = lax.optimization_barrier(
-        (pack(second, theirs, terms, width), got_first, back, home)
+    terms, back_even = chunk_rows(second, weights, back_type, 12)
+    payload, near_first, back_even, home = lax.optimization_barrier(
+        (pack(second, theirs, width, terms), near_first, back_even, home)
     )
-    home = give_back(home, even, back)
+    home = give_back(home, even, back_even)
+    home = give_back(home, odd[-1:], back[-1:])
     got_second = exchange(payload)
-    local_other, first_other = swap(got_local, got_first)
-    sums = weight_sums(got_local, local_other, None, share, None)
-    sums = weight_sums(got_first, first_other, sums, share, None)
+    local_other, first_other = swap(got_local, near_first)
+    sums = weight_sums(got_local, got_local, local_other, None, share, None)
+    sums = weight_sums(got_first, near_first, first_other, sums, share, None)
     got_second, home, sums = lax.optimization_barrier((got_second, home, sums))
-    sums = weight_sums(got_second, swap(got_second)[0], sums, share, scale)
+    sums = weight_sums(got_second, got_second, swap(got_second)[0], sums, share, scale)
 
     grad_input, grad_prob = take(placing, home)
     return (grad_input, grad_prob, *[total[None] for total in sums])

time: 84.5 us -> 89.2 us (1.056)
  waiting for transfers between devices: 27.7 us -> 30.5 us
  starting transfers between devices: 23 us -> 25 us
    ppermute x14 -> x17, waiting for transfers between devices: 0.88 us -> 7.75 us  [flipped(): return lax.ppermute(values, axis, [(i, i ^ mask) for i in range(size)])]
    ppermute x6, waiting for transfers between devices: 26.8 us -> 22.8 us  [shifted(): lax.ppermute(values, axis, [(i, (i + by) % size) for i in range(size)])]
    ppermute x14 -> x17, starting transfers between devices: 13.6 us -> 15 us  [flipped(): return lax.ppermute(values, axis, [(i, i ^ mask) for i in range(size)])]
  transfers between devices with their start and end apart: 20 -> 23, of which waited for: 5 -> 9; matrix products, arithmetic and copies ran while one was open for 0% -> 0% of each run, Pallas kernels for 31% -> 29%
where the time goes in v9:
time: 89.2 us; the launch traced here: 89 us
  waiting for transfers between devices  30.5 us (34%)
  Pallas kernels  30.2 us (34%)
  starting transfers between devices  25 us (28%)
  local copies, waits for them, and re-layouts  2.31 us (3%)
  between operations  0.96 us (1%)
    pallas_call x3, Pallas kernels, chunk_rows(): pl.pallas_call(functools.partial(chunk_kernel, count), out_shape=[jax.Sha...  22.8 us
    ppermute x6, waiting for transfers between devices, shifted(): lax.ppermute(values, axis, [(i, (i + by) % size) for i in range(size)])  22.8 us
    ppermute x17, starting transfers between devices, flipped(): return lax.ppermute(values, axis, [(i, i ^ mask) for i in range(size)])  15 us
    ppermute x6, starting transfers between devices, shifted(): lax.ppermute(values, axis, [(i, (i + by) % size) for i in range(size)])  10 us
    ppermute x17, waiting for transfers between devices, flipped(): return lax.ppermute(values, axis, [(i, i ^ mask) for i in range(size)])  7.75 us
    pallas_call x1, Pallas kernels, place(): pl.pallas_call(functools.partial(place_kernel, n_expert), out_shape=[jax....  3.03 us
    pallas_call x3, Pallas kernels, weight_sums(): pl.pallas_call(functools.partial(sum_kernel, chips, share, units, scale,...  2.89 us
    unnamed x15, local copies, waits for them, and re-layouts  2.12 us
  transfers between devices with their start and end apart: 23, of which 9 were waited for; matrix products, arithmetic and copies ran while one was open for 0% of the time, Pallas kernels for 29%

profile of v9, /device:TPU:0, one launch (start us, length us, event | category | flops | bytes accessed | tf_op | source)
XLA Modules:
  0.0 89.0 jit_solution(1784585233480660908)
XLA Ops:
  0.6 3.0 %shard_map.110 = (bf16[192,128]{1,0:T(8,128)(2,1)}, bf16[48,4224]{1,0:T(8,128)(2,1)}, bf16[48,4224]{1,0:T(8,128)(2,1)}, bf16[48,4224]{1,0:T(8,128)(2,1)}, bf16[48,4224]{1,0:T(8,128)(2,1)}) custom-call(s32[1]{0:T(128)} %bitcast.me_ref, s32[1,128]{1,0:T(1,128)} %bitcast.20, bf16[1,128]{1,0:T(2,128)(2,1)} %bitcast.21, bf16[128,2048]{1,0:T(8,128)(2,1)} %tok_ref.1, ...), custom_call_target="tpu_custom_call" | custom-call | bytes 1024 | tf_op jit(solution)/shard_map/pallas_call | solution.py:202
  5.2 2.6 %collective-permute-start = (bf16[48,4224]{1,0:T(8,128)(2,1)}, bf16[48,4224]{1,0:T(8,128)(2,1)S(1)}, u32[]{:S(2)}, u32[]{:S(2)}) collective-permute-start(bf16[48,4224]{1,0:T(8,128)(2,1)} %get-tuple-element.82), channel_id=1, source_target_pairs={{0,1},{1,2},{2,3},{3,0},{4,5},{5,6},{6,7},{7,4},{8,9},{9,10},{10,1... | collective-permute-start | bytes 1216520 | tf_op jit(solution)/shard_map/ppermute | solution.py:31
  7.8 2.1 %collective-permute-start.1 = (bf16[48,4224]{1,0:T(8,128)(2,1)}, bf16[48,4224]{1,0:T(8,128)(2,1)S(1)}, u32[]{:S(2)}, u32[]{:S(2)}) collective-permute-start(bf16[48,4224]{1,0:T(8,128)(2,1)} %get-tuple-element.83), channel_id=1, source_target_pairs={{0,3},{1,0},{2,1},{3,2},{4,7},{5,4},{6,5},{7,6},{8,11},{9,8},{10,9... | collective-permute-start | bytes 1216520 | tf_op jit(solution)/shard_map/ppermute | solution.py:31
  10.0 1.0 %copy-done.1 = bf16[48,4224]{1,0:T(8,128)(2,1)S(1)} copy-done((bf16[48,4224]{1,0:T(8,128)(2,1)S(1)}, bf16[48,4224]{1,0:T(8,128)(2,1)}, u32[]{:S(2)}) %copy-start.1) | copy-done | bytes 405528
  11.0 7.6 %shard_map.112 = (bf16[48,1536]{1,0:T(8,128)(2,1)S(1)}, bf16[48,2176]{1,0:T(8,128)(2,1)S(1)}) custom-call(bf16[48,4224]{1,0:T(8,128)(2,1)S(1)} %copy-done.1, f32[2048,512]{1,0:T(8,128)} %bitcast.11, f32[2048,512]{1,0:T(8,128)} %bitcast.14, f32[2048,512]{1,0:T(8,128)} %bitcast.17), custom_call_target="tpu_custom_call" | custom-call | flops 7247757312 | bytes 1048576 | tf_op jit(solution)/shard_map/pallas_call | solution.py:303
  18.7 1.7 %collective-permute-start.3 = (bf16[48,2560]{1,0:T(8,128)(2,1)S(1)}, bf16[48,2560]{1,0:T(8,128)(2,1)S(1)}, u32[]{:S(2)}, u32[]{:S(2)}) collective-permute-start(bf16[48,2560]{1,0:T(8,128)(2,1)S(1)} %get-tuple-element.86), channel_id=1, source_target_pairs={{0,8},{4,12},{8,0},{12,4},{16,24},{20,28},{24,16},{28,20},{1,9},{5... | collective-permute-start | bytes 737288 | tf_op jit(solution)/shard_map/ppermute | solution.py:36
  20.3 1.5 %collective-permute-start.4 = (bf16[48,2560]{1,0:T(8,128)(2,1)S(1)}, bf16[48,2560]{1,0:T(8,128)(2,1)S(1)}, u32[]{:S(2)}, u32[]{:S(2)}) collective-permute-start(bf16[48,2560]{1,0:T(8,128)(2,1)S(1)} %get-tuple-element.87), channel_id=1, source_target_pairs={{0,16},{4,20},{8,24},{12,28},{16,0},{20,4},{24,8},{28,12},{1,17},{... | collective-permute-start | bytes 737288 | tf_op jit(solution)/shard_map/ppermute | solution.py:36
  22.2 6.0 %collective-permute-done.1.refs_1_ = bf16[48,4224]{1,0:T(8,128)(2,1)S(1)} collective-permute-done((bf16[48,4224]{1,0:T(8,128)(2,1)}, bf16[48,4224]{1,0:T(8,128)(2,1)S(1)}, u32[]{:S(2)}, u32[]{:S(2)}) %collective-permute-start.1) | collective-permute-done | bytes 405536 | tf_op jit(solution)/shard_map/ppermute | solution.py:31
  28.2 4.9 %collective-permute-done.4.refs_2_.refs_6_ = bf16[48,2560]{1,0:T(8,128)(2,1)S(1)} collective-permute-done((bf16[48,2560]{1,0:T(8,128)(2,1)S(1)}, bf16[48,2560]{1,0:T(8,128)(2,1)S(1)}, u32[]{:S(2)}, u32[]{:S(2)}) %collective-permute-start.4) | collective-permute-done | bytes 245792 | tf_op jit(solution)/shard_map/ppermute | solution.py:36
  35.0 1.3 %collective-permute-start.8 = (bf16[96,1024]{1,0:T(8,128)(2,1)S(1)}, bf16[96,1024]{1,0:T(8,128)(2,1)S(1)}, u32[]{:S(2)}, u32[]{:S(2)}) collective-permute-start(bf16[96,1024]{1,0:T(8,128)(2,1)S(1)} %get-tuple-element.96), channel_id=1, source_target_pairs={{0,8},{4,12},{8,0},{12,4},{16,24},{20,28},{24,16},{28,20},{1,9},{5... | collective-permute-start | bytes 589832 | tf_op jit(solution)/shard_map/ppermute | solution.py:36
  37.2 1.4 %collective-permute-start.10 = (bf16[96,1024]{1,0:T(8,128)(2,1)S(1)}, bf16[96,1024]{1,0:T(8,128)(2,1)S(1)}, u32[]{:S(2)}, u32[]{:S(2)}) collective-permute-start(bf16[96,1024]{1,0:T(8,128)(2,1)S(1)} %get-tuple-element.98), channel_id=1, source_target_pairs={{0,24},{4,28},{8,16},{12,20},{16,8},{20,12},{24,0},{28,4},{1,25},{... | collective-permute-start | bytes 589832 | tf_op jit(solution)/shard_map/ppermute | solution.py:36
  38.6 7.7 %shard_map.114 = (bf16[96,1536]{1,0:T(8,128)(2,1)S(1)}, bf16[48,2176]{1,0:T(8,128)(2,1)S(1)}, bf16[48,2176]{1,0:T(8,128)(2,1)S(1)}) custom-call(bf16[48,4224]{1,0:T(8,128)(2,1)S(1)} %collective-permute-done.refs_0_, bf16[48,4224]{1,0:T(8,128)(2,1)S(1)} %collective-permute-done.1.refs_1_, f32[2048,512]{1,0:T(8,128)} %bitcast.12, f32[2048,512]{1,0:T(8,128)} %bitcast.15, ...), custom_call_target="tpu_custom_call" | custom-call | flops 4831838208 | bytes 1048576 | tf_op jit(solution)/shard_map/pallas_call | solution.py:303
  47.2 1.8 %collective-permute-start.14 = (bf16[96,1536]{1,0:T(8,128)(2,1)S(1)}, bf16[96,1536]{1,0:T(8,128)(2,1)S(1)}, u32[]{:S(2)}, u32[]{:S(2)}) collective-permute-start(bf16[96,1536]{1,0:T(8,128)(2,1)S(1)} %get-tuple-element.125.refs_4_), channel_id=1, source_target_pairs={{0,24},{4,28},{8,16},{12,20},{16,8},{20,12},{24,0},{28,4},{1,25},{... | collective-permute-start | bytes 884744 | tf_op jit(solution)/shard_map/ppermute | solution.py:36
  49.5 1.2 %collective-permute-start.12 = (bf16[96,1536]{1,0:T(8,128)(2,1)S(1)}, bf16[96,1536]{1,0:T(8,128)(2,1)S(1)}, u32[]{:S(2)}, u32[]{:S(2)}) collective-permute-start(bf16[96,1536]{1,0:T(8,128)(2,1)S(1)} %get-tuple-element.125.refs_4_), channel_id=1, source_target_pairs={{0,8},{4,12},{8,0},{12,4},{16,24},{20,28},{24,16},{28,20},{1,9},{5... | collective-permute-start | bytes 884744 | tf_op jit(solution)/shard_map/ppermute | solution.py:36
  50.7 3.1 %collective-permute-done.6.refs_0_ = bf16[48,4224]{1,0:T(8,128)(2,1)S(1)} collective-permute-done((bf16[48,4224]{1,0:T(8,128)(2,1)S(1)}, bf16[48,4224]{1,0:T(8,128)(2,1)S(1)}, u32[]{:S(2)}, u32[]{:S(2)}) %collective-permute-start.6) | collective-permute-done | bytes 405536 | tf_op jit(solution)/shard_map/ppermute | solution.py:31
  53.9 2.7 %collective-permute-start.15 = (bf16[48,2176]{1,0:T(8,128)(2,1)S(1)}, bf16[48,2176]{1,0:T(8,128)(2,1)S(1)}, u32[]{:S(2)}, u32[]{:S(2)}) collective-permute-start(bf16[48,2176]{1,0:T(8,128)(2,1)S(1)} %get-tuple-element.112), channel_id=1, source_target_pairs={{0,3},{1,0},{2,1},{3,2},{4,7},{5,4},{6,5},{7,6},{8,11},{9,8},{10,9... | collective-permute-start | bytes 626696 | tf_op jit(solution)/shard_map/ppermute | solution.py:31
  56.7 7.6 %shard_map.118 = (bf16[48,1536]{1,0:T(8,128)(2,1)S(1)}, bf16[48,2176]{1,0:T(8,128)(2,1)S(1)}) custom-call(bf16[48,4224]{1,0:T(8,128)(2,1)S(1)} %collective-permute-done.6.refs_0_, f32[2048,512]{1,0:T(8,128)} %bitcast.13, f32[2048,512]{1,0:T(8,128)} %bitcast.16, f32[2048,512]{1,0:T(8,128)} %bitcast.19), custom_call_target="tpu_custom_call" | custom-call | flops 2415919104 | bytes 1048576 | tf_op jit(solution)/shard_map/pallas_call | solution.py:303
  64.6 1.3 %collective-permute-start.16 = (bf16[48,2560]{1,0:T(8,128)(2,1)S(1)}, bf16[48,2560]{1,0:T(8,128)(2,1)S(1)}, u32[]{:S(2)}, u32[]{:S(2)}) collective-permute-start(bf16[48,2560]{1,0:T(8,128)(2,1)S(1)} %get-tuple-element.114), channel_id=1, source_target_pairs={{0,8},{4,12},{8,0},{12,4},{16,24},{20,28},{24,16},{28,20},{1,9},{5... | collective-permute-start | bytes 737288 | tf_op jit(solution)/shard_map/ppermute | solution.py:36
  66.7 1.4 %collective-permute-start.18 = (bf16[48,2560]{1,0:T(8,128)(2,1)S(1)}, bf16[48,2560]{1,0:T(8,128)(2,1)S(1)}, u32[]{:S(2)}, u32[]{:S(2)}) collective-permute-start(bf16[48,2560]{1,0:T(8,128)(2,1)S(1)} %get-tuple-element.116), channel_id=1, source_target_pairs={{0,24},{4,28},{8,16},{12,20},{16,8},{20,12},{24,0},{28,4},{1,25},{... | collective-permute-start | bytes 737288 | tf_op jit(solution)/shard_map/ppermute | solution.py:36
  68.3 1.8 %collective-permute-start.19 = (bf16[48,2176]{1,0:T(8,128)(2,1)S(1)}, bf16[48,2176]{1,0:T(8,128)(2,1)S(1)}, u32[]{:S(2)}, u32[]{:S(2)}) collective-permute-start(bf16[48,2176]{1,0:T(8,128)(2,1)S(1)} %get-tuple-element.119), channel_id=1, source_target_pairs={{0,2},{1,3},{2,0},{3,1},{4,6},{5,7},{6,4},{7,5},{8,10},{9,11},{10,... | collective-permute-start | bytes 626696 | tf_op jit(solution)/shard_map/ppermute | solution.py:31
  71.6 6.4 %collective-permute-done.20.refs_3_ = bf16[48,2176]{1,0:T(8,128)(2,1)S(1)} collective-permute-done((bf16[48,2176]{1,0:T(8,128)(2,1)S(1)}, bf16[48,2176]{1,0:T(8,128)(2,1)S(1)}, u32[]{:S(2)}, u32[]{:S(2)}) %collective-permute-start.20) | collective-permute-done | bytes 208928 | tf_op jit(solution)/shard_map/ppermute | solution.py:31
  78.1 7.2 %collective-permute-done.19.refs_2_ = bf16[48,2176]{1,0:T(8,128)(2,1)S(1)} collective-permute-done((bf16[48,2176]{1,0:T(8,128)(2,1)S(1)}, bf16[48,2176]{1,0:T(8,128)(2,1)S(1)}, u32[]{:S(2)}, u32[]{:S(2)}) %collective-permute-start.19) | collective-permute-done | bytes 208928 | tf_op jit(solution)/shard_map/ppermute | solution.py:31
  85.5 1.1 %shard_map.122 = (bf16[128,2048]{1,0:T(8,128)(2,1)}, bf16[1,128]{1,0:T(2,128)(2,1)}) custom-call(bf16[192,128]{1,0:T(8,128)(2,1)S(1)} %copy-done.2, bf16[48,2176]{1,0:T(8,128)(2,1)S(1)} %get-tuple-element.139.refs_0_, bf16[48,2176]{1,0:T(8,128)(2,1)S(1)} %collective-permute-done.15.refs_1_, bf16[48,2176]{1,0:T(8,128)(2,1)S(1)} %collective-permute-done.19.refs_2_, ...), custom_call_target="tpu_custom_call" | custom-call | bytes 1024 | tf_op jit(solution)/shard_map/pallas_call | solution.py:341
  87.5 1.5 %shard_map.123 = (f32[256,512]{1,0:T(8,128)}, f32[256,512]{1,0:T(8,128)}, f32[256,512]{1,0:T(8,128)}) custom-call(bf16[48,2560]{1,0:T(8,128)(2,1)S(1)} %get-tuple-element.145.refs_0_.refs_4_, bf16[48,2560]{1,0:T(8,128)(2,1)S(1)} %collective-permute-done.16.refs_1_.refs_5_, bf16[48,2560]{1,0:T(8,128)(2,1)S(1)} %collective-permute-done.17.refs_2_.refs_6_, ...), custom_call_target="tpu_custom_call" | custom-call | bytes 1024 | tf_op jit(solution)/shard_map/pallas_call | solution.py:162
  (59 shorter events, 10.0 us)
Async XLA Ops:
  4.7 13.9 %collective-permute-start.2 = (bf16[4,48,512]{2,1,0:T(8,128)(2,1)S(1)}, bf16[4,48,512]{2,1,0:T(8,128)(2,1)S(1)}, u32[]{:S(2)}, u32[]{:S(2)}) collective-permute-start(bf16[4,48,512]{2,1,0:T(8,128)(2,1)S(1)} %shard_map.111), channel_id=1, source_target_pairs={{0,4},{4,0},{8,12},{12,8},{16,20},{20,16},{24,28},{28,24},{1,5},{5... | collective-permute-start | bytes 589832 | tf_op jit(solution)/shard_map/ppermute | solution.py:36
  5.2 17.0 %collective-permute-start = (bf16[48,4224]{1,0:T(8,128)(2,1)}, bf16[48,4224]{1,0:T(8,128)(2,1)S(1)}, u32[]{:S(2)}, u32[]{:S(2)}) collective-permute-start(bf16[48,4224]{1,0:T(8,128)(2,1)} %get-tuple-element.82), channel_id=1, source_target_pairs={{0,1},{1,2},{2,3},{3,0},{4,5},{5,6},{6,7},{7,4},{8,9},{9,10},{10,1... | collective-permute-start | bytes 1216520 | tf_op jit(solution)/shard_map/ppermute | solution.py:31
  7.8 20.3 %collective-permute-start.1 = (bf16[48,4224]{1,0:T(8,128)(2,1)}, bf16[48,4224]{1,0:T(8,128)(2,1)S(1)}, u32[]{:S(2)}, u32[]{:S(2)}) collective-permute-start(bf16[48,4224]{1,0:T(8,128)(2,1)} %get-tuple-element.83), channel_id=1, source_target_pairs={{0,3},{1,0},{2,1},{3,2},{4,7},{5,4},{6,5},{7,6},{8,11},{9,8},{10,9... | collective-permute-start | bytes 1216520 | tf_op jit(solution)/shard_map/ppermute | solution.py:31
  18.6 14.7 %copy-start.3 = (bf16[48,4224]{1,0:T(8,128)(2,1)S(1)}, bf16[48,4224]{1,0:T(8,128)(2,1)}, u32[]{:S(2)}) copy-start(bf16[48,4224]{1,0:T(8,128)(2,1)} %get-tuple-element.89) | copy-start | bytes 1216516
  18.7 9.5 %collective-permute-start.3 = (bf16[48,2560]{1,0:T(8,128)(2,1)S(1)}, bf16[48,2560]{1,0:T(8,128)(2,1)S(1)}, u32[]{:S(2)}, u32[]{:S(2)}) collective-permute-start(bf16[48,2560]{1,0:T(8,128)(2,1)S(1)} %get-tuple-element.86), channel_id=1, source_target_pairs={{0,8},{4,12},{8,0},{12,4},{16,24},{20,28},{24,16},{28,20},{1,9},{5... | collective-permute-start | bytes 737288 | tf_op jit(solution)/shard_map/ppermute | solution.py:36
  20.3 12.8 %collective-permute-start.4 = (bf16[48,2560]{1,0:T(8,128)(2,1)S(1)}, bf16[48,2560]{1,0:T(8,128)(2,1)S(1)}, u32[]{:S(2)}, u32[]{:S(2)}) collective-permute-start(bf16[48,2560]{1,0:T(8,128)(2,1)S(1)} %get-tuple-element.87), channel_id=1, source_target_pairs={{0,16},{4,20},{8,24},{12,28},{16,0},{20,4},{24,8},{28,12},{1,17},{... | collective-permute-start | bytes 737288 | tf_op jit(solution)/shard_map/ppermute | solution.py:36
  21.9 11.3 %collective-permute-start.5 = (bf16[48,2560]{1,0:T(8,128)(2,1)S(1)}, bf16[48,2560]{1,0:T(8,128)(2,1)S(1)}, u32[]{:S(2)}, u32[]{:S(2)}) collective-permute-start(bf16[48,2560]{1,0:T(8,128)(2,1)S(1)} %get-tuple-element.88), channel_id=1, source_target_pairs={{0,24},{4,28},{8,16},{12,20},{16,8},{20,12},{24,0},{28,4},{1,25},{... | collective-permute-start | bytes 737288 | tf_op jit(solution)/shard_map/ppermute | solution.py:36
  33.2 1.8 %collective-permute-start.7 = (bf16[4,96,512]{2,1,0:T(8,128)(2,1)S(1)}, bf16[4,96,512]{2,1,0:T(8,128)(2,1)S(1)}, u32[]{:S(2)}, u32[]{:S(2)}) collective-permute-start(bf16[4,96,512]{2,1,0:T(8,128)(2,1)S(1)} %shard_map.115), channel_id=1, source_target_pairs={{0,4},{4,0},{8,12},{12,8},{16,20},{20,16},{24,28},{28,24},{1,5},{5... | collective-permute-start | bytes 1179656 | tf_op jit(solution)/shard_map/ppermute | solution.py:36
  33.3 20.5 %collective-permute-start.6 = (bf16[48,4224]{1,0:T(8,128)(2,1)S(1)}, bf16[48,4224]{1,0:T(8,128)(2,1)S(1)}, u32[]{:S(2)}, u32[]{:S(2)}) collective-permute-start(bf16[48,4224]{1,0:T(8,128)(2,1)S(1)} %copy-done.3), channel_id=1, source_target_pairs={{0,2},{1,3},{2,0},{3,1},{4,6},{5,7},{6,4},{7,5},{8,10},{9,11},{10,... | collective-permute-start | bytes 1216520 | tf_op jit(solution)/shard_map/ppermute | solution.py:31
  35.0 11.2 %collective-permute-start.8 = (bf16[96,1024]{1,0:T(8,128)(2,1)S(1)}, bf16[96,1024]{1,0:T(8,128)(2,1)S(1)}, u32[]{:S(2)}, u32[]{:S(2)}) collective-permute-start(bf16[96,1024]{1,0:T(8,128)(2,1)S(1)} %get-tuple-element.96), channel_id=1, source_target_pairs={{0,8},{4,12},{8,0},{12,4},{16,24},{20,28},{24,16},{28,20},{1,9},{5... | collective-permute-start | bytes 589832 | tf_op jit(solution)/shard_map/ppermute | solution.py:36
  36.3 10.0 %collective-permute-start.9 = (bf16[96,1024]{1,0:T(8,128)(2,1)S(1)}, bf16[96,1024]{1,0:T(8,128)(2,1)S(1)}, u32[]{:S(2)}, u32[]{:S(2)}) collective-permute-start(bf16[96,1024]{1,0:T(8,128)(2,1)S(1)} %get-tuple-element.97), channel_id=1, source_target_pairs={{0,16},{4,20},{8,24},{12,28},{16,0},{20,4},{24,8},{28,12},{1,17},{... | collective-permute-start | bytes 589832 | tf_op jit(solution)/shard_map/ppermute | solution.py:36
  37.2 10.1 %collective-permute-start.10 = (bf16[96,1024]{1,0:T(8,128)(2,1)S(1)}, bf16[96,1024]{1,0:T(8,128)(2,1)S(1)}, u32[]{:S(2)}, u32[]{:S(2)}) collective-permute-start(bf16[96,1024]{1,0:T(8,128)(2,1)S(1)} %get-tuple-element.98), channel_id=1, source_target_pairs={{0,24},{4,28},{8,16},{12,20},{16,8},{20,12},{24,0},{28,4},{1,25},{... | collective-permute-start | bytes 589832 | tf_op jit(solution)/shard_map/ppermute | solution.py:36
  47.2 17.1 %collective-permute-start.14 = (bf16[96,1536]{1,0:T(8,128)(2,1)S(1)}, bf16[96,1536]{1,0:T(8,128)(2,1)S(1)}, u32[]{:S(2)}, u32[]{:S(2)}) collective-permute-start(bf16[96,1536]{1,0:T(8,128)(2,1)S(1)} %get-tuple-element.125.refs_4_), channel_id=1, source_target_pairs={{0,24},{4,28},{8,16},{12,20},{16,8},{20,12},{24,0},{28,4},{1,25},{... | collective-permute-start | bytes 884744 | tf_op jit(solution)/shard_map/ppermute | solution.py:36
  49.0 15.4 %collective-permute-start.13 = (bf16[96,1536]{1,0:T(8,128)(2,1)S(1)}, bf16[96,1536]{1,0:T(8,128)(2,1)S(1)}, u32[]{:S(2)}, u32[]{:S(2)}) collective-permute-start(bf16[96,1536]{1,0:T(8,128)(2,1)S(1)} %get-tuple-element.125.refs_4_), channel_id=1, source_target_pairs={{0,16},{4,20},{8,24},{12,28},{16,0},{20,4},{24,8},{28,12},{1,17},{... | collective-permute-start | bytes 884744 | tf_op jit(solution)/shard_map/ppermute | solution.py:36
  49.5 14.9 %collective-permute-start.12 = (bf16[96,1536]{1,0:T(8,128)(2,1)S(1)}, bf16[96,1536]{1,0:T(8,128)(2,1)S(1)}, u32[]{:S(2)}, u32[]{:S(2)}) collective-permute-start(bf16[96,1536]{1,0:T(8,128)(2,1)S(1)} %get-tuple-element.125.refs_4_), channel_id=1, source_target_pairs={{0,8},{4,12},{8,0},{12,4},{16,24},{20,28},{24,16},{28,20},{1,9},{5... | collective-permute-start | bytes 884744 | tf_op jit(solution)/shard_map/ppermute | solution.py:36
  53.8 10.4 %collective-permute-start.11 = (bf16[4,48,512]{2,1,0:T(8,128)(2,1)S(1)}, bf16[4,48,512]{2,1,0:T(8,128)(2,1)S(1)}, u32[]{:S(2)}, u32[]{:S(2)}) collective-permute-start(bf16[4,48,512]{2,1,0:T(8,128)(2,1)S(1)} %shard_map.117), channel_id=1, source_target_pairs={{0,4},{4,0},{8,12},{12,8},{16,20},{20,16},{24,28},{28,24},{1,5},{5... | collective-permute-start | bytes 589832 | tf_op jit(solution)/shard_map/ppermute | solution.py:36
  53.9 10.4 %collective-permute-start.15 = (bf16[48,2176]{1,0:T(8,128)(2,1)S(1)}, bf16[48,2176]{1,0:T(8,128)(2,1)S(1)}, u32[]{:S(2)}, u32[]{:S(2)}) collective-permute-start(bf16[48,2176]{1,0:T(8,128)(2,1)S(1)} %get-tuple-element.112), channel_id=1, source_target_pairs={{0,3},{1,0},{2,1},{3,2},{4,7},{5,4},{6,5},{7,6},{8,11},{9,8},{10,9... | collective-permute-start | bytes 626696 | tf_op jit(solution)/shard_map/ppermute | solution.py:31
  64.5 3.8 %collective-permute-start.21 = (bf16[576,1536]{1,0:T(8,128)(2,1)S(1)}, bf16[576,1536]{1,0:T(8,128)(2,1)S(1)}, u32[]{:S(2)}, u32[]{:S(2)}) collective-permute-start(bf16[576,1536]{1,0:T(8,128)(2,1)S(1)} %constant_dynamic-update-slice_fusion), channel_id=1, source_target_pairs={{0,4},{4,0},{8,12},{12,8},{16,20},{20,16},{24,28},{28,24},{1,5},{5... | collective-permute-start | bytes 5308424 | tf_op jit(solution)/shard_map/ppermute | solution.py:36
  64.6 20.7 %collective-permute-start.16 = (bf16[48,2560]{1,0:T(8,128)(2,1)S(1)}, bf16[48,2560]{1,0:T(8,128)(2,1)S(1)}, u32[]{:S(2)}, u32[]{:S(2)}) collective-permute-start(bf16[48,2560]{1,0:T(8,128)(2,1)S(1)} %get-tuple-element.114), channel_id=1, source_target_pairs={{0,8},{4,12},{8,0},{12,4},{16,24},{20,28},{24,16},{28,20},{1,9},{5... | collective-permute-start | bytes 737288 | tf_op jit(solution)/shard_map/ppermute | solution.py:36
  65.9 19.4 %collective-permute-start.17 = (bf16[48,2560]{1,0:T(8,128)(2,1)S(1)}, bf16[48,2560]{1,0:T(8,128)(2,1)S(1)}, u32[]{:S(2)}, u32[]{:S(2)}) collective-permute-start(bf16[48,2560]{1,0:T(8,128)(2,1)S(1)} %get-tuple-element.115), channel_id=1, source_target_pairs={{0,16},{4,20},{8,24},{12,28},{16,0},{20,4},{24,8},{28,12},{1,17},{... | collective-permute-start | bytes 737288 | tf_op jit(solution)/shard_map/ppermute | solution.py:36
  66.7 18.6 %collective-permute-start.18 = (bf16[48,2560]{1,0:T(8,128)(2,1)S(1)}, bf16[48,2560]{1,0:T(8,128)(2,1)S(1)}, u32[]{:S(2)}, u32[]{:S(2)}) collective-permute-start(bf16[48,2560]{1,0:T(8,128)(2,1)S(1)} %get-tuple-element.116), channel_id=1, source_target_pairs={{0,24},{4,28},{8,16},{12,20},{16,8},{20,12},{24,0},{28,4},{1,25},{... | collective-permute-start | bytes 737288 | tf_op jit(solution)/shard_map/ppermute | solution.py:36
  68.1 9.9 %collective-permute-start.20 = (bf16[48,2176]{1,0:T(8,128)(2,1)S(1)}, bf16[48,2176]{1,0:T(8,128)(2,1)S(1)}, u32[]{:S(2)}, u32[]{:S(2)}) collective-permute-start(bf16[48,2176]{1,0:T(8,128)(2,1)S(1)} %get-tuple-element.120), channel_id=1, source_target_pairs={{0,1},{1,2},{2,3},{3,0},{4,5},{5,6},{6,7},{7,4},{8,9},{9,10},{10,1... | collective-permute-start | bytes 626696 | tf_op jit(solution)/shard_map/ppermute | solution.py:31
  68.3 17.1 %collective-permute-start.19 = (bf16[48,2176]{1,0:T(8,128)(2,1)S(1)}, bf16[48,2176]{1,0:T(8,128)(2,1)S(1)}, u32[]{:S(2)}, u32[]{:S(2)}) collective-permute-start(bf16[48,2176]{1,0:T(8,128)(2,1)S(1)} %get-tuple-element.119), channel_id=1, source_target_pairs={{0,2},{1,3},{2,0},{3,1},{4,6},{5,7},{6,4},{7,5},{8,10},{9,11},{10,... | collective-permute-start | bytes 626696 | tf_op jit(solution)/shard_map/ppermute | solution.py:31
  85.5 2.1 %collective-permute-start.22 = (bf16[192,1536]{1,0:T(8,128)(2,1)S(1)}, bf16[192,1536]{1,0:T(8,128)(2,1)S(1)}, u32[]{:S(2)}, u32[]{:S(2)}) collective-permute-start(bf16[192,1536]{1,0:T(8,128)(2,1)S(1)} %pad_maximum_fusion), channel_id=1, source_target_pairs={{0,4},{4,0},{8,12},{12,8},{16,20},{20,16},{24,28},{28,24},{1,5},{5... | collective-permute-start | bytes 1769480 | tf_op jit(solution)/shard_map/ppermute | solution.py:36
  (3 other events, 15.9 us)

commit v10 on v8

--- a/solution.py
+++ b/solution.py
@@ -387,10 +387,11 @@
     even = list(range(2, n_expert, 2))
     first = [shifted(pieces[k], "expert", k) for k in odd]
 
-    theirs = flipped(cut(pieces[:1], width), "dp", 1)
     terms, back = chunk_rows(pieces[:1], weights, back_type, 36)
     home[0] = back[0]
-    payload = pack(pieces[:1], theirs, terms, width)
+    own, terms = lax.optimization_barrier((pieces[0], terms))
+    theirs = flipped(cut([own], width), "dp", 1)
+    payload = pack([own], theirs, terms, width)
     late, payload[-1], first, _ = lax.optimization_barrier(
         ([pieces[k] for k in even], payload[-1], first, payload[0])
     )

time: 84.5 us -> 82.9 us (0.981)
  local copies, waits for them, and re-layouts: 2.31 us -> 1.3 us
    ppermute x6, waiting for transfers between devices: 26.8 us -> 24.9 us  [shifted(): lax.ppermute(values, axis, [(i, (i + by) % size) for i in range(size)])]
    ppermute x14, waiting for transfers between devices: 0.88 us -> 2.3 us  [flipped(): return lax.ppermute(values, axis, [(i, i ^ mask) for i in range(size)])]
    unnamed x15 -> x13, local copies, waits for them, and re-layouts: 2.12 us -> 1.12 us
  transfers between devices with their start and end apart: 20 -> 20, of which waited for: 5 -> 6; matrix products, arithmetic and copies ran while one was open for 0% -> 0% of each run, Pallas kernels for 31% -> 31%
where the time goes in v10:
time: 82.9 us; the launch traced here: 82.7 us
  Pallas kernels  30.3 us (37%)
  waiting for transfers between devices  27.2 us (33%)
  starting transfers between devices  22.9 us (28%)
  local copies, waits for them, and re-layouts  1.3 us (2%)
  between operations  0.95 us (1%)
    ppermute x6, waiting for transfers between devices, shifted(): lax.ppermute(values, axis, [(i, (i + by) % size) for i in range(size)])  24.9 us
    pallas_call x3, Pallas kernels, chunk_rows(): pl.pallas_call(functools.partial(chunk_kernel, count), out_shape=[jax.Sha...  22.9 us
    ppermute x14, starting transfers between devices, flipped(): return lax.ppermute(values, axis, [(i, i ^ mask) for i in range(size)])  13.2 us
    ppermute x6, starting transfers between devices, shifted(): lax.ppermute(values, axis, [(i, (i + by) % size) for i in range(size)])  9.74 us
    pallas_call x1, Pallas kernels, place(): pl.pallas_call(functools.partial(place_kernel, n_expert), out_shape=[jax....  3.03 us
    pallas_call x3, Pallas kernels, weight_sums(): pl.pallas_call(functools.partial(sum_kernel, chips, share, units, scale,...  2.9 us
    ppermute x14, waiting for transfers between devices, flipped(): return lax.ppermute(values, axis, [(i, i ^ mask) for i in range(size)])  2.3 us
  transfers between devices with their start and end apart: 20, of which 6 were waited for; matrix products, arithmetic and copies ran while one was open for 0% of the time, Pallas kernels for 31%

profile of v10, /device:TPU:0, one launch (start us, length us, event | category | flops | bytes accessed | tf_op | source)
XLA Modules:
  0.0 82.7 jit_solution(17323296283377548945)
XLA Ops:
  0.6 3.0 %shard_map.110 = (bf16[192,128]{1,0:T(8,128)(2,1)}, bf16[48,4224]{1,0:T(8,128)(2,1)}, bf16[48,4224]{1,0:T(8,128)(2,1)}, bf16[48,4224]{1,0:T(8,128)(2,1)}, bf16[48,4224]{1,0:T(8,128)(2,1)}) custom-call(s32[1]{0:T(128)} %bitcast.me_ref, s32[1,128]{1,0:T(1,128)} %bitcast.20, bf16[1,128]{1,0:T(2,128)(2,1)} %bitcast.21, bf16[128,2048]{1,0:T(8,128)(2,1)} %tok_ref.1, ...), custom_call_target="tpu_custom_call" | custom-call | bytes 1024 | tf_op jit(solution)/shard_map/pallas_call | solution.py:200
  3.7 3.0 %collective-permute-start.1 = (bf16[48,4224]{1,0:T(8,128)(2,1)}, bf16[48,4224]{1,0:T(8,128)(2,1)S(1)}, u32[]{:S(2)}, u32[]{:S(2)}) collective-permute-start(bf16[48,4224]{1,0:T(8,128)(2,1)} %get-tuple-element.87), channel_id=1, source_target_pairs={{0,1},{1,2},{2,3},{3,0},{4,5},{5,6},{6,7},{7,4},{8,9},{9,10},{10,1... | collective-permute-start | bytes 1216520 | tf_op jit(solution)/shard_map/ppermute | solution.py:31
  6.7 2.0 %collective-permute-start.2 = (bf16[48,4224]{1,0:T(8,128)(2,1)}, bf16[48,4224]{1,0:T(8,128)(2,1)S(1)}, u32[]{:S(2)}, u32[]{:S(2)}) collective-permute-start(bf16[48,4224]{1,0:T(8,128)(2,1)} %get-tuple-element.88), channel_id=1, source_target_pairs={{0,3},{1,0},{2,1},{3,2},{4,7},{5,4},{6,5},{7,6},{8,11},{9,8},{10,9... | collective-permute-start | bytes 1216520 | tf_op jit(solution)/shard_map/ppermute | solution.py:31
  8.7 1.0 %copy-done = bf16[48,4224]{1,0:T(8,128)(2,1)S(1)} copy-done((bf16[48,4224]{1,0:T(8,128)(2,1)S(1)}, bf16[48,4224]{1,0:T(8,128)(2,1)}, u32[]{:S(2)}) %copy-start) | copy-done | bytes 405528
  9.7 7.6 %shard_map.111 = (bf16[48,1536]{1,0:T(8,128)(2,1)S(1)}, bf16[48,2176]{1,0:T(8,128)(2,1)S(1)}) custom-call(bf16[48,4224]{1,0:T(8,128)(2,1)S(1)} %copy-done, f32[2048,512]{1,0:T(8,128)} %bitcast.11, f32[2048,512]{1,0:T(8,128)} %bitcast.14, f32[2048,512]{1,0:T(8,128)} %bitcast.17), custom_call_target="tpu_custom_call" | custom-call | flops 7247757312 | bytes 1048576 | tf_op jit(solution)/shard_map/pallas_call | solution.py:301
  17.5 1.4 %collective-permute-done.refs_1_ = bf16[4,48,512]{2,1,0:T(8,128)(2,1)S(1)} collective-permute-done((bf16[4,48,512]{2,1,0:T(8,128)(2,1)S(1)}, bf16[4,48,512]{2,1,0:T(8,128)(2,1)S(1)}, u32[]{:S(2)}, u32[]{:S(2)}) %collective-permute-start) | collective-permute-done | bytes 196640 | tf_op jit(solution)/shard_map/ppermute | solution.py:36
  19.0 1.8 %collective-permute-start.5 = (bf16[48,2560]{1,0:T(8,128)(2,1)S(1)}, bf16[48,2560]{1,0:T(8,128)(2,1)S(1)}, u32[]{:S(2)}, u32[]{:S(2)}) collective-permute-start(bf16[48,2560]{1,0:T(8,128)(2,1)S(1)} %get-tuple-element.100), channel_id=1, source_target_pairs={{0,8},{4,12},{8,0},{12,4},{16,24},{20,28},{24,16},{28,20},{1,9},{5... | collective-permute-start | bytes 737288 | tf_op jit(solution)/shard_map/ppermute | solution.py:36
  20.7 1.5 %collective-permute-start.6 = (bf16[48,2560]{1,0:T(8,128)(2,1)S(1)}, bf16[48,2560]{1,0:T(8,128)(2,1)S(1)}, u32[]{:S(2)}, u32[]{:S(2)}) collective-permute-start(bf16[48,2560]{1,0:T(8,128)(2,1)S(1)} %get-tuple-element.101), channel_id=1, source_target_pairs={{0,16},{4,20},{8,24},{12,28},{16,0},{20,4},{24,8},{28,12},{1,17},{... | collective-permute-start | bytes 737288 | tf_op jit(solution)/shard_map/ppermute | solution.py:36
  22.3 4.2 %collective-permute-done.2.refs_1_ = bf16[48,4224]{1,0:T(8,128)(2,1)S(1)} collective-permute-done((bf16[48,4224]{1,0:T(8,128)(2,1)}, bf16[48,4224]{1,0:T(8,128)(2,1)S(1)}, u32[]{:S(2)}, u32[]{:S(2)}) %collective-permute-start.2) | collective-permute-done | bytes 405536 | tf_op jit(solution)/shard_map/ppermute | solution.py:31
  26.4 2.4 %collective-permute-start.7 = (bf16[48,2560]{1,0:T(8,128)(2,1)S(1)}, bf16[48,2560]{1,0:T(8,128)(2,1)S(1)}, u32[]{:S(2)}, u32[]{:S(2)}) collective-permute-start(bf16[48,2560]{1,0:T(8,128)(2,1)S(1)} %get-tuple-element.102), channel_id=1, source_target_pairs={{0,24},{4,28},{8,16},{12,20},{16,8},{20,12},{24,0},{28,4},{1,25},{... | collective-permute-start | bytes 737288 | tf_op jit(solution)/shard_map/ppermute | solution.py:36
  29.0 1.4 %collective-permute-start.3 = (bf16[48,4224]{1,0:T(8,128)(2,1)}, bf16[48,4224]{1,0:T(8,128)(2,1)S(1)}, u32[]{:S(2)}, u32[]{:S(2)}) collective-permute-start(bf16[48,4224]{1,0:T(8,128)(2,1)} %get-tuple-element.90), channel_id=1, source_target_pairs={{0,2},{1,3},{2,0},{3,1},{4,6},{5,7},{6,4},{7,5},{8,10},{9,11},{10,... | collective-permute-start | bytes 1216520 | tf_op jit(solution)/shard_map/ppermute | solution.py:31
  30.4 7.7 %shard_map.114 = (bf16[96,1536]{1,0:T(8,128)(2,1)S(1)}, bf16[48,2176]{1,0:T(8,128)(2,1)S(1)}, bf16[48,2176]{1,0:T(8,128)(2,1)S(1)}) custom-call(bf16[48,4224]{1,0:T(8,128)(2,1)S(1)} %collective-permute-done.1.refs_0_, bf16[48,4224]{1,0:T(8,128)(2,1)S(1)} %collective-permute-done.2.refs_1_, f32[2048,512]{1,0:T(8,128)} %bitcast.12, f32[2048,512]{1,0:T(8,128)} %bitcast.15, ...), custom_call_target="tpu_custom_call" | custom-call | flops 4831838208 | bytes 1048576 | tf_op jit(solution)/shard_map/pallas_call | solution.py:301
  39.4 2.4 %collective-permute-start.11 = (bf16[96,2560]{1,0:T(8,128)(2,1)S(1)}, bf16[96,2560]{1,0:T(8,128)(2,1)S(1)}, u32[]{:S(2)}, u32[]{:S(2)}) collective-permute-start(bf16[96,2560]{1,0:T(8,128)(2,1)S(1)} %get-tuple-element.106), channel_id=1, source_target_pairs={{0,24},{4,28},{8,16},{12,20},{16,8},{20,12},{24,0},{28,4},{1,25},{... | collective-permute-start | bytes 1474568 | tf_op jit(solution)/shard_map/ppermute | solution.py:36
  41.9 8.7 %collective-permute-done.3.refs_0_ = bf16[48,4224]{1,0:T(8,128)(2,1)S(1)} collective-permute-done((bf16[48,4224]{1,0:T(8,128)(2,1)}, bf16[48,4224]{1,0:T(8,128)(2,1)S(1)}, u32[]{:S(2)}, u32[]{:S(2)}) %collective-permute-start.3) | collective-permute-done | bytes 405536 | tf_op jit(solution)/shard_map/ppermute | solution.py:31
  50.7 2.3 %collective-permute-start.12 = (bf16[48,2176]{1,0:T(8,128)(2,1)S(1)}, bf16[48,2176]{1,0:T(8,128)(2,1)S(1)}, u32[]{:S(2)}, u32[]{:S(2)}) collective-permute-start(bf16[48,2176]{1,0:T(8,128)(2,1)S(1)} %get-tuple-element.115), channel_id=1, source_target_pairs={{0,3},{1,0},{2,1},{3,2},{4,7},{5,4},{6,5},{7,6},{8,11},{9,8},{10,9... | collective-permute-start | bytes 626696 | tf_op jit(solution)/shard_map/ppermute | solution.py:31
  53.0 7.6 %shard_map.118 = (bf16[48,1536]{1,0:T(8,128)(2,1)S(1)}, bf16[48,2176]{1,0:T(8,128)(2,1)S(1)}) custom-call(bf16[48,4224]{1,0:T(8,128)(2,1)S(1)} %collective-permute-done.3.refs_0_, f32[2048,512]{1,0:T(8,128)} %bitcast.13, f32[2048,512]{1,0:T(8,128)} %bitcast.16, f32[2048,512]{1,0:T(8,128)} %bitcast.19), custom_call_target="tpu_custom_call" | custom-call | flops 2415919104 | bytes 1048576 | tf_op jit(solution)/shard_map/pallas_call | solution.py:301
  60.7 2.6 %collective-permute-done.13.refs_3_ = bf16[48,2176]{1,0:T(8,128)(2,1)S(1)} collective-permute-done((bf16[48,2176]{1,0:T(8,128)(2,1)S(1)}, bf16[48,2176]{1,0:T(8,128)(2,1)S(1)}, u32[]{:S(2)}, u32[]{:S(2)}) %collective-permute-start.13) | collective-permute-done | bytes 208928 | tf_op jit(solution)/shard_map/ppermute | solution.py:31
  64.7 2.3 %collective-permute-start.16 = (bf16[48,2560]{1,0:T(8,128)(2,1)S(1)}, bf16[48,2560]{1,0:T(8,128)(2,1)S(1)}, u32[]{:S(2)}, u32[]{:S(2)}) collective-permute-start(bf16[48,2560]{1,0:T(8,128)(2,1)S(1)} %get-tuple-element.120), channel_id=1, source_target_pairs={{0,24},{4,28},{8,16},{12,20},{16,8},{20,12},{24,0},{28,4},{1,25},{... | collective-permute-start | bytes 737288 | tf_op jit(solution)/shard_map/ppermute | solution.py:36
  67.0 1.0 %collective-permute-start.17 = (bf16[48,2176]{1,0:T(8,128)(2,1)S(1)}, bf16[48,2176]{1,0:T(8,128)(2,1)S(1)}, u32[]{:S(2)}, u32[]{:S(2)}) collective-permute-start(bf16[48,2176]{1,0:T(8,128)(2,1)S(1)} %get-tuple-element.123), channel_id=1, source_target_pairs={{0,2},{1,3},{2,0},{3,1},{4,6},{5,7},{6,4},{7,5},{8,10},{9,11},{10,... | collective-permute-start | bytes 626696 | tf_op jit(solution)/shard_map/ppermute | solution.py:31
  68.8 0.8 shard_map.121
  69.6 9.4 %collective-permute-done.17.refs_2_ = bf16[48,2176]{1,0:T(8,128)(2,1)S(1)} collective-permute-done((bf16[48,2176]{1,0:T(8,128)(2,1)S(1)}, bf16[48,2176]{1,0:T(8,128)(2,1)S(1)}, u32[]{:S(2)}, u32[]{:S(2)}) %collective-permute-start.17) | collective-permute-done | bytes 208928 | tf_op jit(solution)/shard_map/ppermute | solution.py:31
  79.3 1.1 %shard_map.122 = (bf16[128,2048]{1,0:T(8,128)(2,1)}, bf16[1,128]{1,0:T(2,128)(2,1)}) custom-call(bf16[192,128]{1,0:T(8,128)(2,1)S(1)} %copy-done.2, bf16[48,2176]{1,0:T(8,128)(2,1)S(1)} %get-tuple-element.139.refs_0_, bf16[48,2176]{1,0:T(8,128)(2,1)S(1)} %collective-permute-done.12.refs_1_, bf16[48,2176]{1,0:T(8,128)(2,1)S(1)} %collective-permute-done.17.refs_2_, ...), custom_call_target="tpu_custom_call" | custom-call | bytes 1024 | tf_op jit(solution)/shard_map/pallas_call | solution.py:339
  80.4 0.8 %collective-permute-done.19.refs_4_ = bf16[192,1536]{1,0:T(8,128)(2,1)S(1)} collective-permute-done((bf16[192,1536]{1,0:T(8,128)(2,1)S(1)}, bf16[192,1536]{1,0:T(8,128)(2,1)S(1)}, u32[]{:S(2)}, u32[]{:S(2)}) %collective-permute-start.19) | collective-permute-done | bytes 589856 | tf_op jit(solution)/shard_map/ppermute | solution.py:36
  81.3 1.5 %shard_map.123 = (f32[256,512]{1,0:T(8,128)}, f32[256,512]{1,0:T(8,128)}, f32[256,512]{1,0:T(8,128)}) custom-call(bf16[48,2560]{1,0:T(8,128)(2,1)S(1)} %get-tuple-element.145.refs_0_, bf16[48,2560]{1,0:T(8,128)(2,1)S(1)} %collective-permute-done.14.refs_1_, bf16[48,2560]{1,0:T(8,128)(2,1)S(1)} %collective-permute-done.15.refs_2_, ...), custom_call_target="tpu_custom_call" | custom-call | bytes 1024 | tf_op jit(solution)/shard_map/pallas_call | solution.py:160
  (51 shorter events, 4.0 us)
Async XLA Ops:
  3.7 18.6 %collective-permute-start.1 = (bf16[48,4224]{1,0:T(8,128)(2,1)}, bf16[48,4224]{1,0:T(8,128)(2,1)S(1)}, u32[]{:S(2)}, u32[]{:S(2)}) collective-permute-start(bf16[48,4224]{1,0:T(8,128)(2,1)} %get-tuple-element.87), channel_id=1, source_target_pairs={{0,1},{1,2},{2,3},{3,0},{4,5},{5,6},{6,7},{7,4},{8,9},{9,10},{10,1... | collective-permute-start | bytes 1216520 | tf_op jit(solution)/shard_map/ppermute | solution.py:31
  6.7 19.7 %collective-permute-start.2 = (bf16[48,4224]{1,0:T(8,128)(2,1)}, bf16[48,4224]{1,0:T(8,128)(2,1)S(1)}, u32[]{:S(2)}, u32[]{:S(2)}) collective-permute-start(bf16[48,4224]{1,0:T(8,128)(2,1)} %get-tuple-element.88), channel_id=1, source_target_pairs={{0,3},{1,0},{2,1},{3,2},{4,7},{5,4},{6,5},{7,6},{8,11},{9,8},{10,9... | collective-permute-start | bytes 1216520 | tf_op jit(solution)/shard_map/ppermute | solution.py:31
  8.7 1.0 %copy-start = (bf16[48,4224]{1,0:T(8,128)(2,1)S(1)}, bf16[48,4224]{1,0:T(8,128)(2,1)}, u32[]{:S(2)}) copy-start(bf16[48,4224]{1,0:T(8,128)(2,1)} %get-tuple-element.84.refs_0_) | copy-start | bytes 1216516
  9.7 7.6 %copy-start.1 = (bf16[48,4224]{1,0:T(8,128)(2,1)S(1)}, bf16[48,4224]{1,0:T(8,128)(2,1)}, u32[]{:S(2)}) copy-start(bf16[48,4224]{1,0:T(8,128)(2,1)} %get-tuple-element.84.refs_0_) | copy-start | bytes 1216516
  17.4 1.5 %collective-permute-start = (bf16[4,48,512]{2,1,0:T(8,128)(2,1)S(1)}, bf16[4,48,512]{2,1,0:T(8,128)(2,1)S(1)}, u32[]{:S(2)}, u32[]{:S(2)}) collective-permute-start(bf16[4,48,512]{2,1,0:T(8,128)(2,1)S(1)} %shard_map.112), channel_id=1, source_target_pairs={{0,4},{4,0},{8,12},{12,8},{16,20},{20,16},{24,28},{28,24},{1,5},{5... | collective-permute-start | bytes 589832 | tf_op jit(solution)/shard_map/ppermute | solution.py:36
  19.0 19.3 %collective-permute-start.5 = (bf16[48,2560]{1,0:T(8,128)(2,1)S(1)}, bf16[48,2560]{1,0:T(8,128)(2,1)S(1)}, u32[]{:S(2)}, u32[]{:S(2)}) collective-permute-start(bf16[48,2560]{1,0:T(8,128)(2,1)S(1)} %get-tuple-element.100), channel_id=1, source_target_pairs={{0,8},{4,12},{8,0},{12,4},{16,24},{20,28},{24,16},{28,20},{1,9},{5... | collective-permute-start | bytes 737288 | tf_op jit(solution)/shard_map/ppermute | solution.py:36
  20.7 17.5 %collective-permute-start.6 = (bf16[48,2560]{1,0:T(8,128)(2,1)S(1)}, bf16[48,2560]{1,0:T(8,128)(2,1)S(1)}, u32[]{:S(2)}, u32[]{:S(2)}) collective-permute-start(bf16[48,2560]{1,0:T(8,128)(2,1)S(1)} %get-tuple-element.101), channel_id=1, source_target_pairs={{0,16},{4,20},{8,24},{12,28},{16,0},{20,4},{24,8},{28,12},{1,17},{... | collective-permute-start | bytes 737288 | tf_op jit(solution)/shard_map/ppermute | solution.py:36
  26.4 11.8 %collective-permute-start.7 = (bf16[48,2560]{1,0:T(8,128)(2,1)S(1)}, bf16[48,2560]{1,0:T(8,128)(2,1)S(1)}, u32[]{:S(2)}, u32[]{:S(2)}) collective-permute-start(bf16[48,2560]{1,0:T(8,128)(2,1)S(1)} %get-tuple-element.102), channel_id=1, source_target_pairs={{0,24},{4,28},{8,16},{12,20},{16,8},{20,12},{24,0},{28,4},{1,25},{... | collective-permute-start | bytes 737288 | tf_op jit(solution)/shard_map/ppermute | solution.py:36
  28.9 9.2 %collective-permute-start.4 = (bf16[4,96,512]{2,1,0:T(8,128)(2,1)S(1)}, bf16[4,96,512]{2,1,0:T(8,128)(2,1)S(1)}, u32[]{:S(2)}, u32[]{:S(2)}) collective-permute-start(bf16[4,96,512]{2,1,0:T(8,128)(2,1)S(1)} %shard_map.115), channel_id=1, source_target_pairs={{0,4},{4,0},{8,12},{12,8},{16,20},{20,16},{24,28},{28,24},{1,5},{5... | collective-permute-start | bytes 1179656 | tf_op jit(solution)/shard_map/ppermute | solution.py:36
  29.0 21.6 %collective-permute-start.3 = (bf16[48,4224]{1,0:T(8,128)(2,1)}, bf16[48,4224]{1,0:T(8,128)(2,1)S(1)}, u32[]{:S(2)}, u32[]{:S(2)}) collective-permute-start(bf16[48,4224]{1,0:T(8,128)(2,1)} %get-tuple-element.90), channel_id=1, source_target_pairs={{0,2},{1,3},{2,0},{3,1},{4,6},{5,7},{6,4},{7,5},{8,10},{9,11},{10,... | collective-permute-start | bytes 1216520 | tf_op jit(solution)/shard_map/ppermute | solution.py:31
  38.3 25.0 %collective-permute-start.9 = (bf16[96,2560]{1,0:T(8,128)(2,1)S(1)}, bf16[96,2560]{1,0:T(8,128)(2,1)S(1)}, u32[]{:S(2)}, u32[]{:S(2)}) collective-permute-start(bf16[96,2560]{1,0:T(8,128)(2,1)S(1)} %get-tuple-element.104), channel_id=1, source_target_pairs={{0,8},{4,12},{8,0},{12,4},{16,24},{20,28},{24,16},{28,20},{1,9},{5... | collective-permute-start | bytes 1474568 | tf_op jit(solution)/shard_map/ppermute | solution.py:36
  38.9 24.4 %collective-permute-start.10 = (bf16[96,2560]{1,0:T(8,128)(2,1)S(1)}, bf16[96,2560]{1,0:T(8,128)(2,1)S(1)}, u32[]{:S(2)}, u32[]{:S(2)}) collective-permute-start(bf16[96,2560]{1,0:T(8,128)(2,1)S(1)} %get-tuple-element.105), channel_id=1, source_target_pairs={{0,16},{4,20},{8,24},{12,28},{16,0},{20,4},{24,8},{28,12},{1,17},{... | collective-permute-start | bytes 1474568 | tf_op jit(solution)/shard_map/ppermute | solution.py:36
  39.4 23.9 %collective-permute-start.11 = (bf16[96,2560]{1,0:T(8,128)(2,1)S(1)}, bf16[96,2560]{1,0:T(8,128)(2,1)S(1)}, u32[]{:S(2)}, u32[]{:S(2)}) collective-permute-start(bf16[96,2560]{1,0:T(8,128)(2,1)S(1)} %get-tuple-element.106), channel_id=1, source_target_pairs={{0,24},{4,28},{8,16},{12,20},{16,8},{20,12},{24,0},{28,4},{1,25},{... | collective-permute-start | bytes 1474568 | tf_op jit(solution)/shard_map/ppermute | solution.py:36
  50.6 2.4 %collective-permute-start.8 = (bf16[4,48,512]{2,1,0:T(8,128)(2,1)S(1)}, bf16[4,48,512]{2,1,0:T(8,128)(2,1)S(1)}, u32[]{:S(2)}, u32[]{:S(2)}) collective-permute-start(bf16[4,48,512]{2,1,0:T(8,128)(2,1)S(1)} %shard_map.117), channel_id=1, source_target_pairs={{0,4},{4,0},{8,12},{12,8},{16,20},{20,16},{24,28},{28,24},{1,5},{5... | collective-permute-start | bytes 589832 | tf_op jit(solution)/shard_map/ppermute | solution.py:36
  50.7 10.0 %collective-permute-start.12 = (bf16[48,2176]{1,0:T(8,128)(2,1)S(1)}, bf16[48,2176]{1,0:T(8,128)(2,1)S(1)}, u32[]{:S(2)}, u32[]{:S(2)}) collective-permute-start(bf16[48,2176]{1,0:T(8,128)(2,1)S(1)} %get-tuple-element.115), channel_id=1, source_target_pairs={{0,3},{1,0},{2,1},{3,2},{4,7},{5,4},{6,5},{7,6},{8,11},{9,8},{10,9... | collective-permute-start | bytes 626696 | tf_op jit(solution)/shard_map/ppermute | solution.py:31
  53.0 10.2 %collective-permute-start.13 = (bf16[48,2176]{1,0:T(8,128)(2,1)S(1)}, bf16[48,2176]{1,0:T(8,128)(2,1)S(1)}, u32[]{:S(2)}, u32[]{:S(2)}) collective-permute-start(bf16[48,2176]{1,0:T(8,128)(2,1)S(1)} %get-tuple-element.116), channel_id=1, source_target_pairs={{0,1},{1,2},{2,3},{3,0},{4,5},{5,6},{6,7},{7,4},{8,9},{9,10},{10,1... | collective-permute-start | bytes 626696 | tf_op jit(solution)/shard_map/ppermute | solution.py:31
  63.4 4.7 %collective-permute-start.18 = (bf16[576,1536]{1,0:T(8,128)(2,1)S(1)}, bf16[576,1536]{1,0:T(8,128)(2,1)S(1)}, u32[]{:S(2)}, u32[]{:S(2)}) collective-permute-start(bf16[576,1536]{1,0:T(8,128)(2,1)S(1)} %slice_dynamic-update-slice_fusion), channel_id=1, source_target_pairs={{0,4},{4,0},{8,12},{12,8},{16,20},{20,16},{24,28},{28,24},{1,5},{5... | collective-permute-start | bytes 5308424 | tf_op jit(solution)/shard_map/ppermute | solution.py:36
  63.5 15.6 %collective-permute-start.14 = (bf16[48,2560]{1,0:T(8,128)(2,1)S(1)}, bf16[48,2560]{1,0:T(8,128)(2,1)S(1)}, u32[]{:S(2)}, u32[]{:S(2)}) collective-permute-start(bf16[48,2560]{1,0:T(8,128)(2,1)S(1)} %get-tuple-element.118), channel_id=1, source_target_pairs={{0,8},{4,12},{8,0},{12,4},{16,24},{20,28},{24,16},{28,20},{1,9},{5... | collective-permute-start | bytes 737288 | tf_op jit(solution)/shard_map/ppermute | solution.py:36
  64.2 14.9 %collective-permute-start.15 = (bf16[48,2560]{1,0:T(8,128)(2,1)S(1)}, bf16[48,2560]{1,0:T(8,128)(2,1)S(1)}, u32[]{:S(2)}, u32[]{:S(2)}) collective-permute-start(bf16[48,2560]{1,0:T(8,128)(2,1)S(1)} %get-tuple-element.119), channel_id=1, source_target_pairs={{0,16},{4,20},{8,24},{12,28},{16,0},{20,4},{24,8},{28,12},{1,17},{... | collective-permute-start | bytes 737288 | tf_op jit(solution)/shard_map/ppermute | solution.py:36
  64.7 14.4 %collective-permute-start.16 = (bf16[48,2560]{1,0:T(8,128)(2,1)S(1)}, bf16[48,2560]{1,0:T(8,128)(2,1)S(1)}, u32[]{:S(2)}, u32[]{:S(2)}) collective-permute-start(bf16[48,2560]{1,0:T(8,128)(2,1)S(1)} %get-tuple-element.120), channel_id=1, source_target_pairs={{0,24},{4,28},{8,16},{12,20},{16,8},{20,12},{24,0},{28,4},{1,25},{... | collective-permute-start | bytes 737288 | tf_op jit(solution)/shard_map/ppermute | solution.py:36
  67.0 12.1 %collective-permute-start.17 = (bf16[48,2176]{1,0:T(8,128)(2,1)S(1)}, bf16[48,2176]{1,0:T(8,128)(2,1)S(1)}, u32[]{:S(2)}, u32[]{:S(2)}) collective-permute-start(bf16[48,2176]{1,0:T(8,128)(2,1)S(1)} %get-tuple-element.123), channel_id=1, source_target_pairs={{0,2},{1,3},{2,0},{3,1},{4,6},{5,7},{6,4},{7,5},{8,10},{9,11},{10,... | collective-permute-start | bytes 626696 | tf_op jit(solution)/shard_map/ppermute | solution.py:31
  69.6 9.7 %copy-start.2 = (bf16[192,128]{1,0:T(8,128)(2,1)S(1)}, bf16[192,128]{1,0:T(8,128)(2,1)}, u32[]{:S(2)}) copy-start(bf16[192,128]{1,0:T(8,128)(2,1)} %get-tuple-element.80.placing_ref) | copy-start | bytes 147460
  79.2 2.1 %collective-permute-start.19 = (bf16[192,1536]{1,0:T(8,128)(2,1)S(1)}, bf16[192,1536]{1,0:T(8,128)(2,1)S(1)}, u32[]{:S(2)}, u32[]{:S(2)}) collective-permute-start(bf16[192,1536]{1,0:T(8,128)(2,1)S(1)} %pad_maximum_fusion), channel_id=1, source_target_pairs={{0,4},{4,0},{8,12},{12,8},{16,20},{20,16},{24,28},{28,24},{1,5},{5... | collective-permute-start | bytes 1769480 | tf_op jit(solution)/shard_map/ppermute | solution.py:36

commit v11 on v9

--- a/solution.py
+++ b/solution.py
@@ -367,7 +367,7 @@
     home = [None] * n_expert
 
     def exchange(payload):
-        return [payload[0]] + [flipped(payload[k], "dp", 2 * k) for k in chips[1:]]
+        return [payload[0]] + [flipped(part, "dp", 2 * k) for k, part in enumerate(payload) if k]
 
     def swap(*groups):
         terms = [near[:, -3 * units :] for group in groups for near in group]
@@ -390,14 +390,16 @@
     even = list(range(2, n_expert, 2))
     first = [shifted(pieces[k], "expert", k) for k in odd]
 
-    theirs = flipped(cut(pieces[:1], width), "dp", 1)
     terms, back = chunk_rows(pieces[:1], weights, back_type, 36)
     home[0] = back[0]
-    payload = pack(pieces[:1], theirs, width, terms)
-    got_local = exchange(payload)
-    late, first, got_local[1:] = lax.optimization_barrier(
-        ([pieces[k] for k in even], first, got_local[1:])
+    own, terms = lax.optimization_barrier((pieces[0], terms))
+    theirs = flipped(cut([own], width), "dp", 1)
+    payload = pack([own], theirs, width, terms)
+    near_local = exchange(payload[:-1])
+    late, first, near_local, payload[-1] = lax.optimization_barrier(
+        ([pieces[k] for k in even], first, near_local, payload[-1])
     )
+    got_local = near_local + [flipped(payload[-1], "dp", 2 * chips[-1])]
     second = [shifted(piece, "expert", k) for piece, k in zip(late, even)]
 
     theirs = flipped(cut(first, width), "dp", 1)
@@ -407,14 +409,13 @@
     near_first = exchange([terms] * len(chips))
 
     second, back, _ = lax.optimization_barrier((second, back, terms))
-    home = give_back(home, odd[:-1], back[:-1])
+    home = give_back(home, odd, back)
     theirs = flipped(cut(second, width), "dp", 1)
     terms, back_even = chunk_rows(second, weights, back_type, 12)
     payload, near_first, back_even, home = lax.optimization_barrier(
         (pack(second, theirs, width, terms), near_first, back_even, home)
     )
     home = give_back(home, even, back_even)
-    home = give_back(home, odd[-1:], back[-1:])
     got_second = exchange(payload)
     local_other, first_other = swap(got_local, near_first)
     sums = weight_sums(got_local, got_local, local_other, None, share, None)

time: 89.2 us -> 91.6 us (1.027)
  starting transfers between devices: 25 us -> 27.1 us
  waiting for transfers between devices: 30.5 us -> 31.8 us
  local copies, waits for them, and re-layouts: 2.31 us -> 1.32 us
    ppermute x6, waiting for transfers between devices: 22.8 us -> 28.3 us  [shifted(): lax.ppermute(values, axis, [(i, (i + by) % size) for i in range(size)])]
    ppermute x17, waiting for transfers between devices: 7.75 us -> 3.45 us  [flipped(): return lax.ppermute(values, axis, [(i, i ^ mask) for i in range(size)])]
    ppermute x17, starting transfers between devices: 15 us -> 17 us  [flipped(): return lax.ppermute(values, axis, [(i, i ^ mask) for i in range(size)])]
    unnamed x15 -> x19, local copies, waits for them, and re-layouts: 2.12 us -> 1.13 us
  transfers between devices with their start and end apart: 23 -> 23, of which waited for: 9 -> 7; matrix products, arithmetic and copies ran while one was open for 0% -> 0% of each run, Pallas kernels for 29% -> 20%
where the time goes in v11:
time: 91.6 us; the launch traced here: 91.5 us
  waiting for transfers between devices  31.8 us (35%)
  Pallas kernels  30.3 us (33%)
  starting transfers between devices  27.1 us (30%)
  local copies, waits for them, and re-layouts  1.32 us (1%)
  between operations  0.95 us (1%)
    ppermute x6, waiting for transfers between devices, shifted(): lax.ppermute(values, axis, [(i, (i + by) % size) for i in range(size)])  28.3 us
    pallas_call x3, Pallas kernels, chunk_rows(): pl.pallas_call(functools.partial(chunk_kernel, count), out_shape=[jax.Sha...  22.9 us
    ppermute x17, starting transfers between devices, flipped(): return lax.ppermute(values, axis, [(i, i ^ mask) for i in range(size)])  17 us
    ppermute x6, starting transfers between devices, shifted(): lax.ppermute(values, axis, [(i, (i + by) % size) for i in range(size)])  10.1 us
    ppermute x17, waiting for transfers between devices, flipped(): return lax.ppermute(values, axis, [(i, i ^ mask) for i in range(size)])  3.45 us
    pallas_call x1, Pallas kernels, place(): pl.pallas_call(functools.partial(place_kernel, n_expert), out_shape=[jax....  3.03 us
    pallas_call x3, Pallas kernels, weight_sums(): pl.pallas_call(functools.partial(sum_kernel, chips, share, units, scale,...  2.9 us
  transfers between devices with their start and end apart: 23, of which 7 were waited for; matrix products, arithmetic and copies ran while one was open for 0% of the time, Pallas kernels for 20%

profile of v11, /device:TPU:0, one launch (start us, length us, event | category | flops | bytes accessed | tf_op | source)
XLA Modules:
  0.0 91.5 jit_solution(16329847089859277373)
XLA Ops:
  0.6 3.0 %shard_map.110 = (bf16[192,128]{1,0:T(8,128)(2,1)}, bf16[48,4224]{1,0:T(8,128)(2,1)}, bf16[48,4224]{1,0:T(8,128)(2,1)}, bf16[48,4224]{1,0:T(8,128)(2,1)}, bf16[48,4224]{1,0:T(8,128)(2,1)}) custom-call(s32[1]{0:T(128)} %bitcast.me_ref, s32[1,128]{1,0:T(1,128)} %bitcast.20, bf16[1,128]{1,0:T(2,128)(2,1)} %bitcast.21, bf16[128,2048]{1,0:T(8,128)(2,1)} %tok_ref.1, ...), custom_call_target="tpu_custom_call" | custom-call | bytes 1024 | tf_op jit(solution)/shard_map/pallas_call | solution.py:202
  3.7 1.0 %copy-done = bf16[48,4224]{1,0:T(8,128)(2,1)S(1)} copy-done((bf16[48,4224]{1,0:T(8,128)(2,1)S(1)}, bf16[48,4224]{1,0:T(8,128)(2,1)}, u32[]{:S(2)}) %copy-start) | copy-done | bytes 405528
  4.7 7.7 %shard_map.111 = (bf16[48,1536]{1,0:T(8,128)(2,1)S(1)}, bf16[48,2176]{1,0:T(8,128)(2,1)S(1)}) custom-call(bf16[48,4224]{1,0:T(8,128)(2,1)S(1)} %copy-done, f32[2048,512]{1,0:T(8,128)} %bitcast.11, f32[2048,512]{1,0:T(8,128)} %bitcast.14, f32[2048,512]{1,0:T(8,128)} %bitcast.17), custom_call_target="tpu_custom_call" | custom-call | flops 7247757312 | bytes 1048576 | tf_op jit(solution)/shard_map/pallas_call | solution.py:303
  12.9 2.6 %collective-permute-start = (bf16[48,4224]{1,0:T(8,128)(2,1)S(1)}, bf16[48,4224]{1,0:T(8,128)(2,1)S(1)}, u32[]{:S(2)}, u32[]{:S(2)}) collective-permute-start(bf16[48,4224]{1,0:T(8,128)(2,1)S(1)} %copy-done.5), channel_id=1, source_target_pairs={{0,1},{1,2},{2,3},{3,0},{4,5},{5,6},{6,7},{7,4},{8,9},{9,10},{10,1... | collective-permute-start | bytes 1216520 | tf_op jit(solution)/shard_map/ppermute | solution.py:31
  15.6 2.3 %collective-permute-start.1 = (bf16[48,4224]{1,0:T(8,128)(2,1)S(1)}, bf16[48,4224]{1,0:T(8,128)(2,1)S(1)}, u32[]{:S(2)}, u32[]{:S(2)}) collective-permute-start(bf16[48,4224]{1,0:T(8,128)(2,1)S(1)} %copy-done.4), channel_id=1, source_target_pairs={{0,3},{1,0},{2,1},{3,2},{4,7},{5,4},{6,5},{7,6},{8,11},{9,8},{10,9... | collective-permute-start | bytes 1216520 | tf_op jit(solution)/shard_map/ppermute | solution.py:31
  17.9 1.5 %collective-permute-start.3 = (bf16[48,2560]{1,0:T(8,128)(2,1)S(1)}, bf16[48,2560]{1,0:T(8,128)(2,1)S(1)}, u32[]{:S(2)}, u32[]{:S(2)}) collective-permute-start(bf16[48,2560]{1,0:T(8,128)(2,1)S(1)} %get-tuple-element.93), channel_id=1, source_target_pairs={{0,8},{4,12},{8,0},{12,4},{16,24},{20,28},{24,16},{28,20},{1,9},{5... | collective-permute-start | bytes 737288 | tf_op jit(solution)/shard_map/ppermute | solution.py:36
  19.5 1.5 %collective-permute-start.4 = (bf16[48,2560]{1,0:T(8,128)(2,1)S(1)}, bf16[48,2560]{1,0:T(8,128)(2,1)S(1)}, u32[]{:S(2)}, u32[]{:S(2)}) collective-permute-start(bf16[48,2560]{1,0:T(8,128)(2,1)S(1)} %get-tuple-element.94), channel_id=1, source_target_pairs={{0,16},{4,20},{8,24},{12,28},{16,0},{20,4},{24,8},{28,12},{1,17},{... | collective-permute-start | bytes 737288 | tf_op jit(solution)/shard_map/ppermute | solution.py:36
  21.0 6.9 %collective-permute-done.refs_0_ = bf16[48,4224]{1,0:T(8,128)(2,1)S(1)} collective-permute-done((bf16[48,4224]{1,0:T(8,128)(2,1)S(1)}, bf16[48,4224]{1,0:T(8,128)(2,1)S(1)}, u32[]{:S(2)}, u32[]{:S(2)}) %collective-permute-start) | collective-permute-done | bytes 405536 | tf_op jit(solution)/shard_map/ppermute | solution.py:31
  27.9 7.8 %collective-permute-done.1.refs_1_ = bf16[48,4224]{1,0:T(8,128)(2,1)S(1)} collective-permute-done((bf16[48,4224]{1,0:T(8,128)(2,1)S(1)}, bf16[48,4224]{1,0:T(8,128)(2,1)S(1)}, u32[]{:S(2)}, u32[]{:S(2)}) %collective-permute-start.1) | collective-permute-done | bytes 405536 | tf_op jit(solution)/shard_map/ppermute | solution.py:31
  35.8 2.5 %collective-permute-start.10 = (bf16[48,2560]{1,0:T(8,128)(2,1)S(1)}, bf16[48,2560]{1,0:T(8,128)(2,1)S(1)}, u32[]{:S(2)}, u32[]{:S(2)}) collective-permute-start(bf16[48,2560]{1,0:T(8,128)(2,1)S(1)} %get-tuple-element.109), channel_id=1, source_target_pairs={{0,24},{4,28},{8,16},{12,20},{16,8},{20,12},{24,0},{28,4},{1,25},{... | collective-permute-start | bytes 737288 | tf_op jit(solution)/shard_map/ppermute | solution.py:36
  38.3 1.3 %collective-permute-start.5 = (bf16[48,4224]{1,0:T(8,128)(2,1)S(1)}, bf16[48,4224]{1,0:T(8,128)(2,1)S(1)}, u32[]{:S(2)}, u32[]{:S(2)}) collective-permute-start(bf16[48,4224]{1,0:T(8,128)(2,1)S(1)} %copy-done.3), channel_id=1, source_target_pairs={{0,2},{1,3},{2,0},{3,1},{4,6},{5,7},{6,4},{7,5},{8,10},{9,11},{10,... | collective-permute-start | bytes 1216520 | tf_op jit(solution)/shard_map/ppermute | solution.py:31
  40.8 2.4 %collective-permute-start.9 = (bf16[96,1024]{1,0:T(8,128)(2,1)S(1)}, bf16[96,1024]{1,0:T(8,128)(2,1)S(1)}, u32[]{:S(2)}, u32[]{:S(2)}) collective-permute-start(bf16[96,1024]{1,0:T(8,128)(2,1)S(1)} %get-tuple-element.105), channel_id=1, source_target_pairs={{0,24},{4,28},{8,16},{12,20},{16,8},{20,12},{24,0},{28,4},{1,25},{... | collective-permute-start | bytes 589832 | tf_op jit(solution)/shard_map/ppermute | solution.py:36
  43.3 7.7 %shard_map.114 = (bf16[96,1536]{1,0:T(8,128)(2,1)S(1)}, bf16[48,2176]{1,0:T(8,128)(2,1)S(1)}, bf16[48,2176]{1,0:T(8,128)(2,1)S(1)}) custom-call(bf16[48,4224]{1,0:T(8,128)(2,1)S(1)} %collective-permute-done.refs_0_, bf16[48,4224]{1,0:T(8,128)(2,1)S(1)} %collective-permute-done.1.refs_1_, f32[2048,512]{1,0:T(8,128)} %bitcast.12, f32[2048,512]{1,0:T(8,128)} %bitcast.15, ...), custom_call_target="tpu_custom_call" | custom-call | flops 4831838208 | bytes 1048576 | tf_op jit(solution)/shard_map/pallas_call | solution.py:303
  51.0 2.6 %collective-permute-done.9.refs_3_ = bf16[96,1024]{1,0:T(8,128)(2,1)S(1)} collective-permute-done((bf16[96,1024]{1,0:T(8,128)(2,1)S(1)}, bf16[96,1024]{1,0:T(8,128)(2,1)S(1)}, u32[]{:S(2)}, u32[]{:S(2)}) %collective-permute-start.9) | collective-permute-done | bytes 196640 | tf_op jit(solution)/shard_map/ppermute | solution.py:36
  53.6 2.4 %collective-permute-start.14 = (bf16[96,1536]{1,0:T(8,128)(2,1)S(1)}, bf16[96,1536]{1,0:T(8,128)(2,1)S(1)}, u32[]{:S(2)}, u32[]{:S(2)}) collective-permute-start(bf16[96,1536]{1,0:T(8,128)(2,1)S(1)} %get-tuple-element.133.refs_4_), channel_id=1, source_target_pairs={{0,24},{4,28},{8,16},{12,20},{16,8},{20,12},{24,0},{28,4},{1,25},{... | collective-permute-start | bytes 884744 | tf_op jit(solution)/shard_map/ppermute | solution.py:36
  57.0 2.3 %collective-permute-done.5.refs_0_ = bf16[48,4224]{1,0:T(8,128)(2,1)S(1)} collective-permute-done((bf16[48,4224]{1,0:T(8,128)(2,1)S(1)}, bf16[48,4224]{1,0:T(8,128)(2,1)S(1)}, u32[]{:S(2)}, u32[]{:S(2)}) %collective-permute-start.5) | collective-permute-done | bytes 405536 | tf_op jit(solution)/shard_map/ppermute | solution.py:31
  59.5 2.3 %collective-permute-start.15 = (bf16[48,2176]{1,0:T(8,128)(2,1)S(1)}, bf16[48,2176]{1,0:T(8,128)(2,1)S(1)}, u32[]{:S(2)}, u32[]{:S(2)}) collective-permute-start(bf16[48,2176]{1,0:T(8,128)(2,1)S(1)} %get-tuple-element.119), channel_id=1, source_target_pairs={{0,3},{1,0},{2,1},{3,2},{4,7},{5,4},{6,5},{7,6},{8,11},{9,8},{10,9... | collective-permute-start | bytes 626696 | tf_op jit(solution)/shard_map/ppermute | solution.py:31
  62.1 7.6 %shard_map.118 = (bf16[48,1536]{1,0:T(8,128)(2,1)S(1)}, bf16[48,2176]{1,0:T(8,128)(2,1)S(1)}) custom-call(bf16[48,4224]{1,0:T(8,128)(2,1)S(1)} %collective-permute-done.5.refs_0_, f32[2048,512]{1,0:T(8,128)} %bitcast.13, f32[2048,512]{1,0:T(8,128)} %bitcast.16, f32[2048,512]{1,0:T(8,128)} %bitcast.19), custom_call_target="tpu_custom_call" | custom-call | flops 2415919104 | bytes 1048576 | tf_op jit(solution)/shard_map/pallas_call | solution.py:303
  69.8 2.2 %collective-permute-done.16.refs_3_ = bf16[48,2176]{1,0:T(8,128)(2,1)S(1)} collective-permute-done((bf16[48,2176]{1,0:T(8,128)(2,1)S(1)}, bf16[48,2176]{1,0:T(8,128)(2,1)S(1)}, u32[]{:S(2)}, u32[]{:S(2)}) %collective-permute-start.16) | collective-permute-done | bytes 208928 | tf_op jit(solution)/shard_map/ppermute | solution.py:31
  73.3 2.4 %collective-permute-start.19 = (bf16[48,2560]{1,0:T(8,128)(2,1)S(1)}, bf16[48,2560]{1,0:T(8,128)(2,1)S(1)}, u32[]{:S(2)}, u32[]{:S(2)}) collective-permute-start(bf16[48,2560]{1,0:T(8,128)(2,1)S(1)} %get-tuple-element.124), channel_id=1, source_target_pairs={{0,24},{4,28},{8,16},{12,20},{16,8},{20,12},{24,0},{28,4},{1,25},{... | collective-permute-start | bytes 737288 | tf_op jit(solution)/shard_map/ppermute | solution.py:36
  75.7 1.4 %collective-permute-start.20 = (bf16[48,2176]{1,0:T(8,128)(2,1)S(1)}, bf16[48,2176]{1,0:T(8,128)(2,1)S(1)}, u32[]{:S(2)}, u32[]{:S(2)}) collective-permute-start(bf16[48,2176]{1,0:T(8,128)(2,1)S(1)} %get-tuple-element.127), channel_id=1, source_target_pairs={{0,2},{1,3},{2,0},{3,1},{4,6},{5,7},{6,4},{7,5},{8,10},{9,11},{10,... | collective-permute-start | bytes 626696 | tf_op jit(solution)/shard_map/ppermute | solution.py:31
  78.7 9.1 %collective-permute-done.20.refs_2_ = bf16[48,2176]{1,0:T(8,128)(2,1)S(1)} collective-permute-done((bf16[48,2176]{1,0:T(8,128)(2,1)S(1)}, bf16[48,2176]{1,0:T(8,128)(2,1)S(1)}, u32[]{:S(2)}, u32[]{:S(2)}) %collective-permute-start.20) | collective-permute-done | bytes 208928 | tf_op jit(solution)/shard_map/ppermute | solution.py:31
  88.0 1.1 %shard_map.122 = (bf16[128,2048]{1,0:T(8,128)(2,1)}, bf16[1,128]{1,0:T(2,128)(2,1)}) custom-call(bf16[192,128]{1,0:T(8,128)(2,1)S(1)} %copy-done.2, bf16[48,2176]{1,0:T(8,128)(2,1)S(1)} %get-tuple-element.147.refs_0_, bf16[48,2176]{1,0:T(8,128)(2,1)S(1)} %collective-permute-done.15.refs_1_, bf16[48,2176]{1,0:T(8,128)(2,1)S(1)} %collective-permute-done.20.refs_2_, ...), custom_call_target="tpu_custom_call" | custom-call | bytes 1024 | tf_op jit(solution)/shard_map/pallas_call | solution.py:341
  90.0 1.5 %shard_map.123 = (f32[256,512]{1,0:T(8,128)}, f32[256,512]{1,0:T(8,128)}, f32[256,512]{1,0:T(8,128)}) custom-call(bf16[48,2560]{1,0:T(8,128)(2,1)S(1)} %get-tuple-element.153.refs_0_.refs_4_, bf16[48,2560]{1,0:T(8,128)(2,1)S(1)} %collective-permute-done.17.refs_1_.refs_5_, bf16[48,2560]{1,0:T(8,128)(2,1)S(1)} %collective-permute-done.18.refs_2_.refs_6_, ...), custom_call_target="tpu_custom_call" | custom-call | bytes 1024 | tf_op jit(solution)/shard_map/pallas_call | solution.py:162
  (63 shorter events, 7.3 us)
Async XLA Ops:
  12.4 26.0 %copy-start.3 = (bf16[48,4224]{1,0:T(8,128)(2,1)S(1)}, bf16[48,4224]{1,0:T(8,128)(2,1)}, u32[]{:S(2)}) copy-start(bf16[48,4224]{1,0:T(8,128)(2,1)} %get-tuple-element.96) | copy-start | bytes 1216516
  12.4 5.5 %collective-permute-start.2 = (bf16[4,48,512]{2,1,0:T(8,128)(2,1)S(1)}, bf16[4,48,512]{2,1,0:T(8,128)(2,1)S(1)}, u32[]{:S(2)}, u32[]{:S(2)}) collective-permute-start(bf16[4,48,512]{2,1,0:T(8,128)(2,1)S(1)} %shard_map.112), channel_id=1, source_target_pairs={{0,4},{4,0},{8,12},{12,8},{16,20},{20,16},{24,28},{28,24},{1,5},{5... | collective-permute-start | bytes 589832 | tf_op jit(solution)/shard_map/ppermute | solution.py:36
  12.9 15.0 %collective-permute-start = (bf16[48,4224]{1,0:T(8,128)(2,1)S(1)}, bf16[48,4224]{1,0:T(8,128)(2,1)S(1)}, u32[]{:S(2)}, u32[]{:S(2)}) collective-permute-start(bf16[48,4224]{1,0:T(8,128)(2,1)S(1)} %copy-done.5), channel_id=1, source_target_pairs={{0,1},{1,2},{2,3},{3,0},{4,5},{5,6},{6,7},{7,4},{8,9},{9,10},{10,1... | collective-permute-start | bytes 1216520 | tf_op jit(solution)/shard_map/ppermute | solution.py:31
  15.6 20.1 %collective-permute-start.1 = (bf16[48,4224]{1,0:T(8,128)(2,1)S(1)}, bf16[48,4224]{1,0:T(8,128)(2,1)S(1)}, u32[]{:S(2)}, u32[]{:S(2)}) collective-permute-start(bf16[48,4224]{1,0:T(8,128)(2,1)S(1)} %copy-done.4), channel_id=1, source_target_pairs={{0,3},{1,0},{2,1},{3,2},{4,7},{5,4},{6,5},{7,6},{8,11},{9,8},{10,9... | collective-permute-start | bytes 1216520 | tf_op jit(solution)/shard_map/ppermute | solution.py:31
  17.9 17.8 %collective-permute-start.3 = (bf16[48,2560]{1,0:T(8,128)(2,1)S(1)}, bf16[48,2560]{1,0:T(8,128)(2,1)S(1)}, u32[]{:S(2)}, u32[]{:S(2)}) collective-permute-start(bf16[48,2560]{1,0:T(8,128)(2,1)S(1)} %get-tuple-element.93), channel_id=1, source_target_pairs={{0,8},{4,12},{8,0},{12,4},{16,24},{20,28},{24,16},{28,20},{1,9},{5... | collective-permute-start | bytes 737288 | tf_op jit(solution)/shard_map/ppermute | solution.py:36
  19.5 16.2 %collective-permute-start.4 = (bf16[48,2560]{1,0:T(8,128)(2,1)S(1)}, bf16[48,2560]{1,0:T(8,128)(2,1)S(1)}, u32[]{:S(2)}, u32[]{:S(2)}) collective-permute-start(bf16[48,2560]{1,0:T(8,128)(2,1)S(1)} %get-tuple-element.94), channel_id=1, source_target_pairs={{0,16},{4,20},{8,24},{12,28},{16,0},{20,4},{24,8},{28,12},{1,17},{... | collective-permute-start | bytes 737288 | tf_op jit(solution)/shard_map/ppermute | solution.py:36
  35.7 3.9 %collective-permute-start.6 = (bf16[4,96,512]{2,1,0:T(8,128)(2,1)S(1)}, bf16[4,96,512]{2,1,0:T(8,128)(2,1)S(1)}, u32[]{:S(2)}, u32[]{:S(2)}) collective-permute-start(bf16[4,96,512]{2,1,0:T(8,128)(2,1)S(1)} %shard_map.115), channel_id=1, source_target_pairs={{0,4},{4,0},{8,12},{12,8},{16,20},{20,16},{24,28},{28,24},{1,5},{5... | collective-permute-start | bytes 1179656 | tf_op jit(solution)/shard_map/ppermute | solution.py:36
  35.8 15.1 %collective-permute-start.10 = (bf16[48,2560]{1,0:T(8,128)(2,1)S(1)}, bf16[48,2560]{1,0:T(8,128)(2,1)S(1)}, u32[]{:S(2)}, u32[]{:S(2)}) collective-permute-start(bf16[48,2560]{1,0:T(8,128)(2,1)S(1)} %get-tuple-element.109), channel_id=1, source_target_pairs={{0,24},{4,28},{8,16},{12,20},{16,8},{20,12},{24,0},{28,4},{1,25},{... | collective-permute-start | bytes 737288 | tf_op jit(solution)/shard_map/ppermute | solution.py:36
  38.3 21.0 %collective-permute-start.5 = (bf16[48,4224]{1,0:T(8,128)(2,1)S(1)}, bf16[48,4224]{1,0:T(8,128)(2,1)S(1)}, u32[]{:S(2)}, u32[]{:S(2)}) collective-permute-start(bf16[48,4224]{1,0:T(8,128)(2,1)S(1)} %copy-done.3), channel_id=1, source_target_pairs={{0,2},{1,3},{2,0},{3,1},{4,6},{5,7},{6,4},{7,5},{8,10},{9,11},{10,... | collective-permute-start | bytes 1216520 | tf_op jit(solution)/shard_map/ppermute | solution.py:31
  39.7 11.3 %collective-permute-start.7 = (bf16[96,1024]{1,0:T(8,128)(2,1)S(1)}, bf16[96,1024]{1,0:T(8,128)(2,1)S(1)}, u32[]{:S(2)}, u32[]{:S(2)}) collective-permute-start(bf16[96,1024]{1,0:T(8,128)(2,1)S(1)} %get-tuple-element.103), channel_id=1, source_target_pairs={{0,8},{4,12},{8,0},{12,4},{16,24},{20,28},{24,16},{28,20},{1,9},{5... | collective-permute-start | bytes 589832 | tf_op jit(solution)/shard_map/ppermute | solution.py:36
  40.3 10.7 %collective-permute-start.8 = (bf16[96,1024]{1,0:T(8,128)(2,1)S(1)}, bf16[96,1024]{1,0:T(8,128)(2,1)S(1)}, u32[]{:S(2)}, u32[]{:S(2)}) collective-permute-start(bf16[96,1024]{1,0:T(8,128)(2,1)S(1)} %get-tuple-element.104), channel_id=1, source_target_pairs={{0,16},{4,20},{8,24},{12,28},{16,0},{20,4},{24,8},{28,12},{1,17},{... | collective-permute-start | bytes 589832 | tf_op jit(solution)/shard_map/ppermute | solution.py:36
  40.8 12.7 %collective-permute-start.9 = (bf16[96,1024]{1,0:T(8,128)(2,1)S(1)}, bf16[96,1024]{1,0:T(8,128)(2,1)S(1)}, u32[]{:S(2)}, u32[]{:S(2)}) collective-permute-start(bf16[96,1024]{1,0:T(8,128)(2,1)S(1)} %get-tuple-element.105), channel_id=1, source_target_pairs={{0,24},{4,28},{8,16},{12,20},{16,8},{20,12},{24,0},{28,4},{1,25},{... | collective-permute-start | bytes 589832 | tf_op jit(solution)/shard_map/ppermute | solution.py:36
  53.6 18.4 %collective-permute-start.14 = (bf16[96,1536]{1,0:T(8,128)(2,1)S(1)}, bf16[96,1536]{1,0:T(8,128)(2,1)S(1)}, u32[]{:S(2)}, u32[]{:S(2)}) collective-permute-start(bf16[96,1536]{1,0:T(8,128)(2,1)S(1)} %get-tuple-element.133.refs_4_), channel_id=1, source_target_pairs={{0,24},{4,28},{8,16},{12,20},{16,8},{20,12},{24,0},{28,4},{1,25},{... | collective-permute-start | bytes 884744 | tf_op jit(solution)/shard_map/ppermute | solution.py:36
  56.0 16.0 %collective-permute-start.13 = (bf16[96,1536]{1,0:T(8,128)(2,1)S(1)}, bf16[96,1536]{1,0:T(8,128)(2,1)S(1)}, u32[]{:S(2)}, u32[]{:S(2)}) collective-permute-start(bf16[96,1536]{1,0:T(8,128)(2,1)S(1)} %get-tuple-element.133.refs_4_), channel_id=1, source_target_pairs={{0,16},{4,20},{8,24},{12,28},{16,0},{20,4},{24,8},{28,12},{1,17},{... | collective-permute-start | bytes 884744 | tf_op jit(solution)/shard_map/ppermute | solution.py:36
  56.5 15.5 %collective-permute-start.12 = (bf16[96,1536]{1,0:T(8,128)(2,1)S(1)}, bf16[96,1536]{1,0:T(8,128)(2,1)S(1)}, u32[]{:S(2)}, u32[]{:S(2)}) collective-permute-start(bf16[96,1536]{1,0:T(8,128)(2,1)S(1)} %get-tuple-element.133.refs_4_), channel_id=1, source_target_pairs={{0,8},{4,12},{8,0},{12,4},{16,24},{20,28},{24,16},{28,20},{1,9},{5... | collective-permute-start | bytes 884744 | tf_op jit(solution)/shard_map/ppermute | solution.py:36
  59.4 2.4 %collective-permute-start.11 = (bf16[4,48,512]{2,1,0:T(8,128)(2,1)S(1)}, bf16[4,48,512]{2,1,0:T(8,128)(2,1)S(1)}, u32[]{:S(2)}, u32[]{:S(2)}) collective-permute-start(bf16[4,48,512]{2,1,0:T(8,128)(2,1)S(1)} %shard_map.117), channel_id=1, source_target_pairs={{0,4},{4,0},{8,12},{12,8},{16,20},{20,16},{24,28},{28,24},{1,5},{5... | collective-permute-start | bytes 589832 | tf_op jit(solution)/shard_map/ppermute | solution.py:36
  59.5 10.3 %collective-permute-start.15 = (bf16[48,2176]{1,0:T(8,128)(2,1)S(1)}, bf16[48,2176]{1,0:T(8,128)(2,1)S(1)}, u32[]{:S(2)}, u32[]{:S(2)}) collective-permute-start(bf16[48,2176]{1,0:T(8,128)(2,1)S(1)} %get-tuple-element.119), channel_id=1, source_target_pairs={{0,3},{1,0},{2,1},{3,2},{4,7},{5,4},{6,5},{7,6},{8,11},{9,8},{10,9... | collective-permute-start | bytes 626696 | tf_op jit(solution)/shard_map/ppermute | solution.py:31
  61.8 10.2 %collective-permute-start.16 = (bf16[48,2176]{1,0:T(8,128)(2,1)S(1)}, bf16[48,2176]{1,0:T(8,128)(2,1)S(1)}, u32[]{:S(2)}, u32[]{:S(2)}) collective-permute-start(bf16[48,2176]{1,0:T(8,128)(2,1)S(1)} %get-tuple-element.120), channel_id=1, source_target_pairs={{0,1},{1,2},{2,3},{3,0},{4,5},{5,6},{6,7},{7,4},{8,9},{9,10},{10,1... | collective-permute-start | bytes 626696 | tf_op jit(solution)/shard_map/ppermute | solution.py:31
  72.1 5.0 %collective-permute-start.21 = (bf16[576,1536]{1,0:T(8,128)(2,1)S(1)}, bf16[576,1536]{1,0:T(8,128)(2,1)S(1)}, u32[]{:S(2)}, u32[]{:S(2)}) collective-permute-start(bf16[576,1536]{1,0:T(8,128)(2,1)S(1)} %constant_dynamic-update-slice_fusion), channel_id=1, source_target_pairs={{0,4},{4,0},{8,12},{12,8},{16,20},{20,16},{24,28},{28,24},{1,5},{5... | collective-permute-start | bytes 5308424 | tf_op jit(solution)/shard_map/ppermute | solution.py:36
  72.2 15.6 %collective-permute-start.17 = (bf16[48,2560]{1,0:T(8,128)(2,1)S(1)}, bf16[48,2560]{1,0:T(8,128)(2,1)S(1)}, u32[]{:S(2)}, u32[]{:S(2)}) collective-permute-start(bf16[48,2560]{1,0:T(8,128)(2,1)S(1)} %get-tuple-element.122), channel_id=1, source_target_pairs={{0,8},{4,12},{8,0},{12,4},{16,24},{20,28},{24,16},{28,20},{1,9},{5... | collective-permute-start | bytes 737288 | tf_op jit(solution)/shard_map/ppermute | solution.py:36
  72.8 15.0 %collective-permute-start.18 = (bf16[48,2560]{1,0:T(8,128)(2,1)S(1)}, bf16[48,2560]{1,0:T(8,128)(2,1)S(1)}, u32[]{:S(2)}, u32[]{:S(2)}) collective-permute-start(bf16[48,2560]{1,0:T(8,128)(2,1)S(1)} %get-tuple-element.123), channel_id=1, source_target_pairs={{0,16},{4,20},{8,24},{12,28},{16,0},{20,4},{24,8},{28,12},{1,17},{... | collective-permute-start | bytes 737288 | tf_op jit(solution)/shard_map/ppermute | solution.py:36
  73.3 14.5 %collective-permute-start.19 = (bf16[48,2560]{1,0:T(8,128)(2,1)S(1)}, bf16[48,2560]{1,0:T(8,128)(2,1)S(1)}, u32[]{:S(2)}, u32[]{:S(2)}) collective-permute-start(bf16[48,2560]{1,0:T(8,128)(2,1)S(1)} %get-tuple-element.124), channel_id=1, source_target_pairs={{0,24},{4,28},{8,16},{12,20},{16,8},{20,12},{24,0},{28,4},{1,25},{... | collective-permute-start | bytes 737288 | tf_op jit(solution)/shard_map/ppermute | solution.py:36
  75.7 12.1 %collective-permute-start.20 = (bf16[48,2176]{1,0:T(8,128)(2,1)S(1)}, bf16[48,2176]{1,0:T(8,128)(2,1)S(1)}, u32[]{:S(2)}, u32[]{:S(2)}) collective-permute-start(bf16[48,2176]{1,0:T(8,128)(2,1)S(1)} %get-tuple-element.127), channel_id=1, source_target_pairs={{0,2},{1,3},{2,0},{3,1},{4,6},{5,7},{6,4},{7,5},{8,10},{9,11},{10,... | collective-permute-start | bytes 626696 | tf_op jit(solution)/shard_map/ppermute | solution.py:31
  87.9 2.1 %collective-permute-start.22 = (bf16[192,1536]{1,0:T(8,128)(2,1)S(1)}, bf16[192,1536]{1,0:T(8,128)(2,1)S(1)}, u32[]{:S(2)}, u32[]{:S(2)}) collective-permute-start(bf16[192,1536]{1,0:T(8,128)(2,1)S(1)} %pad_maximum_fusion), channel_id=1, source_target_pairs={{0,4},{4,0},{8,12},{12,8},{16,20},{20,16},{24,28},{28,24},{1,5},{5... | collective-permute-start | bytes 1769480 | tf_op jit(solution)/shard_map/ppermute | solution.py:36
  (5 other events, 42.7 us)

commit v12 on v10

--- a/solution.py
+++ b/solution.py
@@ -11,7 +11,7 @@
 HOT = 4
 CAP = 48
 LANES = 128
-BLOCK = 256
+BLOCK = 512
 MIB = 1 << 20
 
 highest = lax.Precision.HIGHEST

time: 82.9 us -> 82.9 us (level)
  no operation moved by 1% of the time
where the time goes in v12:
time: 82.9 us; the launch traced here: 82.7 us
  Pallas kernels  30.1 us (36%)
  waiting for transfers between devices  27.5 us (33%)
  starting transfers between devices  22.9 us (28%)
  local copies, waits for them, and re-layouts  1.3 us (2%)
  between operations  0.95 us (1%)
    ppermute x6, waiting for transfers between devices, shifted(): lax.ppermute(values, axis, [(i, (i + by) % size) for i in range(size)])  25.2 us
    pallas_call x3, Pallas kernels, chunk_rows(): pl.pallas_call(functools.partial(chunk_kernel, count), out_shape=[jax.Sha...  22.7 us
    ppermute x14, starting transfers between devices, flipped(): return lax.ppermute(values, axis, [(i, i ^ mask) for i in range(size)])  13.2 us
    ppermute x6, starting transfers between devices, shifted(): lax.ppermute(values, axis, [(i, (i + by) % size) for i in range(size)])  9.74 us
    pallas_call x1, Pallas kernels, place(): pl.pallas_call(functools.partial(place_kernel, n_expert), out_shape=[jax....  3.03 us
    pallas_call x3, Pallas kernels, weight_sums(): pl.pallas_call(functools.partial(sum_kernel, chips, share, units, scale,...  2.9 us
    ppermute x14, waiting for transfers between devices, flipped(): return lax.ppermute(values, axis, [(i, i ^ mask) for i in range(size)])  2.3 us
  transfers between devices with their start and end apart: 20, of which 6 were waited for; matrix products, arithmetic and copies ran while one was open for 0% of the time, Pallas kernels for 31%

profile of v12, /device:TPU:0, one launch (start us, length us, event | category | flops | bytes accessed | tf_op | source)
XLA Modules:
  0.0 82.7 jit_solution(1593365087766655493)
XLA Ops:
  0.6 3.0 %shard_map.110 = (bf16[192,128]{1,0:T(8,128)(2,1)}, bf16[48,4224]{1,0:T(8,128)(2,1)}, bf16[48,4224]{1,0:T(8,128)(2,1)}, bf16[48,4224]{1,0:T(8,128)(2,1)}, bf16[48,4224]{1,0:T(8,128)(2,1)}) custom-call(s32[1]{0:T(128)} %bitcast.me_ref, s32[1,128]{1,0:T(1,128)} %bitcast.20, bf16[1,128]{1,0:T(2,128)(2,1)} %bitcast.21, bf16[128,2048]{1,0:T(8,128)(2,1)} %tok_ref.1, ...), custom_call_target="tpu_custom_call" | custom-call | bytes 1024 | tf_op jit(solution)/shard_map/pallas_call | solution.py:200
  3.7 3.0 %collective-permute-start.1 = (bf16[48,4224]{1,0:T(8,128)(2,1)}, bf16[48,4224]{1,0:T(8,128)(2,1)S(1)}, u32[]{:S(2)}, u32[]{:S(2)}) collective-permute-start(bf16[48,4224]{1,0:T(8,128)(2,1)} %get-tuple-element.87), channel_id=1, source_target_pairs={{0,1},{1,2},{2,3},{3,0},{4,5},{5,6},{6,7},{7,4},{8,9},{9,10},{10,1... | collective-permute-start | bytes 1216520 | tf_op jit(solution)/shard_map/ppermute | solution.py:31
  6.7 2.0 %collective-permute-start.2 = (bf16[48,4224]{1,0:T(8,128)(2,1)}, bf16[48,4224]{1,0:T(8,128)(2,1)S(1)}, u32[]{:S(2)}, u32[]{:S(2)}) collective-permute-start(bf16[48,4224]{1,0:T(8,128)(2,1)} %get-tuple-element.88), channel_id=1, source_target_pairs={{0,3},{1,0},{2,1},{3,2},{4,7},{5,4},{6,5},{7,6},{8,11},{9,8},{10,9... | collective-permute-start | bytes 1216520 | tf_op jit(solution)/shard_map/ppermute | solution.py:31
  8.7 1.0 %copy-done = bf16[48,4224]{1,0:T(8,128)(2,1)S(1)} copy-done((bf16[48,4224]{1,0:T(8,128)(2,1)S(1)}, bf16[48,4224]{1,0:T(8,128)(2,1)}, u32[]{:S(2)}) %copy-start) | copy-done | bytes 405528
  9.7 7.5 %shard_map.111 = (bf16[48,1536]{1,0:T(8,128)(2,1)S(1)}, bf16[48,2176]{1,0:T(8,128)(2,1)S(1)}) custom-call(bf16[48,4224]{1,0:T(8,128)(2,1)S(1)} %copy-done, f32[2048,512]{1,0:T(8,128)} %bitcast.11, f32[2048,512]{1,0:T(8,128)} %bitcast.14, f32[2048,512]{1,0:T(8,128)} %bitcast.17), custom_call_target="tpu_custom_call" | custom-call | flops 7247757312 | bytes 1048576 | tf_op jit(solution)/shard_map/pallas_call | solution.py:301
  17.4 1.4 %collective-permute-done.refs_1_ = bf16[4,48,512]{2,1,0:T(8,128)(2,1)S(1)} collective-permute-done((bf16[4,48,512]{2,1,0:T(8,128)(2,1)S(1)}, bf16[4,48,512]{2,1,0:T(8,128)(2,1)S(1)}, u32[]{:S(2)}, u32[]{:S(2)}) %collective-permute-start) | collective-permute-done | bytes 196640 | tf_op jit(solution)/shard_map/ppermute | solution.py:36
  18.9 1.8 %collective-permute-start.5 = (bf16[48,2560]{1,0:T(8,128)(2,1)S(1)}, bf16[48,2560]{1,0:T(8,128)(2,1)S(1)}, u32[]{:S(2)}, u32[]{:S(2)}) collective-permute-start(bf16[48,2560]{1,0:T(8,128)(2,1)S(1)} %get-tuple-element.100), channel_id=1, source_target_pairs={{0,8},{4,12},{8,0},{12,4},{16,24},{20,28},{24,16},{28,20},{1,9},{5... | collective-permute-start | bytes 737288 | tf_op jit(solution)/shard_map/ppermute | solution.py:36
  20.7 1.5 %collective-permute-start.6 = (bf16[48,2560]{1,0:T(8,128)(2,1)S(1)}, bf16[48,2560]{1,0:T(8,128)(2,1)S(1)}, u32[]{:S(2)}, u32[]{:S(2)}) collective-permute-start(bf16[48,2560]{1,0:T(8,128)(2,1)S(1)} %get-tuple-element.101), channel_id=1, source_target_pairs={{0,16},{4,20},{8,24},{12,28},{16,0},{20,4},{24,8},{28,12},{1,17},{... | collective-permute-start | bytes 737288 | tf_op jit(solution)/shard_map/ppermute | solution.py:36
  22.2 4.3 %collective-permute-done.2.refs_1_ = bf16[48,4224]{1,0:T(8,128)(2,1)S(1)} collective-permute-done((bf16[48,4224]{1,0:T(8,128)(2,1)}, bf16[48,4224]{1,0:T(8,128)(2,1)S(1)}, u32[]{:S(2)}, u32[]{:S(2)}) %collective-permute-start.2) | collective-permute-done | bytes 405536 | tf_op jit(solution)/shard_map/ppermute | solution.py:31
  26.4 2.4 %collective-permute-start.7 = (bf16[48,2560]{1,0:T(8,128)(2,1)S(1)}, bf16[48,2560]{1,0:T(8,128)(2,1)S(1)}, u32[]{:S(2)}, u32[]{:S(2)}) collective-permute-start(bf16[48,2560]{1,0:T(8,128)(2,1)S(1)} %get-tuple-element.102), channel_id=1, source_target_pairs={{0,24},{4,28},{8,16},{12,20},{16,8},{20,12},{24,0},{28,4},{1,25},{... | collective-permute-start | bytes 737288 | tf_op jit(solution)/shard_map/ppermute | solution.py:36
  29.0 1.4 %collective-permute-start.3 = (bf16[48,4224]{1,0:T(8,128)(2,1)}, bf16[48,4224]{1,0:T(8,128)(2,1)S(1)}, u32[]{:S(2)}, u32[]{:S(2)}) collective-permute-start(bf16[48,4224]{1,0:T(8,128)(2,1)} %get-tuple-element.90), channel_id=1, source_target_pairs={{0,2},{1,3},{2,0},{3,1},{4,6},{5,7},{6,4},{7,5},{8,10},{9,11},{10,... | collective-permute-start | bytes 1216520 | tf_op jit(solution)/shard_map/ppermute | solution.py:31
  30.4 7.6 %shard_map.114 = (bf16[96,1536]{1,0:T(8,128)(2,1)S(1)}, bf16[48,2176]{1,0:T(8,128)(2,1)S(1)}, bf16[48,2176]{1,0:T(8,128)(2,1)S(1)}) custom-call(bf16[48,4224]{1,0:T(8,128)(2,1)S(1)} %collective-permute-done.1.refs_0_, bf16[48,4224]{1,0:T(8,128)(2,1)S(1)} %collective-permute-done.2.refs_1_, f32[2048,512]{1,0:T(8,128)} %bitcast.12, f32[2048,512]{1,0:T(8,128)} %bitcast.15, ...), custom_call_target="tpu_custom_call" | custom-call | flops 4831838208 | bytes 1048576 | tf_op jit(solution)/shard_map/pallas_call | solution.py:301
  39.3 2.4 %collective-permute-start.11 = (bf16[96,2560]{1,0:T(8,128)(2,1)S(1)}, bf16[96,2560]{1,0:T(8,128)(2,1)S(1)}, u32[]{:S(2)}, u32[]{:S(2)}) collective-permute-start(bf16[96,2560]{1,0:T(8,128)(2,1)S(1)} %get-tuple-element.106), channel_id=1, source_target_pairs={{0,24},{4,28},{8,16},{12,20},{16,8},{20,12},{24,0},{28,4},{1,25},{... | collective-permute-start | bytes 1474568 | tf_op jit(solution)/shard_map/ppermute | solution.py:36
  41.8 8.8 %collective-permute-done.3.refs_0_ = bf16[48,4224]{1,0:T(8,128)(2,1)S(1)} collective-permute-done((bf16[48,4224]{1,0:T(8,128)(2,1)}, bf16[48,4224]{1,0:T(8,128)(2,1)S(1)}, u32[]{:S(2)}, u32[]{:S(2)}) %collective-permute-start.3) | collective-permute-done | bytes 405536 | tf_op jit(solution)/shard_map/ppermute | solution.py:31
  50.7 2.3 %collective-permute-start.12 = (bf16[48,2176]{1,0:T(8,128)(2,1)S(1)}, bf16[48,2176]{1,0:T(8,128)(2,1)S(1)}, u32[]{:S(2)}, u32[]{:S(2)}) collective-permute-start(bf16[48,2176]{1,0:T(8,128)(2,1)S(1)} %get-tuple-element.115), channel_id=1, source_target_pairs={{0,3},{1,0},{2,1},{3,2},{4,7},{5,4},{6,5},{7,6},{8,11},{9,8},{10,9... | collective-permute-start | bytes 626696 | tf_op jit(solution)/shard_map/ppermute | solution.py:31
  53.0 7.5 %shard_map.118 = (bf16[48,1536]{1,0:T(8,128)(2,1)S(1)}, bf16[48,2176]{1,0:T(8,128)(2,1)S(1)}) custom-call(bf16[48,4224]{1,0:T(8,128)(2,1)S(1)} %collective-permute-done.3.refs_0_, f32[2048,512]{1,0:T(8,128)} %bitcast.13, f32[2048,512]{1,0:T(8,128)} %bitcast.16, f32[2048,512]{1,0:T(8,128)} %bitcast.19), custom_call_target="tpu_custom_call" | custom-call | flops 2415919104 | bytes 1048576 | tf_op jit(solution)/shard_map/pallas_call | solution.py:301
  60.6 2.6 %collective-permute-done.13.refs_3_ = bf16[48,2176]{1,0:T(8,128)(2,1)S(1)} collective-permute-done((bf16[48,2176]{1,0:T(8,128)(2,1)S(1)}, bf16[48,2176]{1,0:T(8,128)(2,1)S(1)}, u32[]{:S(2)}, u32[]{:S(2)}) %collective-permute-start.13) | collective-permute-done | bytes 208928 | tf_op jit(solution)/shard_map/ppermute | solution.py:31
  64.6 2.4 %collective-permute-start.16 = (bf16[48,2560]{1,0:T(8,128)(2,1)S(1)}, bf16[48,2560]{1,0:T(8,128)(2,1)S(1)}, u32[]{:S(2)}, u32[]{:S(2)}) collective-permute-start(bf16[48,2560]{1,0:T(8,128)(2,1)S(1)} %get-tuple-element.120), channel_id=1, source_target_pairs={{0,24},{4,28},{8,16},{12,20},{16,8},{20,12},{24,0},{28,4},{1,25},{... | collective-permute-start | bytes 737288 | tf_op jit(solution)/shard_map/ppermute | solution.py:36
  67.0 1.0 %collective-permute-start.17 = (bf16[48,2176]{1,0:T(8,128)(2,1)S(1)}, bf16[48,2176]{1,0:T(8,128)(2,1)S(1)}, u32[]{:S(2)}, u32[]{:S(2)}) collective-permute-start(bf16[48,2176]{1,0:T(8,128)(2,1)S(1)} %get-tuple-element.123), channel_id=1, source_target_pairs={{0,2},{1,3},{2,0},{3,1},{4,6},{5,7},{6,4},{7,5},{8,10},{9,11},{10,... | collective-permute-start | bytes 626696 | tf_op jit(solution)/shard_map/ppermute | solution.py:31
  68.8 0.8 shard_map.121
  69.6 9.4 %collective-permute-done.17.refs_2_ = bf16[48,2176]{1,0:T(8,128)(2,1)S(1)} collective-permute-done((bf16[48,2176]{1,0:T(8,128)(2,1)S(1)}, bf16[48,2176]{1,0:T(8,128)(2,1)S(1)}, u32[]{:S(2)}, u32[]{:S(2)}) %collective-permute-start.17) | collective-permute-done | bytes 208928 | tf_op jit(solution)/shard_map/ppermute | solution.py:31
  79.3 1.1 %shard_map.122 = (bf16[128,2048]{1,0:T(8,128)(2,1)}, bf16[1,128]{1,0:T(2,128)(2,1)}) custom-call(bf16[192,128]{1,0:T(8,128)(2,1)S(1)} %copy-done.2, bf16[48,2176]{1,0:T(8,128)(2,1)S(1)} %get-tuple-element.139.refs_0_, bf16[48,2176]{1,0:T(8,128)(2,1)S(1)} %collective-permute-done.12.refs_1_, bf16[48,2176]{1,0:T(8,128)(2,1)S(1)} %collective-permute-done.17.refs_2_, ...), custom_call_target="tpu_custom_call" | custom-call | bytes 1024 | tf_op jit(solution)/shard_map/pallas_call | solution.py:339
  80.4 0.8 %collective-permute-done.19.refs_4_ = bf16[192,1536]{1,0:T(8,128)(2,1)S(1)} collective-permute-done((bf16[192,1536]{1,0:T(8,128)(2,1)S(1)}, bf16[192,1536]{1,0:T(8,128)(2,1)S(1)}, u32[]{:S(2)}, u32[]{:S(2)}) %collective-permute-start.19) | collective-permute-done | bytes 589856 | tf_op jit(solution)/shard_map/ppermute | solution.py:36
  81.3 1.5 %shard_map.123 = (f32[256,512]{1,0:T(8,128)}, f32[256,512]{1,0:T(8,128)}, f32[256,512]{1,0:T(8,128)}) custom-call(bf16[48,2560]{1,0:T(8,128)(2,1)S(1)} %get-tuple-element.145.refs_0_, bf16[48,2560]{1,0:T(8,128)(2,1)S(1)} %collective-permute-done.14.refs_1_, bf16[48,2560]{1,0:T(8,128)(2,1)S(1)} %collective-permute-done.15.refs_2_, ...), custom_call_target="tpu_custom_call" | custom-call | bytes 1024 | tf_op jit(solution)/shard_map/pallas_call | solution.py:160
  (51 shorter events, 3.9 us)
Async XLA Ops:
  3.7 18.5 %collective-permute-start.1 = (bf16[48,4224]{1,0:T(8,128)(2,1)}, bf16[48,4224]{1,0:T(8,128)(2,1)S(1)}, u32[]{:S(2)}, u32[]{:S(2)}) collective-permute-start(bf16[48,4224]{1,0:T(8,128)(2,1)} %get-tuple-element.87), channel_id=1, source_target_pairs={{0,1},{1,2},{2,3},{3,0},{4,5},{5,6},{6,7},{7,4},{8,9},{9,10},{10,1... | collective-permute-start | bytes 1216520 | tf_op jit(solution)/shard_map/ppermute | solution.py:31
  6.7 19.7 %collective-permute-start.2 = (bf16[48,4224]{1,0:T(8,128)(2,1)}, bf16[48,4224]{1,0:T(8,128)(2,1)S(1)}, u32[]{:S(2)}, u32[]{:S(2)}) collective-permute-start(bf16[48,4224]{1,0:T(8,128)(2,1)} %get-tuple-element.88), channel_id=1, source_target_pairs={{0,3},{1,0},{2,1},{3,2},{4,7},{5,4},{6,5},{7,6},{8,11},{9,8},{10,9... | collective-permute-start | bytes 1216520 | tf_op jit(solution)/shard_map/ppermute | solution.py:31
  8.7 1.0 %copy-start = (bf16[48,4224]{1,0:T(8,128)(2,1)S(1)}, bf16[48,4224]{1,0:T(8,128)(2,1)}, u32[]{:S(2)}) copy-start(bf16[48,4224]{1,0:T(8,128)(2,1)} %get-tuple-element.84.refs_0_) | copy-start | bytes 1216516
  9.7 7.6 %copy-start.1 = (bf16[48,4224]{1,0:T(8,128)(2,1)S(1)}, bf16[48,4224]{1,0:T(8,128)(2,1)}, u32[]{:S(2)}) copy-start(bf16[48,4224]{1,0:T(8,128)(2,1)} %get-tuple-element.84.refs_0_) | copy-start | bytes 1216516
  17.3 1.5 %collective-permute-start = (bf16[4,48,512]{2,1,0:T(8,128)(2,1)S(1)}, bf16[4,48,512]{2,1,0:T(8,128)(2,1)S(1)}, u32[]{:S(2)}, u32[]{:S(2)}) collective-permute-start(bf16[4,48,512]{2,1,0:T(8,128)(2,1)S(1)} %shard_map.112), channel_id=1, source_target_pairs={{0,4},{4,0},{8,12},{12,8},{16,20},{20,16},{24,28},{28,24},{1,5},{5... | collective-permute-start | bytes 589832 | tf_op jit(solution)/shard_map/ppermute | solution.py:36
  18.9 19.2 %collective-permute-start.5 = (bf16[48,2560]{1,0:T(8,128)(2,1)S(1)}, bf16[48,2560]{1,0:T(8,128)(2,1)S(1)}, u32[]{:S(2)}, u32[]{:S(2)}) collective-permute-start(bf16[48,2560]{1,0:T(8,128)(2,1)S(1)} %get-tuple-element.100), channel_id=1, source_target_pairs={{0,8},{4,12},{8,0},{12,4},{16,24},{20,28},{24,16},{28,20},{1,9},{5... | collective-permute-start | bytes 737288 | tf_op jit(solution)/shard_map/ppermute | solution.py:36
  20.7 17.5 %collective-permute-start.6 = (bf16[48,2560]{1,0:T(8,128)(2,1)S(1)}, bf16[48,2560]{1,0:T(8,128)(2,1)S(1)}, u32[]{:S(2)}, u32[]{:S(2)}) collective-permute-start(bf16[48,2560]{1,0:T(8,128)(2,1)S(1)} %get-tuple-element.101), channel_id=1, source_target_pairs={{0,16},{4,20},{8,24},{12,28},{16,0},{20,4},{24,8},{28,12},{1,17},{... | collective-permute-start | bytes 737288 | tf_op jit(solution)/shard_map/ppermute | solution.py:36
  26.4 11.7 %collective-permute-start.7 = (bf16[48,2560]{1,0:T(8,128)(2,1)S(1)}, bf16[48,2560]{1,0:T(8,128)(2,1)S(1)}, u32[]{:S(2)}, u32[]{:S(2)}) collective-permute-start(bf16[48,2560]{1,0:T(8,128)(2,1)S(1)} %get-tuple-element.102), channel_id=1, source_target_pairs={{0,24},{4,28},{8,16},{12,20},{16,8},{20,12},{24,0},{28,4},{1,25},{... | collective-permute-start | bytes 737288 | tf_op jit(solution)/shard_map/ppermute | solution.py:36
  28.9 9.1 %collective-permute-start.4 = (bf16[4,96,512]{2,1,0:T(8,128)(2,1)S(1)}, bf16[4,96,512]{2,1,0:T(8,128)(2,1)S(1)}, u32[]{:S(2)}, u32[]{:S(2)}) collective-permute-start(bf16[4,96,512]{2,1,0:T(8,128)(2,1)S(1)} %shard_map.115), channel_id=1, source_target_pairs={{0,4},{4,0},{8,12},{12,8},{16,20},{20,16},{24,28},{28,24},{1,5},{5... | collective-permute-start | bytes 1179656 | tf_op jit(solution)/shard_map/ppermute | solution.py:36
  29.0 21.6 %collective-permute-start.3 = (bf16[48,4224]{1,0:T(8,128)(2,1)}, bf16[48,4224]{1,0:T(8,128)(2,1)S(1)}, u32[]{:S(2)}, u32[]{:S(2)}) collective-permute-start(bf16[48,4224]{1,0:T(8,128)(2,1)} %get-tuple-element.90), channel_id=1, source_target_pairs={{0,2},{1,3},{2,0},{3,1},{4,6},{5,7},{6,4},{7,5},{8,10},{9,11},{10,... | collective-permute-start | bytes 1216520 | tf_op jit(solution)/shard_map/ppermute | solution.py:31
  38.2 25.1 %collective-permute-start.9 = (bf16[96,2560]{1,0:T(8,128)(2,1)S(1)}, bf16[96,2560]{1,0:T(8,128)(2,1)S(1)}, u32[]{:S(2)}, u32[]{:S(2)}) collective-permute-start(bf16[96,2560]{1,0:T(8,128)(2,1)S(1)} %get-tuple-element.104), channel_id=1, source_target_pairs={{0,8},{4,12},{8,0},{12,4},{16,24},{20,28},{24,16},{28,20},{1,9},{5... | collective-permute-start | bytes 1474568 | tf_op jit(solution)/shard_map/ppermute | solution.py:36
  38.8 24.5 %collective-permute-start.10 = (bf16[96,2560]{1,0:T(8,128)(2,1)S(1)}, bf16[96,2560]{1,0:T(8,128)(2,1)S(1)}, u32[]{:S(2)}, u32[]{:S(2)}) collective-permute-start(bf16[96,2560]{1,0:T(8,128)(2,1)S(1)} %get-tuple-element.105), channel_id=1, source_target_pairs={{0,16},{4,20},{8,24},{12,28},{16,0},{20,4},{24,8},{28,12},{1,17},{... | collective-permute-start | bytes 1474568 | tf_op jit(solution)/shard_map/ppermute | solution.py:36
  39.3 24.0 %collective-permute-start.11 = (bf16[96,2560]{1,0:T(8,128)(2,1)S(1)}, bf16[96,2560]{1,0:T(8,128)(2,1)S(1)}, u32[]{:S(2)}, u32[]{:S(2)}) collective-permute-start(bf16[96,2560]{1,0:T(8,128)(2,1)S(1)} %get-tuple-element.106), channel_id=1, source_target_pairs={{0,24},{4,28},{8,16},{12,20},{16,8},{20,12},{24,0},{28,4},{1,25},{... | collective-permute-start | bytes 1474568 | tf_op jit(solution)/shard_map/ppermute | solution.py:36
  50.6 2.4 %collective-permute-start.8 = (bf16[4,48,512]{2,1,0:T(8,128)(2,1)S(1)}, bf16[4,48,512]{2,1,0:T(8,128)(2,1)S(1)}, u32[]{:S(2)}, u32[]{:S(2)}) collective-permute-start(bf16[4,48,512]{2,1,0:T(8,128)(2,1)S(1)} %shard_map.117), channel_id=1, source_target_pairs={{0,4},{4,0},{8,12},{12,8},{16,20},{20,16},{24,28},{28,24},{1,5},{5... | collective-permute-start | bytes 589832 | tf_op jit(solution)/shard_map/ppermute | solution.py:36
  50.7 9.9 %collective-permute-start.12 = (bf16[48,2176]{1,0:T(8,128)(2,1)S(1)}, bf16[48,2176]{1,0:T(8,128)(2,1)S(1)}, u32[]{:S(2)}, u32[]{:S(2)}) collective-permute-start(bf16[48,2176]{1,0:T(8,128)(2,1)S(1)} %get-tuple-element.115), channel_id=1, source_target_pairs={{0,3},{1,0},{2,1},{3,2},{4,7},{5,4},{6,5},{7,6},{8,11},{9,8},{10,9... | collective-permute-start | bytes 626696 | tf_op jit(solution)/shard_map/ppermute | solution.py:31
  53.0 10.2 %collective-permute-start.13 = (bf16[48,2176]{1,0:T(8,128)(2,1)S(1)}, bf16[48,2176]{1,0:T(8,128)(2,1)S(1)}, u32[]{:S(2)}, u32[]{:S(2)}) collective-permute-start(bf16[48,2176]{1,0:T(8,128)(2,1)S(1)} %get-tuple-element.116), channel_id=1, source_target_pairs={{0,1},{1,2},{2,3},{3,0},{4,5},{5,6},{6,7},{7,4},{8,9},{9,10},{10,1... | collective-permute-start | bytes 626696 | tf_op jit(solution)/shard_map/ppermute | solution.py:31
  63.4 4.7 %collective-permute-start.18 = (bf16[576,1536]{1,0:T(8,128)(2,1)S(1)}, bf16[576,1536]{1,0:T(8,128)(2,1)S(1)}, u32[]{:S(2)}, u32[]{:S(2)}) collective-permute-start(bf16[576,1536]{1,0:T(8,128)(2,1)S(1)} %slice_dynamic-update-slice_fusion), channel_id=1, source_target_pairs={{0,4},{4,0},{8,12},{12,8},{16,20},{20,16},{24,28},{28,24},{1,5},{5... | collective-permute-start | bytes 5308424 | tf_op jit(solution)/shard_map/ppermute | solution.py:36
  63.5 15.6 %collective-permute-start.14 = (bf16[48,2560]{1,0:T(8,128)(2,1)S(1)}, bf16[48,2560]{1,0:T(8,128)(2,1)S(1)}, u32[]{:S(2)}, u32[]{:S(2)}) collective-permute-start(bf16[48,2560]{1,0:T(8,128)(2,1)S(1)} %get-tuple-element.118), channel_id=1, source_target_pairs={{0,8},{4,12},{8,0},{12,4},{16,24},{20,28},{24,16},{28,20},{1,9},{5... | collective-permute-start | bytes 737288 | tf_op jit(solution)/shard_map/ppermute | solution.py:36
  64.1 15.0 %collective-permute-start.15 = (bf16[48,2560]{1,0:T(8,128)(2,1)S(1)}, bf16[48,2560]{1,0:T(8,128)(2,1)S(1)}, u32[]{:S(2)}, u32[]{:S(2)}) collective-permute-start(bf16[48,2560]{1,0:T(8,128)(2,1)S(1)} %get-tuple-element.119), channel_id=1, source_target_pairs={{0,16},{4,20},{8,24},{12,28},{16,0},{20,4},{24,8},{28,12},{1,17},{... | collective-permute-start | bytes 737288 | tf_op jit(solution)/shard_map/ppermute | solution.py:36
  64.6 14.5 %collective-permute-start.16 = (bf16[48,2560]{1,0:T(8,128)(2,1)S(1)}, bf16[48,2560]{1,0:T(8,128)(2,1)S(1)}, u32[]{:S(2)}, u32[]{:S(2)}) collective-permute-start(bf16[48,2560]{1,0:T(8,128)(2,1)S(1)} %get-tuple-element.120), channel_id=1, source_target_pairs={{0,24},{4,28},{8,16},{12,20},{16,8},{20,12},{24,0},{28,4},{1,25},{... | collective-permute-start | bytes 737288 | tf_op jit(solution)/shard_map/ppermute | solution.py:36
  67.0 12.1 %collective-permute-start.17 = (bf16[48,2176]{1,0:T(8,128)(2,1)S(1)}, bf16[48,2176]{1,0:T(8,128)(2,1)S(1)}, u32[]{:S(2)}, u32[]{:S(2)}) collective-permute-start(bf16[48,2176]{1,0:T(8,128)(2,1)S(1)} %get-tuple-element.123), channel_id=1, source_target_pairs={{0,2},{1,3},{2,0},{3,1},{4,6},{5,7},{6,4},{7,5},{8,10},{9,11},{10,... | collective-permute-start | bytes 626696 | tf_op jit(solution)/shard_map/ppermute | solution.py:31
  69.6 9.7 %copy-start.2 = (bf16[192,128]{1,0:T(8,128)(2,1)S(1)}, bf16[192,128]{1,0:T(8,128)(2,1)}, u32[]{:S(2)}) copy-start(bf16[192,128]{1,0:T(8,128)(2,1)} %get-tuple-element.80.placing_ref) | copy-start | bytes 147460
  79.2 2.1 %collective-permute-start.19 = (bf16[192,1536]{1,0:T(8,128)(2,1)S(1)}, bf16[192,1536]{1,0:T(8,128)(2,1)S(1)}, u32[]{:S(2)}, u32[]{:S(2)}) collective-permute-start(bf16[192,1536]{1,0:T(8,128)(2,1)S(1)} %pad_maximum_fusion), channel_id=1, source_target_pairs={{0,4},{4,0},{8,12},{12,8},{16,20},{20,16},{24,28},{28,24},{1,5},{5... | collective-permute-start | bytes 1769480 | tf_op jit(solution)/shard_map/ppermute | solution.py:36
